TPU v7x, 32 devices: a whole 2x2x4 slice. The times are simulated.
32 devices in a mesh: seq: 8 (over z, x), fsdp: 4 (over y, core).
Axes of the slice: x: 2, y: 2, z: 4, core: 2. Of those that a mesh axis runs over, the one named last changes fastest.
Arguments:
- inputs: bfloat16 [4, 2048, 2048], P('fsdp', 'seq'), may hold values from -6 to 6
- out_grad: bfloat16 [4, 2048, 2048], P('fsdp', 'seq'), may hold values from -6 to 6
- norm_gain: float32 [2048], replicated, may hold values from 0.5 to 1.5
- w_in: bfloat16 [2048, 6704], P(('seq', 'fsdp')), may hold values from -0.125 to 0.125
- conv_weight: float32 [4, 3584], replicated, may hold values from -3 to 3
- conv_bias: float32 [3584], replicated, may hold values from -0.5 to 0.5
- dt_bias: float32 [48], replicated, may hold values from -4 to 0
- a_log: float32 [48], replicated, may hold values from -7 to 1
- skip_gain: float32 [48], replicated, may hold values from 0.2 to 1
- gated_gain: float32 [3072], replicated, may hold values from 0.5 to 1.5
- w_out: bfloat16 [3072, 2048], P(('seq', 'fsdp')), may hold values from -0.109375 to 0.109375
- w_q: bfloat16 [2048, 1024], P(('seq', 'fsdp')), may hold values from -0.125 to 0.125
- w_k: bfloat16 [2048, 256], P(('seq', 'fsdp')), may hold values from -0.125 to 0.125
- w_v: bfloat16 [2048, 256], P(('seq', 'fsdp')), may hold values from -0.125 to 0.125
- w_o: bfloat16 [1024, 2048], P(('seq', 'fsdp')), may hold values from -1.5 to 1.5
- mid_gain: float32 [2048], replicated, may hold values from 0.5 to 1.5
- w_gate: bfloat16 [2048, 4096], P(('seq', 'fsdp')), may hold values from -0.125 to 0.125
- w_up: bfloat16 [2048, 4096], P(('seq', 'fsdp')), may hold values from -0.125 to 0.125
- w_down: bfloat16 [4096, 2048], P(('seq', 'fsdp')), may hold values from -0.09375 to 0.09375
Outputs:
- output: bfloat16 [4, 2048, 2048], P('fsdp', 'seq')
- input_grad: float32 [4, 2048, 2048], P('fsdp', 'seq')
- grad_norm_gain: float32 [2048], replicated
- grad_w_in: float32 [2048, 6704], P(('seq', 'fsdp'))
- grad_conv_weight: float32 [4, 3584], replicated
- grad_conv_bias: float32 [3584], replicated
- grad_dt_bias: float32 [48], replicated
- grad_a_log: float32 [48], replicated
- grad_skip_gain: float32 [48], replicated
- grad_gated_gain: float32 [3072], replicated
- grad_w_out: float32 [3072, 2048], P(('seq', 'fsdp'))
- grad_w_q: float32 [2048, 1024], P(('seq', 'fsdp'))
- grad_w_k: float32 [2048, 256], P(('seq', 'fsdp'))
- grad_w_v: float32 [2048, 256], P(('seq', 'fsdp'))
- grad_w_o: float32 [1024, 2048], P(('seq', 'fsdp'))
- grad_mid_gain: float32 [2048], replicated
- grad_w_gate: float32 [2048, 4096], P(('seq', 'fsdp'))
- grad_w_up: float32 [2048, 4096], P(('seq', 'fsdp'))
- grad_w_down: float32 [4096, 2048], P(('seq', 'fsdp'))
All inputs are finite; a program needn't handle non-finite values.
Results may differ from a plain program's by a relative error of at most 0.017.
Values may be sent and summed in bfloat16 or wider, within the bound.
No kernel may reach another device: no remote copies, remote signals or barrier semaphores. Data moves between devices by JAX's collectives and lax.ppermute only.
A program may use at most 704 MiB of HBM per device.

v0:
```python
import jax
import jax.numpy as jnp
from jax import lax
from jax.sharding import PartitionSpec as P

MAMBA_HEADS = 48
MAMBA_HEAD = 64
STATE = 256
ATT_HEADS = 8
KV_HEADS = 2
HEAD_DIM = 128
SPAN = 128
INNER = 3072


epsilon = 1e-05
rope_base = 100000000000.0
highest = lax.Precision.HIGHEST
block_limit = 512


def shifted(block, axis, distance):
    devices = range(lax.axis_size(axis))
    route = [(i - distance, i) for i in devices if i - distance in devices]
    return lax.ppermute(block, axis, route)


def prefix(array, axis, combine, identity):
    count, index = (lax.axis_size(axis), lax.axis_index(axis))
    everything = jax.tree.map(
        lambda part, kind: lax.all_gather(part.astype(kind), axis),
        array,
        (jnp.bfloat16, jnp.bfloat16),
    )
    start = jax.tree.map(
        lambda part, zero: jnp.broadcast_to(jnp.asarray(zero, part.dtype), part.shape),
        array,
        identity,
    )

    def prefix_step(k, before):
        reached = k < index
        new = combine(
            before, jax.tree.map(lambda part, own: part[k].astype(own.dtype), everything, array)
        )
        return jax.tree.map(lambda a, b: jnp.where(reached, a, b), new, before)

    return lax.fori_loop(0, count, prefix_step, start)


def entering(array, axis, combine, identity):
    count, index = (lax.axis_size(axis), lax.axis_index(axis))
    everything = jax.tree.map(
        lambda part, kind: lax.all_gather(part.astype(kind), axis),
        array,
        jax.tree.map(lambda a: jnp.bfloat16 if a.dtype == jnp.float32 else a.dtype, array),
    )
    start = jax.tree.map(
        lambda part, zero: jnp.broadcast_to(jnp.asarray(zero, part.dtype), part.shape),
        array,
        identity,
    )

    def entering_step(k, before):
        at = count - 1 - k
        reached = at > index
        new = combine(
            before, jax.tree.map(lambda part, own: part[at].astype(own.dtype), everything, array)
        )
        return jax.tree.map(lambda a, b: jnp.where(reached, a, b), new, before)

    return lax.fori_loop(0, count, entering_step, start)


def as_sent(array):
    return jax.tree.map(lambda a: a.astype(jnp.bfloat16) if a.dtype == jnp.float32 else a, array)


def mat_high(left, right):
    return jnp.dot(left, right, precision=highest, preferred_element_type=jnp.float32)


def low_dot(left, right):
    return jnp.dot(left, right, preferred_element_type=jnp.float32)


def back_dot(grad_rows, weight):
    return lax.dot_general(
        grad_rows, weight, (((1,), (1,)), ((), ())), preferred_element_type=jnp.float32
    )


def weight_grad(left, right):
    return lax.dot_general(
        left, right, (((0,), (0,)), ((), ())), preferred_element_type=jnp.float32
    )


def rms_scale(values, gain):
    return values * lax.rsqrt(jnp.mean(values * values, axis=-1, keepdims=True) + epsilon) * gain


def rotate(values, positions):
    half_dim = values.shape[-1] // 2
    frequencies = rope_base ** (-jnp.arange(half_dim, dtype=jnp.float32) / half_dim)
    angles = positions.astype(jnp.float32)[:, None] * frequencies[None, :]
    cosine = jnp.cos(angles)[:, None, :]
    sine_table = jnp.sin(angles)[:, None, :]
    first_half = values[..., :half_dim]
    second = values[..., half_dim:]
    return jnp.concatenate(
        [first_half * cosine - second * sine_table, second * cosine + first_half * sine_table],
        axis=-1,
    )


def convolve(padded, conv_weight, conv_bias):
    length = padded.shape[0] - conv_weight.shape[0] + 1
    accumulated = conv_bias[None, :] + jnp.zeros((length, padded.shape[1]), jnp.float32)
    for offset in range(conv_weight.shape[0]):
        accumulated = accumulated + padded[offset : offset + length] * conv_weight[offset]
    return jax.nn.silu(accumulated)


def conv_piece(conv_in, edge_rows, conv_weight, conv_bias):
    return convolve(jnp.concatenate([edge_rows, conv_in], 0), conv_weight, conv_bias)


def unpack(mixed, dt_raw, dt_bias, a_log):
    length = mixed.shape[0]
    inputs_ssm = mixed[:, :INNER].reshape(length, MAMBA_HEADS, MAMBA_HEAD)
    b_matrix = mixed[:, INNER : INNER + STATE]
    c_matrix = mixed[:, INNER + STATE :]
    step_size = jax.nn.softplus(dt_raw + dt_bias)
    rates = -jnp.exp(a_log)
    return (inputs_ssm, b_matrix, c_matrix, step_size, rates)


def run_spans(inputs_ssm, b_matrix, c_matrix, step_size, rates):
    length = inputs_ssm.shape[0]
    pieces_count = length // SPAN
    places = jnp.arange(SPAN, dtype=jnp.int32)
    causal = places[:, None] >= places[None, :]

    def span_step(state, pieces):
        part_x, part_b, part_c, part_dt = pieces
        cumulative = jnp.cumsum(part_dt * rates, axis=0)
        spread = cumulative.T[:, :, None] - cumulative.T[:, None, :]
        decay = jnp.exp(jnp.where(causal[None], spread, -jnp.inf))
        intersection = mat_high(part_c, part_b.T)
        weights = intersection[None] * decay * part_dt.T[:, None, :]
        inside = jnp.einsum("hts,shp->thp", weights, part_x, precision=highest)
        carried = jnp.exp(cumulative)[:, :, None] * jnp.einsum(
            "tn,hpn->thp", part_c, state, precision=highest
        )
        tail = jnp.exp(cumulative[-1][None, :] - cumulative) * part_dt
        local_state = jnp.einsum(
            "shp,sn->hpn", tail[:, :, None] * part_x, part_b, precision=highest
        )
        updated = jnp.exp(cumulative[-1])[:, None, None] * state + local_state
        return (updated, inside + carried)

    start_state = jnp.zeros((MAMBA_HEADS, MAMBA_HEAD, STATE), jnp.float32)
    pieces = (
        inputs_ssm.reshape(pieces_count, SPAN, MAMBA_HEADS, MAMBA_HEAD),
        b_matrix.reshape(pieces_count, SPAN, STATE),
        c_matrix.reshape(pieces_count, SPAN, STATE),
        step_size.reshape(pieces_count, SPAN, MAMBA_HEADS),
    )
    final_state, outputs = lax.scan(jax.checkpoint(span_step), start_state, pieces)
    return (outputs.reshape(length, MAMBA_HEADS, MAMBA_HEAD), final_state)


def local_scan(mixed, dt_raw, dt_bias, a_log):
    inputs_ssm, b_matrix, c_matrix, step_size, rates = unpack(mixed, dt_raw, dt_bias, a_log)
    outputs, final_state = run_spans(inputs_ssm, b_matrix, c_matrix, step_size, rates)
    return (outputs, final_state, jnp.exp(jnp.sum(step_size * rates, axis=0)))


def gate_output(values, gate_z, gated_gain):
    flat = values.reshape(values.shape[0], INNER) * jax.nn.silu(gate_z)
    return rms_scale(flat, gated_gain)


def mamba_finish(mixed, dt_raw, dt_bias, a_log, skip_gain, gate_z, gated_gain, outputs, state_in):
    inputs_ssm, b_matrix, c_matrix, step_size, rates = unpack(mixed, dt_raw, dt_bias, a_log)
    cumulative = jnp.cumsum(step_size * rates, axis=0)
    carried = jnp.exp(cumulative)[:, :, None] * jnp.einsum(
        "tn,hpn->thp", c_matrix, state_in, precision=highest
    )
    values_ssm = outputs + carried + skip_gain[:, None] * inputs_ssm
    return gate_output(values_ssm, gate_z, gated_gain)


def swish_product(gate_proj, up_proj):
    return jax.nn.silu(gate_proj) * up_proj


def chain_combine(earlier, later):
    return (earlier[0] * later[0], later[0][:, None, None] * earlier[1] + later[1])


def block_scores(queries, key_rows, value_rows, block_index, block_size, query_first):
    key_block = lax.dynamic_slice_in_dim(key_rows, block_index * block_size, block_size, 0)
    value_block = lax.dynamic_slice_in_dim(value_rows, block_index * block_size, block_size, 0)
    raw_scores = jnp.einsum(
        "lkgd,jkd->lkgj", queries, key_block, preferred_element_type=jnp.float32
    ) * queries.shape[-1] ** (-0.5)
    query_place = query_first + jnp.arange(queries.shape[0], dtype=jnp.int32)
    key_place = block_index * block_size + jnp.arange(block_size, dtype=jnp.int32)
    allowed = query_place[:, None, None, None] >= key_place
    return (jnp.where(allowed, raw_scores, -jnp.inf), key_block, value_block)


def attend_forward(queries, key_rows, value_rows, query_first):
    block_size = min(block_limit, key_rows.shape[0])
    block_count = (query_first + queries.shape[0] + block_size - 1) // block_size
    stat_shape = queries.shape[:3]

    def max_step(block_index, carry):
        running_max, running_sum = carry
        scores, key_block, value_block = block_scores(
            queries, key_rows, value_rows, block_index, block_size, query_first
        )
        new_max = jnp.maximum(running_max, jnp.max(scores, axis=-1))
        running_sum = running_sum * jnp.exp(running_max - new_max) + jnp.sum(
            jnp.exp(scores - new_max[..., None]), axis=-1
        )
        return (new_max, running_sum)

    running_max, running_sum = lax.fori_loop(
        0,
        block_count,
        max_step,
        (jnp.full(stat_shape, -jnp.inf, jnp.float32), jnp.zeros(stat_shape, jnp.float32)),
    )
    log_total = running_max + jnp.log(running_sum)

    def value_step(block_index, accumulated):
        scores, key_block, value_block = block_scores(
            queries, key_rows, value_rows, block_index, block_size, query_first
        )
        probs = jnp.exp(scores - log_total[..., None]).astype(jnp.bfloat16)
        return accumulated + jnp.einsum(
            "lkgj,jkd->lkgd", probs, value_block, preferred_element_type=jnp.float32
        )

    attended = lax.fori_loop(0, block_count, value_step, jnp.zeros(queries.shape, jnp.float32))
    return (attended, log_total)


def attend_backward(queries, key_rows, value_rows, log_total, attended, attended_grad, query_first):
    block_size = min(block_limit, key_rows.shape[0])
    block_count = (query_first + queries.shape[0] + block_size - 1) // block_size
    score_scale = queries.shape[-1] ** (-0.5)
    delta = jnp.sum(attended_grad.astype(jnp.float32) * attended, axis=-1)

    def grad_step(block_index, carry):
        query_grad, key_grads, value_grads = carry
        scores, key_block, value_block = block_scores(
            queries, key_rows, value_rows, block_index, block_size, query_first
        )
        probs = jnp.exp(scores - log_total[..., None])
        prob_grad = jnp.einsum(
            "lkgd,jkd->lkgj", attended_grad, value_block, preferred_element_type=jnp.float32
        )
        score_grad = (probs * (prob_grad - delta[..., None])).astype(jnp.bfloat16)
        query_grad = query_grad + jnp.einsum(
            "lkgj,jkd->lkgd", score_grad, key_block, preferred_element_type=jnp.float32
        )
        key_piece = jnp.einsum(
            "lkgj,lkgd->jkd", score_grad, queries, preferred_element_type=jnp.float32
        )
        value_piece = jnp.einsum(
            "lkgj,lkgd->jkd",
            probs.astype(jnp.bfloat16),
            attended_grad,
            preferred_element_type=jnp.float32,
        )
        key_grads = lax.dynamic_update_slice_in_dim(
            key_grads, key_piece, block_index * block_size, 0
        )
        value_grads = lax.dynamic_update_slice_in_dim(
            value_grads, value_piece, block_index * block_size, 0
        )
        return (query_grad, key_grads, value_grads)

    empty_keys = jnp.zeros(key_rows.shape, jnp.float32)
    query_grad, key_grads, value_grads = lax.fori_loop(
        0, block_count, grad_step, (jnp.zeros(queries.shape, jnp.float32), empty_keys, empty_keys)
    )
    return (query_grad * score_scale, key_grads * score_scale, value_grads)


def body(
    inputs,
    out_grad,
    norm_gain,
    w_in,
    conv_weight,
    conv_bias,
    dt_bias,
    a_log,
    skip_gain,
    gated_gain,
    w_out,
    w_q,
    w_k,
    w_v,
    w_o,
    mid_gain,
    w_gate,
    w_up,
    w_down,
):
    length = inputs.shape[1]
    group_size = ATT_HEADS // KV_HEADS
    query_first = lax.axis_index("seq") * length
    positions = query_first + jnp.arange(length, dtype=jnp.int32)
    edge_count = conv_weight.shape[0] - 1
    full_in, full_out, full_q, full_k, full_v, full_o = (
        lax.all_gather(w_in, ("seq", "fsdp"), axis=0, tiled=True),
        lax.all_gather(w_out, ("seq", "fsdp"), axis=0, tiled=True),
        lax.all_gather(w_q, ("seq", "fsdp"), axis=0, tiled=True),
        lax.all_gather(w_k, ("seq", "fsdp"), axis=0, tiled=True),
        lax.all_gather(w_v, ("seq", "fsdp"), axis=0, tiled=True),
        lax.all_gather(w_o, ("seq", "fsdp"), axis=0, tiled=True),
    )
    resident = inputs[0].astype(jnp.float32)
    normed, norm_back = jax.vjp(rms_scale, resident, norm_gain)
    normed16 = normed.astype(jnp.bfloat16)
    projected = low_dot(normed16, full_in)
    gate_z = projected[:, :INNER]
    conv_in = projected[:, INNER : 2 * INNER + 2 * STATE]
    dt_raw = projected[:, 2 * INNER + 2 * STATE :]
    edge_rows = shifted(conv_in[length - edge_count :].astype(jnp.bfloat16), "seq", 1).astype(
        jnp.float32
    )
    mixed, conv_back_fn = jax.vjp(conv_piece, conv_in, edge_rows, conv_weight, conv_bias)
    local_out, local_back = jax.vjp(local_scan, mixed, dt_raw, dt_bias, a_log)
    identity = (
        jnp.ones((MAMBA_HEADS,), jnp.float32),
        jnp.zeros((MAMBA_HEADS, MAMBA_HEAD, STATE), jnp.float32),
    )
    decay_prefix, state_in = prefix((local_out[2], local_out[1]), "seq", chain_combine, identity)
    gated, gated_back = jax.vjp(
        mamba_finish,
        mixed,
        dt_raw,
        dt_bias,
        a_log,
        skip_gain,
        gate_z,
        gated_gain,
        local_out[0],
        state_in,
    )
    gated16 = gated.astype(jnp.bfloat16)
    query_pre = low_dot(normed16, full_q).reshape(length, ATT_HEADS, HEAD_DIM)
    key_pre = low_dot(normed16, full_k).reshape(length, KV_HEADS, HEAD_DIM)
    value16 = low_dot(normed16, full_v).astype(jnp.bfloat16)
    query16 = (
        rotate(query_pre, positions)
        .astype(jnp.bfloat16)
        .reshape(length, KV_HEADS, group_size, HEAD_DIM)
    )
    key16 = rotate(key_pre, positions).astype(jnp.bfloat16).reshape(length, KV_HEADS * HEAD_DIM)
    key_all, value_all = (
        lax.all_gather(key16, "seq", axis=0, tiled=True),
        lax.all_gather(value16, "seq", axis=0, tiled=True),
    )
    attended, log_total = attend_forward(
        query16,
        key_all.reshape(-1, KV_HEADS, HEAD_DIM),
        value_all.reshape(-1, KV_HEADS, HEAD_DIM),
        query_first,
    )
    attended16 = attended.reshape(length, ATT_HEADS * HEAD_DIM).astype(jnp.bfloat16)
    hidden_state = resident + (low_dot(attended16, full_o) + low_dot(gated16, full_out))
    full_gate, full_up, full_down = (
        lax.all_gather(w_gate, ("seq", "fsdp"), axis=0, tiled=True),
        lax.all_gather(w_up, ("seq", "fsdp"), axis=0, tiled=True),
        lax.all_gather(w_down, ("seq", "fsdp"), axis=0, tiled=True),
    )
    middle, mid_back = jax.vjp(rms_scale, hidden_state, mid_gain)
    middle16 = middle.astype(jnp.bfloat16)
    gate_proj = low_dot(middle16, full_gate)
    up_proj = low_dot(middle16, full_up)
    activated, swish_back = jax.vjp(swish_product, gate_proj, up_proj)
    activated16 = activated.astype(jnp.bfloat16)
    output = (hidden_state + low_dot(activated16, full_down)).astype(jnp.bfloat16)
    cotangent16 = out_grad[0]
    cotangent = cotangent16.astype(jnp.float32)
    act_grad = back_dot(cotangent16, full_down)
    gate_grad, up_grad = swish_back(act_grad)
    gate16 = gate_grad.astype(jnp.bfloat16)
    up16 = up_grad.astype(jnp.bfloat16)
    mid_grad = back_dot(gate16, full_gate) + back_dot(up16, full_up)
    hidden_part, mid_gain_grad = mid_back(mid_grad)
    hidden_grad = cotangent + hidden_part
    grad_down = weight_grad(activated16, cotangent16)
    grad_gate = weight_grad(middle16, gate16)
    grad_up = weight_grad(middle16, up16)
    mlp_grads = (
        lax.psum_scatter(grad_gate, ("seq", "fsdp"), scatter_dimension=0, tiled=True),
        lax.psum_scatter(grad_up, ("seq", "fsdp"), scatter_dimension=0, tiled=True),
        lax.psum_scatter(grad_down, ("seq", "fsdp"), scatter_dimension=0, tiled=True),
    )
    mix16 = hidden_grad.astype(jnp.bfloat16)
    attended_grad16 = (
        back_dot(mix16, full_o).astype(jnp.bfloat16).reshape(length, KV_HEADS, group_size, HEAD_DIM)
    )
    gated_grad = back_dot(mix16, full_out)
    (
        mixed_first,
        dt_raw_first,
        dt_bias_first,
        a_log_first,
        skip_grad,
        gate_z_grad,
        gated_gain_grad,
        outputs_grad,
        state_local_grad,
    ) = gated_back(gated_grad)
    tail_decay, state_out_grad = entering(
        (local_out[2], state_local_grad), "seq", chain_combine, identity
    )
    decay_grad = jnp.sum(state_out_grad * state_in, axis=(1, 2))
    mixed_second, dt_raw_second, dt_bias_second, a_log_second = local_back(
        (outputs_grad, state_out_grad, decay_grad)
    )
    conv_in_grad, edge_grad, conv_weight_grad, conv_bias_grad = conv_back_fn(
        mixed_first + mixed_second
    )
    edge_back = shifted(as_sent(edge_grad), "seq", -1).astype(edge_grad.dtype)
    conv_in_grad = jnp.concatenate(
        [conv_in_grad[: length - edge_count], conv_in_grad[length - edge_count :] + edge_back], 0
    )
    projected_grad16 = jnp.concatenate(
        [gate_z_grad, conv_in_grad, dt_raw_first + dt_raw_second], axis=1
    ).astype(jnp.bfloat16)
    query_grad, key_grads, value_grads = attend_backward(
        query16,
        key_all.reshape(-1, KV_HEADS, HEAD_DIM),
        value_all.reshape(-1, KV_HEADS, HEAD_DIM),
        log_total,
        attended,
        attended_grad16,
        query_first,
    )
    key_grad, value_grad = (
        lax.psum_scatter(
            key_grads.reshape(-1, KV_HEADS * HEAD_DIM).astype(jnp.bfloat16),
            "seq",
            scatter_dimension=0,
            tiled=True,
        ).astype(jnp.float32),
        lax.psum_scatter(
            value_grads.reshape(-1, KV_HEADS * HEAD_DIM).astype(jnp.bfloat16),
            "seq",
            scatter_dimension=0,
            tiled=True,
        ).astype(jnp.float32),
    )
    query_grad16 = (
        rotate(query_grad.reshape(length, ATT_HEADS, HEAD_DIM), -positions)
        .reshape(length, ATT_HEADS * HEAD_DIM)
        .astype(jnp.bfloat16)
    )
    key_grad16 = (
        rotate(key_grad.reshape(length, KV_HEADS, HEAD_DIM), -positions)
        .reshape(length, KV_HEADS * HEAD_DIM)
        .astype(jnp.bfloat16)
    )
    value_grad16 = value_grad.astype(jnp.bfloat16)
    normed_grad = (
        back_dot(projected_grad16, full_in)
        + back_dot(query_grad16, full_q)
        + back_dot(key_grad16, full_k)
        + back_dot(value_grad16, full_v)
    )
    resident_grad, norm_gain_grad = norm_back(normed_grad)
    input_grad = hidden_grad + resident_grad
    grad_in = weight_grad(normed16, projected_grad16)
    grad_q = weight_grad(normed16, query_grad16)
    grad_k = weight_grad(normed16, key_grad16)
    grad_v = weight_grad(normed16, value_grad16)
    grad_o = weight_grad(attended16, mix16)
    grad_out_w = weight_grad(gated16, mix16)
    mixer_grads = (
        lax.psum_scatter(grad_in, ("seq", "fsdp"), scatter_dimension=0, tiled=True),
        lax.psum_scatter(grad_out_w, ("seq", "fsdp"), scatter_dimension=0, tiled=True),
        lax.psum_scatter(grad_q, ("seq", "fsdp"), scatter_dimension=0, tiled=True),
        lax.psum_scatter(grad_k, ("seq", "fsdp"), scatter_dimension=0, tiled=True),
        lax.psum_scatter(grad_v, ("seq", "fsdp"), scatter_dimension=0, tiled=True),
        lax.psum_scatter(grad_o, ("seq", "fsdp"), scatter_dimension=0, tiled=True),
    )
    result_in, result_out, result_q, result_k, result_v, result_o = mixer_grads
    result_gate, result_up, result_down = mlp_grads
    small = lax.psum(
        (
            norm_gain_grad,
            conv_weight_grad,
            conv_bias_grad,
            dt_bias_first + dt_bias_second,
            a_log_first + a_log_second,
            skip_grad,
            gated_gain_grad,
            mid_gain_grad,
        ),
        ("seq", "fsdp"),
    )
    return (
        output[None],
        input_grad[None],
        small[0],
        result_in,
        small[1],
        small[2],
        small[3],
        small[4],
        small[5],
        small[6],
        result_out,
        result_q,
        result_k,
        result_v,
        result_o,
        small[7],
        result_gate,
        result_up,
        result_down,
    )


def solution(mesh):
    return jax.shard_map(
        body,
        mesh=mesh,
        in_specs=(
            P("fsdp", "seq", None),
            P("fsdp", "seq", None),
            P(),
            P(("seq", "fsdp"), None),
            P(),
            P(),
            P(),
            P(),
            P(),
            P(),
            P(("seq", "fsdp"), None),
            P(("seq", "fsdp"), None),
            P(("seq", "fsdp"), None),
            P(("seq", "fsdp"), None),
            P(("seq", "fsdp"), None),
            P(),
            P(("seq", "fsdp"), None),
            P(("seq", "fsdp"), None),
            P(("seq", "fsdp"), None),
        ),
        out_specs=(
            P("fsdp", "seq", None),
            P("fsdp", "seq", None),
            P(),
            P(("seq", "fsdp"), None),
            P(),
            P(),
            P(),
            P(),
            P(),
            P(),
            P(("seq", "fsdp"), None),
            P(("seq", "fsdp"), None),
            P(("seq", "fsdp"), None),
            P(("seq", "fsdp"), None),
            P(("seq", "fsdp"), None),
            P(),
            P(("seq", "fsdp"), None),
            P(("seq", "fsdp"), None),
            P(("seq", "fsdp"), None),
        ),
        check_vma=False,
    )
```

profile of v0, /device:TPU:0, one launch (start us, length us, event | category | flops | bytes accessed | tf_op | source)
XLA Modules:
  0.0 4354.9 jit_solution(5802935089059232485)
XLA Ops:
  12.2 55.2 %all-gather.21.cloned.1.call-done = bf16[2048,256]{1,0:T(8,128)(2,1)} async-done(((bf16[64,256]{1,0:T(8,128)(2,1)}), bf16[2048,256]{1,0:T(8,128)(2,1)}) %all-gather.21.cloned.1.call-update) | async-done | bytes 1048592 | tf_op jit(solution)/shard_map/all_gather | solution.py:325
  70.3 52.7 %all-gather.17.cloned.1.call-done = bf16[2048,256]{1,0:T(8,128)(2,1)} async-done(((bf16[64,256]{1,0:T(8,128)(2,1)}), bf16[2048,256]{1,0:T(8,128)(2,1)}) %all-gather.17.cloned.1.call-update) | async-done | bytes 1048592 | tf_op jit(solution)/shard_map/all_gather | solution.py:326
  126.9 165.1 %all-gather.29.cloned.1.call-done = bf16[2048,6704]{1,0:T(8,128)(2,1)} async-done(((bf16[64,6704]{1,0:T(8,128)(2,1)}), bf16[2048,6704]{1,0:T(8,128)(2,1)}) %all-gather.29.cloned.1.call-update) | async-done | bytes 27459600 | tf_op jit(solution)/shard_map/all_gather | solution.py:322
  355.5 137.1 %while.110 = (s32[]{:T(128)}, f32[48,64,256]{2,1,0:T(8,128)S(1)}, f32[2,128,48,64]{1,0,3,2:T(2,128)}, f32[2,48,64,256]{3,2,1,0:T(8,128)}, f32[2,128,48]{2,1,0:T(...) while((s32[]{:T(128)}, f32[48,64,256]{2,1,0:T(8,128)S(1)}, ...), condition=%wide.region_9.11_spmd.clone, body=%wide.region_7.10_spmd.clone.sunk | while | flops 3079286784 | bytes 42103724 | solution.py:170
  379.0 36.8 dynamic_update_slice.80
  537.4 44.5 %all-reduce.15 = bf16[384]{0:T(512)(128)(2,1)S(1)} all-reduce(bf16[384]{0:T(512)(128)(2,1)S(1)} %dynamic-update-slice), channel_id=2, replica_groups=mesh['seq'=8,'fsdp'=4] {'seq'}, use_global_device_ids=true, to_apply=%add.15 | all-reduce | flops 384 | bytes 1536
  592.1 76.5 %all-gather.39.cloned.1.call-done = bf16[384,64,256]{2,1,0:T(8,128)(2,1)} async-done(((bf16[48,64,256]{2,1,0:T(8,128)(2,1)}), bf16[384,64,256]{2,1,0:T(8,128)(2,1)}) %all-gather.39.cloned.1.call-update) | async-done | bytes 12582928 | tf_op jit(solution)/shard_map/all_gather | solution.py:31
  709.1 56.8 %all-gather.31.cloned.1.call-done = bf16[3072,2048]{1,0:T(8,128)(2,1)} async-done(((bf16[96,2048]{1,0:T(8,128)(2,1)}), bf16[3072,2048]{1,0:T(8,128)(2,1)}) %all-gather.31.cloned.1.call-update) | async-done | bytes 12582928 | tf_op jit(solution)/shard_map/all_gather | solution.py:323
  776.2 52.8 %all-gather.27.cloned.1.call-done = bf16[1024,2048]{1,0:T(8,128)(2,1)} async-done(((bf16[32,2048]{1,0:T(8,128)(2,1)}), bf16[1024,2048]{1,0:T(8,128)(2,1)}) %all-gather.27.cloned.1.call-update) | async-done | bytes 4194320 | tf_op jit(solution)/shard_map/all_gather | solution.py:327
  833.8 111.4 %all-gather.33.cloned.1.call-done = bf16[2048,4096]{1,0:T(8,128)(2,1)} async-done(((bf16[64,4096]{1,0:T(8,128)(2,1)}), bf16[2048,4096]{1,0:T(8,128)(2,1)}) %all-gather.33.cloned.1.call-update) | async-done | bytes 16777232 | tf_op jit(solution)/shard_map/all_gather | solution.py:381
  955.3 105.9 %all-gather.35.cloned.1.call-done = bf16[2048,4096]{1,0:T(8,128)(2,1)} async-done(((bf16[64,4096]{1,0:T(8,128)(2,1)}), bf16[2048,4096]{1,0:T(8,128)(2,1)}) %all-gather.35.cloned.1.call-update) | async-done | bytes 16777232 | tf_op jit(solution)/shard_map/all_gather | solution.py:382
  1071.3 105.7 %all-gather.37.cloned.1.call-done = bf16[4096,2048]{1,0:T(8,128)(2,1)} async-done(((bf16[128,2048]{1,0:T(8,128)(2,1)}), bf16[4096,2048]{1,0:T(8,128)(2,1)}) %all-gather.37.cloned.1.call-update) | async-done | bytes 16777232 | tf_op jit(solution)/shard_map/all_gather | solution.py:383
  1268.8 76.8 %reduce-scatter.12.cloned.1.call-done = bf16[256,256]{0,1:T(8,128)(2,1)} async-done(((bf16[2048,256]{0,1:T(8,128)(2,1)}), bf16[256,256]{0,1:T(8,128)(2,1)}) %reduce-scatter.12.cloned.1.call-update) | async-done | bytes 131088 | tf_op jit(solution)/shard_map/reduce_scatter | solution.py:452
  1348.7 64.1 %reduce-scatter.14.cloned.1.call-done = bf16[256,256]{0,1:T(8,128)(2,1)} async-done(((bf16[2048,256]{0,1:T(8,128)(2,1)}), bf16[256,256]{0,1:T(8,128)(2,1)}) %reduce-scatter.14.cloned.1.call-update) | async-done | bytes 131088 | tf_op jit(solution)/shard_map/reduce_scatter | solution.py:458
  1464.0 126.3 %all-gather.41.cloned.1.call-done = bf16[384,64,256]{2,1,0:T(8,128)(2,1)} async-done(((bf16[48,64,256]{2,1,0:T(8,128)(2,1)}), bf16[384,64,256]{2,1,0:T(8,128)(2,1)}) %all-gather.41.cloned.1.call-update) | async-done | bytes 12582928 | tf_op jit(solution)/shard_map/all_gather | solution.py:54
  1627.8 122.7 %while.113 = (s32[]{:T(128)}, f32[48]{0:T(128)}, f32[48,64,256]{2,1,0:T(8,128)S(1)}, f32[2,128,48,64]{1,3,2,0:T(8,128)}, f32[2,128,256]{2,1,0:T(8,128)}, /*index...) while((s32[]{:T(128)}, f32[48]{0:T(128)}, ...), condition=%wide.region_33.35_spmd.clone, body=%wide.region_21.34_spmd.clone.sunk | while | flops 7420530688 | bytes 152928624 | solution.py:170
  1912.6 98.7 %reduce-scatter.26.cloned.1.call-done = f32[32,2048]{1,0:T(8,128)} async-done(((f32[1024,2048]{1,0:T(8,128)}), f32[32,2048]{1,0:T(8,128)}) %reduce-scatter.26.cloned.1.call-update) | async-done | bytes 262160 | tf_op jit(solution)/shard_map/reduce_scatter | solution.py:496
  2011.3 147.6 %reduce-scatter.20.cloned.1.call-done = f32[64,1024]{1,0:T(8,128)} async-done(((f32[2048,1024]{1,0:T(8,128)}), f32[64,1024]{1,0:T(8,128)}) %reduce-scatter.20.cloned.1.call-update) | async-done | bytes 262160 | tf_op jit(solution)/shard_map/reduce_scatter | solution.py:493
  2158.9 260.1 %all-reduce.19.cloned.1.call-done = (f32[2048]{0:T(1024)}, f32[4,3584]{1,0:T(4,128)}, f32[3584]{0:T(1024)}, f32[48]{0:T(128)}, f32[48]{0:T(128)}, /*index=5*/f32[48]{0:T(128)}, f32[3072]{0:T(1024)}, f32[2048]{0:T(1024)}) async-done(((f32[2048]{0:T(1024)}, f32[4,3584]{1,0:T(4,128)}, f32[3584]{0:T(1024)}, f32[48]{0:T(128)}, f32[48]{0:T(128)}, /*index=5*/f32[48]{0:T(128)}, f32[3072]{0:T(1024)}, ...) | async-done | bytes 100944 | tf_op jit(solution)/shard_map/psum | solution.py:500
  2419.0 256.8 %reduce-scatter.18.cloned.1.call-done = f32[96,2048]{1,0:T(8,128)} async-done(((f32[3072,2048]{1,0:T(8,128)}), f32[96,2048]{1,0:T(8,128)}) %reduce-scatter.18.cloned.1.call-update) | async-done | bytes 786448 | tf_op jit(solution)/shard_map/reduce_scatter | solution.py:492
  2675.9 356.5 %reduce-scatter.28.cloned.1.call-done = f32[64,4096]{1,0:T(8,128)} async-done(((f32[2048,4096]{1,0:T(8,128)}), f32[64,4096]{1,0:T(8,128)}) %reduce-scatter.28.cloned.1.call-update) | async-done | bytes 1048592 | tf_op jit(solution)/shard_map/reduce_scatter | solution.py:405
  3032.4 360.5 %reduce-scatter.30.cloned.1.call-done = f32[64,4096]{1,0:T(8,128)} async-done(((f32[2048,4096]{1,0:T(8,128)}), f32[64,4096]{1,0:T(8,128)}) %reduce-scatter.30.cloned.1.call-update) | async-done | bytes 1048592 | tf_op jit(solution)/shard_map/reduce_scatter | solution.py:406
  3392.9 360.3 %reduce-scatter.32.cloned.1.call-done = f32[128,2048]{1,0:T(8,128)} async-done(((f32[4096,2048]{1,0:T(8,128)}), f32[128,2048]{1,0:T(8,128)}) %reduce-scatter.32.cloned.1.call-update) | async-done | bytes 1048592 | tf_op jit(solution)/shard_map/reduce_scatter | solution.py:407
  3753.2 584.5 %reduce-scatter.16.cloned.1.call-done = f32[64,6704]{1,0:T(8,128)} async-done(((f32[2048,6704]{1,0:T(8,128)}), f32[64,6704]{1,0:T(8,128)}) %reduce-scatter.16.cloned.1.call-update) | async-done | bytes 1716240 | tf_op jit(solution)/shard_map/reduce_scatter | solution.py:491
  (740 shorter events, 848.9 us)
Async XLA Ops:
  7.9 115.1 %all-gather.17.cloned.1.call-start = ((), (), s32[]{:S(2)}) async-start(), calls=%async_computation.11 | async-start | bytes 1081344 | tf_op jit(solution)/shard_map/all_gather | solution.py:326
  8.7 283.3 %all-gather.29.cloned.1.call-start = ((), (), s32[]{:S(2)}) async-start(), calls=%async_computation.17 | async-start | bytes 28655616 | tf_op jit(solution)/shard_map/all_gather | solution.py:322
  9.4 490.3 %all-gather.23.cloned.1.call-start = ((), (), s32[]{:S(2)}) async-start(), calls=%async_computation.14 | async-start | bytes 1179648 | tf_op jit(solution)/shard_map/all_gather | solution.py:369
  70.3 431.8 %all-gather.19.cloned.1.call-start = ((), (), s32[]{:S(2)}) async-start(), calls=%async_computation.12 | async-start | bytes 1179648 | tf_op jit(solution)/shard_map/all_gather | solution.py:370
  125.4 379.0 %all-gather.25.cloned.1.call-start = ((), (), s32[]{:S(2)}) async-start(), calls=%async_computation.15 | async-start | bytes 4325376 | tf_op jit(solution)/shard_map/all_gather | solution.py:324
  126.0 542.6 %all-gather.39.cloned.1.call-start = ((), (), s32[]{:S(2)}) async-start(), calls=%async_computation.33 | async-start | bytes 14155776 | tf_op jit(solution)/shard_map/all_gather | solution.py:31
  494.0 271.9 %all-gather.31.cloned.1.call-start = ((), (), s32[]{:S(2)}) async-start(), calls=%async_computation.18 | async-start | bytes 12976128 | tf_op jit(solution)/shard_map/all_gather | solution.py:323
  494.7 334.3 %all-gather.27.cloned.1.call-start = ((), (), s32[]{:S(2)}) async-start(), calls=%async_computation.16 | async-start | bytes 4325376 | tf_op jit(solution)/shard_map/all_gather | solution.py:327
  495.4 449.8 %all-gather.33.cloned.1.call-start = ((), (), s32[]{:S(2)}) async-start(), calls=%async_computation.19 | async-start | bytes 17301504 | tf_op jit(solution)/shard_map/all_gather | solution.py:381
  496.0 565.1 %all-gather.35.cloned.1.call-start = ((), (), s32[]{:S(2)}) async-start(), calls=%async_computation.20 | async-start | bytes 17301504 | tf_op jit(solution)/shard_map/all_gather | solution.py:382
  496.8 680.2 %all-gather.37.cloned.1.call-start = ((), (), s32[]{:S(2)}) async-start(), calls=%async_computation.21 | async-start | bytes 17301504 | tf_op jit(solution)/shard_map/all_gather | solution.py:383
  497.3 848.2 %reduce-scatter.12.cloned.1.call-start = ((), (), s32[]{:S(2)}) async-start(), calls=%async_computation.22 | async-start | bytes 1179648 | tf_op jit(solution)/shard_map/reduce_scatter | solution.py:452
  1242.6 170.2 %reduce-scatter.14.cloned.1.call-start = ((), (), s32[]{:S(2)}) async-start(), calls=%async_computation.23 | async-start | bytes 1179648 | tf_op jit(solution)/shard_map/reduce_scatter | solution.py:458
  1243.1 347.1 %all-gather.41.cloned.1.call-start = ((), (), s32[]{:S(2)}) async-start(), calls=%async_computation.34 | async-start | bytes 14155776 | tf_op jit(solution)/shard_map/all_gather | solution.py:54
  1268.8 643.8 %reduce-scatter.22.cloned.1.call-start = ((), (), s32[]{:S(2)}) async-start(), calls=%async_computation.27 | async-start | bytes 2162688 | tf_op jit(solution)/shard_map/reduce_scatter | solution.py:494
  1348.6 564.0 %reduce-scatter.24.cloned.1.call-start = ((), (), s32[]{:S(2)}) async-start(), calls=%async_computation.28 | async-start | bytes 2162688 | tf_op jit(solution)/shard_map/reduce_scatter | solution.py:495
  1415.6 595.7 %reduce-scatter.26.cloned.1.call-start = ((), (), s32[]{:S(2)}) async-start(), calls=%async_computation.29 | async-start | bytes 8650752 | tf_op jit(solution)/shard_map/reduce_scatter | solution.py:496
  1420.3 738.6 %reduce-scatter.20.cloned.1.call-start = ((), (), s32[]{:S(2)}) async-start(), calls=%async_computation.26 | async-start | bytes 8650752 | tf_op jit(solution)/shard_map/reduce_scatter | solution.py:493
  1458.2 960.9 %all-reduce.19.cloned.1.call-start = ((), (), s32[]{:S(2)}) async-start(), calls=%async_computation.35 | async-start | bytes 207872 | tf_op jit(solution)/shard_map/psum | solution.py:500
  1813.8 862.1 %reduce-scatter.18.cloned.1.call-start = ((), (), s32[]{:S(2)}) async-start(), calls=%async_computation.25 | async-start | bytes 25952256 | tf_op jit(solution)/shard_map/reduce_scatter | solution.py:492
  1826.4 1206.1 %reduce-scatter.28.cloned.1.call-start = ((), (), s32[]{:S(2)}) async-start(), calls=%async_computation.30 | async-start | bytes 34603008 | tf_op jit(solution)/shard_map/reduce_scatter | solution.py:405
  1842.5 1550.5 %reduce-scatter.30.cloned.1.call-start = ((), (), s32[]{:S(2)}) async-start(), calls=%async_computation.31 | async-start | bytes 34603008 | tf_op jit(solution)/shard_map/reduce_scatter | solution.py:406
  1857.3 1895.9 %reduce-scatter.32.cloned.1.call-start = ((), (), s32[]{:S(2)}) async-start(), calls=%async_computation.32 | async-start | bytes 34603008 | tf_op jit(solution)/shard_map/reduce_scatter | solution.py:407
  1873.5 2464.3 %reduce-scatter.16.cloned.1.call-start = ((), (), s32[]{:S(2)}) async-start(), calls=%async_computation.24 | async-start | bytes 57311232 | tf_op jit(solution)/shard_map/reduce_scatter | solution.py:491
  (182 other events, 5538.3 us)
Sparse Core Ops, SparseCore 0:
  10.9 56.4 all-gather.20
  70.3 52.6 all-gather.16
  125.9 166.0 all-gather.28
  334.8 39.0 all-gather.18
  376.6 60.7 all-gather.24
  494.1 174.4 all-gather.38
  671.5 94.3 all-gather.30
  768.7 60.2 all-gather.26
  831.8 113.4 all-gather.32
  948.1 113.0 all-gather.34
  1063.9 113.0 all-gather.36
  1242.7 102.8 reduce-scatter.11
  1349.8 62.8 reduce-scatter.13
  1414.8 175.4 all-gather.40
  1592.9 135.0 reduce-scatter.21
  1730.8 132.6 reduce-scatter.23
  1866.2 145.0 reduce-scatter.25
  2014.2 144.7 reduce-scatter.19
  2166.3 252.6 all-reduce.18
  2429.1 246.7 reduce-scatter.17
  2678.8 353.6 reduce-scatter.27
  3035.3 357.5 reduce-scatter.29
  3395.6 357.5 reduce-scatter.31
  3756.1 581.6 reduce-scatter.15
  (1 shorter events, 37.6 us)
where the time goes:
time: 4380 us; the launch traced here: 4350 us
  waiting for transfers between devices  3480 us (79%)
  matrix products  387 us (9%)
  local copies, waits for them, and re-layouts  241 us (6%)
  other arithmetic  167 us (4%)
  blocking collectives  44.5 us (1%)
    reduce_scatter x1, waiting for transfers between devices, body(): lax.psum_scatter(grad_in, ('seq', 'fsdp'), scatter_dimension=0, tiled=True)  585 us
    reduce_scatter x1, waiting for transfers between devices, body(): lax.psum_scatter(grad_up, ('seq', 'fsdp'), scatter_dimension=0, tiled=True)  360 us
    reduce_scatter x1, waiting for transfers between devices, body(): lax.psum_scatter(grad_down, ('seq', 'fsdp'), scatter_dimension=0, tiled=T...  360 us
    reduce_scatter x1, waiting for transfers between devices, body(): lax.psum_scatter(grad_gate, ('seq', 'fsdp'), scatter_dimension=0, tiled=T...  357 us
    psum x1, waiting for transfers between devices, body(): lax.psum((norm_gain_grad, conv_weight_grad, conv_bias_grad, dt_bias_first...  260 us
    reduce_scatter x1, waiting for transfers between devices, body(): lax.psum_scatter(grad_out_w, ('seq', 'fsdp'), scatter_dimension=0, tiled=...  257 us
    all_gather x1, waiting for transfers between devices, body(): lax.all_gather(w_in, ('seq', 'fsdp'), axis=0, tiled=True)  165 us
    reduce_scatter x1, waiting for transfers between devices, body(): lax.psum_scatter(grad_q, ('seq', 'fsdp'), scatter_dimension=0, tiled=True)  148 us
  transfers between devices with their start and end apart: 27, of which 20 were waited for; matrix products, arithmetic and copies ran while one was open for 16% of the time, Pallas kernels for 0%

commit v1 on v0

v1 whole, which is shorter than its diff:
```python
import jax
import jax.numpy as jnp
from jax import lax
from jax.sharding import Mesh
from jax.sharding import PartitionSpec as P

D = 2048
MAMBA_HEADS = 48
MAMBA_HEAD = 64
STATE = 256
ATT_HEADS = 8
KV_HEADS = 2
HEAD_DIM = 128
SPAN = 128
INNER = 3072

HEADS = MAMBA_HEADS // 4
PART = HEADS * MAMBA_HEAD
BC = 2 * STATE
DT_PAD = 128
QP = 2 * HEAD_DIM
CONV_COLS = PART + BC
AT_DT = CONV_COLS
AT_Q = AT_DT + DT_PAD
AT_K = AT_Q + QP
AT_V = AT_K + HEAD_DIM
AT_Z = AT_V + HEAD_DIM
MIX_COLS = AT_Z + PART

epsilon = 1e-05
rope_base = 100000000000.0
highest = lax.Precision.HIGHEST
GROUP = ("x", "c")
SHARDS = ("z", "y")
EVERY = ("z", "x", "y", "c")
bf16 = jnp.bfloat16
f32 = jnp.float32


def swap(array, axis):
    return lax.ppermute(array, axis, [(0, 1), (1, 0)])


def shifted(array, distance):
    devices = range(lax.axis_size("z"))
    return lax.ppermute(array, "z", [(i - distance, i) for i in devices if i - distance in devices])


def total(array):
    for axis in EVERY:
        size = lax.axis_size(axis)
        bit = 1
        while bit < size:
            array = array + lax.ppermute(array, axis, [(i, i ^ bit) for i in range(size)])
            bit *= 2
    return array


def group_total(array):
    array = array + swap(array[::-1], "c")
    return array + swap(array, "x")


def low_dot(left, right):
    return jnp.dot(left, right, preferred_element_type=f32)


def back_dot(grad_rows, weight):
    return lax.dot_general(grad_rows, weight, (((1,), (1,)), ((), ())), preferred_element_type=f32)


def weight_grad(left, right):
    return lax.dot_general(left, right, (((0,), (0,)), ((), ())), preferred_element_type=f32)


def rms_scale(values, gain):
    return values * lax.rsqrt(jnp.mean(values * values, axis=-1, keepdims=True) + epsilon) * gain


def rope_tables(positions):
    half_dim = HEAD_DIM // 2
    frequencies = rope_base ** (-jnp.arange(half_dim, dtype=f32) / half_dim)
    angles = positions.astype(f32)[:, None] * frequencies[None, :]
    return (jnp.cos(angles), jnp.sin(angles))


def rotate(values, cosine, sine):
    half_dim = HEAD_DIM // 2
    cosine, sine = cosine[:, None, :], sine[:, None, :]
    first, second = values[..., :half_dim], values[..., half_dim:]
    return jnp.concatenate([first * cosine - second * sine, second * cosine + first * sine], axis=-1)


def convolve(padded, conv_weight, conv_bias):
    taps = conv_weight.shape[0]
    length = padded.shape[1] - taps + 1
    accumulated = conv_bias + padded[:, 0:length] * conv_weight[0]
    for offset in range(1, taps):
        accumulated = accumulated + padded[:, offset : offset + length] * conv_weight[offset]
    return jax.nn.silu(accumulated)


def chunk_parts(mixed, dt_raw, dt_bias, a_log):
    seqs, length = mixed.shape[:2]
    n = length // SPAN
    xs = mixed[..., :PART].reshape(seqs, n, SPAN, HEADS, MAMBA_HEAD)
    bs = mixed[..., PART : PART + STATE].reshape(seqs, n, SPAN, STATE)
    cs = mixed[..., PART + STATE :].reshape(seqs, n, SPAN, STATE)
    dt = jax.nn.softplus(dt_raw + dt_bias).reshape(seqs, n, SPAN, HEADS)
    cum = jnp.cumsum(dt * -jnp.exp(a_log), axis=2)
    return (xs, bs, cs, dt, cum)


def span_states(xs, bs, dt, cum):
    tail = jnp.exp(cum[:, :, -1:] - cum) * dt
    return jnp.einsum("bnshp,bnsm->bnhpm", tail[..., None] * xs, bs, precision=highest)


def local_state(mixed, dt_raw, dt_bias, a_log):
    xs, bs, cs, dt, cum = chunk_parts(mixed, dt_raw, dt_bias, a_log)
    local = span_states(xs, bs, dt, cum)
    state = local[:, 0]
    for i in range(1, local.shape[1]):
        state = jnp.exp(cum[:, i, -1])[:, :, None, None] * state + local[:, i]
    return (state, jnp.exp(jnp.sum(cum[:, :, -1], axis=1)))


def scan_all(mixed, dt_raw, dt_bias, a_log, skip_gain, state_in):
    seqs, length = mixed.shape[:2]
    xs, bs, cs, dt, cum = chunk_parts(mixed, dt_raw, dt_bias, a_log)
    n = length // SPAN
    places = jnp.arange(SPAN, dtype=jnp.int32)
    causal = places[:, None] >= places[None, :]
    cum_h = jnp.moveaxis(cum, 3, 2)
    dt_h = jnp.moveaxis(dt, 3, 2)
    spread = cum_h[..., :, None] - cum_h[..., None, :]
    decay = jnp.exp(jnp.where(causal, spread, -jnp.inf))
    meet = jnp.einsum("bntm,bnsm->bnts", cs, bs, precision=highest)
    weights = meet[:, :, None] * decay * dt_h[..., None, :]
    inside = jnp.einsum("bnhts,bnshp->bnthp", weights, xs, precision=highest)
    local = span_states(xs, bs, dt, cum)
    state, carried = state_in, []
    for i in range(n):
        carried.append(jnp.einsum("btm,bhpm->bthp", cs[:, i], state, precision=highest))
        state = jnp.exp(cum[:, i, -1])[:, :, None, None] * state + local[:, i]
    values = inside + jnp.exp(cum)[..., None] * jnp.stack(carried, 1) + skip_gain[:, None] * xs
    return (values.reshape(seqs, length, PART), state)


def swish_product(gate_proj, up_proj):
    return jax.nn.silu(gate_proj) * up_proj


def gather_tokens(block):
    across = swap(block, "x")
    return (block, swap(block, "c"), across, swap(across, "c"))


def scatter_tokens(blocks):
    near, far = blocks[0], blocks[2]
    sent = swap(jnp.stack([blocks[1].astype(bf16), blocks[3].astype(bf16)]), "c")
    near = near + sent[0].astype(f32)
    far = far + sent[1].astype(f32)
    return near + swap(far.astype(bf16), "x").astype(f32)


def body(
    inputs,
    out_grad,
    norm_gain,
    w_in,
    conv_weight,
    conv_bias,
    dt_bias,
    a_log,
    skip_gain,
    gated_gain,
    w_out,
    w_q,
    w_k,
    w_v,
    w_o,
    mid_gain,
    w_gate,
    w_up,
    w_down,
):
    nz, ny = lax.axis_size("z"), lax.axis_size("y")
    zi, xi, ci = (lax.axis_index(name) for name in ("z", "x", "c"))
    length = inputs.shape[1]
    span_all = 2 * length
    rows = w_in.shape[0]
    ff_rows = w_down.shape[0]
    hidden_part = nz * ny * ff_rows
    edge_count = conv_weight.shape[0] - 1
    out_rows, o_rows = w_out.shape[0], w_o.shape[0]
    aligned = ny == 2 and nz == 4 and MAMBA_HEADS % (4 * nz) == 0
    g = nz if aligned else 1
    hp = HEADS // g

    def heads_mine(array, width):
        lead = array.shape[:-1]
        array = array.reshape(lead + (g, 2, 2, hp * width))
        array = lax.dynamic_index_in_dim(array, xi, len(lead) + 1, keepdims=False)
        array = lax.dynamic_index_in_dim(array, ci, len(lead) + 1, keepdims=False)
        return array.reshape(lead + (HEADS * width,))

    def heads_spread(array, width):
        lead = array.shape[:-1]
        array = array.reshape(lead + (g, 1, 1, hp * width))
        whole = jnp.zeros(lead + (g, 2, 2, hp * width), array.dtype)
        start = (0,) * len(lead) + (0, xi, ci, 0)
        return lax.dynamic_update_slice(whole, array, start).reshape(
            lead + (MAMBA_HEADS * width,)
        )

    def heads_split(array, width):
        n = array.shape[0]
        array = array.reshape(n, g, 2, 2, hp * width)
        return jnp.transpose(array, (2, 3, 0, 1, 4)).reshape(4, n, HEADS * width)

    def heads_join(array, width):
        n = array.shape[1]
        array = array.reshape(2, 2, n, g, hp * width)
        return jnp.transpose(array, (2, 3, 0, 1, 4)).reshape(n, MAMBA_HEADS * width)

    def permuted(array):
        lead = array.shape[:-1]
        array = array.reshape(lead + (nz, 2, ny, 2 * rows))
        return jnp.swapaxes(array, -3, -2).reshape(lead + (D,))

    def restored(array):
        lead = array.shape[:-1]
        array = array.reshape(lead + (nz, ny, 2, 2 * rows))
        return jnp.swapaxes(array, -3, -2).reshape(lead + (D,))

    def to_ranks(array):
        return lax.all_to_all(array, GROUP, 0, 0, tiled=True)

    def in_order(own, other):
        return lax.dynamic_slice_in_dim(
            jnp.concatenate([own, other, own], 0), xi * length, span_all, 0
        )

    def gather_sequences(block):
        own, near, across, far = gather_tokens(block)
        return jnp.stack([in_order(own, across), in_order(near, far)])

    def scatter_sequences(partial):
        mine = partial[0] + swap(partial[1].astype(bf16), "c").astype(f32)
        mine = mine.reshape(2, length, mine.shape[-1])
        own = lax.dynamic_index_in_dim(mine, xi, 0, keepdims=False)
        other = lax.dynamic_index_in_dim(mine, 1 - xi, 0, keepdims=False)
        return own + swap(other.astype(bf16), "x").astype(f32)

    split_q = jnp.transpose(w_q.reshape(rows, 2, 2, 2, HEAD_DIM), (3, 1, 0, 2, 4))
    split_k = jnp.transpose(w_k.reshape(rows, 2, HEAD_DIM), (1, 0, 2))
    split_v = jnp.transpose(w_v.reshape(rows, 2, HEAD_DIM), (1, 0, 2))
    two = lambda a: jnp.broadcast_to(a[None], (2,) + a.shape).reshape(4, rows, a.shape[-1])
    packed_mix = jnp.concatenate(
        [
            heads_split(w_in[:, INNER : 2 * INNER], MAMBA_HEAD),
            jnp.broadcast_to(w_in[None, :, 2 * INNER : 2 * INNER + BC], (4, rows, BC)),
            jnp.pad(
                heads_split(w_in[:, 2 * INNER + BC :], 1), ((0, 0), (0, 0), (0, DT_PAD - HEADS))
            ),
            split_q.reshape(4, rows, QP),
            two(split_k),
            two(split_v),
            heads_split(w_in[:, :INNER], MAMBA_HEAD),
        ],
        axis=2,
    )
    full_mix = lax.all_gather(
        to_ranks(packed_mix).reshape(4 * rows, MIX_COLS), SHARDS, axis=0, tiled=True
    )

    if aligned:
        turn = [(2 * y + c, 2 * c + y) for y in range(2) for c in range(2)]
        place = []
        for z in range(4):
            for y in range(2):
                for c in range(2):
                    place.append(((z * 2 + y) * 2 + c, ((z % 2 * 2 + y) * 2 + c) * 2 + z // 2))
        back_place = [(b, a) for a, b in place]
        sent_out = lax.ppermute(w_out, ("y", "c"), turn)
        sent_o = lax.ppermute(w_o, ("z", "y", "c"), place)
        full_rows = lax.all_gather(
            jnp.concatenate([sent_out, sent_o], 0), SHARDS, axis=0, tiled=True
        ).reshape(nz * ny, out_rows + o_rows, D)
        full_out = full_rows[:, :out_rows].reshape(PART, D)
        full_o = full_rows[:, out_rows:].reshape(QP, D)
    else:
        every_out = lax.all_gather(w_out, EVERY, axis=0, tiled=True)
        every_o = lax.all_gather(w_o, EVERY, axis=0, tiled=True)
        full_out = lax.dynamic_slice_in_dim(every_out, (2 * xi + ci) * PART, PART, 0)
        every_o = every_o.reshape(2, 2, 2, HEAD_DIM, D)
        every_o = lax.dynamic_index_in_dim(every_o, xi, 2, keepdims=False)
        full_o = lax.dynamic_index_in_dim(every_o, ci, 0, keepdims=False).reshape(QP, D)

    def split_ff(w):
        w = w.reshape(rows, nz, 2, ny, 2, ff_rows)
        return jnp.transpose(w, (2, 4, 0, 1, 3, 5)).reshape(4, rows, hidden_part)

    def join_ff(w):
        w = w.reshape(2, 2, rows, nz, ny, ff_rows)
        return jnp.transpose(w, (2, 3, 0, 4, 1, 5)).reshape(rows, 4 * hidden_part)

    packed_ff = jnp.concatenate([split_ff(w_gate), split_ff(w_up)], axis=2)
    full_ff = lax.all_gather(
        to_ranks(packed_ff).reshape(4 * rows, 2 * hidden_part), SHARDS, axis=0, tiled=True
    )
    full_down = lax.all_gather(w_down, SHARDS, axis=0, tiled=True)

    resident = inputs[0].astype(f32)
    normed, norm_back = jax.vjp(rms_scale, resident, norm_gain)
    normed16 = gather_sequences(permuted(normed.astype(bf16)))
    tokens = 2 * span_all
    projected = low_dot(normed16.reshape(tokens, D), full_mix).reshape(2, span_all, MIX_COLS)
    conv_in = projected[..., :CONV_COLS]
    dt_raw = projected[..., AT_DT : AT_DT + HEADS]
    gate_z = projected[..., AT_Z:]
    edge_rows = shifted(conv_in[:, span_all - edge_count :].astype(bf16), 1).astype(f32)

    def rank_channels(array):
        return jnp.concatenate(
            [heads_mine(array[..., :INNER], MAMBA_HEAD), array[..., INNER:]], axis=-1
        )

    conv_w, conv_b = rank_channels(conv_weight), rank_channels(conv_bias)
    dt_b, a_l, skip = (heads_mine(v, 1) for v in (dt_bias, a_log, skip_gain))
    gain = heads_mine(gated_gain, MAMBA_HEAD)

    def conv_piece(conv_in, edge_rows, conv_w, conv_b):
        return convolve(jnp.concatenate([edge_rows, conv_in], 1), conv_w, conv_b)

    mixed, conv_back = jax.vjp(conv_piece, conv_in, edge_rows, conv_w, conv_b)
    own_state, own_decay = local_state(mixed, dt_raw, dt_b, a_l)
    own_state16 = own_state.astype(bf16)

    positions = zi * span_all + jnp.arange(span_all, dtype=jnp.int32)
    cosine, sine = rope_tables(positions)
    query16 = rotate(
        projected[..., AT_Q:AT_K].reshape(2, span_all, 2, HEAD_DIM), cosine, sine
    ).astype(bf16)
    key16 = rotate(projected[..., None, AT_K:AT_V], cosine, sine).astype(bf16)[:, :, 0]
    value16 = projected[..., AT_V:AT_Z].astype(bf16)
    kv16 = jnp.stack([key16, value16])
    kv_all = jnp.concatenate([shifted(kv16, d) for d in range(nz - 1, 0, -1)] + [kv16], axis=2)
    key_all, value_all = kv_all[0], kv_all[1]
    decays = [shifted(own_decay, d) for d in range(1, nz)]
    state_in = jnp.zeros(own_state.shape, f32)
    factor = jnp.ones(own_decay.shape, f32)
    for d in range(1, nz):
        arrived = shifted(own_state16, d).astype(f32)
        state_in = state_in + factor[:, :, None, None] * arrived
        factor = factor * decays[d - 1]

    score_scale = HEAD_DIM ** (-0.5)
    key_place = (zi - nz + 1) * span_all + jnp.arange(nz * span_all, dtype=jnp.int32)
    allowed = (key_place >= 0) & (positions[:, None] >= key_place)
    scores = (
        jnp.einsum("bqhd,bkd->bhqk", query16, key_all, preferred_element_type=f32) * score_scale
    )
    scores = jnp.where(allowed, scores, -jnp.inf)
    peak = jnp.max(scores, axis=-1, keepdims=True)
    unscaled = jnp.exp(scores - peak)
    probs = unscaled * (1.0 / jnp.sum(unscaled, axis=-1, keepdims=True))
    probs16 = probs.astype(bf16)
    attended = jnp.einsum("bhqk,bkd->bqhd", probs16, value_all, preferred_element_type=f32)
    attended16 = attended.reshape(tokens, QP).astype(bf16)

    (scanned, state_out), scan_back = jax.vjp(scan_all, mixed, dt_raw, dt_b, a_l, skip, state_in)
    flat, gate_back = jax.vjp(lambda v, z: v * jax.nn.silu(z), scanned, gate_z)
    square = group_total(jnp.sum(flat * flat, axis=-1, keepdims=True))
    root = lax.rsqrt(square / INNER + epsilon)
    gated16 = (flat * root * gain).astype(bf16).reshape(tokens, PART)
    mixture = low_dot(gated16, full_out) + low_dot(attended16, full_o)
    hidden_state = resident + scatter_sequences(mixture.reshape(2, span_all, D))

    middle, mid_back = jax.vjp(rms_scale, hidden_state, mid_gain)
    middle16 = jnp.concatenate(gather_tokens(permuted(middle.astype(bf16))), 0)
    cotangent16 = jnp.concatenate(gather_tokens(out_grad[0]), 0)
    both = low_dot(middle16, full_ff)
    activated, swish_back = jax.vjp(
        swish_product, both[:, :hidden_part], both[:, hidden_part:]
    )
    activated16 = activated.astype(bf16)
    down = low_dot(activated16, full_down).reshape(4, length, D)
    output = (hidden_state + scatter_tokens(down)).astype(bf16)
    gate_grad, up_grad = swish_back(back_dot(cotangent16, full_down))
    both16 = jnp.concatenate([gate_grad, up_grad], axis=1).astype(bf16)
    mid_grad = restored(scatter_tokens(back_dot(both16, full_ff).reshape(4, length, D)))
    hidden_piece, mid_gain_grad = mid_back(mid_grad)
    hidden_grad = out_grad[0].astype(f32) + hidden_piece

    def to_owners(array):
        return lax.psum_scatter(array.astype(bf16), SHARDS, scatter_dimension=0, tiled=True)

    result_down = to_owners(weight_grad(activated16, cotangent16)).astype(f32)
    ff_parts = to_ranks(to_owners(weight_grad(middle16, both16)).reshape(4, rows, 2 * hidden_part))
    result_gate = join_ff(ff_parts[..., :hidden_part]).astype(f32)
    result_up = join_ff(ff_parts[..., hidden_part:]).astype(f32)

    mix16 = gather_sequences(hidden_grad.astype(bf16)).reshape(tokens, D)
    attended_grad16 = back_dot(mix16, full_o).astype(bf16).reshape(2, span_all, 2, HEAD_DIM)
    gated_grad = back_dot(mix16, full_out).reshape(2, span_all, PART)
    grad_out_w = weight_grad(gated16, mix16)
    grad_o = weight_grad(attended16, mix16)
    if aligned:
        rows_parts = to_owners(
            jnp.concatenate(
                [
                    grad_out_w.reshape(nz * ny, out_rows, D),
                    grad_o.reshape(nz * ny, o_rows, D),
                ],
                axis=1,
            ).reshape(nz * ny * (out_rows + o_rows), D)
        )
        result_out = lax.ppermute(rows_parts[:out_rows], ("y", "c"), turn).astype(f32)
        result_o = lax.ppermute(rows_parts[out_rows:], ("z", "y", "c"), back_place).astype(f32)
    else:
        every_out = lax.dynamic_update_slice_in_dim(
            jnp.zeros((INNER, D), f32), grad_out_w, (2 * xi + ci) * PART, 0
        )
        every_o = lax.dynamic_update_slice(
            jnp.zeros((2, 2, 2, HEAD_DIM, D), f32),
            grad_o.reshape(1, 2, 1, HEAD_DIM, D),
            (ci, 0, xi, 0, 0),
        ).reshape(ATT_HEADS * HEAD_DIM, D)
        result_out = lax.psum_scatter(
            every_out.astype(bf16), EVERY, scatter_dimension=0, tiled=True
        ).astype(f32)
        result_o = lax.psum_scatter(
            every_o.astype(bf16), EVERY, scatter_dimension=0, tiled=True
        ).astype(f32)

    normal = flat * root
    gain_grad = jnp.sum(gated_grad * normal, axis=(0, 1))
    wide = gated_grad * gain
    inner_mean = group_total(jnp.sum(wide * normal, axis=-1, keepdims=True)) / INNER
    flat_grad = root * (wide - normal * inner_mean)
    scanned_grad, gate_z_grad = gate_back(flat_grad)
    state_local_grad = scan_back((scanned_grad, jnp.zeros(state_out.shape, f32)))[5]
    state_local16 = state_local_grad.astype(bf16)
    state_out_grad = jnp.zeros(own_state.shape, f32)
    factor = jnp.ones(own_decay.shape, f32)
    for d in range(1, nz):
        arrived = shifted(state_local16, -d).astype(f32)
        state_out_grad = state_out_grad + factor[:, :, None, None] * arrived
        factor = factor * shifted(own_decay, -d)

    attended_grad32 = attended_grad16.astype(f32)
    delta = jnp.moveaxis(jnp.sum(attended_grad32 * attended, axis=-1), 2, 1)
    prob_grad = jnp.einsum("bqhd,bkd->bhqk", attended_grad16, value_all, preferred_element_type=f32)
    score_grad = (probs * (prob_grad - delta[..., None])).astype(bf16)
    query_grad = score_scale * jnp.einsum(
        "bhqk,bkd->bqhd", score_grad, key_all, preferred_element_type=f32
    )
    key_grads = score_scale * jnp.einsum(
        "bhqk,bqhd->bkd", score_grad, query16, preferred_element_type=f32
    )
    value_grads = jnp.einsum(
        "bhqk,bqhd->bkd", probs16, attended_grad16, preferred_element_type=f32
    )
    kv_grads = jnp.stack([key_grads, value_grads]).reshape(2, 2, nz, span_all, HEAD_DIM)
    kv_grad = kv_grads[:, :, nz - 1]
    for d in range(1, nz):
        kv_grad = kv_grad + shifted(kv_grads[:, :, nz - 1 - d].astype(bf16), -d).astype(f32)

    mixed_grad, dt_raw_grad, dt_bias_grad, a_log_grad, skip_grad, _ = scan_back(
        (scanned_grad, state_out_grad)
    )
    conv_in_grad, edge_grad, conv_w_grad, conv_b_grad = conv_back(mixed_grad)
    edge_back = shifted(edge_grad.astype(bf16), -1).astype(f32)
    conv_in_grad = jnp.concatenate(
        [
            conv_in_grad[:, : span_all - edge_count],
            conv_in_grad[:, span_all - edge_count :] + edge_back,
        ],
        axis=1,
    )
    query_back = rotate(query_grad, cosine, -sine).reshape(2, span_all, QP)
    key_back = rotate(kv_grad[0][:, :, None], cosine, -sine)[:, :, 0]
    projected_grad16 = jnp.concatenate(
        [
            conv_in_grad.astype(bf16),
            jnp.pad(dt_raw_grad, ((0, 0), (0, 0), (0, DT_PAD - HEADS))).astype(bf16),
            query_back.astype(bf16),
            key_back.astype(bf16),
            kv_grad[1].astype(bf16),
            gate_z_grad.astype(bf16),
        ],
        axis=-1,
    ).reshape(tokens, MIX_COLS)
    mix_parts = to_ranks(
        to_owners(weight_grad(normed16.reshape(tokens, D), projected_grad16)).reshape(
            4, rows, MIX_COLS
        )
    ).astype(f32)
    normed_grad = restored(
        scatter_sequences(back_dot(projected_grad16, full_mix).reshape(2, span_all, D))
    )
    resident_grad, norm_gain_grad = norm_back(normed_grad)
    input_grad = hidden_grad + resident_grad

    result_in = jnp.concatenate(
        [
            heads_join(mix_parts[..., AT_Z:], MAMBA_HEAD),
            heads_join(mix_parts[..., :PART], MAMBA_HEAD),
            jnp.sum(mix_parts[..., PART:CONV_COLS], axis=0),
            heads_join(mix_parts[..., AT_DT : AT_DT + HEADS], 1),
        ],
        axis=1,
    )
    result_q = jnp.transpose(
        mix_parts[..., AT_Q:AT_K].reshape(2, 2, rows, 2, HEAD_DIM), (2, 1, 3, 0, 4)
    ).reshape(rows, ATT_HEADS * HEAD_DIM)
    kv_parts = jnp.sum(mix_parts[..., AT_K:AT_Z].reshape(2, 2, rows, 2, HEAD_DIM), axis=0)
    result_k = jnp.transpose(kv_parts[:, :, 0], (1, 0, 2)).reshape(rows, KV_HEADS * HEAD_DIM)
    result_v = jnp.transpose(kv_parts[:, :, 1], (1, 0, 2)).reshape(rows, KV_HEADS * HEAD_DIM)

    def all_channels(array):
        return jnp.concatenate(
            [heads_spread(array[..., :PART], MAMBA_HEAD), array[..., PART:]], axis=-1
        )

    small = [
        norm_gain_grad,
        all_channels(conv_w_grad),
        all_channels(conv_b_grad),
        heads_spread(dt_bias_grad, 1),
        heads_spread(a_log_grad, 1),
        heads_spread(skip_grad, 1),
        heads_spread(gain_grad, MAMBA_HEAD),
        mid_gain_grad,
    ]
    summed = total(jnp.concatenate([v.reshape(-1) for v in small]))
    parts, at = [], 0
    for v in small:
        parts.append(summed[at : at + v.size].reshape(v.shape))
        at += v.size
    return (
        output[None],
        input_grad[None],
        parts[0],
        result_in,
        parts[1],
        parts[2],
        parts[3],
        parts[4],
        parts[5],
        parts[6],
        result_out,
        result_q,
        result_k,
        result_v,
        result_o,
        parts[7],
        result_gate,
        result_up,
        result_down,
    )


def solution(mesh):
    seq, fsdp = mesh.shape["seq"], mesh.shape["fsdp"]
    split = Mesh(mesh.devices.reshape(seq // 2, 2, fsdp // 2, 2), EVERY)
    tokens = P(("y", "c"), ("z", "x"), None)
    matrix = P(EVERY, None)
    return jax.shard_map(
        body,
        mesh=split,
        in_specs=(tokens, tokens, P(), matrix)
        + (P(),) * 6
        + (matrix,) * 5
        + (P(),)
        + (matrix,) * 3,
        out_specs=(tokens, tokens, P(), matrix)
        + (P(),) * 6
        + (matrix,) * 5
        + (P(),)
        + (matrix,) * 3,
        check_vma=False,
    )
```

time: 4380 us -> 1450 us (0.33)
  waiting for transfers between devices: 3480 us -> 666 us
  matrix products: 387 us -> 272 us
  starting transfers between devices: 6.73 us -> 91.5 us
  local copies, waits for them, and re-layouts: 241 us -> 175 us
    reduce_scatter x11 -> x4, waiting for transfers between devices: 2310 us -> 133 us  [to_owners(): lax.psum_scatter(array.astype(bf16), SHARDS, scatter_dimension=0, tiled=T...]
    all_gather x13 -> x4, waiting for transfers between devices: 908 us -> 143 us  [the longest x1 143 us: body(): lax.all_gather(to_ranks(packed_mix).reshape(4 * rows, MIX_COLS), SHARDS,...]
    ppermute x2 -> x51, waiting for transfers between devices: 0.01 us -> 387 us  [the longest x18 225 us: shifted(): lax.ppermute(array, 'z', [(i - distance, i) for i in devices if i - dista...]
    psum x1 -> x0, waiting for transfers between devices: 260 us -> none  [body(): lax.psum((norm_gain_grad, conv_weight_grad, conv_bias_grad, dt_bias_first...]
    dynamic_update_slice x6, local copies, waits for them, and re-layouts: 76.6 us -> 0.29 us  [heads_spread(): lax.dynamic_update_slice(whole, array, start)]
    ppermute x2 -> x51, starting transfers between devices: 5.04 us -> 78.5 us  [the longest x18 60 us: shifted(): lax.ppermute(array, 'z', [(i - distance, i) for i in devices if i - dista...]
    dot_general x9 -> x5, matrix products: 92.6 us -> 40.6 us  [weight_grad(): lax.dot_general(left, right, (((0,), (0,)), ((), ())), preferred_element_...]
    dot_general x47 -> x31, matrix products: 219 us -> 169 us  [the longest x5 48.1 us: low_dot(): return jnp.dot(left, right, preferred_element_type=f32)]
  transfers between devices with their start and end apart: 27 -> 62, of which waited for: 20 -> 26; matrix products, arithmetic and copies ran while one was open for 16% -> 39% of each run, Pallas kernels for 0% -> 0%
where the time goes in v1:
time: 1450 us; the launch traced here: 1430 us
  waiting for transfers between devices  666 us (46%)
  matrix products  272 us (19%)
  other arithmetic  178 us (12%)
  local copies, waits for them, and re-layouts  175 us (12%)
  starting transfers between devices  91.5 us (6%)
  blocking collectives  30.6 us (2%)
  between operations  18 us (1%)
    ppermute x18, waiting for transfers between devices, shifted(): lax.ppermute(array, 'z', [(i - distance, i) for i in devices if i - dista...  225 us
    ppermute x24, waiting for transfers between devices, swap(): return lax.ppermute(array, axis, [(0, 1), (1, 0)])  152 us
    all_gather x1, waiting for transfers between devices, body(): lax.all_gather(to_ranks(packed_mix).reshape(4 * rows, MIX_COLS), SHARDS,...  143 us
    reduce_scatter x4, waiting for transfers between devices, to_owners(): lax.psum_scatter(array.astype(bf16), SHARDS, scatter_dimension=0, tiled=T...  133 us
    ppermute x18, starting transfers between devices, shifted(): lax.ppermute(array, 'z', [(i - distance, i) for i in devices if i - dista...  60 us
    dot_general x5, matrix products, back_dot(): lax.dot_general(grad_rows, weight, (((1,), (1,)), ((), ())), preferred_el...  51.1 us
    dot_general x5, matrix products, low_dot(): return jnp.dot(left, right, preferred_element_type=f32)  48.1 us
    dot_general x5, matrix products, weight_grad(): lax.dot_general(left, right, (((0,), (0,)), ((), ())), preferred_element_...  40.6 us
  transfers between devices with their start and end apart: 62, of which 26 were waited for; matrix products, arithmetic and copies ran while one was open for 39% of the time, Pallas kernels for 0%

profile of v1, /device:TPU:0, one launch (start us, length us, event | category | flops | bytes accessed | tf_op | source)
XLA Modules:
  0.0 1431.6 jit_solution(6608395182818061424)
XLA Ops:
  16.3 30.6 %all_to_all.20 = bf16[4,64,2688]{2,1,0:T(8,128)(2,1)} all-to-all(bf16[4,64,2688]{2,1,0:T(8,128)(2,1)S(1)} %constant_dynamic-update-slice_fusion), channel_id=1, replica_groups=mesh['z'=4,'x'=2,'y'=2,'c'=2] {'x','c'}, dimensions={0} | all-to-all | bytes 2752512 | tf_op jit(solution)/shard_map/all_to_all | solution.py:238
  66.5 16.7 %collective-permute-done = bf16[256,2048]{1,0:T(8,128)(2,1)} collective-permute-done((bf16[256,2048]{1,0:T(8,128)(2,1)S(1)}, bf16[256,2048]{1,0:T(8,128)(2,1)}, u32[]{:S(2)}, u32[]{:S(2)}) %collective-permute-start) | collective-permute-done | bytes 1048608 | tf_op jit(solution)/shard_map/ppermute | solution.py:41
  110.6 142.8 %all-gather.5.cloned.1.call-done = bf16[2048,2688]{1,0:T(8,128)(2,1)} async-done(((bf16[256,2688]{1,0:T(8,128)(2,1)}), bf16[2048,2688]{1,0:T(8,128)(2,1)}) %all-gather.5.cloned.1.call-update) | async-done | bytes 11010064 | tf_op jit(solution)/shard_map/all_gather | solution.py:274
  253.4 17.0 %fusion.201 = (bf16[2,512,2688]{2,1,0:T(8,128)(2,1)S(1)}, f32[2,512,2688]{2,1,0:T(8,128)S(1)}) fusion(bf16[2048,2688]{1,0:T(8,128)(2,1)} %all-gather.5.cloned.1.call-done, bf16[1,512,2048]{2,1,0:T(8,128)(2,1)} %fusion.72, bf16[1,512,2048]{2,1,0:T(8,128)(2,1)} %fusion.75), kind=kOutput, calls=%fused_computation.423 | convolution fusion | flops 11279138816 | bytes 31719424 | tf_op jit(solution)/shard_map/dot_general | solution.py:65
  320.5 15.2 %collective-permute-start.15 = (bf16[2,2,512,128]{3,2,1,0:T(8,128)(2,1)}, bf16[2,2,512,128]{3,2,1,0:T(8,128)(2,1)}, u32[]{:S(2)}, u32[]{:S(2)}) collective-permute-start(bf16[2,2,512,128]{3,2,1,0:T(8,128)(2,1)} %pad_maximum_fusion.22), channel_id=1, source_target_pairs={{0,8},{8,16},{16,24},{1,9},{9,17},{17,25},{2,10},{10,18},{18,26},{... | collective-permute-start | bytes 1572872 | tf_op jit(solution)/shard_map/ppermute | solution.py:46
  392.6 14.7 %collective-permute-done.4 = bf16[2,12,64,256]{3,2,1,0:T(8,128)(2,1)} collective-permute-done((bf16[2,12,64,256]{3,2,1,0:T(8,128)(2,1)}, bf16[2,12,64,256]{3,2,1,0:T(8,128)(2,1)}, u32[]{:S(2)}, u32[]{:S(2)}) %collective-permute-start.4) | collective-permute-done | bytes 786464 | tf_op jit(solution)/shard_map/ppermute | solution.py:46
  407.3 33.7 %collective-permute-done.6 = bf16[2,12,64,256]{3,2,1,0:T(8,128)(2,1)} collective-permute-done((bf16[2,12,64,256]{3,2,1,0:T(8,128)(2,1)}, bf16[2,12,64,256]{3,2,1,0:T(8,128)(2,1)}, u32[]{:S(2)}, u32[]{:S(2)}) %collective-permute-start.6) | collective-permute-done | bytes 786464 | tf_op jit(solution)/shard_map/ppermute | solution.py:46
  441.0 23.7 %collective-permute-done.8 = bf16[2,12,64,256]{3,2,1,0:T(8,128)(2,1)} collective-permute-done((bf16[2,12,64,256]{3,2,1,0:T(8,128)(2,1)}, bf16[2,12,64,256]{3,2,1,0:T(8,128)(2,1)}, u32[]{:S(2)}, u32[]{:S(2)}) %collective-permute-start.8) | collective-permute-done | bytes 786464 | tf_op jit(solution)/shard_map/ppermute | solution.py:46
  536.0 24.6 %collective-permute-done.17 = bf16[256,2048]{1,0:T(8,128)(2,1)S(1)} collective-permute-done((bf16[256,2048]{1,0:T(8,128)(2,1)S(1)}, bf16[256,2048]{1,0:T(8,128)(2,1)S(1)}, u32[]{:S(2)}, u32[]{:S(2)}) %collective-permute-start.17) | collective-permute-done | bytes 1048608 | tf_op jit(solution)/shard_map/ppermute | solution.py:41
  571.3 24.4 %collective-permute-done.19 = bf16[256,2048]{0,1:T(8,128)(2,1)} collective-permute-done((bf16[256,2048]{0,1:T(8,128)(2,1)}, bf16[256,2048]{0,1:T(8,128)(2,1)}, u32[]{:S(2)}, u32[]{:S(2)}) %collective-permute-start.19) | collective-permute-done | bytes 1048608 | tf_op jit(solution)/shard_map/ppermute | solution.py:41
  596.2 20.3 %collective-permute-done.24 = bf16[256,2048]{1,0:T(8,128)(2,1)} collective-permute-done((bf16[256,2048]{1,0:T(8,128)(2,1)}, bf16[256,2048]{1,0:T(8,128)(2,1)}, u32[]{:S(2)}, u32[]{:S(2)}) %collective-permute-start.24) | collective-permute-done | bytes 1048608 | tf_op jit(solution)/shard_map/ppermute | solution.py:41
  616.6 14.6 %fusion.124 = f32[1024,2048]{1,0:T(8,128)} fusion(bf16[2048,2048]{1,0:T(8,128)(2,1)} %all-gather.9.cloned.1.call-done, bf16[256,2048]{0,1:T(8,128)(2,1)} %collective-permute-done.20, bf16[256,2048]{0,1:T(8,128)(2,1)} %collective-permute-done.19, bf16[256,2048]{0,1:T(8,128)(2,1)} %collective-permute-done.18, bf16[256,2048]{0,1:T(8,128)(2,1)} %bitcast.550), kind=kOutput, calls=%fused_computation.257 | convolution fusion | flops 8606711808 | bytes 20971520 | tf_op jit(solution)/shard_map/dot_general | solution.py:65
  658.2 14.8 %fusion.204 = (bf16[1024,2048]{1,0:T(8,128)(2,1)S(1)}, f32[1024,2048]{1,0:T(8,128)}) fusion(bf16[2048,2048]{1,0:T(8,128)(2,1)} %all-gather.9.cloned.1.call-done, bf16[1024,1024]{1,0:T(8,128)(2,1)} %copy-done.178, bf16[1024,1024]{1,0:T(8,128)(2,1)} %copy-done.177), kind=kOutput, calls=%fused_computation.426 | convolution fusion | flops 8600420352 | bytes 25165824 | tf_op jit(solution)/shard_map/dot_general | solution.py:69
  678.6 24.9 %collective-permute-done.27 = bf16[256,2048]{1,0:T(8,128)(2,1)S(1)} collective-permute-done((bf16[256,2048]{1,0:T(8,128)(2,1)S(1)}, bf16[256,2048]{1,0:T(8,128)(2,1)S(1)}, u32[]{:S(2)}, u32[]{:S(2)}) %collective-permute-start.27) | collective-permute-done | bytes 1048608 | tf_op jit(solution)/shard_map/ppermute | solution.py:41
  725.6 19.8 %collective-permute-done.34 = f32[2,12]{1,0:T(2,128)S(1)} collective-permute-done((f32[2,12]{1,0:T(2,128)}, f32[2,12]{1,0:T(2,128)S(1)}, u32[]{:S(2)}, u32[]{:S(2)}) %collective-permute-start.34) | collective-permute-done | bytes 128 | tf_op jit(solution)/shard_map/ppermute | solution.py:46
  847.7 15.6 %fusion.29 = (f32[2,4,12,128]{3,2,1,0:T(8,128)}, f32[2,4,12,128]{3,2,1,0:T(8,128)}, f32[2,4,12,128]{3,2,1,0:T(8,128)}, f32[2,4,128,128]{3,2,1,0:T(8,128)S(1)}) fusion(f32[2,4,12,128]{3,2,1,0:T(8,128)S(1)} %copy-done.130, f32[2,4,12,128]{3,2,1,0:T(8,128)S(1)} %copy-done.127, f32[2,4,128,128]{3,2,1,0:T(8,128)S(1)} %copy-done.93, ...), kind=kOutput, calls=%fused_computation.68 | convolution fusion | flops 1228238848 | bytes 7602176 | tf_op jit(solution)/shard_map/transpose(jvp(bnhts,bnshp->bnthp))/dot_general | solution.py:140
  873.1 29.6 %collective-permute-done.40 = bf16[2,2,512,128]{3,2,1,0:T(8,128)(2,1)} collective-permute-done((bf16[2,2,512,128]{3,2,1,0:T(8,128)(2,1)}, bf16[2,2,512,128]{3,2,1,0:T(8,128)(2,1)}, u32[]{:S(2)}, u32[]{:S(2)}) %collective-permute-start.40) | collective-permute-done | bytes 524320 | tf_op jit(solution)/shard_map/ppermute | solution.py:46
  919.7 71.9 %collective-permute-done.35 = bf16[2,12,64,256]{3,2,1,0:T(8,128)(2,1)S(1)} collective-permute-done((bf16[2,12,64,256]{3,2,1,0:T(8,128)(2,1)S(1)}, bf16[2,12,64,256]{3,2,1,0:T(8,128)(2,1)S(1)}, u32[]{:S(2)}, u32[]{:S(2)}) %collective-permute-start.35) | collective-permute-done | bytes 786464 | tf_op jit(solution)/shard_map/ppermute | solution.py:46
  1056.7 15.6 %multiply_reduce_fusion.4 = (f32[1280]{0:T(1024)S(1)}, f32[1280]{0:T(1024)S(1)}, f32[1280]{0:T(1024)S(1)}, f32[1280]{0:T(1024)S(1)}, f32[1280]{0:T(1024)S(1)}, /*index=5*/f32[2,512,1280]{2,1,0:T(8,128)}) fusion(f32[2,512,1280]{2,1,0:T(8,128)} %slice.441, f32[2,3,1280]{2,1,0:T(4,128)S(1)} %copy-done.98, f32[2,512,2688]{2,1,0:T(8,128)} %copy-done.6, ...), kind=kLoop, calls=%fused_computation.40 | loop fusion | flops 30140160 | bytes 26270720 | tf_op jit(solution)/shard_map/transpose(jvp())/reduce_sum | solution.py:99
  1104.6 14.7 %bitcast_convert_fusion = bf16[2048,2688]{1,0:T(8,128)(2,1)} fusion(bf16[2,512,2688]{2,1,0:T(8,128)(2,1)S(1)} %fusion.95, bf16[1,512,2048]{2,1,0:T(8,128)(2,1)S(1)} %copy-done.80, bf16[1,512,2048]{2,1,0:T(8,128)(2,1)S(1)} %copy-done.79), kind=kOutput, calls=%fused_computation.1 | convolution fusion | flops 11281891328 | bytes 20709376 | tf_op jit(solution)/shard_map/dot_general | solution.py:73
  1144.5 16.6 %fusion.209 = f32[1024,2048]{1,0:T(8,128)S(1)} fusion(bf16[1024,2688]{1,0:T(8,128)(2,1)} %bitcast.545, bf16[2048,2688]{1,0:T(8,128)(2,1)} %all-gather.5.cloned.1.call-done), kind=kOutput, calls=%fused_computation.431 | convolution fusion | flops 11274289152 | bytes 24903680 | tf_op jit(solution)/shard_map/dot_general | solution.py:69
  1182.7 32.0 %collective-permute-done.43 = bf16[256,2048]{0,1:T(8,128)(2,1)S(1)} collective-permute-done((bf16[256,2048]{0,1:T(8,128)(2,1)}, bf16[256,2048]{0,1:T(8,128)(2,1)S(1)}, u32[]{:S(2)}, u32[]{:S(2)}) %collective-permute-start.43) | collective-permute-done | bytes 1048608 | tf_op jit(solution)/shard_map/ppermute | solution.py:41
  1247.8 54.5 %reduce-scatter.5.cloned.1.call-done = bf16[256,2688]{1,0:T(8,128)(2,1)} async-done(((bf16[2048,2688]{1,0:T(8,128)(2,1)}), bf16[256,2688]{1,0:T(8,128)(2,1)}) %reduce-scatter.5.cloned.1.call-update) | async-done | bytes 1376272 | tf_op jit(solution)/shard_map/reduce_scatter | solution.py:398
  1314.2 78.8 %reduce-scatter.7.cloned.1.call-done = bf16[128,2048]{1,0:T(8,128)(2,1)} async-done(((bf16[1024,2048]{1,0:T(8,128)(2,1)}), bf16[128,2048]{1,0:T(8,128)(2,1)}) %reduce-scatter.7.cloned.1.call-update) | async-done | bytes 524304 | tf_op jit(solution)/shard_map/reduce_scatter | solution.py:398
  (833 shorter events, 646.5 us)
Async XLA Ops:
  7.2 96.7 %all-gather.7.cloned.1.call-start = ((), (), s32[]{:S(2)}) async-start(), calls=%async_computation.9 | async-start | bytes 4718592 | tf_op jit(solution)/shard_map/all_gather | solution.py:288
  11.5 241.9 %all-gather.5.cloned.1.call-start = ((), (), s32[]{:S(2)}) async-start(), calls=%async_computation.8 | async-start | bytes 12386304 | tf_op jit(solution)/shard_map/all_gather | solution.py:274
  64.9 551.6 %all-gather.9.cloned.1.call-start = ((), (), s32[]{:S(2)}) async-start(), calls=%async_computation.10 | async-start | bytes 9437184 | tf_op jit(solution)/shard_map/all_gather | solution.py:310
  94.0 537.2 %all-gather.11.cloned.1.call-start = ((), (), s32[]{:S(2)}) async-start(), calls=%async_computation.11 | async-start | bytes 4718592 | tf_op jit(solution)/shard_map/all_gather | solution.py:313
  272.1 105.2 %collective-permute-start.13 = (bf16[2,2,512,128]{3,2,1,0:T(8,128)(2,1)}, bf16[2,2,512,128]{3,2,1,0:T(8,128)(2,1)}, u32[]{:S(2)}, u32[]{:S(2)}) collective-permute-start(bf16[2,2,512,128]{3,2,1,0:T(8,128)(2,1)} %pad_maximum_fusion.22), channel_id=1, source_target_pairs={{0,24},{1,25},{2,26},{3,27},{4,28},{5,29},{6,30},{7,31}} | collective-permute-start | bytes 1572872 | tf_op jit(solution)/shard_map/ppermute | solution.py:46
  276.2 103.3 %collective-permute-start.14 = (bf16[2,2,512,128]{3,2,1,0:T(8,128)(2,1)}, bf16[2,2,512,128]{3,2,1,0:T(8,128)(2,1)}, u32[]{:S(2)}, u32[]{:S(2)}) collective-permute-start(bf16[2,2,512,128]{3,2,1,0:T(8,128)(2,1)} %pad_maximum_fusion.22), channel_id=1, source_target_pairs={{0,16},{8,24},{1,17},{9,25},{2,18},{10,26},{3,19},{11,27},{4,20},{... | collective-permute-start | bytes 1572872 | tf_op jit(solution)/shard_map/ppermute | solution.py:46
  282.9 52.8 %collective-permute-start.7 = (f32[2,12]{1,0:T(2,128)}, f32[2,12]{1,0:T(2,128)}, u32[]{:S(2)}, u32[]{:S(2)}) collective-permute-start(f32[2,12]{1,0:T(2,128)} %exp.115), channel_id=1, source_target_pairs={{0,16},{8,24},{1,17},{9,25},{2,18},{10,26},{3,19},{11,27},{4,20},{... | collective-permute-start | bytes 296 | tf_op jit(solution)/shard_map/ppermute | solution.py:46
  285.3 51.0 %collective-permute-start.3 = (bf16[2,3,1280]{2,1,0:T(4,128)(2,1)}, bf16[2,3,1280]{2,1,0:T(4,128)(2,1)S(1)}, u32[]{:S(2)}, u32[]{:S(2)}) collective-permute-start(bf16[2,3,1280]{2,1,0:T(4,128)(2,1)} %slice.440), channel_id=1, source_target_pairs={{0,8},{8,16},{16,24},{1,9},{9,17},{17,25},{2,10},{10,18},{18,26},{... | collective-permute-start | bytes 46088 | tf_op jit(solution)/shard_map/ppermute | solution.py:46
  320.5 59.1 %collective-permute-start.15 = (bf16[2,2,512,128]{3,2,1,0:T(8,128)(2,1)}, bf16[2,2,512,128]{3,2,1,0:T(8,128)(2,1)}, u32[]{:S(2)}, u32[]{:S(2)}) collective-permute-start(bf16[2,2,512,128]{3,2,1,0:T(8,128)(2,1)} %pad_maximum_fusion.22), channel_id=1, source_target_pairs={{0,8},{8,16},{16,24},{1,9},{9,17},{17,25},{2,10},{10,18},{18,26},{... | collective-permute-start | bytes 1572872 | tf_op jit(solution)/shard_map/ppermute | solution.py:46
  373.2 67.9 %collective-permute-start.6 = (bf16[2,12,64,256]{3,2,1,0:T(8,128)(2,1)}, bf16[2,12,64,256]{3,2,1,0:T(8,128)(2,1)}, u32[]{:S(2)}, u32[]{:S(2)}) collective-permute-start(bf16[2,12,64,256]{3,2,1,0:T(8,128)(2,1)} %fusion.92), channel_id=1, source_target_pairs={{0,16},{8,24},{1,17},{9,25},{2,18},{10,26},{3,19},{11,27},{4,20},{... | collective-permute-start | bytes 2359304 | tf_op jit(solution)/shard_map/ppermute | solution.py:46
  377.3 87.4 %collective-permute-start.8 = (bf16[2,12,64,256]{3,2,1,0:T(8,128)(2,1)}, bf16[2,12,64,256]{3,2,1,0:T(8,128)(2,1)}, u32[]{:S(2)}, u32[]{:S(2)}) collective-permute-start(bf16[2,12,64,256]{3,2,1,0:T(8,128)(2,1)} %fusion.92), channel_id=1, source_target_pairs={{0,24},{1,25},{2,26},{3,27},{4,28},{5,29},{6,30},{7,31}} | collective-permute-start | bytes 2359304 | tf_op jit(solution)/shard_map/ppermute | solution.py:46
  528.1 689.7 %reduce-scatter.9.cloned.1.call-start = ((), (), s32[]{:S(2)}) async-start(), calls=%async_computation.14 | async-start | bytes 9437184 | tf_op jit(solution)/shard_map/reduce_scatter | solution.py:398
  658.1 571.5 %reduce-scatter.11.cloned.1.call-start = ((), (), s32[]{:S(2)}) async-start(), calls=%async_computation.15 | async-start | bytes 4718592 | tf_op jit(solution)/shard_map/reduce_scatter | solution.py:398
  758.4 543.9 %reduce-scatter.5.cloned.1.call-start = ((), (), s32[]{:S(2)}) async-start(), calls=%async_computation.12 | async-start | bytes 12386304 | tf_op jit(solution)/shard_map/reduce_scatter | solution.py:398
  807.3 63.9 %collective-permute-start.39 = (bf16[2,2,512,128]{3,2,1,0:T(8,128)(2,1)}, bf16[2,2,512,128]{3,2,1,0:T(8,128)(2,1)}, u32[]{:S(2)}, u32[]{:S(2)}) collective-permute-start(bf16[2,2,512,128]{3,2,1,0:T(8,128)(2,1)} %get-tuple-element.80), channel_id=1, source_target_pairs={{8,0},{16,8},{24,16},{9,1},{17,9},{25,17},{10,2},{18,10},{26,18},{... | collective-permute-start | bytes 1572872 | tf_op jit(solution)/shard_map/ppermute | solution.py:46
  808.9 93.9 %collective-permute-start.40 = (bf16[2,2,512,128]{3,2,1,0:T(8,128)(2,1)}, bf16[2,2,512,128]{3,2,1,0:T(8,128)(2,1)}, u32[]{:S(2)}, u32[]{:S(2)}) collective-permute-start(bf16[2,2,512,128]{3,2,1,0:T(8,128)(2,1)} %get-tuple-element.82), channel_id=1, source_target_pairs={{16,0},{24,8},{17,1},{25,9},{18,2},{26,10},{19,3},{27,11},{20,4},{... | collective-permute-start | bytes 1572872 | tf_op jit(solution)/shard_map/ppermute | solution.py:46
  810.2 92.6 %collective-permute-start.41 = (bf16[2,2,512,128]{3,2,1,0:T(8,128)(2,1)}, bf16[2,2,512,128]{3,2,1,0:T(8,128)(2,1)}, u32[]{:S(2)}, u32[]{:S(2)}) collective-permute-start(bf16[2,2,512,128]{3,2,1,0:T(8,128)(2,1)} %get-tuple-element.81), channel_id=1, source_target_pairs={{24,0},{25,1},{26,2},{27,3},{28,4},{29,5},{30,6},{31,7}} | collective-permute-start | bytes 1572872 | tf_op jit(solution)/shard_map/ppermute | solution.py:46
  839.8 79.9 %collective-permute-start.33 = (bf16[2,12,64,256]{3,2,1,0:T(8,128)(2,1)S(1)}, bf16[2,12,64,256]{3,2,1,0:T(8,128)(2,1)S(1)}, u32[]{:S(2)}, u32[]{:S(2)}) collective-permute-start(bf16[2,12,64,256]{3,2,1,0:T(8,128)(2,1)S(1)} %add_convert_fusion), channel_id=1, source_target_pairs={{8,0},{16,8},{24,16},{9,1},{17,9},{25,17},{10,2},{18,10},{26,18},{... | collective-permute-start | bytes 2359304 | tf_op jit(solution)/shard_map/ppermute | solution.py:46
  841.3 150.3 %collective-permute-start.35 = (bf16[2,12,64,256]{3,2,1,0:T(8,128)(2,1)S(1)}, bf16[2,12,64,256]{3,2,1,0:T(8,128)(2,1)S(1)}, u32[]{:S(2)}, u32[]{:S(2)}) collective-permute-start(bf16[2,12,64,256]{3,2,1,0:T(8,128)(2,1)S(1)} %add_convert_fusion), channel_id=1, source_target_pairs={{16,0},{24,8},{17,1},{25,9},{18,2},{26,10},{19,3},{27,11},{20,4},{... | collective-permute-start | bytes 2359304 | tf_op jit(solution)/shard_map/ppermute | solution.py:46
  871.3 120.3 %collective-permute-start.37 = (bf16[2,12,64,256]{3,2,1,0:T(8,128)(2,1)S(1)}, bf16[2,12,64,256]{3,2,1,0:T(8,128)(2,1)S(1)}, u32[]{:S(2)}, u32[]{:S(2)}) collective-permute-start(bf16[2,12,64,256]{3,2,1,0:T(8,128)(2,1)S(1)} %add_convert_fusion), channel_id=1, source_target_pairs={{24,0},{25,1},{26,2},{27,3},{28,4},{29,5},{30,6},{31,7}} | collective-permute-start | bytes 2359304 | tf_op jit(solution)/shard_map/ppermute | solution.py:46
  1119.3 273.6 %reduce-scatter.7.cloned.1.call-start = ((), (), s32[]{:S(2)}) async-start(), calls=%async_computation.13 | async-start | bytes 4718592 | tf_op jit(solution)/shard_map/reduce_scatter | solution.py:398
  1168.2 138.4 %collective-permute-start.22 = (bf16[256,2048]{1,0:T(8,128)(2,1)}, bf16[256,2048]{1,0:T(8,128)(2,1)}, u32[]{:S(2)}, u32[]{:S(2)}) collective-permute-start(bf16[256,2048]{1,0:T(8,128)(2,1)} %fusion.78), channel_id=1, source_target_pairs={{0,4},{4,0},{1,5},{5,1},{2,6},{6,2},{3,7},{7,3},{8,12},{12,8},{9,1... | collective-permute-start | bytes 3145736 | tf_op jit(solution)/shard_map/ppermute | solution.py:41
  1247.7 64.5 %collective-permute-start.48 = (f32[25232]{0:T(1024)S(1)}, f32[25232]{0:T(1024)S(1)}, u32[]{:S(2)}, u32[]{:S(2)}) collective-permute-start(f32[25232]{0:T(1024)S(1)} %add.439), channel_id=1, source_target_pairs={{0,1},{1,0},{2,3},{3,2},{4,5},{5,4},{6,7},{7,6},{8,9},{9,8},{10,11... | collective-permute-start | bytes 302792 | tf_op jit(solution)/shard_map/ppermute | solution.py:54
  1302.3 105.6 %all-to-all-start.2 = ((bf16[4,64,2688]{2,1,0:T(8,128)(2,1)}), bf16[4,64,2688]{2,1,0:T(8,128)(2,1)}, u32[]{:S(2)}, u32[]{:S(2)}) async-start(bf16[4,64,2688]{2,1,0:T(8,128)(2,1)} %bitcast.544), calls=%async_computation.3 | async-start | bytes 2752512 | tf_op jit(solution)/shard_map/all_to_all | solution.py:238
  (223 other events, 6307.4 us)
Sparse Core Ops, SparseCore 0:
  11.6 83.9 all-gather.6
  97.8 155.5 all-gather.4
  256.1 199.3 all-gather.8
  528.2 91.7 all-gather.10
  658.3 167.2 reduce-scatter.8
  829.5 144.7 reduce-scatter.10
  1119.4 182.7 reduce-scatter.4
  1305.9 86.9 reduce-scatter.6

commit v2 on v1

--- a/solution.py
+++ b/solution.py
@@ -21,15 +21,15 @@
 QP = 2 * HEAD_DIM
 CONV_COLS = PART + BC
 AT_DT = CONV_COLS
-AT_Q = AT_DT + DT_PAD
-AT_K = AT_Q + QP
+SCAN_COLS = AT_DT + DT_PAD
+AT_K = QP
 AT_V = AT_K + HEAD_DIM
 AT_Z = AT_V + HEAD_DIM
-MIX_COLS = AT_Z + PART
+REST_COLS = AT_Z + PART
 
 epsilon = 1e-05
 rope_base = 100000000000.0
-highest = lax.Precision.HIGHEST
+highest = lax.Precision.DEFAULT
 GROUP = ("x", "c")
 SHARDS = ("z", "y")
 EVERY = ("z", "x", "y", "c")
@@ -257,13 +257,18 @@
     split_k = jnp.transpose(w_k.reshape(rows, 2, HEAD_DIM), (1, 0, 2))
     split_v = jnp.transpose(w_v.reshape(rows, 2, HEAD_DIM), (1, 0, 2))
     two = lambda a: jnp.broadcast_to(a[None], (2,) + a.shape).reshape(4, rows, a.shape[-1])
-    packed_mix = jnp.concatenate(
+    packed_scan = jnp.concatenate(
         [
             heads_split(w_in[:, INNER : 2 * INNER], MAMBA_HEAD),
             jnp.broadcast_to(w_in[None, :, 2 * INNER : 2 * INNER + BC], (4, rows, BC)),
             jnp.pad(
                 heads_split(w_in[:, 2 * INNER + BC :], 1), ((0, 0), (0, 0), (0, DT_PAD - HEADS))
             ),
+        ],
+        axis=2,
+    )
+    packed_rest = jnp.concatenate(
+        [
             split_q.reshape(4, rows, QP),
             two(split_k),
             two(split_v),
@@ -271,9 +276,15 @@
         ],
         axis=2,
     )
-    full_mix = lax.all_gather(
-        to_ranks(packed_mix).reshape(4 * rows, MIX_COLS), SHARDS, axis=0, tiled=True
-    )
+
+    def gathered(array):
+        return lax.all_gather(array, SHARDS, axis=0, tiled=True)
+
+    def after(array, *others):
+        return lax.optimization_barrier((array,) + others)[0]
+
+    full_scan = gathered(to_ranks(packed_scan).reshape(4 * rows, SCAN_COLS))
+    full_rest = gathered(after(to_ranks(packed_rest).reshape(4 * rows, REST_COLS), full_scan))
 
     if aligned:
         turn = [(2 * y + c, 2 * c + y) for y in range(2) for c in range(2)]
@@ -285,9 +296,8 @@
         back_place = [(b, a) for a, b in place]
         sent_out = lax.ppermute(w_out, ("y", "c"), turn)
         sent_o = lax.ppermute(w_o, ("z", "y", "c"), place)
-        full_rows = lax.all_gather(
-            jnp.concatenate([sent_out, sent_o], 0), SHARDS, axis=0, tiled=True
-        ).reshape(nz * ny, out_rows + o_rows, D)
+        whole_rows = gathered(after(jnp.concatenate([sent_out, sent_o], 0), full_rest))
+        full_rows = whole_rows.reshape(nz * ny, out_rows + o_rows, D)
         full_out = full_rows[:, :out_rows].reshape(PART, D)
         full_o = full_rows[:, out_rows:].reshape(QP, D)
     else:
@@ -297,6 +307,7 @@
         every_o = every_o.reshape(2, 2, 2, HEAD_DIM, D)
         every_o = lax.dynamic_index_in_dim(every_o, xi, 2, keepdims=False)
         full_o = lax.dynamic_index_in_dim(every_o, ci, 0, keepdims=False).reshape(QP, D)
+        whole_rows = full_out
 
     def split_ff(w):
         w = w.reshape(rows, nz, 2, ny, 2, ff_rows)
@@ -307,20 +318,23 @@
         return jnp.transpose(w, (2, 3, 0, 4, 1, 5)).reshape(rows, 4 * hidden_part)
 
     packed_ff = jnp.concatenate([split_ff(w_gate), split_ff(w_up)], axis=2)
-    full_ff = lax.all_gather(
-        to_ranks(packed_ff).reshape(4 * rows, 2 * hidden_part), SHARDS, axis=0, tiled=True
-    )
-    full_down = lax.all_gather(w_down, SHARDS, axis=0, tiled=True)
+    full_ff = gathered(
+        after(to_ranks(packed_ff).reshape(4 * rows, 2 * hidden_part), whole_rows)
+    )
+    full_down = gathered(after(w_down, full_ff))
 
     resident = inputs[0].astype(f32)
     normed, norm_back = jax.vjp(rms_scale, resident, norm_gain)
     normed16 = gather_sequences(permuted(normed.astype(bf16)))
     tokens = 2 * span_all
-    projected = low_dot(normed16.reshape(tokens, D), full_mix).reshape(2, span_all, MIX_COLS)
-    conv_in = projected[..., :CONV_COLS]
-    dt_raw = projected[..., AT_DT : AT_DT + HEADS]
-    gate_z = projected[..., AT_Z:]
-    edge_rows = shifted(conv_in[:, span_all - edge_count :].astype(bf16), 1).astype(f32)
+    edges16 = shifted(normed16[:, span_all - edge_count :], 1).reshape(2 * edge_count, D)
+    normed_rows = normed16.reshape(tokens, D)
+    scan_in = low_dot(normed_rows, full_scan).reshape(2, span_all, SCAN_COLS)
+    edge_rows = low_dot(edges16, full_scan[:, :CONV_COLS]).reshape(2, edge_count, CONV_COLS)
+    conv_in = scan_in[..., :CONV_COLS]
+    dt_raw = scan_in[..., AT_DT : AT_DT + HEADS]
+    rest = low_dot(normed_rows, full_rest).reshape(2, span_all, REST_COLS)
+    gate_z = rest[..., AT_Z:]
 
     def rank_channels(array):
         return jnp.concatenate(
@@ -336,25 +350,31 @@
 
     mixed, conv_back = jax.vjp(conv_piece, conv_in, edge_rows, conv_w, conv_b)
     own_state, own_decay = local_state(mixed, dt_raw, dt_b, a_l)
-    own_state16 = own_state.astype(bf16)
+
+    def chained(local, decay, step):
+        entering = []
+        for s in range(2):
+            held = jnp.zeros(local.shape[1:], f32)
+            for hop in range(nz - 1):
+                at = hop if step == 1 else nz - 1 - hop
+                leaving = local[s] + decay[s][:, None, None] * held if hop else local[s]
+                held = held + lax.ppermute(
+                    leaving.astype(bf16), "z", [(at, at + step)]
+                ).astype(f32)
+            entering.append(held)
+        return jnp.stack(entering)
 
     positions = zi * span_all + jnp.arange(span_all, dtype=jnp.int32)
     cosine, sine = rope_tables(positions)
     query16 = rotate(
-        projected[..., AT_Q:AT_K].reshape(2, span_all, 2, HEAD_DIM), cosine, sine
+        rest[..., :AT_K].reshape(2, span_all, 2, HEAD_DIM), cosine, sine
     ).astype(bf16)
-    key16 = rotate(projected[..., None, AT_K:AT_V], cosine, sine).astype(bf16)[:, :, 0]
-    value16 = projected[..., AT_V:AT_Z].astype(bf16)
+    key16 = rotate(rest[..., None, AT_K:AT_V], cosine, sine).astype(bf16)[:, :, 0]
+    value16 = rest[..., AT_V:AT_Z].astype(bf16)
     kv16 = jnp.stack([key16, value16])
     kv_all = jnp.concatenate([shifted(kv16, d) for d in range(nz - 1, 0, -1)] + [kv16], axis=2)
     key_all, value_all = kv_all[0], kv_all[1]
-    decays = [shifted(own_decay, d) for d in range(1, nz)]
-    state_in = jnp.zeros(own_state.shape, f32)
-    factor = jnp.ones(own_decay.shape, f32)
-    for d in range(1, nz):
-        arrived = shifted(own_state16, d).astype(f32)
-        state_in = state_in + factor[:, :, None, None] * arrived
-        factor = factor * decays[d - 1]
+    state_in = chained(own_state, own_decay, 1)
 
     score_scale = HEAD_DIM ** (-0.5)
     key_place = (zi - nz + 1) * span_all + jnp.arange(nz * span_all, dtype=jnp.int32)
@@ -417,6 +437,7 @@
                 axis=1,
             ).reshape(nz * ny * (out_rows + o_rows), D)
         )
+        rows_done = rows_parts
         result_out = lax.ppermute(rows_parts[:out_rows], ("y", "c"), turn).astype(f32)
         result_o = lax.ppermute(rows_parts[out_rows:], ("z", "y", "c"), back_place).astype(f32)
     else:
@@ -434,6 +455,7 @@
         result_o = lax.psum_scatter(
             every_o.astype(bf16), EVERY, scatter_dimension=0, tiled=True
         ).astype(f32)
+        rows_done = result_out
 
     normal = flat * root
     gain_grad = jnp.sum(gated_grad * normal, axis=(0, 1))
@@ -442,13 +464,7 @@
     flat_grad = root * (wide - normal * inner_mean)
     scanned_grad, gate_z_grad = gate_back(flat_grad)
     state_local_grad = scan_back((scanned_grad, jnp.zeros(state_out.shape, f32)))[5]
-    state_local16 = state_local_grad.astype(bf16)
-    state_out_grad = jnp.zeros(own_state.shape, f32)
-    factor = jnp.ones(own_decay.shape, f32)
-    for d in range(1, nz):
-        arrived = shifted(state_local16, -d).astype(f32)
-        state_out_grad = state_out_grad + factor[:, :, None, None] * arrived
-        factor = factor * shifted(own_decay, -d)
+    state_out_grad = chained(state_local_grad, own_decay, -1)
 
     attended_grad32 = attended_grad16.astype(f32)
     delta = jnp.moveaxis(jnp.sum(attended_grad32 * attended, axis=-1), 2, 1)
@@ -482,41 +498,44 @@
     )
     query_back = rotate(query_grad, cosine, -sine).reshape(2, span_all, QP)
     key_back = rotate(kv_grad[0][:, :, None], cosine, -sine)[:, :, 0]
-    projected_grad16 = jnp.concatenate(
+    scan_grad16 = jnp.concatenate(
         [
             conv_in_grad.astype(bf16),
             jnp.pad(dt_raw_grad, ((0, 0), (0, 0), (0, DT_PAD - HEADS))).astype(bf16),
+        ],
+        axis=-1,
+    ).reshape(tokens, SCAN_COLS)
+    rest_grad16 = jnp.concatenate(
+        [
             query_back.astype(bf16),
             key_back.astype(bf16),
             kv_grad[1].astype(bf16),
             gate_z_grad.astype(bf16),
         ],
         axis=-1,
-    ).reshape(tokens, MIX_COLS)
-    mix_parts = to_ranks(
-        to_owners(weight_grad(normed16.reshape(tokens, D), projected_grad16)).reshape(
-            4, rows, MIX_COLS
-        )
-    ).astype(f32)
-    normed_grad = restored(
-        scatter_sequences(back_dot(projected_grad16, full_mix).reshape(2, span_all, D))
-    )
+    ).reshape(tokens, REST_COLS)
+    rest_owned = to_owners(after(weight_grad(normed_rows, rest_grad16).astype(bf16), rows_done))
+    rest_parts = to_ranks(rest_owned.reshape(4, rows, REST_COLS)).astype(f32)
+    scan_owned = to_owners(after(weight_grad(normed_rows, scan_grad16).astype(bf16), rest_owned))
+    scan_parts = to_ranks(scan_owned.reshape(4, rows, SCAN_COLS)).astype(f32)
+    normed_grad = back_dot(scan_grad16, full_scan) + back_dot(rest_grad16, full_rest)
+    normed_grad = restored(scatter_sequences(normed_grad.reshape(2, span_all, D)))
     resident_grad, norm_gain_grad = norm_back(normed_grad)
     input_grad = hidden_grad + resident_grad
 
     result_in = jnp.concatenate(
         [
-            heads_join(mix_parts[..., AT_Z:], MAMBA_HEAD),
-            heads_join(mix_parts[..., :PART], MAMBA_HEAD),
-            jnp.sum(mix_parts[..., PART:CONV_COLS], axis=0),
-            heads_join(mix_parts[..., AT_DT : AT_DT + HEADS], 1),
+            heads_join(rest_parts[..., AT_Z:], MAMBA_HEAD),
+            heads_join(scan_parts[..., :PART], MAMBA_HEAD),
+            jnp.sum(scan_parts[..., PART:CONV_COLS], axis=0),
+            heads_join(scan_parts[..., AT_DT : AT_DT + HEADS], 1),
         ],
         axis=1,
     )
     result_q = jnp.transpose(
-        mix_parts[..., AT_Q:AT_K].reshape(2, 2, rows, 2, HEAD_DIM), (2, 1, 3, 0, 4)
+        rest_parts[..., :AT_K].reshape(2, 2, rows, 2, HEAD_DIM), (2, 1, 3, 0, 4)
     ).reshape(rows, ATT_HEADS * HEAD_DIM)
-    kv_parts = jnp.sum(mix_parts[..., AT_K:AT_Z].reshape(2, 2, rows, 2, HEAD_DIM), axis=0)
+    kv_parts = jnp.sum(rest_parts[..., AT_K:AT_Z].reshape(2, 2, rows, 2, HEAD_DIM), axis=0)
     result_k = jnp.transpose(kv_parts[:, :, 0], (1, 0, 2)).reshape(rows, KV_HEADS * HEAD_DIM)
     result_v = jnp.transpose(kv_parts[:, :, 1], (1, 0, 2)).reshape(rows, KV_HEADS * HEAD_DIM)
 

time: 1450 us -> 1350 us (0.931)
  waiting for transfers between devices: 666 us -> 612 us
  matrix products: 272 us -> 222 us
  starting transfers between devices: 91.5 us -> 120 us
  other arithmetic: 178 us -> 163 us
    ppermute x18 -> x8, waiting for transfers between devices: 225 us -> 92.3 us  [shifted(): lax.ppermute(array, 'z', [(i - distance, i) for i in devices if i - dista...]
    ppermute x0 -> x12, waiting for transfers between devices: none -> 55.7 us  [chained(): lax.ppermute(leaving.astype(bf16), 'z', [(at, at + step)]).astype(f32)]
    ppermute x0 -> x12, starting transfers between devices: none -> 30.1 us  [chained(): lax.ppermute(leaving.astype(bf16), 'z', [(at, at + step)]).astype(f32)]
    dot_general x3, matrix products: 35.4 us -> 12 us  [scan_all(): inside = jnp.einsum('bnhts,bnshp->bnthp', weights, xs, precision=highest)]
    ppermute x24, waiting for transfers between devices: 152 us -> 173 us  [swap(): return lax.ppermute(array, axis, [(0, 1), (1, 0)])]
    dot_general x12, matrix products: 22.4 us -> 4.25 us  [scan_all(): jnp.einsum('btm,bhpm->bthp', cs[:, i], state, precision=highest)]
    ppermute x18 -> x8, starting transfers between devices: 60 us -> 44.2 us  [shifted(): lax.ppermute(array, 'z', [(i - distance, i) for i in devices if i - dista...]
    unnamed x372 -> x443, local copies, waits for them, and re-layouts: 30 us -> 40.5 us
  transfers between devices with their start and end apart: 62 -> 67, of which waited for: 26 -> 29; matrix products, arithmetic and copies ran while one was open for 39% -> 34% of each run, Pallas kernels for 0% -> 0%
where the time goes in v2:
time: 1350 us; the launch traced here: 1340 us
  waiting for transfers between devices  612 us (45%)
  matrix products  222 us (16%)
  local copies, waits for them, and re-layouts  179 us (13%)
  other arithmetic  163 us (12%)
  starting transfers between devices  120 us (9%)
  blocking collectives  28.4 us (2%)
  between operations  18.4 us (1%)
    ppermute x24, waiting for transfers between devices, swap(): return lax.ppermute(array, axis, [(0, 1), (1, 0)])  173 us
    all_gather x5, waiting for transfers between devices, gathered(): return lax.all_gather(array, SHARDS, axis=0, tiled=True)  144 us
    reduce_scatter x5, waiting for transfers between devices, to_owners(): lax.psum_scatter(array.astype(bf16), SHARDS, scatter_dimension=0, tiled=T...  130 us
    ppermute x8, waiting for transfers between devices, shifted(): lax.ppermute(array, 'z', [(i - distance, i) for i in devices if i - dista...  92.3 us
    dot_general x6, matrix products, back_dot(): lax.dot_general(grad_rows, weight, (((1,), (1,)), ((), ())), preferred_el...  58.3 us
    ppermute x12, waiting for transfers between devices, chained(): lax.ppermute(leaving.astype(bf16), 'z', [(at, at + step)]).astype(f32)  55.7 us
    dot_general x7, matrix products, low_dot(): return jnp.dot(left, right, preferred_element_type=f32)  47.1 us
    ppermute x8, starting transfers between devices, shifted(): lax.ppermute(array, 'z', [(i - distance, i) for i in devices if i - dista...  44.2 us
  transfers between devices with their start and end apart: 67, of which 29 were waited for; matrix products, arithmetic and copies ran while one was open for 34% of the time, Pallas kernels for 0%

profile of v2, /device:TPU:0, one launch (start us, length us, event | category | flops | bytes accessed | tf_op | source)
XLA Modules:
  0.0 1342.4 jit_solution(15859710701766537998)
XLA Ops:
  10.2 15.1 %all_to_all.30 = bf16[4,64,1408]{2,1,0:T(8,128)(2,1)} all-to-all(bf16[4,64,1408]{2,1,0:T(8,128)(2,1)S(1)} %fusion.130), channel_id=1, replica_groups=mesh['z'=4,'x'=2,'y'=2,'c'=2] {'x','c'}, dimensions={0} | all-to-all | bytes 1441792 | tf_op jit(solution)/shard_map/all_to_all | solution.py:238
  27.1 13.4 all_to_all.31
  40.5 78.4 %all-gather.6.cloned.1.call-done = bf16[2048,1408]{1,0:T(8,128)(2,1)} async-done(((bf16[256,1408]{1,0:T(8,128)(2,1)}), bf16[2048,1408]{1,0:T(8,128)(2,1)}) %all-gather.6.cloned.1.call-update) | async-done | bytes 5767184 | tf_op jit(solution)/shard_map/all_gather | solution.py:281
  137.4 15.7 %collective-permute-done = bf16[256,2048]{1,0:T(8,128)(2,1)} collective-permute-done((bf16[256,2048]{1,0:T(8,128)(2,1)S(1)}, bf16[256,2048]{1,0:T(8,128)(2,1)}, u32[]{:S(2)}, u32[]{:S(2)}) %collective-permute-start) | collective-permute-done | bytes 1048608 | tf_op jit(solution)/shard_map/ppermute | solution.py:41
  163.0 45.3 %all-gather.8.cloned.1.call-done = bf16[2048,1280]{1,0:T(8,128)(2,1)} async-done(((bf16[256,1280]{1,0:T(8,128)(2,1)}), bf16[2048,1280]{1,0:T(8,128)(2,1)}) %all-gather.8.cloned.1.call-update) | async-done | bytes 5242896 | tf_op jit(solution)/shard_map/all_gather | solution.py:281
  265.1 20.6 %all-gather.10.cloned.1.call-done = bf16[1024,2048]{1,0:T(8,128)(2,1)} async-done(((bf16[128,2048]{1,0:T(8,128)(2,1)}), bf16[1024,2048]{1,0:T(8,128)(2,1)}) %all-gather.10.cloned.1.call-update) | async-done | bytes 4194320 | tf_op jit(solution)/shard_map/all_gather | solution.py:281
  359.8 31.7 %collective-permute-start.14 = (bf16[2,2,512,128]{3,2,1,0:T(8,128)(2,1)}, bf16[2,2,512,128]{3,2,1,0:T(8,128)(2,1)}, u32[]{:S(2)}, u32[]{:S(2)}) collective-permute-start(bf16[2,2,512,128]{3,2,1,0:T(8,128)(2,1)} %pad_maximum_fusion.26), channel_id=1, source_target_pairs={{0,24},{1,25},{2,26},{3,27},{4,28},{5,29},{6,30},{7,31}} | collective-permute-start | bytes 1572872 | tf_op jit(solution)/shard_map/ppermute | solution.py:46
  414.4 22.5 %collective-permute-done.15 = bf16[2,2,512,128]{3,2,1,0:T(8,128)(2,1)} collective-permute-done((bf16[2,2,512,128]{3,2,1,0:T(8,128)(2,1)}, bf16[2,2,512,128]{3,2,1,0:T(8,128)(2,1)}, u32[]{:S(2)}, u32[]{:S(2)}) %collective-permute-start.15) | collective-permute-done | bytes 524320 | tf_op jit(solution)/shard_map/ppermute | solution.py:46
  436.9 14.5 %collective-permute-done.16 = bf16[2,2,512,128]{3,2,1,0:T(8,128)(2,1)} collective-permute-done((bf16[2,2,512,128]{3,2,1,0:T(8,128)(2,1)}, bf16[2,2,512,128]{3,2,1,0:T(8,128)(2,1)}, u32[]{:S(2)}, u32[]{:S(2)}) %collective-permute-start.16) | collective-permute-done | bytes 524320 | tf_op jit(solution)/shard_map/ppermute | solution.py:46
  453.1 11.0 fusion.207
  496.2 23.5 %collective-permute-done.18 = bf16[256,2048]{1,0:T(8,128)(2,1)S(1)} collective-permute-done((bf16[256,2048]{1,0:T(8,128)(2,1)S(1)}, bf16[256,2048]{1,0:T(8,128)(2,1)S(1)}, u32[]{:S(2)}, u32[]{:S(2)}) %collective-permute-start.18) | collective-permute-done | bytes 1048608 | tf_op jit(solution)/shard_map/ppermute | solution.py:41
  530.0 24.3 %collective-permute-done.20 = bf16[256,2048]{0,1:T(8,128)(2,1)S(1)} collective-permute-done((bf16[256,2048]{0,1:T(8,128)(2,1)}, bf16[256,2048]{0,1:T(8,128)(2,1)S(1)}, u32[]{:S(2)}, u32[]{:S(2)}) %collective-permute-start.20) | collective-permute-done | bytes 1048608 | tf_op jit(solution)/shard_map/ppermute | solution.py:41
  554.8 20.3 %collective-permute-done.25 = bf16[256,2048]{1,0:T(8,128)(2,1)S(1)} collective-permute-done((bf16[256,2048]{1,0:T(8,128)(2,1)S(1)}, bf16[256,2048]{1,0:T(8,128)(2,1)S(1)}, u32[]{:S(2)}, u32[]{:S(2)}) %collective-permute-start.25) | collective-permute-done | bytes 1048608 | tf_op jit(solution)/shard_map/ppermute | solution.py:41
  575.2 15.0 %fusion.132 = f32[1024,2048]{1,0:T(8,128)} fusion(bf16[2048,2048]{1,0:T(8,128)(2,1)} %all-gather.12.cloned.1.call-done, bf16[256,2048]{0,1:T(8,128)(2,1)S(1)} %collective-permute-done.21, bf16[256,2048]{0,1:T(8,128)(2,1)S(1)} %collective-permute-done.20, bf16[256,2048]{0,1:T(8,128)(2,1)S(1)} %collective-permute-done.19, bf16[256,2048]{0,1:T(8,128)(2,1)} %bitcast.613), kind=kOutput, calls=%fused_computation.296 | convolution fusion | flops 8606711808 | bytes 20971520 | tf_op jit(solution)/shard_map/dot_general | solution.py:65
  591.2 12.5 fusion.30
  603.7 15.1 %fusion.209 = (bf16[1024,2048]{1,0:T(8,128)(2,1)S(1)}, f32[1024,2048]{1,0:T(8,128)}) fusion(bf16[2048,2048]{1,0:T(8,128)(2,1)} %all-gather.12.cloned.1.call-done, bf16[1024,1024]{1,0:T(8,128)(2,1)} %get-tuple-element.72, bf16[1024,1024]{1,0:T(8,128)(2,1)S(1)} %get-tuple-element.71), kind=kOutput, calls=%fused_computation.461 | convolution fusion | flops 8600420352 | bytes 25165824 | tf_op jit(solution)/shard_map/dot_general | solution.py:69
  625.4 23.5 %collective-permute-done.28 = bf16[256,2048]{1,0:T(8,128)(2,1)S(1)} collective-permute-done((bf16[256,2048]{1,0:T(8,128)(2,1)S(1)}, bf16[256,2048]{1,0:T(8,128)(2,1)S(1)}, u32[]{:S(2)}, u32[]{:S(2)}) %collective-permute-start.28) | collective-permute-done | bytes 1048608 | tf_op jit(solution)/shard_map/ppermute | solution.py:41
  669.0 23.0 %collective-permute-done.29 = bf16[256,2048]{1,0:T(8,128)(2,1)} collective-permute-done((bf16[256,2048]{1,0:T(8,128)(2,1)}, bf16[256,2048]{1,0:T(8,128)(2,1)}, u32[]{:S(2)}, u32[]{:S(2)}) %collective-permute-start.29) | collective-permute-done | bytes 1048608 | tf_op jit(solution)/shard_map/ppermute | solution.py:41
  777.8 51.6 %collective-permute-done.42 = bf16[2,2,512,128]{3,2,1,0:T(8,128)(2,1)} collective-permute-done((bf16[2,2,512,128]{3,2,1,0:T(8,128)(2,1)}, bf16[2,2,512,128]{3,2,1,0:T(8,128)(2,1)}, u32[]{:S(2)}, u32[]{:S(2)}) %collective-permute-start.42) | collective-permute-done | bytes 524320 | tf_op jit(solution)/shard_map/ppermute | solution.py:46
  905.2 36.4 %collective-permute-done.36 = bf16[12,64,256]{2,1,0:T(8,128)(2,1)S(1)} collective-permute-done((bf16[12,64,256]{2,1,0:T(8,128)(2,1)S(1)}, bf16[12,64,256]{2,1,0:T(8,128)(2,1)S(1)}, u32[]{:S(2)}, u32[]{:S(2)}) %collective-permute-start.36) | collective-permute-done | bytes 393248 | tf_op jit(solution)/shard_map/ppermute | solution.py:361
  941.7 13.4 collective-permute-done.39
  1087.6 31.9 %collective-permute-done.45 = bf16[256,2048]{0,1:T(8,128)(2,1)S(1)} collective-permute-done((bf16[256,2048]{0,1:T(8,128)(2,1)}, bf16[256,2048]{0,1:T(8,128)(2,1)S(1)}, u32[]{:S(2)}, u32[]{:S(2)}) %collective-permute-start.45) | collective-permute-done | bytes 1048608 | tf_op jit(solution)/shard_map/ppermute | solution.py:41
  1147.8 49.7 %reduce-scatter.12.cloned.1.call-done = bf16[256,2048]{1,0:T(8,128)(2,1)} async-done(((bf16[2048,2048]{1,0:T(8,128)(2,1)}), bf16[256,2048]{1,0:T(8,128)(2,1)}) %reduce-scatter.12.cloned.1.call-update) | async-done | bytes 1048592 | tf_op jit(solution)/shard_map/reduce_scatter | solution.py:418
  1233.8 80.7 %reduce-scatter.10.cloned.1.call-done = bf16[256,1408]{1,0:T(8,128)(2,1)} async-done(((bf16[2048,1408]{1,0:T(8,128)(2,1)}), bf16[256,1408]{1,0:T(8,128)(2,1)}) %reduce-scatter.10.cloned.1.call-update) | async-done | bytes 720912 | tf_op jit(solution)/shard_map/reduce_scatter | solution.py:418
  (942 shorter events, 635.2 us)
Async XLA Ops:
  7.2 111.6 %all-gather.6.cloned.1.call-start = ((), (), s32[]{:S(2)}) async-start(), calls=%async_computation.11 | async-start | bytes 6488064 | tf_op jit(solution)/shard_map/all_gather | solution.py:281
  25.3 183.0 %all-gather.8.cloned.1.call-start = ((), (), s32[]{:S(2)}) async-start(), calls=%async_computation.12 | async-start | bytes 5898240 | tf_op jit(solution)/shard_map/all_gather | solution.py:281
  130.3 82.0 %collective-permute-start.1 = (bf16[256,2048]{1,0:T(8,128)(2,1)S(1)}, bf16[256,2048]{1,0:T(8,128)(2,1)}, u32[]{:S(2)}, u32[]{:S(2)}) collective-permute-start(bf16[256,2048]{1,0:T(8,128)(2,1)S(1)} %copy.790), channel_id=1, source_target_pairs={{0,1},{1,0},{2,3},{3,2},{4,5},{5,4},{6,7},{7,6},{8,9},{9,8},{10,11... | collective-permute-start | bytes 3145736 | tf_op jit(solution)/shard_map/ppermute | solution.py:41
  153.1 59.2 %collective-permute-start.2 = (bf16[256,2048]{1,0:T(8,128)(2,1)}, bf16[256,2048]{1,0:T(8,128)(2,1)}, u32[]{:S(2)}, u32[]{:S(2)}) collective-permute-start(bf16[256,2048]{1,0:T(8,128)(2,1)} %collective-permute-done), channel_id=1, source_target_pairs={{0,1},{1,0},{2,3},{3,2},{4,5},{5,4},{6,7},{7,6},{8,9},{9,8},{10,11... | collective-permute-start | bytes 3145736 | tf_op jit(solution)/shard_map/ppermute | solution.py:41
  154.2 110.9 %all-to-all-start.2 = ((bf16[4,64,2048]{2,1,0:T(8,128)(2,1)}), bf16[4,64,2048]{2,1,0:T(8,128)(2,1)}, u32[]{:S(2)}, u32[]{:S(2)}) async-start(bf16[4,64,2048]{2,1,0:T(8,128)(2,1)} %pad_maximum_fusion.17), calls=%async_computation.2 | async-start | bytes 2097152 | tf_op jit(solution)/shard_map/all_to_all | solution.py:238
  158.5 127.3 %all-gather.10.cloned.1.call-start = ((), (), s32[]{:S(2)}) async-start(), calls=%async_computation.13 | async-start | bytes 4718592 | tf_op jit(solution)/shard_map/all_gather | solution.py:281
  208.3 278.8 %all-gather.12.cloned.1.call-start = ((), (), s32[]{:S(2)}) async-start(), calls=%async_computation.14 | async-start | bytes 9437184 | tf_op jit(solution)/shard_map/all_gather | solution.py:281
  285.8 305.4 %all-gather.14.cloned.1.call-start = ((), (), s32[]{:S(2)}) async-start(), calls=%async_computation.15 | async-start | bytes 4718592 | tf_op jit(solution)/shard_map/all_gather | solution.py:281
  359.8 54.7 %collective-permute-start.14 = (bf16[2,2,512,128]{3,2,1,0:T(8,128)(2,1)}, bf16[2,2,512,128]{3,2,1,0:T(8,128)(2,1)}, u32[]{:S(2)}, u32[]{:S(2)}) collective-permute-start(bf16[2,2,512,128]{3,2,1,0:T(8,128)(2,1)} %pad_maximum_fusion.26), channel_id=1, source_target_pairs={{0,24},{1,25},{2,26},{3,27},{4,28},{5,29},{6,30},{7,31}} | collective-permute-start | bytes 1572872 | tf_op jit(solution)/shard_map/ppermute | solution.py:46
  391.4 45.4 %collective-permute-start.15 = (bf16[2,2,512,128]{3,2,1,0:T(8,128)(2,1)}, bf16[2,2,512,128]{3,2,1,0:T(8,128)(2,1)}, u32[]{:S(2)}, u32[]{:S(2)}) collective-permute-start(bf16[2,2,512,128]{3,2,1,0:T(8,128)(2,1)} %pad_maximum_fusion.26), channel_id=1, source_target_pairs={{0,16},{8,24},{1,17},{9,25},{2,18},{10,26},{3,19},{11,27},{4,20},{... | collective-permute-start | bytes 1572872 | tf_op jit(solution)/shard_map/ppermute | solution.py:46
  393.5 57.8 %collective-permute-start.16 = (bf16[2,2,512,128]{3,2,1,0:T(8,128)(2,1)}, bf16[2,2,512,128]{3,2,1,0:T(8,128)(2,1)}, u32[]{:S(2)}, u32[]{:S(2)}) collective-permute-start(bf16[2,2,512,128]{3,2,1,0:T(8,128)(2,1)} %pad_maximum_fusion.26), channel_id=1, source_target_pairs={{0,8},{8,16},{16,24},{1,9},{9,17},{17,25},{2,10},{10,18},{18,26},{... | collective-permute-start | bytes 1572872 | tf_op jit(solution)/shard_map/ppermute | solution.py:46
  487.1 353.7 %reduce-scatter.6.cloned.1.call-start = ((), (), s32[]{:S(2)}) async-start(), calls=%async_computation.16 | async-start | bytes 4718592 | tf_op jit(solution)/shard_map/reduce_scatter | solution.py:418
  529.7 45.5 %collective-permute-start.25 = (bf16[256,2048]{1,0:T(8,128)(2,1)S(1)}, bf16[256,2048]{1,0:T(8,128)(2,1)S(1)}, u32[]{:S(2)}, u32[]{:S(2)}) collective-permute-start(bf16[256,2048]{1,0:T(8,128)(2,1)S(1)} %bitcast.590), channel_id=1, source_target_pairs={{0,4},{4,0},{1,5},{5,1},{2,6},{6,2},{3,7},{7,3},{8,12},{12,8},{9,1... | collective-permute-start | bytes 3145736 | tf_op jit(solution)/shard_map/ppermute | solution.py:41
  530.0 45.1 %collective-permute-start.19 = (bf16[256,2048]{0,1:T(8,128)(2,1)}, bf16[256,2048]{0,1:T(8,128)(2,1)S(1)}, u32[]{:S(2)}, u32[]{:S(2)}) collective-permute-start(bf16[256,2048]{0,1:T(8,128)(2,1)} %bitcast.612), channel_id=1, source_target_pairs={{0,1},{1,0},{2,3},{3,2},{4,5},{5,4},{6,7},{7,6},{8,9},{9,8},{10,11... | collective-permute-start | bytes 3145736 | tf_op jit(solution)/shard_map/ppermute | solution.py:41
  710.7 329.9 %reduce-scatter.8.cloned.1.call-start = ((), (), s32[]{:S(2)}) async-start(), calls=%async_computation.17 | async-start | bytes 5898240 | tf_op jit(solution)/shard_map/reduce_scatter | solution.py:418
  746.2 83.3 %collective-permute-start.42 = (bf16[2,2,512,128]{3,2,1,0:T(8,128)(2,1)}, bf16[2,2,512,128]{3,2,1,0:T(8,128)(2,1)}, u32[]{:S(2)}, u32[]{:S(2)}) collective-permute-start(bf16[2,2,512,128]{3,2,1,0:T(8,128)(2,1)} %get-tuple-element.91), channel_id=1, source_target_pairs={{16,0},{24,8},{17,1},{25,9},{18,2},{26,10},{19,3},{27,11},{20,4},{... | collective-permute-start | bytes 1572872 | tf_op jit(solution)/shard_map/ppermute | solution.py:46
  747.5 82.0 %collective-permute-start.43 = (bf16[2,2,512,128]{3,2,1,0:T(8,128)(2,1)}, bf16[2,2,512,128]{3,2,1,0:T(8,128)(2,1)}, u32[]{:S(2)}, u32[]{:S(2)}) collective-permute-start(bf16[2,2,512,128]{3,2,1,0:T(8,128)(2,1)} %get-tuple-element.90), channel_id=1, source_target_pairs={{24,0},{25,1},{26,2},{27,3},{28,4},{29,5},{30,6},{31,7}} | collective-permute-start | bytes 1572872 | tf_op jit(solution)/shard_map/ppermute | solution.py:46
  840.9 287.7 %reduce-scatter.14.cloned.1.call-start = ((), (), s32[]{:S(2)}) async-start(), calls=%async_computation.20 | async-start | bytes 4718592 | tf_op jit(solution)/shard_map/reduce_scatter | solution.py:418
  851.2 346.3 %reduce-scatter.12.cloned.1.call-start = ((), (), s32[]{:S(2)}) async-start(), calls=%async_computation.19 | async-start | bytes 9437184 | tf_op jit(solution)/shard_map/reduce_scatter | solution.py:418
  875.8 438.6 %reduce-scatter.10.cloned.1.call-start = ((), (), s32[]{:S(2)}) async-start(), calls=%async_computation.18 | async-start | bytes 6488064 | tf_op jit(solution)/shard_map/reduce_scatter | solution.py:418
  901.0 40.5 %collective-permute-start.36 = (bf16[12,64,256]{2,1,0:T(8,128)(2,1)S(1)}, bf16[12,64,256]{2,1,0:T(8,128)(2,1)S(1)}, u32[]{:S(2)}, u32[]{:S(2)}) collective-permute-start(bf16[12,64,256]{2,1,0:T(8,128)(2,1)S(1)} %get-tuple-element.96), channel_id=1, source_target_pairs={{8,0},{9,1},{10,2},{11,3},{12,4},{13,5},{14,6},{15,7}} | collective-permute-start | bytes 1179656 | tf_op jit(solution)/shard_map/ppermute | solution.py:361
  902.5 52.5 %collective-permute-start.39 = (bf16[12,64,256]{2,1,0:T(8,128)(2,1)S(1)}, bf16[12,64,256]{2,1,0:T(8,128)(2,1)S(1)}, u32[]{:S(2)}, u32[]{:S(2)}) collective-permute-start(bf16[12,64,256]{2,1,0:T(8,128)(2,1)S(1)} %add_convert_fusion.2), channel_id=1, source_target_pairs={{8,0},{9,1},{10,2},{11,3},{12,4},{13,5},{14,6},{15,7}} | collective-permute-start | bytes 1179656 | tf_op jit(solution)/shard_map/ppermute | solution.py:361
  1072.8 129.0 %collective-permute-start.23 = (bf16[256,2048]{1,0:T(8,128)(2,1)}, bf16[256,2048]{1,0:T(8,128)(2,1)}, u32[]{:S(2)}, u32[]{:S(2)}) collective-permute-start(bf16[256,2048]{1,0:T(8,128)(2,1)} %fusion.83), channel_id=1, source_target_pairs={{0,4},{4,0},{1,5},{5,1},{2,6},{6,2},{3,7},{7,3},{8,12},{12,8},{9,1... | collective-permute-start | bytes 3145736 | tf_op jit(solution)/shard_map/ppermute | solution.py:41
  1147.8 59.8 %collective-permute-start.50 = (f32[25232]{0:T(1024)S(1)}, f32[25232]{0:T(1024)S(1)}, u32[]{:S(2)}, u32[]{:S(2)}) collective-permute-start(f32[25232]{0:T(1024)S(1)} %add.493), channel_id=1, source_target_pairs={{0,1},{1,0},{2,3},{3,2},{4,5},{5,4},{6,7},{7,6},{8,9},{9,8},{10,11... | collective-permute-start | bytes 302792 | tf_op jit(solution)/shard_map/ppermute | solution.py:54
  (269 other events, 4132.7 us)
Sparse Core Ops, SparseCore 0:
  25.4 93.4 all-gather.5
  121.0 87.2 all-gather.7
  211.0 74.6 all-gather.9
  287.7 158.9 all-gather.11
  487.2 85.9 all-gather.13
  710.9 120.0 reduce-scatter.5
  841.0 111.6 reduce-scatter.7
  956.8 86.3 reduce-scatter.13
  1046.8 150.6 reduce-scatter.11
  1201.4 112.9 reduce-scatter.9

commit v3 on v2

v3 whole, which is shorter than its diff:
```python
import jax
import jax.numpy as jnp
from jax import lax
from jax.experimental import pallas as pl
from jax.experimental.pallas import tpu as pltpu
from jax.sharding import Mesh
from jax.sharding import PartitionSpec as P

D = 2048
MAMBA_HEADS = 48
MAMBA_HEAD = 64
STATE = 256
ATT_HEADS = 8
KV_HEADS = 2
HEAD_DIM = 128
SPAN = 128
INNER = 3072

HEADS = MAMBA_HEADS // 4
PART = HEADS * MAMBA_HEAD
BC = 2 * STATE
DT_PAD = 128
QP = 2 * HEAD_DIM
CONV_COLS = PART + BC
SCAN_COLS = CONV_COLS + DT_PAD
AT_Q = PART
AT_K = AT_Q + QP
AT_V = AT_K + HEAD_DIM
REST_COLS = AT_V + HEAD_DIM
HALF = D // 2

epsilon = 1e-05
rope_base = 100000000000.0
GROUP = ("x", "c")
SHARDS = ("z", "y")
EVERY = ("z", "x", "y", "c")
bf16 = jnp.bfloat16
f32 = jnp.float32


def swap(array, axis):
    return lax.ppermute(array, axis, [(0, 1), (1, 0)])


def shifted(array, distance):
    devices = range(lax.axis_size("z"))
    return lax.ppermute(array, "z", [(i - distance, i) for i in devices if i - distance in devices])


def total(array):
    for axis in EVERY:
        size = lax.axis_size(axis)
        bit = 1
        while bit < size:
            array = array + lax.ppermute(array, axis, [(i, i ^ bit) for i in range(size)])
            bit *= 2
    return array


def group_total(array):
    array = array + swap(array[::-1], "c")
    return array + swap(array, "x")


def low_dot(left, right):
    return jnp.dot(left, right, preferred_element_type=f32)


def back_dot(grad_rows, weight):
    return lax.dot_general(grad_rows, weight, (((1,), (1,)), ((), ())), preferred_element_type=f32)


def weight_grad(left, right):
    return lax.dot_general(left, right, (((0,), (0,)), ((), ())), preferred_element_type=f32)


def rms_scale(values, gain):
    return values * lax.rsqrt(jnp.mean(values * values, axis=-1, keepdims=True) + epsilon) * gain


def rope_tables(positions):
    half_dim = HEAD_DIM // 2
    frequencies = rope_base ** (-jnp.arange(half_dim, dtype=f32) / half_dim)
    angles = positions.astype(f32)[:, None] * frequencies[None, :]
    return (jnp.cos(angles), jnp.sin(angles))


def rotate(values, cosine, sine):
    half_dim = HEAD_DIM // 2
    cosine, sine = cosine[:, None, :], sine[:, None, :]
    first, second = values[..., :half_dim], values[..., half_dim:]
    return jnp.concatenate([first * cosine - second * sine, second * cosine + first * sine], axis=-1)


def exact(left, right):
    return jnp.dot(left, right, precision=lax.Precision.HIGHEST, preferred_element_type=f32)


def over_lanes(left, right):
    return lax.dot_general(left, right, (((1,), (1,)), ((), ())), preferred_element_type=f32)


def over_rows(left, right):
    return lax.dot_general(left, right, (((0,), (0,)), ((), ())), preferred_element_type=f32)


def widen(values, lift):
    return exact(values, lift)


def narrow(values, lift):
    return lax.dot_general(
        values,
        lift,
        (((1,), (1,)), ((), ())),
        precision=lax.Precision.HIGHEST,
        preferred_element_type=f32,
    )


def sig(values):
    return 1.0 / (1.0 + jnp.exp(-values))


def soft(values):
    return jnp.maximum(values, 0.0) + jnp.log1p(jnp.exp(-jnp.abs(values)))


def square_places():
    return (
        lax.broadcasted_iota(jnp.int32, (SPAN, SPAN), 0),
        lax.broadcasted_iota(jnp.int32, (SPAN, SPAN), 1),
    )


def pre_conv(current, before, taps, bias):
    extended = jnp.concatenate([before, current], axis=0)
    pre = bias + extended[5 : 5 + SPAN] * taps[0:1]
    for k in range(1, 4):
        pre = pre + extended[5 + k : 5 + k + SPAN] * taps[k : k + 1]
    return (pre, extended)


def states_kernel(
    scan_in, before, taps, bias, dt_bias, rates, lift, mixed, steps, starts, prefix, last, held, sofar
):
    @pl.when(pl.program_id(1) == 0)
    def _():
        held[...] = jnp.zeros_like(held)
        sofar[...] = jnp.zeros_like(sofar)

    pre, _ = pre_conv(scan_in[0, :, :CONV_COLS], before[0, 0], taps[...], bias[...])
    mix = pre * sig(pre)
    mixed[0] = mix
    dt = soft(scan_in[0, :, CONV_COLS:] + dt_bias[...])
    row, column = square_places()
    cum = exact(jnp.where(row >= column, 1.0, 0.0), dt * rates[...])
    steps[0, :, :DT_PAD] = dt
    steps[0, :, DT_PAD:] = cum
    starts[0, 0] = sofar[...]
    prefix[0, 0] = held[...]
    end = cum[SPAN - 1 : SPAN]
    tail = jnp.exp(end - cum) * dt
    fed = (mix[:, :PART] * widen(tail, lift[...])).astype(bf16)
    added = over_rows(mix[:, PART : PART + STATE].astype(bf16), fed)
    whole = widen(jnp.broadcast_to(jnp.exp(end), (8, DT_PAD)), lift[...])[0:1]
    held[...] = whole * held[...] + added
    sofar[...] = sofar[...] + end
    last[0] = held[...]


def values_kernel(
    mixed, steps, starts, prefix, state_in, gate, skip, lift, values, flat, square
):
    x = mixed[0, :, :PART]
    b16 = mixed[0, :, PART : PART + STATE].astype(bf16)
    c16 = mixed[0, :, PART + STATE :].astype(bf16)
    dt = steps[0, :, :DT_PAD]
    cum = steps[0, :, DT_PAD:]
    dt_t, cum_t = dt.T, cum.T
    state = prefix[0, 0] + widen(jnp.exp(starts[0, 0]), lift[...])[0:1] * state_in[0]
    meet = over_lanes(c16, b16)
    carried = low_dot(c16, state.astype(bf16)) * widen(jnp.exp(cum), lift[...])
    row, column = square_places()
    first = column < MAMBA_HEAD
    inside = []
    for k in range(HEADS // 2):
        pair = x[:, 2 * MAMBA_HEAD * k : 2 * MAMBA_HEAD * (k + 1)]
        weights = []
        for h in (2 * k, 2 * k + 1):
            spread = cum[:, h : h + 1] - cum_t[h : h + 1, :]
            decay = jnp.exp(jnp.where(row >= column, spread, -1e30))
            weights.append((meet * decay * dt_t[h : h + 1, :]).astype(bf16))
        split = [
            jnp.where(first, pair, 0.0).astype(bf16),
            jnp.where(first, 0.0, pair).astype(bf16),
        ]
        inside.append(low_dot(jnp.concatenate(weights, 1), jnp.concatenate(split, 0)))
    value = jnp.concatenate(inside, 1) + carried + skip[...] * x
    values[0] = value
    z = gate[0]
    product = value * (z * sig(z))
    flat[0] = product
    square[0] = jnp.broadcast_to(
        jnp.sum(product * product, axis=1, keepdims=True), (SPAN, 128)
    )


def gate_back_kernel(
    gated_grad, values, gate, root, mean, gain, c_part, steps, lift,
    value_grad, gate_grad, gain_grad, suffix, first_grad, held,
):
    @pl.when(pl.program_id(1) == 0)
    def _():
        held[...] = jnp.zeros_like(held)

    @pl.when((pl.program_id(0) == 0) & (pl.program_id(1) == 0))
    def _():
        gain_grad[...] = jnp.zeros_like(gain_grad)

    z, value, grad = gate[0], values[0], gated_grad[0]
    s = sig(z)
    silu = z * s
    scale = root[0, :, 0:1]
    normal = value * silu * scale
    flat_grad = scale * (grad * gain[...] - normal * mean[0, :, 0:1])
    d_value = flat_grad * silu
    value_grad[0] = d_value
    gate_grad[0] = (flat_grad * value * (s * (1.0 + z * (1.0 - s)))).astype(bf16)
    gain_grad[0:1] = gain_grad[0:1] + jnp.sum(grad * normal, axis=0, keepdims=True)
    grown = widen(jnp.exp(steps[0, :, DT_PAD:]), lift[...])
    suffix[0, 0] = held[...]
    held[...] = grown[SPAN - 1 : SPAN] * held[...] + over_rows(
        c_part[0].astype(bf16), (grown * d_value).astype(bf16)
    )
    first_grad[0] = held[...]


def scan_back_kernel(
    scan_in, before, mixed, steps, starts, prefix, state_in, suffix, state_grad, value_grad,
    skip, taps, bias, dt_bias, rates, lift,
    scan_grad, edge_grad, conv_grad, small_grad,
    later, after_pre, columns,
):
    @pl.when(pl.program_id(1) == 0)
    def _():
        later[...] = jnp.zeros_like(later)
        after_pre[...] = jnp.zeros_like(after_pre)

    @pl.when((pl.program_id(0) == 0) & (pl.program_id(1) == 0))
    def _():
        conv_grad[...] = jnp.zeros_like(conv_grad)
        small_grad[...] = jnp.zeros_like(small_grad)
        columns[...] = jnp.zeros_like(columns)

    up = lift[...]
    x = mixed[0, :, :PART]
    b16 = mixed[0, :, PART : PART + STATE].astype(bf16)
    c16 = mixed[0, :, PART + STATE :].astype(bf16)
    dt = steps[0, :, :DT_PAD]
    cum = steps[0, :, DT_PAD:]
    dt_t, cum_t = dt.T, cum.T
    end = cum[SPAN - 1 : SPAN]
    dy = value_grad[0]
    state = prefix[0, 0] + widen(jnp.exp(starts[0, 0]), up)[0:1] * state_in[0]
    ending = suffix[0, 0] + widen(jnp.exp(later[...]), up)[0:1] * state_grad[0]
    later[...] = later[...] + end
    state16, ending16 = state.astype(bf16), ending.astype(bf16)
    grown = widen(jnp.exp(cum), up)
    tail_wide = widen(jnp.exp(end - cum), up)
    dt_wide = widen(dt, up)
    grown_dy = grown * dy
    reach = low_dot(c16, state16)
    pull = tail_wide * low_dot(b16, ending16)
    d_c = over_lanes(grown_dy.astype(bf16), state16)
    d_b = over_lanes((tail_wide * dt_wide * x).astype(bf16), ending16)
    meet = over_lanes(c16, b16)
    row, column = square_places()
    first = column < MAMBA_HEAD
    d_meet = jnp.zeros((SPAN, SPAN), f32)
    rows_sum = jnp.zeros((SPAN, DT_PAD), f32)
    back = []
    for k in range(HEADS // 2):
        at = slice(2 * MAMBA_HEAD * k, 2 * MAMBA_HEAD * (k + 1))
        x16, dy_pair = x[:, at].astype(bf16), dy[:, at]
        split = [
            jnp.where(first, dy_pair, 0.0).astype(bf16),
            jnp.where(first, 0.0, dy_pair).astype(bf16),
        ]
        weights = []
        for j in range(2):
            h = 2 * k + j
            spread = cum[:, h : h + 1] - cum_t[h : h + 1, :]
            decay = jnp.exp(jnp.where(row >= column, spread, -1e30))
            d_weight = over_lanes(split[j], x16) * decay
            scaled = d_weight * dt_t[h : h + 1, :]
            d_meet = d_meet + scaled
            rows_sum = rows_sum + jnp.where(
                column == h, jnp.sum(scaled * meet, axis=1, keepdims=True), 0.0
            )
            columns[h : h + 1, :] = jnp.sum(d_weight * meet, axis=0, keepdims=True)
            weights.append((meet * decay).astype(bf16))
        back.append(over_rows(jnp.concatenate(weights, 0), jnp.concatenate(split, 0)))
    d_meet16 = d_meet.astype(bf16)
    d_c = d_c + low_dot(d_meet16, b16)
    d_b = d_b + over_rows(d_meet16, c16)
    d_x = dt_wide * (jnp.concatenate(back, 1) + pull) + skip[...] * dy
    tail_dt = narrow(x * pull, up)
    inner_dt = columns[...].T
    d_cum = rows_sum + narrow(grown_dy * reach, up) - dt * (inner_dt + tail_dt)
    kept = narrow(
        jnp.broadcast_to(jnp.sum(state * ending, axis=0, keepdims=True), (8, PART)), up
    )[0:1]
    extra = jnp.sum(dt * tail_dt, axis=0, keepdims=True) + jnp.exp(end) * kept
    d_log = exact(jnp.where(row <= column, 1.0, 0.0), d_cum) + extra
    rate = rates[...]
    d_raw = (inner_dt + tail_dt + d_log * rate) * sig(
        scan_in[0, :, CONV_COLS:] + dt_bias[...]
    )
    small_grad[0:1] = small_grad[0:1] + jnp.sum(d_raw, axis=0, keepdims=True)
    small_grad[1:2] = small_grad[1:2] + jnp.sum(d_log * dt * rate, axis=0, keepdims=True)
    small_grad[2:3] = small_grad[2:3] + jnp.sum(narrow(dy * x, up), axis=0, keepdims=True)

    pre, extended = pre_conv(scan_in[0, :, :CONV_COLS], before[0, 0], taps[...], bias[...])
    s = sig(pre)
    d_pre = jnp.concatenate([d_x, d_b, d_c], axis=1) * (s * (1.0 + pre * (1.0 - s)))
    for k in range(4):
        conv_grad[k : k + 1] = conv_grad[k : k + 1] + jnp.sum(
            d_pre * extended[5 + k : 5 + k + SPAN], axis=0, keepdims=True
        )
    conv_grad[4:5] = conv_grad[4:5] + jnp.sum(d_pre, axis=0, keepdims=True)
    following = jnp.concatenate([d_pre, after_pre[...]], axis=0)
    d_in = following[0:SPAN] * taps[3:4]
    for k in range(3):
        d_in = d_in + following[3 - k : 3 - k + SPAN] * taps[k : k + 1]
    scan_grad[0, :, :CONV_COLS] = d_in.astype(bf16)
    scan_grad[0, :, CONV_COLS:] = d_raw.astype(bf16)
    front = d_pre[0:8]
    after_pre[...] = front
    padded = jnp.concatenate([jnp.zeros((8, CONV_COLS), f32), front, jnp.zeros((8, CONV_COLS), f32)], 0)
    edge = padded[0:8] * taps[3:4]
    for k in range(3):
        edge = edge + padded[3 - k : 11 - k] * taps[k : k + 1]
    edge_grad[0] = edge


def one(shape):
    return pl.BlockSpec(shape, lambda b, i: (0,) * len(shape))


def by_span(width, column=0, reverse=None):
    if reverse is None:
        return pl.BlockSpec((1, SPAN, width), lambda b, i: (b, i, column))
    return pl.BlockSpec((1, SPAN, width), lambda b, i: (b, reverse - 1 - i, column))


def by_piece(rows, width, reverse=None):
    if reverse is None:
        return pl.BlockSpec((1, 1, rows, width), lambda b, i: (b, i, 0, 0))
    return pl.BlockSpec((1, 1, rows, width), lambda b, i: (b, reverse - 1 - i, 0, 0))


def by_sequence(rows, width):
    return pl.BlockSpec((1, rows, width), lambda b, i: (b, 0, 0))


def grid_call(kernel, spans, ins, outs, scratch, flops, moved):
    return pl.pallas_call(
        kernel,
        grid=(2, spans),
        in_specs=ins,
        out_specs=[spec for spec, _ in outs],
        out_shape=[shape for _, shape in outs],
        scratch_shapes=scratch,
        compiler_params=pltpu.CompilerParams(
            dimension_semantics=("arbitrary", "arbitrary"), vmem_limit_bytes=50 * 2**20
        ),
        cost_estimate=pl.CostEstimate(flops=flops, bytes_accessed=moved, transcendentals=0),
    )


def like(shape, kind=f32):
    return jax.ShapeDtypeStruct(shape, kind)


def scan_states(scan_in, before, taps, bias, dt_bias, rates, lift):
    length = scan_in.shape[1]
    n = length // SPAN
    return grid_call(
        states_kernel,
        n,
        [
            by_span(SCAN_COLS),
            by_piece(8, CONV_COLS),
            one((4, CONV_COLS)),
            one((1, CONV_COLS)),
            one((1, DT_PAD)),
            one((1, DT_PAD)),
            one((DT_PAD, PART)),
        ],
        [
            (by_span(CONV_COLS), like((2, length, CONV_COLS))),
            (by_span(2 * DT_PAD), like((2, length, 2 * DT_PAD))),
            (by_piece(8, DT_PAD), like((2, n, 8, DT_PAD))),
            (by_piece(STATE, PART), like((2, n, STATE, PART))),
            (by_sequence(STATE, PART), like((2, STATE, PART))),
        ],
        [pltpu.VMEM((STATE, PART), f32), pltpu.VMEM((8, DT_PAD), f32)],
        8 * 10**9,
        30 * 10**6,
    )(scan_in, before, taps, bias, dt_bias, rates, lift)


def scan_values(mixed, steps, starts, prefix, state_in, rest, gate_at, skip, lift):
    length = mixed.shape[1]
    n = length // SPAN
    return grid_call(
        values_kernel,
        n,
        [
            by_span(CONV_COLS),
            by_span(2 * DT_PAD),
            by_piece(8, DT_PAD),
            by_piece(STATE, PART),
            by_sequence(STATE, PART),
            by_span(PART, gate_at),
            one((1, PART)),
            one((DT_PAD, PART)),
        ],
        [
            (by_span(PART), like((2, length, PART))),
            (by_span(PART), like((2, length, PART))),
            (by_span(128), like((2, length, 128))),
        ],
        [],
        12 * 10**9,
        30 * 10**6,
    )(mixed, steps, starts, prefix, state_in, rest, skip, lift)


def gate_backward(gated_grad, values, rest, gate_at, root, mean, gain, mixed, steps, lift):
    length = mixed.shape[1]
    n = length // SPAN
    return grid_call(
        gate_back_kernel,
        n,
        [
            by_span(PART, 0, n),
            by_span(PART, 0, n),
            by_span(PART, gate_at, n),
            by_span(128, 0, n),
            by_span(128, 0, n),
            one((1, PART)),
            by_span(STATE, (PART + STATE) // STATE, n),
            by_span(2 * DT_PAD, 0, n),
            one((DT_PAD, PART)),
        ],
        [
            (by_span(PART, 0, n), like((2, length, PART))),
            (by_span(PART, 0, n), like((2, length, PART), bf16)),
            (one((8, PART)), like((8, PART))),
            (by_piece(STATE, PART, n), like((2, n, STATE, PART))),
            (by_sequence(STATE, PART), like((2, STATE, PART))),
        ],
        [pltpu.VMEM((STATE, PART), f32)],
        8 * 10**9,
        30 * 10**6,
    )(gated_grad, values, rest, root, mean, gain, mixed, steps, lift)


def scan_backward(
    scan_in, before, mixed, steps, starts, prefix, state_in, suffix, state_grad, value_grad,
    skip, taps, bias, dt_bias, rates, lift,
):
    length = mixed.shape[1]
    n = length // SPAN
    return grid_call(
        scan_back_kernel,
        n,
        [
            by_span(SCAN_COLS, 0, n),
            by_piece(8, CONV_COLS, n),
            by_span(CONV_COLS, 0, n),
            by_span(2 * DT_PAD, 0, n),
            by_piece(8, DT_PAD, n),
            by_piece(STATE, PART, n),
            by_sequence(STATE, PART),
            by_piece(STATE, PART, n),
            by_sequence(STATE, PART),
            by_span(PART, 0, n),
            one((1, PART)),
            one((4, CONV_COLS)),
            one((1, CONV_COLS)),
            one((1, DT_PAD)),
            one((1, DT_PAD)),
            one((DT_PAD, PART)),
        ],
        [
            (by_span(SCAN_COLS, 0, n), like((2, length, SCAN_COLS), bf16)),
            (by_sequence(8, CONV_COLS), like((2, 8, CONV_COLS))),
            (one((8, CONV_COLS)), like((8, CONV_COLS))),
            (one((8, DT_PAD)), like((8, DT_PAD))),
        ],
        [
            pltpu.VMEM((8, DT_PAD), f32),
            pltpu.VMEM((8, CONV_COLS), f32),
            pltpu.VMEM((SPAN, SPAN), f32),
        ],
        30 * 10**9,
        50 * 10**6,
    )(
        scan_in, before, mixed, steps, starts, prefix, state_in, suffix, state_grad, value_grad,
        skip, taps, bias, dt_bias, rates, lift,
    )


def attend_kernel(query, key, value, query_place, key_place, attended, log_sum):
    scores = over_lanes(query[0], key[0]) * HEAD_DIM ** (-0.5)
    seen = (key_place[0:1] >= 0) & (query_place[:, 0:1] >= key_place[0:1])
    scores = jnp.where(seen, scores, -1e30)
    peak = jnp.max(scores, axis=1, keepdims=True)
    unscaled = jnp.exp(scores - peak)
    whole = jnp.sum(unscaled, axis=1, keepdims=True)
    probs = (unscaled * (1.0 / whole)).astype(bf16)
    attended[0] = low_dot(probs, value[0])
    log_sum[0] = jnp.broadcast_to(peak + jnp.log(whole), log_sum.shape[1:])


def attend_back_kernel(
    query, key, value, grad, attended, log_sum, query_place, key_place, query_grad, kv_grad
):
    @pl.when((pl.program_id(1) == 0) & (pl.program_id(2) == 0))
    def _():
        kv_grad[...] = jnp.zeros_like(kv_grad)

    scale = HEAD_DIM ** (-0.5)
    scores = over_lanes(query[0], key[0]) * scale
    seen = (key_place[0:1] >= 0) & (query_place[:, 0:1] >= key_place[0:1])
    probs = jnp.exp(jnp.where(seen, scores, -1e30) - log_sum[0, :, 0:1])
    delta = jnp.sum(grad[0].astype(f32) * attended[0], axis=1, keepdims=True)
    score_grad = (probs * (over_lanes(grad[0], value[0]) - delta)).astype(bf16)
    query_grad[0] = low_dot(score_grad, key[0]) * scale
    kv_grad[0, 0] = kv_grad[0, 0] + over_rows(score_grad, query[0]) * scale
    kv_grad[1, 0] = kv_grad[1, 0] + over_rows(probs.astype(bf16), grad[0])


def attend_specs(block, keys):
    by_query = pl.BlockSpec((1, block, HEAD_DIM), lambda b, h, i: (b, i, h))
    whole_key = pl.BlockSpec((1, keys, HEAD_DIM), lambda b, h, i: (b, 0, 0))
    place = pl.BlockSpec((block, 128), lambda b, h, i: (i, 0))
    key_at = pl.BlockSpec((8, keys), lambda b, h, i: (0, 0))
    return (by_query, whole_key, place, key_at)


def attend(query, key, value, query_place, key_place):
    length, keys = query.shape[1], key.shape[1]
    block = 256 if keys <= 4096 else 128
    by_query, whole_key, place, key_at = attend_specs(block, keys)
    return pl.pallas_call(
        attend_kernel,
        grid=(2, 2, length // block),
        in_specs=[by_query, whole_key, whole_key, place, key_at],
        out_specs=[by_query, by_query],
        out_shape=[like((2, length, QP)), like((2, length, QP))],
        compiler_params=pltpu.CompilerParams(
            dimension_semantics=("arbitrary",) * 3, vmem_limit_bytes=50 * 2**20
        ),
        cost_estimate=pl.CostEstimate(
            flops=12 * 10**9, bytes_accessed=20 * 10**6, transcendentals=0
        ),
    )(query, key, value, query_place, key_place)


def attend_backward(query, key, value, grad, attended, log_sum, query_place, key_place):
    length, keys = query.shape[1], key.shape[1]
    block = 256 if keys <= 4096 else 128
    by_query, whole_key, place, key_at = attend_specs(block, keys)
    return pl.pallas_call(
        attend_back_kernel,
        grid=(2, 2, length // block),
        in_specs=[by_query, whole_key, whole_key, by_query, by_query, by_query, place, key_at],
        out_specs=[
            by_query,
            pl.BlockSpec((2, 1, keys, HEAD_DIM), lambda b, h, i: (0, b, 0, 0)),
        ],
        out_shape=[like((2, length, QP)), like((2, 2, keys, HEAD_DIM))],
        compiler_params=pltpu.CompilerParams(
            dimension_semantics=("arbitrary",) * 3, vmem_limit_bytes=50 * 2**20
        ),
        cost_estimate=pl.CostEstimate(
            flops=20 * 10**9, bytes_accessed=30 * 10**6, transcendentals=0
        ),
    )(query, key, value, grad, attended, log_sum, query_place, key_place)


def swish_product(gate_proj, up_proj):
    return jax.nn.silu(gate_proj) * up_proj


def gather_tokens(block):
    across = swap(block, "x")
    return (block, swap(block, "c"), across, swap(across, "c"))


def scatter_tokens(blocks):
    near, far = blocks[0], blocks[2]
    sent = swap(jnp.stack([blocks[1].astype(bf16), blocks[3].astype(bf16)]), "c")
    near = near + sent[0].astype(f32)
    far = far + sent[1].astype(f32)
    return near + swap(far.astype(bf16), "x").astype(f32)


def body(
    inputs,
    out_grad,
    norm_gain,
    w_in,
    conv_weight,
    conv_bias,
    dt_bias,
    a_log,
    skip_gain,
    gated_gain,
    w_out,
    w_q,
    w_k,
    w_v,
    w_o,
    mid_gain,
    w_gate,
    w_up,
    w_down,
):
    nz, ny = lax.axis_size("z"), lax.axis_size("y")
    zi, xi, ci = (lax.axis_index(name) for name in ("z", "x", "c"))
    length = inputs.shape[1]
    span_all = 2 * length
    rows = w_in.shape[0]
    ff_rows = w_down.shape[0]
    hidden_part = nz * ny * ff_rows
    edge_count = conv_weight.shape[0] - 1
    out_rows, o_rows = w_out.shape[0], w_o.shape[0]
    aligned = ny == 2 and nz == 4 and MAMBA_HEADS % (4 * nz) == 0
    g = nz if aligned else 1
    hp = HEADS // g

    def heads_mine(array, width):
        lead = array.shape[:-1]
        array = array.reshape(lead + (g, 2, 2, hp * width))
        array = lax.dynamic_index_in_dim(array, xi, len(lead) + 1, keepdims=False)
        array = lax.dynamic_index_in_dim(array, ci, len(lead) + 1, keepdims=False)
        return array.reshape(lead + (HEADS * width,))

    def heads_spread(array, width):
        lead = array.shape[:-1]
        array = array.reshape(lead + (g, 1, 1, hp * width))
        whole = jnp.zeros(lead + (g, 2, 2, hp * width), array.dtype)
        start = (0,) * len(lead) + (0, xi, ci, 0)
        return lax.dynamic_update_slice(whole, array, start).reshape(
            lead + (MAMBA_HEADS * width,)
        )

    def heads_split(array, width):
        n = array.shape[0]
        array = array.reshape(n, g, 2, 2, hp * width)
        return jnp.transpose(array, (2, 3, 0, 1, 4)).reshape(4, n, HEADS * width)

    def heads_join(array, width):
        n = array.shape[1]
        array = array.reshape(2, 2, n, g, hp * width)
        return jnp.transpose(array, (2, 3, 0, 1, 4)).reshape(n, MAMBA_HEADS * width)

    def reordered(array, first, second):
        width = 2 * rows
        return jnp.concatenate(
            [
                array[..., at * width : (at + 1) * width]
                for z in range(nz)
                for at in (
                    (z * first + i) * second + j for j in range(second) for i in range(first)
                )
            ],
            axis=-1,
        )

    def permuted(array):
        return reordered(array, 2, ny)

    def restored(array):
        return reordered(array, ny, 2)

    def to_ranks(array):
        return lax.all_to_all(array, GROUP, 0, 0, tiled=True)

    def in_order(own, other):
        return lax.dynamic_slice_in_dim(
            jnp.concatenate([own, other, own], 0), xi * length, span_all, 0
        )

    def gather_sequences(block):
        own, near, across, far = gather_tokens(block)
        return jnp.stack([in_order(own, across), in_order(near, far)])

    def scatter_sequences(partial):
        mine = partial[0] + swap(partial[1].astype(bf16), "c").astype(f32)
        mine = mine.reshape(2, length, mine.shape[-1])
        own = lax.dynamic_index_in_dim(mine, xi, 0, keepdims=False)
        other = lax.dynamic_index_in_dim(mine, 1 - xi, 0, keepdims=False)
        return own + swap(other.astype(bf16), "x").astype(f32)

    split_q = jnp.transpose(w_q.reshape(rows, 2, 2, 2, HEAD_DIM), (3, 1, 0, 2, 4))
    split_k = jnp.transpose(w_k.reshape(rows, 2, HEAD_DIM), (1, 0, 2))
    split_v = jnp.transpose(w_v.reshape(rows, 2, HEAD_DIM), (1, 0, 2))
    two = lambda a: jnp.broadcast_to(a[None], (2,) + a.shape).reshape(4, rows, a.shape[-1])
    packed_scan = jnp.concatenate(
        [
            heads_split(w_in[:, INNER : 2 * INNER], MAMBA_HEAD),
            jnp.broadcast_to(w_in[None, :, 2 * INNER : 2 * INNER + BC], (4, rows, BC)),
            jnp.pad(
                heads_split(w_in[:, 2 * INNER + BC :], 1), ((0, 0), (0, 0), (0, DT_PAD - HEADS))
            ),
        ],
        axis=2,
    )
    packed_rest = jnp.concatenate(
        [
            heads_split(w_in[:, :INNER], MAMBA_HEAD),
            split_q.reshape(4, rows, QP),
            two(split_k),
            two(split_v),
        ],
        axis=2,
    )

    def gathered(array):
        return lax.all_gather(array, SHARDS, axis=0, tiled=True)

    def after(array, *others):
        return lax.optimization_barrier((array,) + others)[0]

    def split_ff(w):
        w = w.reshape(rows, nz, 2, ny, 2, ff_rows)
        return jnp.transpose(w, (2, 4, 0, 1, 3, 5)).reshape(4, rows, hidden_part)

    def join_ff(w):
        w = w.reshape(2, 2, rows, nz, ny, ff_rows)
        return jnp.transpose(w, (2, 3, 0, 4, 1, 5)).reshape(rows, 4 * hidden_part)

    full_scan = gathered(to_ranks(packed_scan).reshape(4 * rows, SCAN_COLS))

    tokens = 2 * span_all
    resident = inputs[0].astype(f32)
    normed, norm_back = jax.vjp(rms_scale, resident, norm_gain)
    normed16 = gather_sequences(permuted(normed.astype(bf16)))
    edges16 = shifted(normed16[:, span_all - 8 :], 1).reshape(16, D)
    normed_rows = normed16.reshape(tokens, D)

    rest_mine = to_ranks(packed_rest).reshape(4 * rows, REST_COLS)
    if aligned:
        turn = [(2 * y + c, 2 * c + y) for y in range(2) for c in range(2)]
        place = []
        for z in range(4):
            for y in range(2):
                for c in range(2):
                    place.append(((z * 2 + y) * 2 + c, ((z % 2 * 2 + y) * 2 + c) * 2 + z // 2))
        back_place = [(b, a) for a, b in place]
        sent_out = lax.ppermute(w_out, ("y", "c"), turn)
        sent_o = lax.ppermute(w_o, ("z", "y", "c"), place)
        sent_rows = jnp.concatenate([sent_out, sent_o], 0).reshape(2 * rows, 2, HALF)
        second = jnp.concatenate(
            [rest_mine, jnp.swapaxes(sent_rows, 0, 1).reshape(4 * rows, HALF)], axis=1
        )
        whole_second = gathered(after(second, normed_rows, edges16))
        full_rest = whole_second[:, :REST_COLS]
        full_rows = jnp.swapaxes(
            whole_second[:, REST_COLS:].reshape(nz * ny, 2, 2 * rows, HALF), 1, 2
        ).reshape(nz * ny, 2 * rows, D)
        full_out = full_rows[:, :out_rows].reshape(PART, D)
        full_o = full_rows[:, out_rows:].reshape(QP, D)
    else:
        full_rest = gathered(after(rest_mine, normed_rows, edges16))
        every_out = lax.all_gather(w_out, EVERY, axis=0, tiled=True)
        every_o = lax.all_gather(w_o, EVERY, axis=0, tiled=True)
        full_out = lax.dynamic_slice_in_dim(every_out, (2 * xi + ci) * PART, PART, 0)
        every_o = every_o.reshape(2, 2, 2, HEAD_DIM, D)
        every_o = lax.dynamic_index_in_dim(every_o, xi, 2, keepdims=False)
        full_o = lax.dynamic_index_in_dim(every_o, ci, 0, keepdims=False).reshape(QP, D)

    scan_in = low_dot(normed_rows, full_scan).reshape(2, span_all, SCAN_COLS)
    edge_rows = low_dot(edges16, full_scan).reshape(2, 1, 8, SCAN_COLS)
    n = span_all // SPAN
    before = jnp.concatenate(
        [edge_rows, scan_in.reshape(2, n, SPAN, SCAN_COLS)[:, : n - 1, SPAN - 8 :]], axis=1
    )[..., :CONV_COLS]

    def rank_channels(array):
        return jnp.concatenate(
            [heads_mine(array[..., :INNER], MAMBA_HEAD), array[..., INNER:]], axis=-1
        )

    def per_head(array):
        return jnp.pad(heads_mine(array, 1), (0, DT_PAD - HEADS))[None]

    taps, bias = rank_channels(conv_weight), rank_channels(conv_bias)[None]
    dt_b, rates = per_head(dt_bias), per_head(-jnp.exp(a_log))
    skip = jnp.repeat(heads_mine(skip_gain, 1), MAMBA_HEAD)[None]
    gain = heads_mine(gated_gain, MAMBA_HEAD)[None]
    lift = (
        jnp.arange(DT_PAD, dtype=jnp.int32)[:, None]
        == jnp.arange(PART, dtype=jnp.int32)[None] // MAMBA_HEAD
    ).astype(f32)
    mixed, steps, starts, prefix, own_state = scan_states(
        scan_in, before, taps, bias, dt_b, rates, lift
    )
    log_decay = starts[:, n - 1, 0] + steps[:, span_all - 1, DT_PAD:]
    own_decay = jnp.repeat(jnp.exp(log_decay[:, :HEADS]), MAMBA_HEAD, axis=-1)

    def chained(local, step):
        entering = []
        for s in range(2):
            held = jnp.zeros(local.shape[1:], f32)
            for hop in range(nz - 1):
                at = hop if step == 1 else nz - 1 - hop
                leaving = local[s] + own_decay[s][None] * held if hop else local[s]
                held = held + lax.ppermute(
                    leaving.astype(bf16), "z", [(at, at + step)]
                ).astype(f32)
            entering.append(held)
        return jnp.stack(entering)

    state_in = chained(own_state, 1)
    packed_ff = jnp.concatenate([split_ff(w_gate), split_ff(w_up)], axis=2)
    rest = low_dot(normed_rows, full_rest).reshape(2, span_all, REST_COLS)

    positions = zi * span_all + jnp.arange(span_all, dtype=jnp.int32)
    cosine, sine = rope_tables(positions)
    query16 = (
        rotate(rest[..., AT_Q:AT_K].reshape(2, span_all, 2, HEAD_DIM), cosine, sine)
        .astype(bf16)
        .reshape(2, span_all, QP)
    )
    key16 = rotate(rest[..., None, AT_K:AT_V], cosine, sine).astype(bf16)[:, :, 0]
    kv16 = jnp.stack([key16, rest[..., AT_V:].astype(bf16)])
    kv_all = jnp.concatenate([shifted(kv16, d) for d in range(nz - 1, 0, -1)] + [kv16], axis=2)
    keys_at = (zi - nz + 1) * span_all + jnp.arange(nz * span_all, dtype=jnp.int32)
    query_place = jnp.broadcast_to(positions[:, None], (span_all, 128))
    key_place = jnp.broadcast_to(keys_at[None], (8, nz * span_all))
    attended, log_sum = attend(query16, kv_all[0], kv_all[1], query_place, key_place)
    attended16 = attended.reshape(tokens, QP).astype(bf16)

    values, flat, square = scan_values(
        mixed, steps, starts, prefix, state_in, rest, 0, skip, lift
    )
    root = lax.rsqrt(group_total(square[..., :1]) / INNER + epsilon)
    gated16 = (flat * root * gain).astype(bf16).reshape(tokens, PART)
    third = jnp.concatenate(
        [to_ranks(packed_ff).reshape(4 * rows, 2 * hidden_part), w_down], axis=0
    )
    whole_third = gathered(after(third, flat, attended)).reshape(nz * ny, 4 * rows + ff_rows, D)
    full_ff = whole_third[:, : 4 * rows].reshape(D, 2 * hidden_part)
    full_down = whole_third[:, 4 * rows :].reshape(hidden_part, D)
    mixture = low_dot(gated16, full_out) + low_dot(attended16, full_o)
    hidden_state = resident + scatter_sequences(mixture.reshape(2, span_all, D))

    middle, mid_back = jax.vjp(rms_scale, hidden_state, mid_gain)
    middle16 = jnp.concatenate(gather_tokens(permuted(middle.astype(bf16))), 0)
    cotangent16 = jnp.concatenate(gather_tokens(out_grad[0]), 0)
    both = low_dot(middle16, full_ff)
    activated, swish_back = jax.vjp(
        swish_product, both[:, :hidden_part], both[:, hidden_part:]
    )
    activated16 = activated.astype(bf16)
    down = low_dot(activated16, full_down).reshape(4, length, D)
    output = (hidden_state + scatter_tokens(down)).astype(bf16)
    gate_grad, up_grad = swish_back(back_dot(cotangent16, full_down))
    both16 = jnp.concatenate([gate_grad, up_grad], axis=1).astype(bf16)
    mid_grad = restored(scatter_tokens(back_dot(both16, full_ff).reshape(4, length, D)))
    hidden_piece, mid_gain_grad = mid_back(mid_grad)
    hidden_grad = out_grad[0].astype(f32) + hidden_piece

    def to_owners(array):
        return lax.psum_scatter(array.astype(bf16), SHARDS, scatter_dimension=0, tiled=True)

    down_owned = to_owners(weight_grad(activated16, cotangent16))
    result_down = down_owned.astype(f32)
    ff_owned = to_owners(after(weight_grad(middle16, both16).astype(bf16), down_owned))
    ff_parts = to_ranks(ff_owned.reshape(4, rows, 2 * hidden_part))
    result_gate = join_ff(ff_parts[..., :hidden_part]).astype(f32)
    result_up = join_ff(ff_parts[..., hidden_part:]).astype(f32)

    mix16 = gather_sequences(hidden_grad.astype(bf16)).reshape(tokens, D)
    attended_grad16 = back_dot(mix16, full_o).astype(bf16).reshape(2, span_all, QP)
    gated_grad = back_dot(mix16, full_out).reshape(2, span_all, PART)
    grad_out_w = weight_grad(gated16, mix16).astype(bf16)
    grad_o = weight_grad(attended16, mix16).astype(bf16)

    inner = jnp.sum(gated_grad * gain * flat, axis=-1, keepdims=True) * root
    inner_mean = group_total(inner) / INNER
    wide = (2, span_all, 128)
    value_grad, gate_z_grad, gain_grad, suffix, first_grad = gate_backward(
        gated_grad,
        values,
        rest,
        0,
        jnp.broadcast_to(root, wide),
        jnp.broadcast_to(inner_mean, wide),
        gain,
        mixed,
        steps,
        lift,
    )
    state_grad = chained(first_grad, -1)

    query_grad, kv_grads = attend_backward(
        query16,
        kv_all[0],
        kv_all[1],
        attended_grad16,
        attended,
        log_sum,
        query_place,
        key_place,
    )
    kv_grads = kv_grads.reshape(2, 2, nz, span_all, HEAD_DIM)
    kv_grad = kv_grads[:, :, nz - 1]
    for d in range(1, nz):
        kv_grad = kv_grad + shifted(kv_grads[:, :, nz - 1 - d].astype(bf16), -d).astype(f32)
    query_back = rotate(
        query_grad.reshape(2, span_all, 2, HEAD_DIM), cosine, -sine
    ).reshape(2, span_all, QP)
    key_back = rotate(kv_grad[0][:, :, None], cosine, -sine)[:, :, 0]
    rest_grad16 = jnp.concatenate(
        [
            gate_z_grad,
            query_back.astype(bf16),
            key_back.astype(bf16),
            kv_grad[1].astype(bf16),
        ],
        axis=-1,
    ).reshape(tokens, REST_COLS)

    scan_grad16, edge_grad, conv_grad, small_grad = scan_backward(
        scan_in,
        before,
        mixed,
        steps,
        starts,
        prefix,
        state_in,
        suffix,
        state_grad,
        after(value_grad, down_owned),
        skip,
        taps,
        bias,
        dt_b,
        rates,
        lift,
    )
    edge_back = shifted(edge_grad[:, 8 - edge_count :].astype(bf16), -1).astype(f32)
    last_rows = scan_grad16[:, span_all - edge_count :, :CONV_COLS].astype(f32) + edge_back
    scan_grad16 = lax.dynamic_update_slice(
        scan_grad16, last_rows.astype(bf16), (0, span_all - edge_count, 0)
    ).reshape(tokens, SCAN_COLS)
    grads = [
        weight_grad(normed_rows, scan_grad16).astype(bf16),
        weight_grad(normed_rows, rest_grad16).astype(bf16),
    ]
    if aligned:
        rows_grad = jnp.concatenate(
            [grad_out_w.reshape(nz * ny, out_rows, D), grad_o.reshape(nz * ny, o_rows, D)], axis=1
        ).reshape(nz * ny, 2 * rows, 2, HALF)
        grads.append(jnp.swapaxes(rows_grad, 1, 2).reshape(D, HALF))
    mix_owned = to_owners(after(jnp.concatenate(grads, axis=1), ff_owned))
    scan_parts = to_ranks(mix_owned[:, :SCAN_COLS].reshape(4, rows, SCAN_COLS)).astype(f32)
    rest_parts = to_ranks(
        mix_owned[:, SCAN_COLS : SCAN_COLS + REST_COLS].reshape(4, rows, REST_COLS)
    ).astype(f32)
    if aligned:
        rows_parts = jnp.swapaxes(
            mix_owned[:, SCAN_COLS + REST_COLS :].reshape(2, 2 * rows, HALF), 0, 1
        ).reshape(2 * rows, D)
        result_out = lax.ppermute(rows_parts[:out_rows], ("y", "c"), turn).astype(f32)
        result_o = lax.ppermute(rows_parts[out_rows:], ("z", "y", "c"), back_place).astype(f32)
    else:
        every_out = lax.dynamic_update_slice_in_dim(
            jnp.zeros((INNER, D), bf16), grad_out_w, (2 * xi + ci) * PART, 0
        )
        every_o = lax.dynamic_update_slice(
            jnp.zeros((2, 2, 2, HEAD_DIM, D), bf16),
            grad_o.reshape(1, 2, 1, HEAD_DIM, D),
            (ci, 0, xi, 0, 0),
        ).reshape(ATT_HEADS * HEAD_DIM, D)
        result_out = lax.psum_scatter(every_out, EVERY, scatter_dimension=0, tiled=True)
        result_o = lax.psum_scatter(every_o, EVERY, scatter_dimension=0, tiled=True)
        result_out, result_o = result_out.astype(f32), result_o.astype(f32)

    normed_grad = back_dot(scan_grad16, full_scan) + back_dot(rest_grad16, full_rest)
    normed_grad = restored(scatter_sequences(normed_grad.reshape(2, span_all, D)))
    resident_grad, norm_gain_grad = norm_back(normed_grad)
    input_grad = hidden_grad + resident_grad

    result_in = jnp.concatenate(
        [
            heads_join(rest_parts[..., :PART], MAMBA_HEAD),
            heads_join(scan_parts[..., :PART], MAMBA_HEAD),
            jnp.sum(scan_parts[..., PART:CONV_COLS], axis=0),
            heads_join(scan_parts[..., CONV_COLS : CONV_COLS + HEADS], 1),
        ],
        axis=1,
    )
    result_q = jnp.transpose(
        rest_parts[..., AT_Q:AT_K].reshape(2, 2, rows, 2, HEAD_DIM), (2, 1, 3, 0, 4)
    ).reshape(rows, ATT_HEADS * HEAD_DIM)
    kv_parts = jnp.sum(rest_parts[..., AT_K:].reshape(2, 2, rows, 2, HEAD_DIM), axis=0)
    result_k = jnp.transpose(kv_parts[:, :, 0], (1, 0, 2)).reshape(rows, KV_HEADS * HEAD_DIM)
    result_v = jnp.transpose(kv_parts[:, :, 1], (1, 0, 2)).reshape(rows, KV_HEADS * HEAD_DIM)

    def all_channels(array):
        return jnp.concatenate(
            [heads_spread(array[..., :PART], MAMBA_HEAD), array[..., PART:]], axis=-1
        )

    small = [
        norm_gain_grad,
        all_channels(conv_grad[:4]),
        all_channels(conv_grad[4]),
        heads_spread(small_grad[0, :HEADS], 1),
        heads_spread(small_grad[1, :HEADS], 1),
        heads_spread(small_grad[2, :HEADS], 1),
        heads_spread(gain_grad[0], MAMBA_HEAD),
        mid_gain_grad,
    ]
    summed = total(jnp.concatenate([v.reshape(-1) for v in small]))
    parts, at = [], 0
    for v in small:
        parts.append(summed[at : at + v.size].reshape(v.shape))
        at += v.size
    return (
        output[None],
        input_grad[None],
        parts[0],
        result_in,
        parts[1],
        parts[2],
        parts[3],
        parts[4],
        parts[5],
        parts[6],
        result_out,
        result_q,
        result_k,
        result_v,
        result_o,
        parts[7],
        result_gate,
        result_up,
        result_down,
    )


def solution(mesh):
    seq, fsdp = mesh.shape["seq"], mesh.shape["fsdp"]
    split = Mesh(mesh.devices.reshape(seq // 2, 2, fsdp // 2, 2), EVERY)
    tokens = P(("y", "c"), ("z", "x"), None)
    matrix = P(EVERY, None)
    return jax.shard_map(
        body,
        mesh=split,
        in_specs=(tokens, tokens, P(), matrix)
        + (P(),) * 6
        + (matrix,) * 5
        + (P(),)
        + (matrix,) * 3,
        out_specs=(tokens, tokens, P(), matrix)
        + (P(),) * 6
        + (matrix,) * 5
        + (P(),)
        + (matrix,) * 3,
        check_vma=False,
    )
```

time: 1350 us -> 1330 us (0.985)
  Pallas kernels: 0 us -> 123 us
  matrix products: 222 us -> 149 us
  other arithmetic: 163 us -> 121 us
    pallas_call x0 -> x6, Pallas kernels: none -> 123 us  [the longest x1 51 us: scan_backward(): grid_call(scan_back_kernel, n, [by_span(SCAN_COLS, 0, n), by_piece(8, CON...]
    ppermute x8, waiting for transfers between devices: 92.3 us -> 3.64 us  [shifted(): lax.ppermute(array, 'z', [(i - distance, i) for i in devices if i - dista...]
    dot_general x26 -> x0, matrix products: 64.9 us -> none  [the longest x3 12 us: scan_all(): inside = jnp.einsum('bnhts,bnshp->bnthp', weights, xs, precision=highest)]
    ppermute x12, waiting for transfers between devices: 55.7 us -> 98.5 us  [chained(): lax.ppermute(leaving.astype(bf16), 'z', [(at, at + step)]).astype(f32)]
    reshape x25 -> x9, local copies, waits for them, and re-layouts: 51.7 us -> 19 us  [the longest x1 7.87 us: body(): grads.append(jnp.swapaxes(rows_grad, 1, 2).reshape(D, HALF))]
    concatenate x0 -> x8, local copies, waits for them, and re-layouts: none -> 32.3 us  [the longest x4 31.6 us: body(): jnp.concatenate([grad_out_w.reshape(nz * ny, out_rows, D), grad_o.reshape...]
    reduce_sum x12 -> x1, other arithmetic: 27.3 us -> 0.18 us  [body(): jnp.sum(rest_parts[..., AT_K:].reshape(2, 2, rows, 2, HEAD_DIM), axis=0)]
    ppermute x5, waiting for transfers between devices: 8.2 us -> 30 us  [total(): lax.ppermute(array, axis, [(i, i ^ bit) for i in range(size)])]
  transfers between devices with their start and end apart: 67 -> 64, of which waited for: 29 -> 27; matrix products, arithmetic and copies ran while one was open for 34% -> 28% of each run, Pallas kernels for 0% -> 8%
where the time goes in v3:
time: 1330 us; the launch traced here: 1320 us
  waiting for transfers between devices  599 us (45%)
  local copies, waits for them, and re-layouts  179 us (13%)
  matrix products  149 us (11%)
  Pallas kernels  123 us (9%)
  other arithmetic  121 us (9%)
  starting transfers between devices  116 us (9%)
  between operations  17.6 us (1%)
  blocking collectives  15.1 us (1%)
    ppermute x24, waiting for transfers between devices, swap(): return lax.ppermute(array, axis, [(0, 1), (1, 0)])  156 us
    all_gather x3, waiting for transfers between devices, gathered(): return lax.all_gather(array, SHARDS, axis=0, tiled=True)  151 us
    reduce_scatter x3, waiting for transfers between devices, to_owners(): lax.psum_scatter(array.astype(bf16), SHARDS, scatter_dimension=0, tiled=T...  150 us
    ppermute x12, waiting for transfers between devices, chained(): lax.ppermute(leaving.astype(bf16), 'z', [(at, at + step)]).astype(f32)  98.5 us
    dot_general x6, matrix products, back_dot(): lax.dot_general(grad_rows, weight, (((1,), (1,)), ((), ())), preferred_el...  58.4 us
    pallas_call x1, Pallas kernels, scan_backward(): grid_call(scan_back_kernel, n, [by_span(SCAN_COLS, 0, n), by_piece(8, CON...  51 us
    ppermute x8, starting transfers between devices, shifted(): lax.ppermute(array, 'z', [(i - distance, i) for i in devices if i - dista...  49.6 us
    dot_general x6, matrix products, weight_grad(): lax.dot_general(left, right, (((0,), (0,)), ((), ())), preferred_element_...  46.9 us
  transfers between devices with their start and end apart: 64, of which 27 were waited for; matrix products, arithmetic and copies ran while one was open for 28% of the time, Pallas kernels for 8%

profile of v3, /device:TPU:0, one launch (start us, length us, event | category | flops | bytes accessed | tf_op | source)
XLA Modules:
  0.0 1319.3 jit_solution(15094188158083866576)
XLA Ops:
  10.2 15.1 %all_to_all.30 = bf16[4,64,1408]{2,1,0:T(8,128)(2,1)} all-to-all(bf16[4,64,1408]{2,1,0:T(8,128)(2,1)S(1)} %fusion.65), channel_id=1, replica_groups=mesh['z'=4,'x'=2,'y'=2,'c'=2] {'x','c'}, dimensions={0} | all-to-all | bytes 1441792 | tf_op jit(solution)/shard_map/all_to_all | solution.py:693
  37.1 15.5 %collective-permute-done = bf16[256,2048]{1,0:T(8,128)(2,1)} collective-permute-done((bf16[256,2048]{1,0:T(8,128)(2,1)S(1)}, bf16[256,2048]{1,0:T(8,128)(2,1)}, u32[]{:S(2)}, u32[]{:S(2)}) %collective-permute-start) | collective-permute-done | bytes 1048608 | tf_op jit(solution)/shard_map/ppermute | solution.py:42
  88.6 32.2 %all-gather.4.cloned.1.call-done = bf16[2048,1408]{1,0:T(8,128)(2,1)} async-done(((bf16[256,1408]{1,0:T(8,128)(2,1)}), bf16[2048,1408]{1,0:T(8,128)(2,1)}) %all-gather.4.cloned.1.call-update) | async-done | bytes 5767184 | tf_op jit(solution)/shard_map/all_gather | solution.py:736
  133.8 15.1 %shard_map.330 = (f32[2,512,1280]{2,1,0:T(8,128)}, f32[2,512,256]{2,1,0:T(8,128)S(1)}, f32[2,4,8,128]{3,2,1,0:T(8,128)S(1)}, f32[2,4,256,768]{3,2,1,0:T(8,128)}, f32[2,256,768]{2,1,0:T(8,128)S(1)}) custom-call(f32[2,512,1408]{2,1,0:T(8,128)} %bitcast.350, f32[2,4,8,1280]{3,2,1,0:T(8,128)S(1)} %pad_maximum_fusion.26.before, ...), custom_call_target="tpu_custom_call" | custom-call | flops 8000000000 | bytes 30000000 | tf_op jit(solution)/shard_map/pallas_call | solution.py:389
  155.3 15.8 %collective-permute-done.4 = bf16[256,768]{1,0:T(8,128)(2,1)} collective-permute-done((bf16[256,768]{1,0:T(8,128)(2,1)}, bf16[256,768]{1,0:T(8,128)(2,1)}, u32[]{:S(2)}, u32[]{:S(2)}) %collective-permute-start.4) | collective-permute-done | bytes 393248 | tf_op jit(solution)/shard_map/ppermute | solution.py:825
  171.1 14.8 %collective-permute-done.7 = bf16[256,768]{1,0:T(8,128)(2,1)S(1)} collective-permute-done((bf16[256,768]{1,0:T(8,128)(2,1)}, bf16[256,768]{1,0:T(8,128)(2,1)S(1)}, u32[]{:S(2)}, u32[]{:S(2)}) %collective-permute-start.7) | collective-permute-done | bytes 393248 | tf_op jit(solution)/shard_map/ppermute | solution.py:825
  203.0 69.7 %all-gather.6.cloned.1.call-done = bf16[2048,2304]{1,0:T(8,128)(2,1)} async-done(((bf16[256,2304]{1,0:T(8,128)(2,1)}), bf16[2048,2304]{1,0:T(8,128)(2,1)}) %all-gather.6.cloned.1.call-update) | async-done | bytes 9437200 | tf_op jit(solution)/shard_map/all_gather | solution.py:736
  283.5 33.9 %collective-permute-start.14 = (bf16[2,2,512,128]{3,2,1,0:T(8,128)(2,1)}, bf16[2,2,512,128]{3,2,1,0:T(8,128)(2,1)}, u32[]{:S(2)}, u32[]{:S(2)}) collective-permute-start(bf16[2,2,512,128]{3,2,1,0:T(8,128)(2,1)} %pad_maximum_fusion.24), channel_id=1, source_target_pairs={{0,24},{1,25},{2,26},{3,27},{4,28},{5,29},{6,30},{7,31}} | collective-permute-start | bytes 1572872 | tf_op jit(solution)/shard_map/ppermute | solution.py:47
  424.2 25.1 %collective-permute-done.18 = bf16[256,2048]{1,0:T(8,128)(2,1)S(1)} collective-permute-done((bf16[256,2048]{1,0:T(8,128)(2,1)S(1)}, bf16[256,2048]{1,0:T(8,128)(2,1)S(1)}, u32[]{:S(2)}, u32[]{:S(2)}) %collective-permute-start.18) | collective-permute-done | bytes 1048608 | tf_op jit(solution)/shard_map/ppermute | solution.py:42
  460.7 24.4 %collective-permute-done.20 = bf16[256,2048]{1,0:T(8,128)(2,1)} collective-permute-done((bf16[256,2048]{1,0:T(8,128)(2,1)}, bf16[256,2048]{1,0:T(8,128)(2,1)}, u32[]{:S(2)}, u32[]{:S(2)}) %collective-permute-start.20) | collective-permute-done | bytes 1048608 | tf_op jit(solution)/shard_map/ppermute | solution.py:42
  485.6 20.2 %collective-permute-done.25 = bf16[256,2048]{1,0:T(8,128)(2,1)} collective-permute-done((bf16[256,2048]{1,0:T(8,128)(2,1)S(1)}, bf16[256,2048]{1,0:T(8,128)(2,1)}, u32[]{:S(2)}, u32[]{:S(2)}) %collective-permute-start.25) | collective-permute-done | bytes 1048608 | tf_op jit(solution)/shard_map/ppermute | solution.py:42
  505.8 48.8 %all-gather.8.cloned.1.call-done = bf16[3072,2048]{1,0:T(8,128)(2,1)} async-done(((bf16[384,2048]{1,0:T(8,128)(2,1)}), bf16[3072,2048]{1,0:T(8,128)(2,1)}) %all-gather.8.cloned.1.call-update) | async-done | bytes 12582928 | tf_op jit(solution)/shard_map/all_gather | solution.py:736
  594.5 15.7 %fusion.101 = (bf16[1024,2048]{1,0:T(8,128)(2,1)S(1)}, f32[1024,2048]{1,0:T(8,128)}) fusion(bf16[2048,2048]{1,0:T(8,128)(2,1)} %bitcast.302, bf16[1024,1024]{1,0:T(8,128)(2,1)} %get-tuple-element.81, bf16[1024,1024]{1,0:T(8,128)(2,1)} %get-tuple-element.80), kind=kOutput, calls=%fused_computation.322 | convolution fusion | flops 8600420352 | bytes 25165824 | tf_op jit(solution)/shard_map/dot_general | solution.py:70
  629.0 15.4 %collective-permute-done.28 = bf16[256,2048]{1,0:T(8,128)(2,1)} collective-permute-done((bf16[256,2048]{1,0:T(8,128)(2,1)}, bf16[256,2048]{1,0:T(8,128)(2,1)}, u32[]{:S(2)}, u32[]{:S(2)}) %collective-permute-start.28) | collective-permute-done | bytes 1048608 | tf_op jit(solution)/shard_map/ppermute | solution.py:42
  653.4 23.0 %collective-permute-done.29 = bf16[256,2048]{1,0:T(8,128)(2,1)S(1)} collective-permute-done((bf16[256,2048]{1,0:T(8,128)(2,1)}, bf16[256,2048]{1,0:T(8,128)(2,1)S(1)}, u32[]{:S(2)}, u32[]{:S(2)}) %collective-permute-start.29) | collective-permute-done | bytes 1048608 | tf_op jit(solution)/shard_map/ppermute | solution.py:42
  676.4 14.3 %convolution_convert_fusion = bf16[2048,2048]{1,0:T(8,128)(2,1)} fusion(bf16[1024,1024]{1,0:T(8,128)(2,1)} %get-tuple-element.81, bf16[1024,1024]{1,0:T(8,128)(2,1)} %get-tuple-element.80, bf16[256,2048]{1,0:T(8,128)(2,1)} %collective-permute-done.21, bf16[256,2048]{1,0:T(8,128)(2,1)} %collective-permute-done.20, ...), kind=kOutput, calls=%fused_computation.3 | convolution fusion | flops 8619294720 | bytes 16777216 | tf_op jit(solution)/shard_map/dot_general | solution.py:74
  700.2 14.2 %reduce-scatter.4.cloned.1.call-done = bf16[128,2048]{1,0:T(8,128)(2,1)} async-done(((bf16[1024,2048]{1,0:T(8,128)(2,1)}), bf16[128,2048]{1,0:T(8,128)(2,1)}) %reduce-scatter.4.cloned.1.call-update) | async-done | bytes 524304 | tf_op jit(solution)/shard_map/reduce_scatter | solution.py:882
  738.8 18.9 %shard_map.335 = (f32[2,512,256]{2,1,0:T(8,128)S(1)}, f32[2,2,2048,128]{3,2,1,0:T(8,128)}) custom-call(bf16[2,512,256]{2,1,0:T(8,128)(2,1)S(1)} %copy-done.9, bf16[2,2048,128]{2,1,0:T(8,128)(2,1)S(1)} %copy-done.7, bf16[2,2048,128]{2,1,0:T(8,128)(2,1)} %get-tuple-element.92.value, bf16[2,512,256]{2,1,0:T(8,128)(2,1)S(1)} %bitcast.292, ...), custom_call_target="tpu_custom_call" | custom-call | flops 20000000000 | bytes 30000000 | tf_op jit(solution)/shard_map/pallas_call | solution.py:578
  772.9 15.7 %copy.230 = bf16[8,96,2,1024]{1,2,0,3:T(2,128)(2,1)} copy(bf16[8,96,2,1024]{3,2,1,0:T(2,128)(2,1)} %concatenate.150) | data formatting | bytes 6291456 | tf_op jit(solution)/shard_map/concatenate | solution.py:970
  856.7 63.2 %collective-permute-done.36 = bf16[256,768]{1,0:T(8,128)(2,1)S(1)} collective-permute-done((bf16[256,768]{1,0:T(8,128)(2,1)S(1)}, bf16[256,768]{1,0:T(8,128)(2,1)S(1)}, u32[]{:S(2)}, u32[]{:S(2)}) %collective-permute-start.36) | collective-permute-done | bytes 393248 | tf_op jit(solution)/shard_map/ppermute | solution.py:825
  928.3 51.0 %shard_map.334 = (bf16[2,512,1408]{2,1,0:T(8,128)(2,1)}, f32[2,8,1280]{2,1,0:T(8,128)S(1)}, f32[8,1280]{1,0:T(8,128)S(1)}, f32[8,128]{1,0:T(8,128)S(1)}) custom-call(f32[2,512,1408]{2,1,0:T(8,128)} %bitcast.351, f32[2,4,8,1280]{3,2,1,0:T(8,128)S(1)} %copy-done.11, f32[2,512,1280]{2,1,0:T(8,128)} %get-tuple-element.45.mixed.c_part, ...), custom_call_target="tpu_custom_call" | custom-call | flops 30000001024 | bytes 50000000 | tf_op jit(solution)/shard_map/pallas_call | solution.py:477
  1046.7 18.7 %collective-permute-done.45 = bf16[256,2048]{1,0:T(8,128)(2,1)S(1)} collective-permute-done((bf16[256,2048]{1,0:T(8,128)(2,1)S(1)}, bf16[256,2048]{1,0:T(8,128)(2,1)S(1)}, u32[]{:S(2)}, u32[]{:S(2)}) %collective-permute-start.45) | collective-permute-done | bytes 1048608 | tf_op jit(solution)/shard_map/ppermute | solution.py:42
  1083.8 14.7 %collective-permute-done.47 = f32[25232]{0:T(1024)S(1)} collective-permute-done((f32[25232]{0:T(1024)S(1)}, f32[25232]{0:T(1024)S(1)}, u32[]{:S(2)}, u32[]{:S(2)}) %collective-permute-start.47) | collective-permute-done | bytes 100960 | tf_op jit(solution)/shard_map/ppermute | solution.py:55
  1119.1 136.2 %reduce-scatter.8.cloned.1.call-done = bf16[256,3712]{0,1:T(8,128)(2,1)} async-done(((bf16[2048,3712]{0,1:T(8,128)(2,1)}), bf16[256,3712]{0,1:T(8,128)(2,1)}) %reduce-scatter.8.cloned.1.call-update) | async-done | bytes 1900560 | tf_op jit(solution)/shard_map/reduce_scatter | solution.py:882
  (718 shorter events, 570.2 us)
Async XLA Ops:
  7.2 113.5 %all-gather.4.cloned.1.call-start = ((), (), s32[]{:S(2)}) async-start(), calls=%async_computation.9 | async-start | bytes 6488064 | tf_op jit(solution)/shard_map/all_gather | solution.py:736
  36.0 236.8 %all-gather.6.cloned.1.call-start = ((), (), s32[]{:S(2)}) async-start(), calls=%async_computation.10 | async-start | bytes 10616832 | tf_op jit(solution)/shard_map/all_gather | solution.py:736
  73.3 124.5 %all-to-all-start.2 = ((bf16[4,64,2048]{2,1,0:T(8,128)(2,1)}), bf16[4,64,2048]{2,1,0:T(8,128)(2,1)}, u32[]{:S(2)}, u32[]{:S(2)}) async-start(bf16[4,64,2048]{2,1,0:T(8,128)(2,1)} %pad_maximum_fusion.16), calls=%async_computation.2 | async-start | bytes 2097152 | tf_op jit(solution)/shard_map/all_to_all | solution.py:693
  81.5 473.1 %all-gather.8.cloned.1.call-start = ((), (), s32[]{:S(2)}) async-start(), calls=%async_computation.11 | async-start | bytes 14155776 | tf_op jit(solution)/shard_map/all_gather | solution.py:736
  83.3 48.0 %collective-permute-start.3 = (bf16[2,8,2048]{2,1,0:T(8,128)(2,1)S(1)}, bf16[2,8,2048]{2,1,0:T(8,128)(2,1)S(1)}, u32[]{:S(2)}, u32[]{:S(2)}) collective-permute-start(bf16[2,8,2048]{2,1,0:T(8,128)(2,1)S(1)} %fusion.76), channel_id=1, source_target_pairs={{0,8},{8,16},{16,24},{1,9},{9,17},{17,25},{2,10},{10,18},{18,26},{... | collective-permute-start | bytes 196616 | tf_op jit(solution)/shard_map/ppermute | solution.py:47
  153.7 32.2 %collective-permute-start.7 = (bf16[256,768]{1,0:T(8,128)(2,1)}, bf16[256,768]{1,0:T(8,128)(2,1)S(1)}, u32[]{:S(2)}, u32[]{:S(2)}) collective-permute-start(bf16[256,768]{1,0:T(8,128)(2,1)} %get-tuple-element.109), channel_id=1, source_target_pairs={{0,8},{1,9},{2,10},{3,11},{4,12},{5,13},{6,14},{7,15}} | collective-permute-start | bytes 1179656 | tf_op jit(solution)/shard_map/ppermute | solution.py:825
  283.5 62.6 %collective-permute-start.14 = (bf16[2,2,512,128]{3,2,1,0:T(8,128)(2,1)}, bf16[2,2,512,128]{3,2,1,0:T(8,128)(2,1)}, u32[]{:S(2)}, u32[]{:S(2)}) collective-permute-start(bf16[2,2,512,128]{3,2,1,0:T(8,128)(2,1)} %pad_maximum_fusion.24), channel_id=1, source_target_pairs={{0,24},{1,25},{2,26},{3,27},{4,28},{5,29},{6,30},{7,31}} | collective-permute-start | bytes 1572872 | tf_op jit(solution)/shard_map/ppermute | solution.py:47
  366.7 347.8 %reduce-scatter.4.cloned.1.call-start = ((), (), s32[]{:S(2)}) async-start(), calls=%async_computation.12 | async-start | bytes 4718592 | tf_op jit(solution)/shard_map/reduce_scatter | solution.py:882
  458.9 46.9 %collective-permute-start.25 = (bf16[256,2048]{1,0:T(8,128)(2,1)S(1)}, bf16[256,2048]{1,0:T(8,128)(2,1)}, u32[]{:S(2)}, u32[]{:S(2)}) collective-permute-start(bf16[256,2048]{1,0:T(8,128)(2,1)S(1)} %bitcast.314), channel_id=1, source_target_pairs={{0,4},{4,0},{1,5},{5,1},{2,6},{6,2},{3,7},{7,3},{8,12},{12,8},{9,1... | collective-permute-start | bytes 3145736 | tf_op jit(solution)/shard_map/ppermute | solution.py:42
  460.7 105.2 %collective-permute-start.19 = (bf16[256,2048]{1,0:T(8,128)(2,1)}, bf16[256,2048]{1,0:T(8,128)(2,1)}, u32[]{:S(2)}, u32[]{:S(2)}) collective-permute-start(bf16[256,2048]{1,0:T(8,128)(2,1)} %constant_dynamic-update-slice_fusion.10), channel_id=1, source_target_pairs={{0,1},{1,0},{2,3},{3,2},{4,5},{5,4},{6,7},{7,6},{8,9},{9,8},{10,11... | collective-permute-start | bytes 3145736 | tf_op jit(solution)/shard_map/ppermute | solution.py:42
  485.1 80.8 %collective-permute-start.21 = (bf16[256,2048]{1,0:T(8,128)(2,1)}, bf16[256,2048]{1,0:T(8,128)(2,1)}, u32[]{:S(2)}, u32[]{:S(2)}) collective-permute-start(bf16[256,2048]{1,0:T(8,128)(2,1)} %collective-permute-done.20), channel_id=1, source_target_pairs={{0,1},{1,0},{2,3},{3,2},{4,5},{5,4},{6,7},{7,6},{8,9},{9,8},{10,11... | collective-permute-start | bytes 3145736 | tf_op jit(solution)/shard_map/ppermute | solution.py:42
  485.1 98.1 %collective-permute-start.24 = (bf16[256,2048]{1,0:T(8,128)(2,1)S(1)}, bf16[256,2048]{1,0:T(8,128)(2,1)}, u32[]{:S(2)}, u32[]{:S(2)}) collective-permute-start(bf16[256,2048]{1,0:T(8,128)(2,1)S(1)} %bitcast.315), channel_id=1, source_target_pairs={{0,1},{1,0},{2,3},{3,2},{4,5},{5,4},{6,7},{7,6},{8,9},{9,8},{10,11... | collective-permute-start | bytes 3145736 | tf_op jit(solution)/shard_map/ppermute | solution.py:42
  505.8 77.3 %collective-permute-start.26 = (bf16[256,2048]{1,0:T(8,128)(2,1)}, bf16[256,2048]{1,0:T(8,128)(2,1)}, u32[]{:S(2)}, u32[]{:S(2)}) collective-permute-start(bf16[256,2048]{1,0:T(8,128)(2,1)} %collective-permute-done.25), channel_id=1, source_target_pairs={{0,1},{1,0},{2,3},{3,2},{4,5},{5,4},{6,7},{7,6},{8,9},{9,8},{10,11... | collective-permute-start | bytes 3145736 | tf_op jit(solution)/shard_map/ppermute | solution.py:42
  629.0 378.3 %reduce-scatter.6.cloned.1.call-start = ((), (), s32[]{:S(2)}) async-start(), calls=%async_computation.13 | async-start | bytes 9437184 | tf_op jit(solution)/shard_map/reduce_scatter | solution.py:882
  653.3 42.1 %collective-permute-start.30 = (bf16[256,2048]{1,0:T(8,128)(2,1)}, bf16[256,2048]{1,0:T(8,128)(2,1)}, u32[]{:S(2)}, u32[]{:S(2)}) collective-permute-start(bf16[256,2048]{1,0:T(8,128)(2,1)} %fusion.94), channel_id=1, source_target_pairs={{0,1},{1,0},{2,3},{3,2},{4,5},{5,4},{6,7},{7,6},{8,9},{9,8},{10,11... | collective-permute-start | bytes 3145736 | tf_op jit(solution)/shard_map/ppermute | solution.py:42
  714.5 540.7 %reduce-scatter.8.cloned.1.call-start = ((), (), s32[]{:S(2)}) async-start(), calls=%async_computation.14 | async-start | bytes 17104896 | tf_op jit(solution)/shard_map/reduce_scatter | solution.py:882
  726.6 71.8 %collective-permute-start.32 = (f32[2,512,1]{2,1,0:T(8,128)}, f32[2,512,1]{2,1,0:T(8,128)}, u32[]{:S(2)}, u32[]{:S(2)}) collective-permute-start(f32[2,512,1]{2,1,0:T(8,128)} %rev.7), channel_id=1, source_target_pairs={{0,1},{1,0},{2,3},{3,2},{4,5},{5,4},{6,7},{7,6},{8,9},{9,8},{10,11... | collective-permute-start | bytes 12296 | tf_op jit(solution)/shard_map/ppermute | solution.py:42
  762.4 87.8 %collective-permute-start.41 = (bf16[2,2,512,128]{3,2,1,0:T(8,128)(2,1)}, bf16[2,2,512,128]{3,2,1,0:T(8,128)(2,1)}, u32[]{:S(2)}, u32[]{:S(2)}) collective-permute-start(bf16[2,2,512,128]{3,2,1,0:T(8,128)(2,1)} %get-tuple-element.89), channel_id=1, source_target_pairs={{8,0},{16,8},{24,16},{9,1},{17,9},{25,17},{10,2},{18,10},{26,18},{... | collective-permute-start | bytes 1572872 | tf_op jit(solution)/shard_map/ppermute | solution.py:47
  763.7 86.5 %collective-permute-start.42 = (bf16[2,2,512,128]{3,2,1,0:T(8,128)(2,1)}, bf16[2,2,512,128]{3,2,1,0:T(8,128)(2,1)}, u32[]{:S(2)}, u32[]{:S(2)}) collective-permute-start(bf16[2,2,512,128]{3,2,1,0:T(8,128)(2,1)} %get-tuple-element.91), channel_id=1, source_target_pairs={{16,0},{24,8},{17,1},{25,9},{18,2},{26,10},{19,3},{27,11},{20,4},{... | collective-permute-start | bytes 1572872 | tf_op jit(solution)/shard_map/ppermute | solution.py:47
  765.0 85.2 %collective-permute-start.43 = (bf16[2,2,512,128]{3,2,1,0:T(8,128)(2,1)}, bf16[2,2,512,128]{3,2,1,0:T(8,128)(2,1)}, u32[]{:S(2)}, u32[]{:S(2)}) collective-permute-start(bf16[2,2,512,128]{3,2,1,0:T(8,128)(2,1)} %get-tuple-element.90), channel_id=1, source_target_pairs={{24,0},{25,1},{26,2},{27,3},{28,4},{29,5},{30,6},{31,7}} | collective-permute-start | bytes 1572872 | tf_op jit(solution)/shard_map/ppermute | solution.py:47
  853.6 66.3 %collective-permute-start.36 = (bf16[256,768]{1,0:T(8,128)(2,1)S(1)}, bf16[256,768]{1,0:T(8,128)(2,1)S(1)}, u32[]{:S(2)}, u32[]{:S(2)}) collective-permute-start(bf16[256,768]{1,0:T(8,128)(2,1)S(1)} %get-tuple-element.96), channel_id=1, source_target_pairs={{8,0},{9,1},{10,2},{11,3},{12,4},{13,5},{14,6},{15,7}} | collective-permute-start | bytes 1179656 | tf_op jit(solution)/shard_map/ppermute | solution.py:825
  855.2 70.6 %collective-permute-start.39 = (bf16[256,768]{1,0:T(8,128)(2,1)S(1)}, bf16[256,768]{1,0:T(8,128)(2,1)S(1)}, u32[]{:S(2)}, u32[]{:S(2)}) collective-permute-start(bf16[256,768]{1,0:T(8,128)(2,1)S(1)} %get-tuple-element.97), channel_id=1, source_target_pairs={{8,0},{9,1},{10,2},{11,3},{12,4},{13,5},{14,6},{15,7}} | collective-permute-start | bytes 1179656 | tf_op jit(solution)/shard_map/ppermute | solution.py:825
  1044.2 68.4 %collective-permute-start.23 = (bf16[256,2048]{1,0:T(8,128)(2,1)}, bf16[256,2048]{1,0:T(8,128)(2,1)}, u32[]{:S(2)}, u32[]{:S(2)}) collective-permute-start(bf16[256,2048]{1,0:T(8,128)(2,1)} %fusion.42), channel_id=1, source_target_pairs={{0,4},{4,0},{1,5},{5,1},{2,6},{6,2},{3,7},{7,3},{8,12},{12,8},{9,1... | collective-permute-start | bytes 3145736 | tf_op jit(solution)/shard_map/ppermute | solution.py:42
  1108.4 156.1 %all-to-all-start.5 = ((bf16[4,64,2048]{2,1,0:T(8,128)(2,1)}), bf16[4,64,2048]{2,1,0:T(8,128)(2,1)}, u32[]{:S(2)}, u32[]{:S(2)}) async-start(bf16[4,64,2048]{2,1,0:T(8,128)(2,1)} %bitcast.336), calls=%async_computation.8 | async-start | bytes 2097152 | tf_op jit(solution)/shard_map/all_to_all | solution.py:693
  (173 other events, 3135.6 us)
Sparse Core Ops, SparseCore 0:
  25.4 95.3 all-gather.3
  122.9 149.7 all-gather.5
  366.8 187.7 all-gather.7
  629.1 85.3 reduce-scatter.3
  718.4 192.6 reduce-scatter.5
  1007.4 247.7 reduce-scatter.7

commit v4 on v3

--- a/solution.py
+++ b/solution.py
@@ -27,7 +27,6 @@
 AT_K = AT_Q + QP
 AT_V = AT_K + HEAD_DIM
 REST_COLS = AT_V + HEAD_DIM
-HALF = D // 2
 
 epsilon = 1e-05
 rope_base = 100000000000.0
@@ -92,8 +91,18 @@
     return jnp.concatenate([first * cosine - second * sine, second * cosine + first * sine], axis=-1)
 
 
-def exact(left, right):
-    return jnp.dot(left, right, precision=lax.Precision.HIGHEST, preferred_element_type=f32)
+def pieces(values, count):
+    parts = []
+    for _ in range(count):
+        part = values.astype(bf16)
+        parts.append(part)
+        values = values - part.astype(f32)
+    return parts
+
+
+def running(mask, values):
+    mask16 = mask.astype(bf16)
+    return sum(low_dot(mask16, part) for part in pieces(values, 3))
 
 
 def over_lanes(left, right):
@@ -105,17 +114,11 @@
 
 
 def widen(values, lift):
-    return exact(values, lift)
+    return sum(low_dot(part, lift) for part in pieces(values, 2))
 
 
 def narrow(values, lift):
-    return lax.dot_general(
-        values,
-        lift,
-        (((1,), (1,)), ((), ())),
-        precision=lax.Precision.HIGHEST,
-        preferred_element_type=f32,
-    )
+    return sum(over_lanes(part, lift) for part in pieces(values, 2))
 
 
 def sig(values):
@@ -154,7 +157,7 @@
     mixed[0] = mix
     dt = soft(scan_in[0, :, CONV_COLS:] + dt_bias[...])
     row, column = square_places()
-    cum = exact(jnp.where(row >= column, 1.0, 0.0), dt * rates[...])
+    cum = running(jnp.where(row >= column, 1.0, 0.0), dt * rates[...])
     steps[0, :, :DT_PAD] = dt
     steps[0, :, DT_PAD:] = cum
     starts[0, 0] = sofar[...]
@@ -237,20 +240,12 @@
 
 
 def scan_back_kernel(
-    scan_in, before, mixed, steps, starts, prefix, state_in, suffix, state_grad, value_grad,
-    skip, taps, bias, dt_bias, rates, lift,
-    scan_grad, edge_grad, conv_grad, small_grad,
-    later, after_pre, columns,
+    mixed, steps, starts, prefix, state_in, suffix, value_grad, skip, lift,
+    mixed_grad, step_grad, skip_grad, columns,
 ):
-    @pl.when(pl.program_id(1) == 0)
-    def _():
-        later[...] = jnp.zeros_like(later)
-        after_pre[...] = jnp.zeros_like(after_pre)
-
     @pl.when((pl.program_id(0) == 0) & (pl.program_id(1) == 0))
     def _():
-        conv_grad[...] = jnp.zeros_like(conv_grad)
-        small_grad[...] = jnp.zeros_like(small_grad)
+        skip_grad[...] = jnp.zeros_like(skip_grad)
         columns[...] = jnp.zeros_like(columns)
 
     up = lift[...]
@@ -263,13 +258,11 @@
     end = cum[SPAN - 1 : SPAN]
     dy = value_grad[0]
     state = prefix[0, 0] + widen(jnp.exp(starts[0, 0]), up)[0:1] * state_in[0]
-    ending = suffix[0, 0] + widen(jnp.exp(later[...]), up)[0:1] * state_grad[0]
-    later[...] = later[...] + end
+    ending = suffix[0, 0]
     state16, ending16 = state.astype(bf16), ending.astype(bf16)
-    grown = widen(jnp.exp(cum), up)
+    grown_dy = widen(jnp.exp(cum), up) * dy
     tail_wide = widen(jnp.exp(end - cum), up)
     dt_wide = widen(dt, up)
-    grown_dy = grown * dy
     reach = low_dot(c16, state16)
     pull = tail_wide * low_dot(b16, ending16)
     d_c = over_lanes(grown_dy.astype(bf16), state16)
@@ -302,9 +295,9 @@
             weights.append((meet * decay).astype(bf16))
         back.append(over_rows(jnp.concatenate(weights, 0), jnp.concatenate(split, 0)))
     d_meet16 = d_meet.astype(bf16)
-    d_c = d_c + low_dot(d_meet16, b16)
-    d_b = d_b + over_rows(d_meet16, c16)
-    d_x = dt_wide * (jnp.concatenate(back, 1) + pull) + skip[...] * dy
+    mixed_grad[0, :, :PART] = dt_wide * (jnp.concatenate(back, 1) + pull) + skip[...] * dy
+    mixed_grad[0, :, PART : PART + STATE] = d_b + over_rows(d_meet16, c16)
+    mixed_grad[0, :, PART + STATE :] = d_c + low_dot(d_meet16, b16)
     tail_dt = narrow(x * pull, up)
     inner_dt = columns[...].T
     d_cum = rows_sum + narrow(grown_dy * reach, up) - dt * (inner_dt + tail_dt)
@@ -312,14 +305,59 @@
         jnp.broadcast_to(jnp.sum(state * ending, axis=0, keepdims=True), (8, PART)), up
     )[0:1]
     extra = jnp.sum(dt * tail_dt, axis=0, keepdims=True) + jnp.exp(end) * kept
-    d_log = exact(jnp.where(row <= column, 1.0, 0.0), d_cum) + extra
+    step_grad[0, :, :DT_PAD] = inner_dt + tail_dt
+    step_grad[0, :, DT_PAD:] = running(jnp.where(row <= column, 1.0, 0.0), d_cum) + extra
+    skip_grad[0:1] = skip_grad[0:1] + jnp.sum(narrow(dy * x, up), axis=0, keepdims=True)
+
+
+def finish_back_kernel(
+    scan_in, before, mixed, steps, starts, prefix, state_in, state_grad, mixed_grad, step_grad,
+    taps, bias, dt_bias, rates, lift,
+    scan_grad, edge_grad, conv_grad, small_grad,
+    later, after_pre,
+):
+    @pl.when(pl.program_id(1) == 0)
+    def _():
+        later[...] = jnp.zeros_like(later)
+        after_pre[...] = jnp.zeros_like(after_pre)
+
+    @pl.when((pl.program_id(0) == 0) & (pl.program_id(1) == 0))
+    def _():
+        conv_grad[...] = jnp.zeros_like(conv_grad)
+        small_grad[...] = jnp.zeros_like(small_grad)
+
+    up = lift[...]
+    x = mixed[0, :, :PART]
+    b16 = mixed[0, :, PART : PART + STATE].astype(bf16)
+    dt = steps[0, :, :DT_PAD]
+    cum = steps[0, :, DT_PAD:]
+    end = cum[SPAN - 1 : SPAN]
+    state = prefix[0, 0] + widen(jnp.exp(starts[0, 0]), up)[0:1] * state_in[0]
+    ending = widen(jnp.exp(later[...]), up)[0:1] * state_grad[0]
+    later[...] = later[...] + end
+    ending16 = ending.astype(bf16)
+    tail_wide = widen(jnp.exp(end - cum), up)
+    dt_wide = widen(dt, up)
+    pull = tail_wide * low_dot(b16, ending16)
+    d_x = mixed_grad[0, :, :PART] + dt_wide * pull
+    d_b = mixed_grad[0, :, PART : PART + STATE] + over_lanes(
+        (tail_wide * dt_wide * x).astype(bf16), ending16
+    )
+    d_c = mixed_grad[0, :, PART + STATE :]
+    tail_dt = narrow(x * pull, up)
+    kept = narrow(
+        jnp.broadcast_to(jnp.sum(state * ending, axis=0, keepdims=True), (8, PART)), up
+    )[0:1]
+    row, column = square_places()
+    fed = dt * tail_dt
+    earlier = running(jnp.where(row > column, 1.0, 0.0), fed)
+    d_log = step_grad[0, :, DT_PAD:] + earlier + jnp.exp(end) * kept
     rate = rates[...]
-    d_raw = (inner_dt + tail_dt + d_log * rate) * sig(
+    d_raw = (step_grad[0, :, :DT_PAD] + tail_dt + d_log * rate) * sig(
         scan_in[0, :, CONV_COLS:] + dt_bias[...]
     )
     small_grad[0:1] = small_grad[0:1] + jnp.sum(d_raw, axis=0, keepdims=True)
     small_grad[1:2] = small_grad[1:2] + jnp.sum(d_log * dt * rate, axis=0, keepdims=True)
-    small_grad[2:3] = small_grad[2:3] + jnp.sum(narrow(dy * x, up), axis=0, keepdims=True)
 
     pre, extended = pre_conv(scan_in[0, :, :CONV_COLS], before[0, 0], taps[...], bias[...])
     s = sig(pre)
@@ -337,7 +375,8 @@
     scan_grad[0, :, CONV_COLS:] = d_raw.astype(bf16)
     front = d_pre[0:8]
     after_pre[...] = front
-    padded = jnp.concatenate([jnp.zeros((8, CONV_COLS), f32), front, jnp.zeros((8, CONV_COLS), f32)], 0)
+    nothing = jnp.zeros((8, CONV_COLS), f32)
+    padded = jnp.concatenate([nothing, front, nothing], 0)
     edge = padded[0:8] * taps[3:4]
     for k in range(3):
         edge = edge + padded[3 - k : 11 - k] * taps[k : k + 1]
@@ -468,14 +507,42 @@
     )(gated_grad, values, rest, root, mean, gain, mixed, steps, lift)
 
 
-def scan_backward(
-    scan_in, before, mixed, steps, starts, prefix, state_in, suffix, state_grad, value_grad,
-    skip, taps, bias, dt_bias, rates, lift,
+def scan_backward(mixed, steps, starts, prefix, state_in, suffix, value_grad, skip, lift):
+    length = mixed.shape[1]
+    n = length // SPAN
+    return grid_call(
+        scan_back_kernel,
+        n,
+        [
+            by_span(CONV_COLS),
+            by_span(2 * DT_PAD),
+            by_piece(8, DT_PAD),
+            by_piece(STATE, PART),
+            by_sequence(STATE, PART),
+            by_piece(STATE, PART),
+            by_span(PART),
+            one((1, PART)),
+            one((DT_PAD, PART)),
+        ],
+        [
+            (by_span(CONV_COLS), like((2, length, CONV_COLS))),
+            (by_span(2 * DT_PAD), like((2, length, 2 * DT_PAD))),
+            (one((8, DT_PAD)), like((8, DT_PAD))),
+        ],
+        [pltpu.VMEM((SPAN, SPAN), f32)],
+        30 * 10**9,
+        40 * 10**6,
+    )(mixed, steps, starts, prefix, state_in, suffix, value_grad, skip, lift)
+
+
+def finish_backward(
+    scan_in, before, mixed, steps, starts, prefix, state_in, state_grad, mixed_grad, step_grad,
+    taps, bias, dt_bias, rates, lift,
 ):
     length = mixed.shape[1]
     n = length // SPAN
     return grid_call(
-        scan_back_kernel,
+        finish_back_kernel,
         n,
         [
             by_span(SCAN_COLS, 0, n),
@@ -485,10 +552,9 @@
             by_piece(8, DT_PAD, n),
             by_piece(STATE, PART, n),
             by_sequence(STATE, PART),
-            by_piece(STATE, PART, n),
             by_sequence(STATE, PART),
-            by_span(PART, 0, n),
-            one((1, PART)),
+            by_span(CONV_COLS, 0, n),
+            by_span(2 * DT_PAD, 0, n),
             one((4, CONV_COLS)),
             one((1, CONV_COLS)),
             one((1, DT_PAD)),
@@ -501,16 +567,12 @@
             (one((8, CONV_COLS)), like((8, CONV_COLS))),
             (one((8, DT_PAD)), like((8, DT_PAD))),
         ],
-        [
-            pltpu.VMEM((8, DT_PAD), f32),
-            pltpu.VMEM((8, CONV_COLS), f32),
-            pltpu.VMEM((SPAN, SPAN), f32),
-        ],
-        30 * 10**9,
+        [pltpu.VMEM((8, DT_PAD), f32), pltpu.VMEM((8, CONV_COLS), f32)],
+        15 * 10**9,
         50 * 10**6,
     )(
-        scan_in, before, mixed, steps, starts, prefix, state_in, suffix, state_grad, value_grad,
-        skip, taps, bias, dt_bias, rates, lift,
+        scan_in, before, mixed, steps, starts, prefix, state_in, state_grad, mixed_grad, step_grad,
+        taps, bias, dt_bias, rates, lift,
     )
 
 
@@ -766,25 +828,9 @@
         back_place = [(b, a) for a, b in place]
         sent_out = lax.ppermute(w_out, ("y", "c"), turn)
         sent_o = lax.ppermute(w_o, ("z", "y", "c"), place)
-        sent_rows = jnp.concatenate([sent_out, sent_o], 0).reshape(2 * rows, 2, HALF)
-        second = jnp.concatenate(
-            [rest_mine, jnp.swapaxes(sent_rows, 0, 1).reshape(4 * rows, HALF)], axis=1
-        )
-        whole_second = gathered(after(second, normed_rows, edges16))
-        full_rest = whole_second[:, :REST_COLS]
-        full_rows = jnp.swapaxes(
-            whole_second[:, REST_COLS:].reshape(nz * ny, 2, 2 * rows, HALF), 1, 2
-        ).reshape(nz * ny, 2 * rows, D)
-        full_out = full_rows[:, :out_rows].reshape(PART, D)
-        full_o = full_rows[:, out_rows:].reshape(QP, D)
-    else:
-        full_rest = gathered(after(rest_mine, normed_rows, edges16))
-        every_out = lax.all_gather(w_out, EVERY, axis=0, tiled=True)
-        every_o = lax.all_gather(w_o, EVERY, axis=0, tiled=True)
-        full_out = lax.dynamic_slice_in_dim(every_out, (2 * xi + ci) * PART, PART, 0)
-        every_o = every_o.reshape(2, 2, 2, HEAD_DIM, D)
-        every_o = lax.dynamic_index_in_dim(every_o, xi, 2, keepdims=False)
-        full_o = lax.dynamic_index_in_dim(every_o, ci, 0, keepdims=False).reshape(QP, D)
+        sent_rows = jnp.concatenate([sent_out, sent_o], 0)
+    full_rest = gathered(after(rest_mine, normed_rows, edges16))
+    cotangent16 = jnp.concatenate(gather_tokens(out_grad[0]), 0)
 
     scan_in = low_dot(normed_rows, full_scan).reshape(2, span_all, SCAN_COLS)
     edge_rows = low_dot(edges16, full_scan).reshape(2, 1, 8, SCAN_COLS)
@@ -808,27 +854,40 @@
     lift = (
         jnp.arange(DT_PAD, dtype=jnp.int32)[:, None]
         == jnp.arange(PART, dtype=jnp.int32)[None] // MAMBA_HEAD
-    ).astype(f32)
+    ).astype(bf16)
     mixed, steps, starts, prefix, own_state = scan_states(
         scan_in, before, taps, bias, dt_b, rates, lift
     )
     log_decay = starts[:, n - 1, 0] + steps[:, span_all - 1, DT_PAD:]
     own_decay = jnp.repeat(jnp.exp(log_decay[:, :HEADS]), MAMBA_HEAD, axis=-1)
 
-    def chained(local, step):
+    if aligned:
+        full_rows = gathered(after(sent_rows, mixed, cotangent16)).reshape(nz * ny, 2 * rows, D)
+        full_out = full_rows[:, :out_rows].reshape(PART, D)
+        full_o = full_rows[:, out_rows:].reshape(QP, D)
+    else:
+        every_out = lax.all_gather(w_out, EVERY, axis=0, tiled=True)
+        every_o = lax.all_gather(w_o, EVERY, axis=0, tiled=True)
+        full_out = lax.dynamic_slice_in_dim(every_out, (2 * xi + ci) * PART, PART, 0)
+        every_o = every_o.reshape(2, 2, 2, HEAD_DIM, D)
+        every_o = lax.dynamic_index_in_dim(every_o, xi, 2, keepdims=False)
+        full_o = lax.dynamic_index_in_dim(every_o, ci, 0, keepdims=False).reshape(QP, D)
+
+    def chained(local, step, pin=None):
         entering = []
         for s in range(2):
             held = jnp.zeros(local.shape[1:], f32)
             for hop in range(nz - 1):
                 at = hop if step == 1 else nz - 1 - hop
                 leaving = local[s] + own_decay[s][None] * held if hop else local[s]
+                if pin is not None and hop == nz - 2:
+                    leaving = after(leaving, pin)
                 held = held + lax.ppermute(
                     leaving.astype(bf16), "z", [(at, at + step)]
                 ).astype(f32)
             entering.append(held)
         return jnp.stack(entering)
 
-    state_in = chained(own_state, 1)
     packed_ff = jnp.concatenate([split_ff(w_gate), split_ff(w_up)], axis=2)
     rest = low_dot(normed_rows, full_rest).reshape(2, span_all, REST_COLS)
 
@@ -841,6 +900,7 @@
     )
     key16 = rotate(rest[..., None, AT_K:AT_V], cosine, sine).astype(bf16)[:, :, 0]
     kv16 = jnp.stack([key16, rest[..., AT_V:].astype(bf16)])
+    state_in = chained(own_state, 1, kv16)
     kv_all = jnp.concatenate([shifted(kv16, d) for d in range(nz - 1, 0, -1)] + [kv16], axis=2)
     keys_at = (zi - nz + 1) * span_all + jnp.arange(nz * span_all, dtype=jnp.int32)
     query_place = jnp.broadcast_to(positions[:, None], (span_all, 128))
@@ -853,18 +913,15 @@
     )
     root = lax.rsqrt(group_total(square[..., :1]) / INNER + epsilon)
     gated16 = (flat * root * gain).astype(bf16).reshape(tokens, PART)
-    third = jnp.concatenate(
-        [to_ranks(packed_ff).reshape(4 * rows, 2 * hidden_part), w_down], axis=0
-    )
-    whole_third = gathered(after(third, flat, attended)).reshape(nz * ny, 4 * rows + ff_rows, D)
-    full_ff = whole_third[:, : 4 * rows].reshape(D, 2 * hidden_part)
-    full_down = whole_third[:, 4 * rows :].reshape(hidden_part, D)
+    full_ff = gathered(
+        after(to_ranks(packed_ff).reshape(4 * rows, 2 * hidden_part), flat, attended)
+    )
     mixture = low_dot(gated16, full_out) + low_dot(attended16, full_o)
     hidden_state = resident + scatter_sequences(mixture.reshape(2, span_all, D))
 
     middle, mid_back = jax.vjp(rms_scale, hidden_state, mid_gain)
     middle16 = jnp.concatenate(gather_tokens(permuted(middle.astype(bf16))), 0)
-    cotangent16 = jnp.concatenate(gather_tokens(out_grad[0]), 0)
+    full_down = gathered(after(w_down, middle16))
     both = low_dot(middle16, full_ff)
     activated, swish_back = jax.vjp(
         swish_product, both[:, :hidden_part], both[:, hidden_part:]
@@ -872,23 +929,25 @@
     activated16 = activated.astype(bf16)
     down = low_dot(activated16, full_down).reshape(4, length, D)
     output = (hidden_state + scatter_tokens(down)).astype(bf16)
-    gate_grad, up_grad = swish_back(back_dot(cotangent16, full_down))
+
+    def to_owners(array):
+        return lax.psum_scatter(array, SHARDS, scatter_dimension=0, tiled=True)
+
+    down_grad = weight_grad(activated16, cotangent16).astype(bf16)
+    down_owned = to_owners(down_grad)
+    result_down = down_owned.astype(f32)
+    gate_grad, up_grad = swish_back(back_dot(after(cotangent16, down_grad), full_down))
     both16 = jnp.concatenate([gate_grad, up_grad], axis=1).astype(bf16)
     mid_grad = restored(scatter_tokens(back_dot(both16, full_ff).reshape(4, length, D)))
     hidden_piece, mid_gain_grad = mid_back(mid_grad)
     hidden_grad = out_grad[0].astype(f32) + hidden_piece
-
-    def to_owners(array):
-        return lax.psum_scatter(array.astype(bf16), SHARDS, scatter_dimension=0, tiled=True)
-
-    down_owned = to_owners(weight_grad(activated16, cotangent16))
-    result_down = down_owned.astype(f32)
-    ff_owned = to_owners(after(weight_grad(middle16, both16).astype(bf16), down_owned))
+    ff_grad = weight_grad(middle16, both16).astype(bf16)
+    ff_owned = to_owners(after(ff_grad, down_owned))
     ff_parts = to_ranks(ff_owned.reshape(4, rows, 2 * hidden_part))
     result_gate = join_ff(ff_parts[..., :hidden_part]).astype(f32)
     result_up = join_ff(ff_parts[..., hidden_part:]).astype(f32)
 
-    mix16 = gather_sequences(hidden_grad.astype(bf16)).reshape(tokens, D)
+    mix16 = gather_sequences(after(hidden_grad.astype(bf16), ff_grad)).reshape(tokens, D)
     attended_grad16 = back_dot(mix16, full_o).astype(bf16).reshape(2, span_all, QP)
     gated_grad = back_dot(mix16, full_out).reshape(2, span_all, PART)
     grad_out_w = weight_grad(gated16, mix16).astype(bf16)
@@ -898,7 +957,7 @@
     inner_mean = group_total(inner) / INNER
     wide = (2, span_all, 128)
     value_grad, gate_z_grad, gain_grad, suffix, first_grad = gate_backward(
-        gated_grad,
+        after(gated_grad, down_owned),
         values,
         rest,
         0,
@@ -939,7 +998,10 @@
         axis=-1,
     ).reshape(tokens, REST_COLS)
 
-    scan_grad16, edge_grad, conv_grad, small_grad = scan_backward(
+    mixed_grad, step_grad, skip_grad = scan_backward(
+        mixed, steps, starts, prefix, state_in, suffix, value_grad, skip, lift
+    )
+    scan_grad16, edge_grad, conv_grad, small_grad = finish_backward(
         scan_in,
         before,
         mixed,
@@ -947,10 +1009,9 @@
         starts,
         prefix,
         state_in,
-        suffix,
-        state_grad,
-        after(value_grad, down_owned),
-        skip,
+        after(state_grad, ff_owned),
+        mixed_grad,
+        step_grad,
         taps,
         bias,
         dt_b,
@@ -962,26 +1023,13 @@
     scan_grad16 = lax.dynamic_update_slice(
         scan_grad16, last_rows.astype(bf16), (0, span_all - edge_count, 0)
     ).reshape(tokens, SCAN_COLS)
-    grads = [
-        weight_grad(normed_rows, scan_grad16).astype(bf16),
-        weight_grad(normed_rows, rest_grad16).astype(bf16),
-    ]
     if aligned:
         rows_grad = jnp.concatenate(
             [grad_out_w.reshape(nz * ny, out_rows, D), grad_o.reshape(nz * ny, o_rows, D)], axis=1
-        ).reshape(nz * ny, 2 * rows, 2, HALF)
-        grads.append(jnp.swapaxes(rows_grad, 1, 2).reshape(D, HALF))
-    mix_owned = to_owners(after(jnp.concatenate(grads, axis=1), ff_owned))
-    scan_parts = to_ranks(mix_owned[:, :SCAN_COLS].reshape(4, rows, SCAN_COLS)).astype(f32)
-    rest_parts = to_ranks(
-        mix_owned[:, SCAN_COLS : SCAN_COLS + REST_COLS].reshape(4, rows, REST_COLS)
-    ).astype(f32)
-    if aligned:
-        rows_parts = jnp.swapaxes(
-            mix_owned[:, SCAN_COLS + REST_COLS :].reshape(2, 2 * rows, HALF), 0, 1
-        ).reshape(2 * rows, D)
-        result_out = lax.ppermute(rows_parts[:out_rows], ("y", "c"), turn).astype(f32)
-        result_o = lax.ppermute(rows_parts[out_rows:], ("z", "y", "c"), back_place).astype(f32)
+        ).reshape(nz * ny * 2 * rows, D)
+        rows_owned = to_owners(after(rows_grad, ff_owned))
+        result_out = lax.ppermute(rows_owned[:out_rows], ("y", "c"), turn).astype(f32)
+        result_o = lax.ppermute(rows_owned[out_rows:], ("z", "y", "c"), back_place).astype(f32)
     else:
         every_out = lax.dynamic_update_slice_in_dim(
             jnp.zeros((INNER, D), bf16), grad_out_w, (2 * xi + ci) * PART, 0
@@ -994,6 +1042,15 @@
         result_out = lax.psum_scatter(every_out, EVERY, scatter_dimension=0, tiled=True)
         result_o = lax.psum_scatter(every_o, EVERY, scatter_dimension=0, tiled=True)
         result_out, result_o = result_out.astype(f32), result_o.astype(f32)
+        rows_owned = result_out
+    rest_owned = to_owners(
+        after(weight_grad(normed_rows, rest_grad16).astype(bf16), rows_owned)
+    )
+    rest_parts = to_ranks(rest_owned.reshape(4, rows, REST_COLS)).astype(f32)
+    scan_owned = to_owners(
+        after(weight_grad(normed_rows, scan_grad16).astype(bf16), rest_owned)
+    )
+    scan_parts = to_ranks(scan_owned.reshape(4, rows, SCAN_COLS)).astype(f32)
 
     normed_grad = back_dot(scan_grad16, full_scan) + back_dot(rest_grad16, full_rest)
     normed_grad = restored(scatter_sequences(normed_grad.reshape(2, span_all, D)))
@@ -1027,7 +1084,7 @@
         all_channels(conv_grad[4]),
         heads_spread(small_grad[0, :HEADS], 1),
         heads_spread(small_grad[1, :HEADS], 1),
-        heads_spread(small_grad[2, :HEADS], 1),
+        heads_spread(skip_grad[0, :HEADS], 1),
         heads_spread(gain_grad[0], MAMBA_HEAD),
         mid_gain_grad,
     ]

time: 1330 us -> 1250 us (0.940)
  local copies, waits for them, and re-layouts: 179 us -> 97.6 us
  waiting for transfers between devices: 599 us -> 647 us
  other arithmetic: 121 us -> 98.1 us
  starting transfers between devices: 116 us -> 102 us
    ppermute x8, waiting for transfers between devices: 3.64 us -> 74.2 us  [shifted(): lax.ppermute(array, 'z', [(i - distance, i) for i in devices if i - dista...]
    concatenate x4 -> x0, local copies, waits for them, and re-layouts: 31.6 us -> none  [body(): jnp.concatenate([grad_out_w.reshape(nz * ny, out_rows, D), grad_o.reshape...]
    ppermute x8, starting transfers between devices: 49.6 us -> 26.3 us  [shifted(): lax.ppermute(array, 'z', [(i - distance, i) for i in devices if i - dista...]
    reduce_scatter x3 -> x5, waiting for transfers between devices: 150 us -> 129 us  [to_owners(): return lax.psum_scatter(array, SHARDS, scatter_dimension=0, tiled=True)]
    slice x14 -> x4, local copies, waits for them, and re-layouts: 21.7 us -> 1.98 us  [the longest x1 1.03 us: body(): rows_owned[:out_rows]]
    ppermute x24, waiting for transfers between devices: 156 us -> 176 us  [swap(): return lax.ppermute(array, axis, [(0, 1), (1, 0)])]
    ppermute x5, waiting for transfers between devices: 30 us -> 13.2 us  [total(): lax.ppermute(array, axis, [(i, i ^ bit) for i in range(size)])]
    reshape x4 -> x0, local copies, waits for them, and re-layouts: 14.5 us -> none  [the longest x1 7.87 us: body(): grads.append(jnp.swapaxes(rows_grad, 1, 2).reshape(D, HALF))]
  transfers between devices with their start and end apart: 64 -> 68, of which waited for: 27 -> 34; matrix products, arithmetic and copies ran while one was open for 28% -> 25% of each run, Pallas kernels for 8% -> 9%
where the time goes in v4:
time: 1250 us; the launch traced here: 1240 us
  waiting for transfers between devices  647 us (52%)
  matrix products  147 us (12%)
  Pallas kernels  112 us (9%)
  starting transfers between devices  102 us (8%)
  other arithmetic  98.1 us (8%)
  local copies, waits for them, and re-layouts  97.6 us (8%)
  between operations  17.2 us (1%)
  blocking collectives  15.2 us (1%)
    ppermute x24, waiting for transfers between devices, swap(): return lax.ppermute(array, axis, [(0, 1), (1, 0)])  176 us
    all_gather x5, waiting for transfers between devices, gathered(): return lax.all_gather(array, SHARDS, axis=0, tiled=True)  138 us
    reduce_scatter x5, waiting for transfers between devices, to_owners(): return lax.psum_scatter(array, SHARDS, scatter_dimension=0, tiled=True)  129 us
    ppermute x12, waiting for transfers between devices, chained(): lax.ppermute(leaving.astype(bf16), 'z', [(at, at + step)]).astype(f32)  100 us
    ppermute x8, waiting for transfers between devices, shifted(): lax.ppermute(array, 'z', [(i - distance, i) for i in devices if i - dista...  74.2 us
    dot_general x6, matrix products, back_dot(): lax.dot_general(grad_rows, weight, (((1,), (1,)), ((), ())), preferred_el...  59 us
    dot_general x6, matrix products, weight_grad(): lax.dot_general(left, right, (((0,), (0,)), ((), ())), preferred_element_...  44.4 us
    dot_general x7, matrix products, low_dot(): return jnp.dot(left, right, preferred_element_type=f32)  43.5 us
  transfers between devices with their start and end apart: 68, of which 34 were waited for; matrix products, arithmetic and copies ran while one was open for 25% of the time, Pallas kernels for 9%

profile of v4, /device:TPU:0, one launch (start us, length us, event | category | flops | bytes accessed | tf_op | source)
XLA Modules:
  0.0 1236.2 jit_solution(1817737940146216422)
XLA Ops:
  10.9 15.2 %all_to_all.30 = bf16[4,64,1408]{2,1,0:T(8,128)(2,1)} all-to-all(bf16[4,64,1408]{2,1,0:T(8,128)(2,1)S(1)} %fusion.57), channel_id=1, replica_groups=mesh['z'=4,'x'=2,'y'=2,'c'=2] {'x','c'}, dimensions={0} | all-to-all | bytes 1441792 | tf_op jit(solution)/shard_map/all_to_all | solution.py:755
  28.2 24.6 %collective-permute-done = bf16[256,2048]{1,0:T(8,128)(2,1)} collective-permute-done((bf16[256,2048]{1,0:T(8,128)(2,1)S(1)}, bf16[256,2048]{1,0:T(8,128)(2,1)}, u32[]{:S(2)}, u32[]{:S(2)}) %collective-permute-start) | collective-permute-done | bytes 1048608 | tf_op jit(solution)/shard_map/ppermute | solution.py:41
  109.1 14.8 %all-gather.6.cloned.1.call-done = bf16[2048,1408]{1,0:T(8,128)(2,1)} async-done(((bf16[256,1408]{1,0:T(8,128)(2,1)}), bf16[2048,1408]{1,0:T(8,128)(2,1)}) %all-gather.6.cloned.1.call-update) | async-done | bytes 5767184 | tf_op jit(solution)/shard_map/all_gather | solution.py:798
  137.0 13.8 %shard_map.330 = (f32[2,512,1280]{2,1,0:T(8,128)}, f32[2,512,256]{2,1,0:T(8,128)S(1)}, f32[2,4,8,128]{3,2,1,0:T(8,128)S(1)}, f32[2,4,256,768]{3,2,1,0:T(8,128)}, f32[2,256,768]{2,1,0:T(8,128)S(1)}) custom-call(f32[2,512,1408]{2,1,0:T(8,128)} %bitcast.320, f32[2,4,8,1280]{3,2,1,0:T(8,128)S(1)} %pad_maximum_fusion.20.before, ...), custom_call_target="tpu_custom_call" | custom-call | flops 8000000000 | bytes 30000000 | tf_op jit(solution)/shard_map/pallas_call | solution.py:428
  168.2 16.1 %collective-permute-done.7 = bf16[256,768]{1,0:T(8,128)(2,1)} collective-permute-done((bf16[256,768]{1,0:T(8,128)(2,1)}, bf16[256,768]{1,0:T(8,128)(2,1)}, u32[]{:S(2)}, u32[]{:S(2)}) %collective-permute-start.7) | collective-permute-done | bytes 393248 | tf_op jit(solution)/shard_map/ppermute | solution.py:885
  189.7 27.5 %all-gather.8.cloned.1.call-done = bf16[2048,1280]{1,0:T(8,128)(2,1)} async-done(((bf16[256,1280]{1,0:T(8,128)(2,1)}), bf16[2048,1280]{1,0:T(8,128)(2,1)}) %all-gather.8.cloned.1.call-update) | async-done | bytes 5242896 | tf_op jit(solution)/shard_map/all_gather | solution.py:798
  261.6 15.5 %collective-permute-done.18 = bf16[2,2,512,128]{3,2,1,0:T(8,128)(2,1)} collective-permute-done((bf16[2,2,512,128]{3,2,1,0:T(8,128)(2,1)}, bf16[2,2,512,128]{3,2,1,0:T(8,128)(2,1)}, u32[]{:S(2)}, u32[]{:S(2)}) %collective-permute-start.18) | collective-permute-done | bytes 524320 | tf_op jit(solution)/shard_map/ppermute | solution.py:46
  277.1 22.0 %collective-permute-done.17 = bf16[2,2,512,128]{3,2,1,0:T(8,128)(2,1)} collective-permute-done((bf16[2,2,512,128]{3,2,1,0:T(8,128)(2,1)}, bf16[2,2,512,128]{3,2,1,0:T(8,128)(2,1)}, u32[]{:S(2)}, u32[]{:S(2)}) %collective-permute-start.17) | collective-permute-done | bytes 524320 | tf_op jit(solution)/shard_map/ppermute | solution.py:46
  302.1 12.9 %shard_map.332 = (f32[2,512,256]{2,1,0:T(8,128)S(1)}, f32[2,512,256]{2,1,0:T(8,128)S(1)}) custom-call(bf16[2,512,256]{2,1,0:T(8,128)(2,1)S(1)} %convert_element_type.349.query, bf16[2,2048,128]{2,1,0:T(8,128)(2,1)S(1)} %get-tuple-element.115.key, bf16[2,2048,128]{2,1,0:T(8,128)(2,1)} %get-tuple-element.114.value, ...), custom_call_target="tpu_custom_call" | custom-call | flops 12000000000 | bytes 20000000 | tf_op jit(solution)/shard_map/pallas_call | solution.py:621
  382.6 23.5 %collective-permute-done.21 = bf16[256,2048]{1,0:T(8,128)(2,1)} collective-permute-done((bf16[256,2048]{1,0:T(8,128)(2,1)}, bf16[256,2048]{1,0:T(8,128)(2,1)}, u32[]{:S(2)}, u32[]{:S(2)}) %collective-permute-start.21) | collective-permute-done | bytes 1048608 | tf_op jit(solution)/shard_map/ppermute | solution.py:41
  411.9 22.7 %collective-permute-done.23 = bf16[256,2048]{1,0:T(8,128)(2,1)S(1)} collective-permute-done((bf16[256,2048]{1,0:T(8,128)(2,1)S(1)}, bf16[256,2048]{1,0:T(8,128)(2,1)S(1)}, u32[]{:S(2)}, u32[]{:S(2)}) %collective-permute-start.23) | collective-permute-done | bytes 1048608 | tf_op jit(solution)/shard_map/ppermute | solution.py:41
  437.4 48.1 %all-gather.12.cloned.1.call-done = bf16[2048,2048]{1,0:T(8,128)(2,1)} async-done(((bf16[256,2048]{1,0:T(8,128)(2,1)}), bf16[2048,2048]{1,0:T(8,128)(2,1)}) %all-gather.12.cloned.1.call-update) | async-done | bytes 8388624 | tf_op jit(solution)/shard_map/all_gather | solution.py:798
  511.1 48.0 %all-gather.14.cloned.1.call-done = bf16[1024,2048]{1,0:T(8,128)(2,1)} async-done(((bf16[128,2048]{1,0:T(8,128)(2,1)}), bf16[1024,2048]{1,0:T(8,128)(2,1)}) %all-gather.14.cloned.1.call-update) | async-done | bytes 4194320 | tf_op jit(solution)/shard_map/all_gather | solution.py:798
  585.5 63.2 %reduce-scatter.6.cloned.1.call-done = bf16[128,2048]{1,0:T(8,128)(2,1)} async-done(((bf16[1024,2048]{1,0:T(8,128)(2,1)}), bf16[128,2048]{1,0:T(8,128)(2,1)}) %reduce-scatter.6.cloned.1.call-update) | async-done | bytes 524304 | tf_op jit(solution)/shard_map/reduce_scatter | solution.py:934
  648.8 15.0 %fusion.89 = (bf16[1024,2048]{1,0:T(8,128)(2,1)S(1)}, f32[1024,2048]{1,0:T(8,128)}) fusion(bf16[2048,2048]{1,0:T(8,128)(2,1)} %all-gather.12.cloned.1.call-done, bf16[1024,1024]{1,0:T(8,128)(2,1)} %copy-done.116, bf16[1024,1024]{1,0:T(8,128)(2,1)} %copy-done.115), kind=kOutput, calls=%fused_computation.311 | convolution fusion | flops 8600420352 | bytes 25165824 | tf_op jit(solution)/shard_map/dot_general | solution.py:69
  670.2 23.7 %collective-permute-done.28 = bf16[256,2048]{1,0:T(8,128)(2,1)S(1)} collective-permute-done((bf16[256,2048]{1,0:T(8,128)(2,1)S(1)}, bf16[256,2048]{1,0:T(8,128)(2,1)S(1)}, u32[]{:S(2)}, u32[]{:S(2)}) %collective-permute-start.28) | collective-permute-done | bytes 1048608 | tf_op jit(solution)/shard_map/ppermute | solution.py:41
  699.7 22.9 %collective-permute-done.29 = bf16[256,2048]{1,0:T(8,128)(2,1)S(1)} collective-permute-done((bf16[256,2048]{1,0:T(8,128)(2,1)S(1)}, bf16[256,2048]{1,0:T(8,128)(2,1)S(1)}, u32[]{:S(2)}, u32[]{:S(2)}) %collective-permute-start.29) | collective-permute-done | bytes 1048608 | tf_op jit(solution)/shard_map/ppermute | solution.py:41
  736.2 65.4 %reduce-scatter.8.cloned.1.call-done = bf16[256,2048]{1,0:T(8,128)(2,1)} async-done(((bf16[2048,2048]{1,0:T(8,128)(2,1)}), bf16[256,2048]{1,0:T(8,128)(2,1)}) %reduce-scatter.8.cloned.1.call-update) | async-done | bytes 1048592 | tf_op jit(solution)/shard_map/reduce_scatter | solution.py:934
  817.6 18.9 %shard_map.336 = (f32[2,512,256]{2,1,0:T(8,128)S(1)}, f32[2,2,2048,128]{3,2,1,0:T(8,128)}) custom-call(bf16[2,512,256]{2,1,0:T(8,128)(2,1)S(1)} %convert_element_type.349.query, bf16[2,2048,128]{2,1,0:T(8,128)(2,1)S(1)} %copy-done.4, bf16[2,2048,128]{2,1,0:T(8,128)(2,1)} %get-tuple-element.114.value, bf16[2,512,256]{2,1,0:T(8,128)(2,1)S(1)} %bitcast.271, ...), custom_call_target="tpu_custom_call" | custom-call | flops 20000000000 | bytes 30000000 | tf_op jit(solution)/shard_map/pallas_call | solution.py:640
  865.9 26.2 %collective-permute-done.42 = bf16[2,2,512,128]{3,2,1,0:T(8,128)(2,1)} collective-permute-done((bf16[2,2,512,128]{3,2,1,0:T(8,128)(2,1)}, bf16[2,2,512,128]{3,2,1,0:T(8,128)(2,1)}, u32[]{:S(2)}, u32[]{:S(2)}) %collective-permute-start.42) | collective-permute-done | bytes 524320 | tf_op jit(solution)/shard_map/ppermute | solution.py:46
  926.9 21.8 %shard_map.334 = (f32[2,512,1280]{2,1,0:T(8,128)}, f32[2,512,256]{2,1,0:T(8,128)S(1)}, f32[8,128]{1,0:T(8,128)S(1)}) custom-call(f32[2,512,1280]{2,1,0:T(8,128)} %get-tuple-element.57.mixed.c_part, f32[2,512,256]{2,1,0:T(8,128)S(1)} %get-tuple-element.58.steps, f32[2,4,8,128]{3,2,1,0:T(8,128)S(1)} %get-tuple-element.59.starts, ...), custom_call_target="tpu_custom_call" | custom-call | flops 30000001024 | bytes 40000000 | tf_op jit(solution)/shard_map/pallas_call | solution.py:513
  948.7 69.4 %collective-permute-done.39 = bf16[256,768]{1,0:T(8,128)(2,1)S(1)} collective-permute-done((bf16[256,768]{1,0:T(8,128)(2,1)S(1)}, bf16[256,768]{1,0:T(8,128)(2,1)S(1)}, u32[]{:S(2)}, u32[]{:S(2)}) %collective-permute-start.39) | collective-permute-done | bytes 393248 | tf_op jit(solution)/shard_map/ppermute | solution.py:885
  1027.0 21.8 %shard_map.335 = (bf16[2,512,1408]{2,1,0:T(8,128)(2,1)}, f32[2,8,1280]{2,1,0:T(8,128)S(1)}, f32[8,1280]{1,0:T(8,128)S(1)}, f32[8,128]{1,0:T(8,128)S(1)}) custom-call(f32[2,512,1408]{2,1,0:T(8,128)} %bitcast.321, f32[2,4,8,1280]{3,2,1,0:T(8,128)S(1)} %copy-done.6, f32[2,512,1280]{2,1,0:T(8,128)} %get-tuple-element.57.mixed.c_part, ...), custom_call_target="tpu_custom_call" | custom-call | flops 15000000512 | bytes 50000000 | tf_op jit(solution)/shard_map/pallas_call | solution.py:544
  1115.9 14.2 %collective-permute-done.45 = bf16[256,2048]{1,0:T(8,128)(2,1)S(1)} collective-permute-done((bf16[256,2048]{1,0:T(8,128)(2,1)S(1)}, bf16[256,2048]{1,0:T(8,128)(2,1)S(1)}, u32[]{:S(2)}, u32[]{:S(2)}) %collective-permute-start.45) | collective-permute-done | bytes 1048608 | tf_op jit(solution)/shard_map/ppermute | solution.py:41
  (692 shorter events, 551.6 us)
Async XLA Ops:
  7.2 116.7 %all-gather.6.cloned.1.call-start = ((), (), s32[]{:S(2)}) async-start(), calls=%async_computation.11 | async-start | bytes 6488064 | tf_op jit(solution)/shard_map/all_gather | solution.py:798
  58.9 158.3 %all-gather.8.cloned.1.call-start = ((), (), s32[]{:S(2)}) async-start(), calls=%async_computation.12 | async-start | bytes 5898240 | tf_op jit(solution)/shard_map/all_gather | solution.py:798
  82.7 248.8 %all-to-all-start.2 = ((bf16[4,64,2048]{2,1,0:T(8,128)(2,1)}), bf16[4,64,2048]{2,1,0:T(8,128)(2,1)}, u32[]{:S(2)}, u32[]{:S(2)}) async-start(bf16[4,64,2048]{2,1,0:T(8,128)(2,1)} %pad_maximum_fusion.14), calls=%async_computation.2 | async-start | bytes 2097152 | tf_op jit(solution)/shard_map/all_to_all | solution.py:755
  87.1 267.4 %all-gather.10.cloned.1.call-start = ((), (), s32[]{:S(2)}) async-start(), calls=%async_computation.13 | async-start | bytes 4718592 | tf_op jit(solution)/shard_map/all_gather | solution.py:798
  159.7 325.8 %all-gather.12.cloned.1.call-start = ((), (), s32[]{:S(2)}) async-start(), calls=%async_computation.14 | async-start | bytes 9437184 | tf_op jit(solution)/shard_map/all_gather | solution.py:798
  186.5 69.1 %collective-permute-start.5 = (bf16[256,768]{1,0:T(8,128)(2,1)}, bf16[256,768]{1,0:T(8,128)(2,1)}, u32[]{:S(2)}, u32[]{:S(2)}) collective-permute-start(bf16[256,768]{1,0:T(8,128)(2,1)} %get-tuple-element.128), channel_id=1, source_target_pairs={{8,16},{9,17},{10,18},{11,19},{12,20},{13,21},{14,22},{15,23}} | collective-permute-start | bytes 1179656 | tf_op jit(solution)/shard_map/ppermute | solution.py:885
  187.9 67.6 %collective-permute-start.8 = (bf16[256,768]{1,0:T(8,128)(2,1)}, bf16[256,768]{1,0:T(8,128)(2,1)}, u32[]{:S(2)}, u32[]{:S(2)}) collective-permute-start(bf16[256,768]{1,0:T(8,128)(2,1)} %get-tuple-element.129), channel_id=1, source_target_pairs={{8,16},{9,17},{10,18},{11,19},{12,20},{13,21},{14,22},{15,23}} | collective-permute-start | bytes 1179656 | tf_op jit(solution)/shard_map/ppermute | solution.py:885
  238.6 38.5 %collective-permute-start.18 = (bf16[2,2,512,128]{3,2,1,0:T(8,128)(2,1)}, bf16[2,2,512,128]{3,2,1,0:T(8,128)(2,1)}, u32[]{:S(2)}, u32[]{:S(2)}) collective-permute-start(bf16[2,2,512,128]{3,2,1,0:T(8,128)(2,1)} %pad_maximum_fusion.16), channel_id=1, source_target_pairs={{0,16},{8,24},{1,17},{9,25},{2,18},{10,26},{3,19},{11,27},{4,20},{... | collective-permute-start | bytes 1572872 | tf_op jit(solution)/shard_map/ppermute | solution.py:46
  244.2 54.9 %collective-permute-start.17 = (bf16[2,2,512,128]{3,2,1,0:T(8,128)(2,1)}, bf16[2,2,512,128]{3,2,1,0:T(8,128)(2,1)}, u32[]{:S(2)}, u32[]{:S(2)}) collective-permute-start(bf16[2,2,512,128]{3,2,1,0:T(8,128)(2,1)} %pad_maximum_fusion.16), channel_id=1, source_target_pairs={{0,24},{1,25},{2,26},{3,27},{4,28},{5,29},{6,30},{7,31}} | collective-permute-start | bytes 1572872 | tf_op jit(solution)/shard_map/ppermute | solution.py:46
  257.3 58.8 %collective-permute-start.9 = (bf16[256,768]{1,0:T(8,128)(2,1)S(1)}, bf16[256,768]{1,0:T(8,128)(2,1)S(1)}, u32[]{:S(2)}, u32[]{:S(2)}) collective-permute-start(bf16[256,768]{1,0:T(8,128)(2,1)S(1)} %get-tuple-element.64), channel_id=1, source_target_pairs={{16,24},{17,25},{18,26},{19,27},{20,28},{21,29},{22,30},{23,31}} | collective-permute-start | bytes 1179656 | tf_op jit(solution)/shard_map/ppermute | solution.py:885
  258.0 59.7 %collective-permute-start.6 = (bf16[256,768]{1,0:T(8,128)(2,1)S(1)}, bf16[256,768]{1,0:T(8,128)(2,1)S(1)}, u32[]{:S(2)}, u32[]{:S(2)}) collective-permute-start(bf16[256,768]{1,0:T(8,128)(2,1)S(1)} %get-tuple-element.63), channel_id=1, source_target_pairs={{16,24},{17,25},{18,26},{19,27},{20,28},{21,29},{22,30},{23,31}} | collective-permute-start | bytes 1179656 | tf_op jit(solution)/shard_map/ppermute | solution.py:885
  331.6 227.4 %all-gather.14.cloned.1.call-start = ((), (), s32[]{:S(2)}) async-start(), calls=%async_computation.15 | async-start | bytes 4718592 | tf_op jit(solution)/shard_map/all_gather | solution.py:798
  382.4 266.3 %reduce-scatter.6.cloned.1.call-start = ((), (), s32[]{:S(2)}) async-start(), calls=%async_computation.16 | async-start | bytes 4718592 | tf_op jit(solution)/shard_map/reduce_scatter | solution.py:934
  510.8 290.8 %reduce-scatter.8.cloned.1.call-start = ((), (), s32[]{:S(2)}) async-start(), calls=%async_computation.17 | async-start | bytes 9437184 | tf_op jit(solution)/shard_map/reduce_scatter | solution.py:934
  648.7 270.3 %reduce-scatter.10.cloned.1.call-start = ((), (), s32[]{:S(2)}) async-start(), calls=%async_computation.18 | async-start | bytes 4718592 | tf_op jit(solution)/shard_map/reduce_scatter | solution.py:934
  801.6 283.2 %reduce-scatter.12.cloned.1.call-start = ((), (), s32[]{:S(2)}) async-start(), calls=%async_computation.19 | async-start | bytes 5898240 | tf_op jit(solution)/shard_map/reduce_scatter | solution.py:934
  813.6 34.4 %collective-permute-start.32 = (f32[2,512,1]{2,1,0:T(8,128)}, f32[2,512,1]{2,1,0:T(8,128)}, u32[]{:S(2)}, u32[]{:S(2)}) collective-permute-start(f32[2,512,1]{2,1,0:T(8,128)} %rev.7), channel_id=1, source_target_pairs={{0,1},{1,0},{2,3},{3,2},{4,5},{5,4},{6,7},{7,6},{8,9},{9,8},{10,11... | collective-permute-start | bytes 12296 | tf_op jit(solution)/shard_map/ppermute | solution.py:41
  840.9 51.2 %collective-permute-start.42 = (bf16[2,2,512,128]{3,2,1,0:T(8,128)(2,1)}, bf16[2,2,512,128]{3,2,1,0:T(8,128)(2,1)}, u32[]{:S(2)}, u32[]{:S(2)}) collective-permute-start(bf16[2,2,512,128]{3,2,1,0:T(8,128)(2,1)} %get-tuple-element.113), channel_id=1, source_target_pairs={{16,0},{24,8},{17,1},{25,9},{18,2},{26,10},{19,3},{27,11},{20,4},{... | collective-permute-start | bytes 1572872 | tf_op jit(solution)/shard_map/ppermute | solution.py:46
  842.2 49.9 %collective-permute-start.41 = (bf16[2,2,512,128]{3,2,1,0:T(8,128)(2,1)}, bf16[2,2,512,128]{3,2,1,0:T(8,128)(2,1)}, u32[]{:S(2)}, u32[]{:S(2)}) collective-permute-start(bf16[2,2,512,128]{3,2,1,0:T(8,128)(2,1)} %get-tuple-element.111), channel_id=1, source_target_pairs={{8,0},{16,8},{24,16},{9,1},{17,9},{25,17},{10,2},{18,10},{26,18},{... | collective-permute-start | bytes 1572872 | tf_op jit(solution)/shard_map/ppermute | solution.py:46
  919.0 283.4 %reduce-scatter.14.cloned.1.call-start = ((), (), s32[]{:S(2)}) async-start(), calls=%async_computation.20 | async-start | bytes 6488064 | tf_op jit(solution)/shard_map/reduce_scatter | solution.py:934
  924.2 93.9 %collective-permute-start.39 = (bf16[256,768]{1,0:T(8,128)(2,1)S(1)}, bf16[256,768]{1,0:T(8,128)(2,1)S(1)}, u32[]{:S(2)}, u32[]{:S(2)}) collective-permute-start(bf16[256,768]{1,0:T(8,128)(2,1)S(1)} %get-tuple-element.119), channel_id=1, source_target_pairs={{8,0},{9,1},{10,2},{11,3},{12,4},{13,5},{14,6},{15,7}} | collective-permute-start | bytes 1179656 | tf_op jit(solution)/shard_map/ppermute | solution.py:885
  925.5 100.0 %collective-permute-start.36 = (bf16[256,768]{1,0:T(8,128)(2,1)S(1)}, bf16[256,768]{1,0:T(8,128)(2,1)S(1)}, u32[]{:S(2)}, u32[]{:S(2)}) collective-permute-start(bf16[256,768]{1,0:T(8,128)(2,1)S(1)} %get-tuple-element.118), channel_id=1, source_target_pairs={{8,0},{9,1},{10,2},{11,3},{12,4},{13,5},{14,6},{15,7}} | collective-permute-start | bytes 1179656 | tf_op jit(solution)/shard_map/ppermute | solution.py:885
  1109.2 78.0 %collective-permute-start.26 = (bf16[256,2048]{1,0:T(8,128)(2,1)}, bf16[256,2048]{1,0:T(8,128)(2,1)}, u32[]{:S(2)}, u32[]{:S(2)}) collective-permute-start(bf16[256,2048]{1,0:T(8,128)(2,1)} %fusion.36), channel_id=1, source_target_pairs={{0,4},{4,0},{1,5},{5,1},{2,6},{6,2},{3,7},{7,3},{8,12},{12,8},{9,1... | collective-permute-start | bytes 3145736 | tf_op jit(solution)/shard_map/ppermute | solution.py:41
  1112.2 51.6 %all-to-all-start.5 = ((bf16[4,64,2048]{2,1,0:T(8,128)(2,1)}), bf16[4,64,2048]{2,1,0:T(8,128)(2,1)S(1)}, u32[]{:S(2)}, u32[]{:S(2)}) async-start(bf16[4,64,2048]{2,1,0:T(8,128)(2,1)} %bitcast.104), calls=%async_computation.10 | async-start | bytes 2097152 | tf_op jit(solution)/shard_map/all_to_all | solution.py:755
  (166 other events, 2749.0 us)
Sparse Core Ops, SparseCore 0:
  26.2 97.6 all-gather.5
  126.7 90.5 all-gather.7
  219.4 101.5 all-gather.9
  331.7 153.6 all-gather.11
  487.4 71.5 all-gather.13
  562.5 86.1 reduce-scatter.5
  652.8 148.7 reduce-scatter.7
  805.2 97.6 reduce-scatter.9
  919.1 137.9 reduce-scatter.11
  1084.9 111.0 reduce-scatter.13

commit v5 on v4

--- a/solution.py
+++ b/solution.py
@@ -694,7 +694,7 @@
     w_down,
 ):
     nz, ny = lax.axis_size("z"), lax.axis_size("y")
-    zi, xi, ci = (lax.axis_index(name) for name in ("z", "x", "c"))
+    zi, xi, yi, ci = (lax.axis_index(name) for name in ("z", "x", "y", "c"))
     length = inputs.shape[1]
     span_all = 2 * length
     rows = w_in.shape[0]
@@ -861,10 +861,21 @@
     log_decay = starts[:, n - 1, 0] + steps[:, span_all - 1, DT_PAD:]
     own_decay = jnp.repeat(jnp.exp(log_decay[:, :HEADS]), MAMBA_HEAD, axis=-1)
 
+    def turned(array, distance):
+        return lax.ppermute(array, "z", [(i, (i + distance) % nz) for i in range(nz)])
+
     if aligned:
-        full_rows = gathered(after(sent_rows, mixed, cotangent16)).reshape(nz * ny, 2 * rows, D)
-        full_out = full_rows[:, :out_rows].reshape(PART, D)
-        full_o = full_rows[:, out_rows:].reshape(QP, D)
+        first_rows = after(sent_rows, full_scan)
+        along_z = jnp.stack([turned(first_rows, d) for d in range(nz - 1, 0, -1)] + [first_rows])
+        along_z = lax.dynamic_slice_in_dim(
+            jnp.concatenate([along_z, along_z], 0), nz - 1 - zi, nz, 0
+        )
+        other_y = swap(along_z, "y")
+        full_rows = jnp.where(
+            yi == 0, jnp.stack([along_z, other_y], 1), jnp.stack([other_y, along_z], 1)
+        )
+        full_out = full_rows[:, :, :out_rows].reshape(PART, D)
+        full_o = full_rows[:, :, out_rows:].reshape(QP, D)
     else:
         every_out = lax.all_gather(w_out, EVERY, axis=0, tiled=True)
         every_o = lax.all_gather(w_o, EVERY, axis=0, tiled=True)
@@ -905,23 +916,23 @@
     keys_at = (zi - nz + 1) * span_all + jnp.arange(nz * span_all, dtype=jnp.int32)
     query_place = jnp.broadcast_to(positions[:, None], (span_all, 128))
     key_place = jnp.broadcast_to(keys_at[None], (8, nz * span_all))
-    attended, log_sum = attend(query16, kv_all[0], kv_all[1], query_place, key_place)
-    attended16 = attended.reshape(tokens, QP).astype(bf16)
-
     values, flat, square = scan_values(
         mixed, steps, starts, prefix, state_in, rest, 0, skip, lift
     )
+    attended, log_sum = attend(after(query16, flat), kv_all[0], kv_all[1], query_place, key_place)
+    attended16 = attended.reshape(tokens, QP).astype(bf16)
+
     root = lax.rsqrt(group_total(square[..., :1]) / INNER + epsilon)
     gated16 = (flat * root * gain).astype(bf16).reshape(tokens, PART)
     full_ff = gathered(
-        after(to_ranks(packed_ff).reshape(4 * rows, 2 * hidden_part), flat, attended)
+        after(to_ranks(packed_ff).reshape(4 * rows, 2 * hidden_part), mixed, cotangent16)
     )
     mixture = low_dot(gated16, full_out) + low_dot(attended16, full_o)
     hidden_state = resident + scatter_sequences(mixture.reshape(2, span_all, D))
 
     middle, mid_back = jax.vjp(rms_scale, hidden_state, mid_gain)
     middle16 = jnp.concatenate(gather_tokens(permuted(middle.astype(bf16))), 0)
-    full_down = gathered(after(w_down, middle16))
+    full_down = gathered(after(w_down, hidden_state))
     both = low_dot(middle16, full_ff)
     activated, swish_back = jax.vjp(
         swish_product, both[:, :hidden_part], both[:, hidden_part:]
@@ -942,12 +953,11 @@
     hidden_piece, mid_gain_grad = mid_back(mid_grad)
     hidden_grad = out_grad[0].astype(f32) + hidden_piece
     ff_grad = weight_grad(middle16, both16).astype(bf16)
-    ff_owned = to_owners(after(ff_grad, down_owned))
+    mix16 = gather_sequences(after(hidden_grad.astype(bf16), ff_grad)).reshape(tokens, D)
+    ff_owned = to_owners(after(ff_grad, down_owned, mix16))
     ff_parts = to_ranks(ff_owned.reshape(4, rows, 2 * hidden_part))
     result_gate = join_ff(ff_parts[..., :hidden_part]).astype(f32)
     result_up = join_ff(ff_parts[..., hidden_part:]).astype(f32)
-
-    mix16 = gather_sequences(after(hidden_grad.astype(bf16), ff_grad)).reshape(tokens, D)
     attended_grad16 = back_dot(mix16, full_o).astype(bf16).reshape(2, span_all, QP)
     gated_grad = back_dot(mix16, full_out).reshape(2, span_all, PART)
     grad_out_w = weight_grad(gated16, mix16).astype(bf16)
@@ -971,7 +981,7 @@
     state_grad = chained(first_grad, -1)
 
     query_grad, kv_grads = attend_backward(
-        query16,
+        after(query16, first_grad),
         kv_all[0],
         kv_all[1],
         attended_grad16,
@@ -1025,9 +1035,17 @@
     ).reshape(tokens, SCAN_COLS)
     if aligned:
         rows_grad = jnp.concatenate(
-            [grad_out_w.reshape(nz * ny, out_rows, D), grad_o.reshape(nz * ny, o_rows, D)], axis=1
-        ).reshape(nz * ny * 2 * rows, D)
-        rows_owned = to_owners(after(rows_grad, ff_owned))
+            [grad_out_w.reshape(nz, 2, out_rows, D), grad_o.reshape(nz, 2, o_rows, D)], axis=2
+        )
+        other_y = lax.dynamic_index_in_dim(rows_grad, 1 - yi, 1, keepdims=False)
+        both_y = lax.dynamic_index_in_dim(rows_grad, yi, 1, keepdims=False).astype(f32) + swap(
+            other_y, "y"
+        ).astype(f32)
+        rows_owned = lax.dynamic_index_in_dim(both_y, zi, 0, keepdims=False)
+        for d in range(1, nz):
+            leaving = lax.dynamic_index_in_dim(both_y, (zi + d) % nz, 0, keepdims=False)
+            rows_owned = rows_owned + turned(leaving.astype(bf16), d).astype(f32)
+        rows_owned = rows_owned.astype(bf16)
         result_out = lax.ppermute(rows_owned[:out_rows], ("y", "c"), turn).astype(f32)
         result_o = lax.ppermute(rows_owned[out_rows:], ("z", "y", "c"), back_place).astype(f32)
     else:
@@ -1042,9 +1060,8 @@
         result_out = lax.psum_scatter(every_out, EVERY, scatter_dimension=0, tiled=True)
         result_o = lax.psum_scatter(every_o, EVERY, scatter_dimension=0, tiled=True)
         result_out, result_o = result_out.astype(f32), result_o.astype(f32)
-        rows_owned = result_out
     rest_owned = to_owners(
-        after(weight_grad(normed_rows, rest_grad16).astype(bf16), rows_owned)
+        after(weight_grad(normed_rows, rest_grad16).astype(bf16), ff_owned, mixed_grad)
     )
     rest_parts = to_ranks(rest_owned.reshape(4, rows, REST_COLS)).astype(f32)
     scan_owned = to_owners(

time: 1250 us -> 1200 us (0.960)
  waiting for transfers between devices: 647 us -> 547 us
  local copies, waits for them, and re-layouts: 97.6 us -> 125 us
    all_gather x5 -> x4, waiting for transfers between devices: 138 us -> 64.4 us  [gathered(): return lax.all_gather(array, SHARDS, axis=0, tiled=True)]
    ppermute x0 -> x6, waiting for transfers between devices: none -> 68.2 us  [turned(): lax.ppermute(array, 'z', [(i, (i + distance) % nz) for i in range(nz)])]
    reduce_scatter x5 -> x4, waiting for transfers between devices: 129 us -> 65.5 us  [to_owners(): return lax.psum_scatter(array, SHARDS, scatter_dimension=0, tiled=True)]
    ppermute x24 -> x26, waiting for transfers between devices: 176 us -> 135 us  [swap(): return lax.ppermute(array, axis, [(0, 1), (1, 0)])]
    unnamed x283 -> x288, local copies, waits for them, and re-layouts: 29.3 us -> 53.3 us
    ppermute x12, waiting for transfers between devices: 100 us -> 118 us  [chained(): lax.ppermute(leaving.astype(bf16), 'z', [(at, at + step)]).astype(f32)]
  transfers between devices with their start and end apart: 68 -> 74, of which waited for: 34 -> 32; matrix products, arithmetic and copies ran while one was open for 25% -> 27% of each run, Pallas kernels for 9% -> 10%
where the time goes in v5:
time: 1200 us; the launch traced here: 1190 us
  waiting for transfers between devices  547 us (46%)
  matrix products  155 us (13%)
  local copies, waits for them, and re-layouts  125 us (10%)
  Pallas kernels  113 us (9%)
  starting transfers between devices  108 us (9%)
  other arithmetic  104 us (9%)
  between operations  17.3 us (1%)
  blocking collectives  15.1 us (1%)
    ppermute x26, waiting for transfers between devices, swap(): return lax.ppermute(array, axis, [(0, 1), (1, 0)])  135 us
    ppermute x12, waiting for transfers between devices, chained(): lax.ppermute(leaving.astype(bf16), 'z', [(at, at + step)]).astype(f32)  118 us
    ppermute x8, waiting for transfers between devices, shifted(): lax.ppermute(array, 'z', [(i - distance, i) for i in devices if i - dista...  69.4 us
    ppermute x6, waiting for transfers between devices, turned(): lax.ppermute(array, 'z', [(i, (i + distance) % nz) for i in range(nz)])  68.2 us
    reduce_scatter x4, waiting for transfers between devices, to_owners(): return lax.psum_scatter(array, SHARDS, scatter_dimension=0, tiled=True)  65.5 us
    all_gather x4, waiting for transfers between devices, gathered(): return lax.all_gather(array, SHARDS, axis=0, tiled=True)  64.4 us
    dot_general x6, matrix products, back_dot(): lax.dot_general(grad_rows, weight, (((1,), (1,)), ((), ())), preferred_el...  60.8 us
    unnamed x288, local copies, waits for them, and re-layouts  53.3 us
  transfers between devices with their start and end apart: 74, of which 32 were waited for; matrix products, arithmetic and copies ran while one was open for 27% of the time, Pallas kernels for 10%

profile of v5, /device:TPU:0, one launch (start us, length us, event | category | flops | bytes accessed | tf_op | source)
XLA Modules:
  0.0 1185.7 jit_solution(1251447151181240703)
XLA Ops:
  10.9 15.1 %all_to_all.30 = bf16[4,64,1408]{2,1,0:T(8,128)(2,1)} all-to-all(bf16[4,64,1408]{2,1,0:T(8,128)(2,1)S(1)} %fusion.64), channel_id=1, replica_groups=mesh['z'=4,'x'=2,'y'=2,'c'=2] {'x','c'}, dimensions={0} | all-to-all | bytes 1441792 | tf_op jit(solution)/shard_map/all_to_all | solution.py:755
  35.5 24.8 %collective-permute-done = bf16[256,2048]{1,0:T(8,128)(2,1)} collective-permute-done((bf16[256,2048]{1,0:T(8,128)(2,1)}, bf16[256,2048]{1,0:T(8,128)(2,1)}, u32[]{:S(2)}, u32[]{:S(2)}) %collective-permute-start) | collective-permute-done | bytes 1048608 | tf_op jit(solution)/shard_map/ppermute | solution.py:41
  143.2 14.1 %shard_map.330 = (f32[2,512,1280]{2,1,0:T(8,128)}, f32[2,512,256]{2,1,0:T(8,128)S(1)}, f32[2,4,8,128]{3,2,1,0:T(8,128)S(1)}, f32[2,4,256,768]{3,2,1,0:T(8,128)}, f32[2,256,768]{2,1,0:T(8,128)S(1)}) custom-call(f32[2,512,1408]{2,1,0:T(8,128)} %bitcast.358, f32[2,4,8,1280]{3,2,1,0:T(8,128)S(1)} %pad_maximum_fusion.21.before, ...), custom_call_target="tpu_custom_call" | custom-call | flops 8000000000 | bytes 30000000 | tf_op jit(solution)/shard_map/pallas_call | solution.py:428
  164.4 27.8 %collective-permute-done.4 = bf16[256,768]{1,0:T(8,128)(2,1)S(1)} collective-permute-done((bf16[256,768]{1,0:T(8,128)(2,1)}, bf16[256,768]{1,0:T(8,128)(2,1)S(1)}, u32[]{:S(2)}, u32[]{:S(2)}) %collective-permute-start.4) | collective-permute-done | bytes 393248 | tf_op jit(solution)/shard_map/ppermute | solution.py:896
  220.6 24.0 %all-gather.7.cloned.1.call-done = bf16[2048,1280]{1,0:T(8,128)(2,1)} async-done(((bf16[256,1280]{1,0:T(8,128)(2,1)}), bf16[2048,1280]{1,0:T(8,128)(2,1)}) %all-gather.7.cloned.1.call-update) | async-done | bytes 5242896 | tf_op jit(solution)/shard_map/all_gather | solution.py:798
  256.6 13.9 %collective-permute-start.20 = (bf16[2,2,512,128]{3,2,1,0:T(8,128)(2,1)}, bf16[2,2,512,128]{3,2,1,0:T(8,128)(2,1)}, u32[]{:S(2)}, u32[]{:S(2)}) collective-permute-start(bf16[2,2,512,128]{3,2,1,0:T(8,128)(2,1)} %pad_maximum_fusion.17), channel_id=1, source_target_pairs={{0,8},{8,16},{16,24},{1,9},{9,17},{17,25},{2,10},{10,18},{18,26},{... | collective-permute-start | bytes 1572872 | tf_op jit(solution)/shard_map/ppermute | solution.py:46
  294.3 21.6 %collective-permute-done.19 = bf16[2,2,512,128]{3,2,1,0:T(8,128)(2,1)} collective-permute-done((bf16[2,2,512,128]{3,2,1,0:T(8,128)(2,1)}, bf16[2,2,512,128]{3,2,1,0:T(8,128)(2,1)}, u32[]{:S(2)}, u32[]{:S(2)}) %collective-permute-start.19) | collective-permute-done | bytes 524320 | tf_op jit(solution)/shard_map/ppermute | solution.py:46
  315.9 21.1 %collective-permute-done.18 = bf16[2,2,512,128]{3,2,1,0:T(8,128)(2,1)} collective-permute-done((bf16[2,2,512,128]{3,2,1,0:T(8,128)(2,1)}, bf16[2,2,512,128]{3,2,1,0:T(8,128)(2,1)}, u32[]{:S(2)}, u32[]{:S(2)}) %collective-permute-start.18) | collective-permute-done | bytes 524320 | tf_op jit(solution)/shard_map/ppermute | solution.py:46
  396.5 25.3 %collective-permute-done.22 = bf16[256,2048]{1,0:T(8,128)(2,1)S(1)} collective-permute-done((bf16[256,2048]{1,0:T(8,128)(2,1)S(1)}, bf16[256,2048]{1,0:T(8,128)(2,1)S(1)}, u32[]{:S(2)}, u32[]{:S(2)}) %collective-permute-start.22) | collective-permute-done | bytes 1048608 | tf_op jit(solution)/shard_map/ppermute | solution.py:41
  436.0 24.5 %collective-permute-done.24 = bf16[256,2048]{1,0:T(8,128)(2,1)S(1)} collective-permute-done((bf16[256,2048]{1,0:T(8,128)(2,1)}, bf16[256,2048]{1,0:T(8,128)(2,1)S(1)}, u32[]{:S(2)}, u32[]{:S(2)}) %collective-permute-start.24) | collective-permute-done | bytes 1048608 | tf_op jit(solution)/shard_map/ppermute | solution.py:41
  490.0 34.1 %all-gather.11.cloned.1.call-done = bf16[1024,2048]{1,0:T(8,128)(2,1)} async-done(((bf16[128,2048]{1,0:T(8,128)(2,1)}), bf16[1024,2048]{1,0:T(8,128)(2,1)}) %all-gather.11.cloned.1.call-update) | async-done | bytes 4194320 | tf_op jit(solution)/shard_map/all_gather | solution.py:798
  537.2 14.7 %fusion.100 = (bf16[1024,2048]{1,0:T(8,128)(2,1)S(1)}, f32[1024,2048]{1,0:T(8,128)}) fusion(bf16[2048,2048]{1,0:T(8,128)(2,1)} %all-gather.9.cloned.1.call-done, bf16[1024,1024]{1,0:T(8,128)(2,1)} %get-tuple-element.106, bf16[1024,1024]{1,0:T(8,128)(2,1)S(1)} %get-tuple-element.105), kind=kOutput, calls=%fused_computation.340 | convolution fusion | flops 8600420352 | bytes 25165824 | tf_op jit(solution)/shard_map/dot_general | solution.py:69
  562.9 13.6 %convolution_convert_fusion = bf16[2048,2048]{1,0:T(8,128)(2,1)} fusion(bf16[1024,1024]{1,0:T(8,128)(2,1)} %get-tuple-element.106, bf16[1024,1024]{1,0:T(8,128)(2,1)S(1)} %copy-done.115, bf16[256,2048]{1,0:T(8,128)(2,1)} %collective-permute-done.25, bf16[256,2048]{1,0:T(8,128)(2,1)S(1)} %copy-done.112, bf16[256,2048]{1,0:T(8,128)(2,1)} %collective-permute-done.23, ...), kind=kOutput, calls=%fused_computation.2 | convolution fusion | flops 8619294720 | bytes 16777216 | tf_op jit(solution)/shard_map/dot_general | solution.py:73
  593.8 23.0 %collective-permute-done.33 = bf16[256,2048]{1,0:T(8,128)(2,1)S(1)} collective-permute-done((bf16[256,2048]{1,0:T(8,128)(2,1)S(1)}, bf16[256,2048]{1,0:T(8,128)(2,1)S(1)}, u32[]{:S(2)}, u32[]{:S(2)}) %collective-permute-start.33) | collective-permute-done | bytes 1048608 | tf_op jit(solution)/shard_map/ppermute | solution.py:41
  625.8 14.2 %reduce-scatter.5.cloned.1.call-done = bf16[128,2048]{1,0:T(8,128)(2,1)} async-done(((bf16[1024,2048]{1,0:T(8,128)(2,1)}), bf16[128,2048]{1,0:T(8,128)(2,1)}) %reduce-scatter.5.cloned.1.call-update) | async-done | bytes 524304 | tf_op jit(solution)/shard_map/reduce_scatter | solution.py:945
  678.6 18.8 %shard_map.336 = (f32[2,512,256]{2,1,0:T(8,128)S(1)}, f32[2,2,2048,128]{3,2,1,0:T(8,128)}) custom-call(bf16[2,512,256]{2,1,0:T(8,128)(2,1)S(1)} %convert_element_type.388.query, bf16[2,2048,128]{2,1,0:T(8,128)(2,1)S(1)} %copy-done.7, bf16[2,2048,128]{2,1,0:T(8,128)(2,1)} %get-tuple-element.119.value, bf16[2,512,256]{2,1,0:T(8,128)(2,1)S(1)} %bitcast.309, ...), custom_call_target="tpu_custom_call" | custom-call | flops 20000000000 | bytes 30000000 | tf_op jit(solution)/shard_map/pallas_call | solution.py:640
  705.0 22.0 %shard_map.334 = (f32[2,512,1280]{2,1,0:T(8,128)}, f32[2,512,256]{2,1,0:T(8,128)S(1)}, f32[8,128]{1,0:T(8,128)S(1)}) custom-call(f32[2,512,1280]{2,1,0:T(8,128)} %get-tuple-element.58.mixed.c_part, f32[2,512,256]{2,1,0:T(8,128)S(1)} %copy-done.4, f32[2,4,8,128]{3,2,1,0:T(8,128)S(1)} %copy-done.20, f32[2,4,256,768]{3,2,1,0:T(8,128)} %get-tuple-element.61.prefix, ...), custom_call_target="tpu_custom_call" | custom-call | flops 30000001024 | bytes 40000000 | tf_op jit(solution)/shard_map/pallas_call | solution.py:513
  734.2 21.5 %collective-permute-done.46 = bf16[2,2,512,128]{3,2,1,0:T(8,128)(2,1)} collective-permute-done((bf16[2,2,512,128]{3,2,1,0:T(8,128)(2,1)}, bf16[2,2,512,128]{3,2,1,0:T(8,128)(2,1)}, u32[]{:S(2)}, u32[]{:S(2)}) %collective-permute-start.46) | collective-permute-done | bytes 524320 | tf_op jit(solution)/shard_map/ppermute | solution.py:46
  767.4 51.3 %reduce-scatter.7.cloned.1.call-done = bf16[256,2048]{1,0:T(8,128)(2,1)} async-done(((bf16[2048,2048]{1,0:T(8,128)(2,1)}), bf16[256,2048]{1,0:T(8,128)(2,1)}) %reduce-scatter.7.cloned.1.call-update) | async-done | bytes 1048592 | tf_op jit(solution)/shard_map/reduce_scatter | solution.py:945
  846.2 72.0 %collective-permute-done.43 = bf16[256,768]{1,0:T(8,128)(2,1)S(1)} collective-permute-done((bf16[256,768]{1,0:T(8,128)(2,1)S(1)}, bf16[256,768]{1,0:T(8,128)(2,1)S(1)}, u32[]{:S(2)}, u32[]{:S(2)}) %collective-permute-start.43) | collective-permute-done | bytes 393248 | tf_op jit(solution)/shard_map/ppermute | solution.py:896
  927.4 22.1 %shard_map.335 = (bf16[2,512,1408]{2,1,0:T(8,128)(2,1)}, f32[2,8,1280]{2,1,0:T(8,128)S(1)}, f32[8,1280]{1,0:T(8,128)S(1)}, f32[8,128]{1,0:T(8,128)S(1)}) custom-call(f32[2,512,1408]{2,1,0:T(8,128)} %bitcast.359, f32[2,4,8,1280]{3,2,1,0:T(8,128)S(1)} %copy-done.9, f32[2,512,1280]{2,1,0:T(8,128)} %get-tuple-element.58.mixed.c_part, ...), custom_call_target="tpu_custom_call" | custom-call | flops 15000000512 | bytes 50000000 | tf_op jit(solution)/shard_map/pallas_call | solution.py:544
  1011.9 21.7 %collective-permute-done.58 = bf16[128,2048]{1,0:T(8,128)(2,1)S(1)} collective-permute-done((bf16[128,2048]{1,0:T(8,128)(2,1)S(1)}, bf16[128,2048]{1,0:T(8,128)(2,1)S(1)}, u32[]{:S(2)}, u32[]{:S(2)}) %collective-permute-start.58) | collective-permute-done | bytes 524320 | tf_op jit(solution)/shard_map/ppermute | solution.py:865
  1033.6 46.5 %collective-permute-done.57 = bf16[128,2048]{1,0:T(8,128)(2,1)S(1)} collective-permute-done((bf16[128,2048]{1,0:T(8,128)(2,1)S(1)}, bf16[128,2048]{1,0:T(8,128)(2,1)S(1)}, u32[]{:S(2)}, u32[]{:S(2)}) %collective-permute-start.57) | collective-permute-done | bytes 524320 | tf_op jit(solution)/shard_map/ppermute | solution.py:865
  1105.6 13.9 %collective-permute-done.51 = f32[25232]{0:T(1024)S(1)} collective-permute-done((f32[25232]{0:T(1024)S(1)}, f32[25232]{0:T(1024)S(1)}, u32[]{:S(2)}, u32[]{:S(2)}) %collective-permute-start.51) | collective-permute-done | bytes 100960 | tf_op jit(solution)/shard_map/ppermute | solution.py:54
  (714 shorter events, 567.1 us)
Async XLA Ops:
  7.2 116.6 %all-gather.5.cloned.1.call-start = ((), (), s32[]{:S(2)}) async-start(), calls=%async_computation.10 | async-start | bytes 6488064 | tf_op jit(solution)/shard_map/all_gather | solution.py:798
  66.4 178.1 %all-gather.7.cloned.1.call-start = ((), (), s32[]{:S(2)}) async-start(), calls=%async_computation.11 | async-start | bytes 5898240 | tf_op jit(solution)/shard_map/all_gather | solution.py:798
  94.3 70.1 %all-to-all-start.2 = ((bf16[4,64,2048]{2,1,0:T(8,128)(2,1)}), bf16[4,64,2048]{2,1,0:T(8,128)(2,1)}, u32[]{:S(2)}, u32[]{:S(2)}) async-start(bf16[4,64,2048]{2,1,0:T(8,128)(2,1)} %pad_maximum_fusion.13), calls=%async_computation.2 | async-start | bytes 2097152 | tf_op jit(solution)/shard_map/all_to_all | solution.py:755
  98.8 365.5 %all-gather.9.cloned.1.call-start = ((), (), s32[]{:S(2)}) async-start(), calls=%async_computation.12 | async-start | bytes 9437184 | tf_op jit(solution)/shard_map/all_gather | solution.py:798
  123.8 85.1 %collective-permute-start.14 = (bf16[128,2048]{1,0:T(8,128)(2,1)}, bf16[128,2048]{1,0:T(8,128)(2,1)}, u32[]{:S(2)}, u32[]{:S(2)}) collective-permute-start(bf16[128,2048]{1,0:T(8,128)(2,1)} %pad_maximum_fusion.18), channel_id=1, source_target_pairs={{0,24},{8,0},{16,8},{24,16},{1,25},{9,1},{17,9},{25,17},{2,26},{10... | collective-permute-start | bytes 1572872 | tf_op jit(solution)/shard_map/ppermute | solution.py:865
  127.5 82.5 %collective-permute-start.15 = (bf16[128,2048]{1,0:T(8,128)(2,1)}, bf16[128,2048]{1,0:T(8,128)(2,1)}, u32[]{:S(2)}, u32[]{:S(2)}) collective-permute-start(bf16[128,2048]{1,0:T(8,128)(2,1)} %pad_maximum_fusion.18), channel_id=1, source_target_pairs={{0,16},{8,24},{16,0},{24,8},{1,17},{9,25},{17,1},{25,9},{2,18},{10... | collective-permute-start | bytes 1572872 | tf_op jit(solution)/shard_map/ppermute | solution.py:865
  128.3 82.8 %collective-permute-start.16 = (bf16[128,2048]{1,0:T(8,128)(2,1)}, bf16[128,2048]{1,0:T(8,128)(2,1)}, u32[]{:S(2)}, u32[]{:S(2)}) collective-permute-start(bf16[128,2048]{1,0:T(8,128)(2,1)} %pad_maximum_fusion.18), channel_id=1, source_target_pairs={{0,8},{8,16},{16,24},{24,0},{1,9},{9,17},{17,25},{25,1},{2,10},{10... | collective-permute-start | bytes 1572872 | tf_op jit(solution)/shard_map/ppermute | solution.py:865
  164.4 359.8 %all-gather.11.cloned.1.call-start = ((), (), s32[]{:S(2)}) async-start(), calls=%async_computation.13 | async-start | bytes 4718592 | tf_op jit(solution)/shard_map/all_gather | solution.py:798
  205.5 78.4 %collective-permute-start.5 = (bf16[256,768]{1,0:T(8,128)(2,1)}, bf16[256,768]{1,0:T(8,128)(2,1)}, u32[]{:S(2)}, u32[]{:S(2)}) collective-permute-start(bf16[256,768]{1,0:T(8,128)(2,1)} %get-tuple-element.133), channel_id=1, source_target_pairs={{8,16},{9,17},{10,18},{11,19},{12,20},{13,21},{14,22},{15,23}} | collective-permute-start | bytes 1179656 | tf_op jit(solution)/shard_map/ppermute | solution.py:896
  207.0 79.8 %collective-permute-start.8 = (bf16[256,768]{1,0:T(8,128)(2,1)}, bf16[256,768]{1,0:T(8,128)(2,1)}, u32[]{:S(2)}, u32[]{:S(2)}) collective-permute-start(bf16[256,768]{1,0:T(8,128)(2,1)} %get-tuple-element.134), channel_id=1, source_target_pairs={{8,16},{9,17},{10,18},{11,19},{12,20},{13,21},{14,22},{15,23}} | collective-permute-start | bytes 1179656 | tf_op jit(solution)/shard_map/ppermute | solution.py:896
  276.2 60.7 %collective-permute-start.18 = (bf16[2,2,512,128]{3,2,1,0:T(8,128)(2,1)}, bf16[2,2,512,128]{3,2,1,0:T(8,128)(2,1)}, u32[]{:S(2)}, u32[]{:S(2)}) collective-permute-start(bf16[2,2,512,128]{3,2,1,0:T(8,128)(2,1)} %pad_maximum_fusion.17), channel_id=1, source_target_pairs={{0,24},{1,25},{2,26},{3,27},{4,28},{5,29},{6,30},{7,31}} | collective-permute-start | bytes 1572872 | tf_op jit(solution)/shard_map/ppermute | solution.py:46
  283.9 90.2 %collective-permute-start.17 = (bf16[4,128,2048]{2,1,0:T(8,128)(2,1)}, bf16[4,128,2048]{2,1,0:T(8,128)(2,1)}, u32[]{:S(2)}, u32[]{:S(2)}) collective-permute-start(bf16[4,128,2048]{2,1,0:T(8,128)(2,1)} %constant_dynamic-slice_fusion), channel_id=1, source_target_pairs={{0,2},{2,0},{1,3},{3,1},{4,6},{6,4},{5,7},{7,5},{8,10},{10,8},{9,1... | collective-permute-start | bytes 6291464 | tf_op jit(solution)/shard_map/ppermute | solution.py:41
  428.2 211.8 %reduce-scatter.5.cloned.1.call-start = ((), (), s32[]{:S(2)}) async-start(), calls=%async_computation.14 | async-start | bytes 4718592 | tf_op jit(solution)/shard_map/reduce_scatter | solution.py:945
  553.5 265.2 %reduce-scatter.7.cloned.1.call-start = ((), (), s32[]{:S(2)}) async-start(), calls=%async_computation.15 | async-start | bytes 9437184 | tf_op jit(solution)/shard_map/reduce_scatter | solution.py:945
  640.0 340.9 %reduce-scatter.9.cloned.1.call-start = ((), (), s32[]{:S(2)}) async-start(), calls=%async_computation.16 | async-start | bytes 5898240 | tf_op jit(solution)/shard_map/reduce_scatter | solution.py:945
  818.8 340.9 %reduce-scatter.11.cloned.1.call-start = ((), (), s32[]{:S(2)}) async-start(), calls=%async_computation.17 | async-start | bytes 6488064 | tf_op jit(solution)/shard_map/reduce_scatter | solution.py:945
  833.0 164.8 %collective-permute-start.29 = (bf16[2,256,2048]{2,1,0:T(8,128)(2,1)}, bf16[2,256,2048]{2,1,0:T(8,128)(2,1)}, u32[]{:S(2)}, u32[]{:S(2)}) collective-permute-start(bf16[2,256,2048]{2,1,0:T(8,128)(2,1)} %pad_maximum_fusion.8), channel_id=1, source_target_pairs={{0,1},{1,0},{2,3},{3,2},{4,5},{5,4},{6,7},{7,6},{8,9},{9,8},{10,11... | collective-permute-start | bytes 6291464 | tf_op jit(solution)/shard_map/ppermute | solution.py:41
  839.2 79.0 %collective-permute-start.43 = (bf16[256,768]{1,0:T(8,128)(2,1)S(1)}, bf16[256,768]{1,0:T(8,128)(2,1)S(1)}, u32[]{:S(2)}, u32[]{:S(2)}) collective-permute-start(bf16[256,768]{1,0:T(8,128)(2,1)S(1)} %get-tuple-element.124), channel_id=1, source_target_pairs={{8,0},{9,1},{10,2},{11,3},{12,4},{13,5},{14,6},{15,7}} | collective-permute-start | bytes 1179656 | tf_op jit(solution)/shard_map/ppermute | solution.py:896
  842.0 83.9 %collective-permute-start.40 = (bf16[256,768]{1,0:T(8,128)(2,1)S(1)}, bf16[256,768]{1,0:T(8,128)(2,1)S(1)}, u32[]{:S(2)}, u32[]{:S(2)}) collective-permute-start(bf16[256,768]{1,0:T(8,128)(2,1)S(1)} %get-tuple-element.123), channel_id=1, source_target_pairs={{8,0},{9,1},{10,2},{11,3},{12,4},{13,5},{14,6},{15,7}} | collective-permute-start | bytes 1179656 | tf_op jit(solution)/shard_map/ppermute | solution.py:896
  844.8 157.2 %collective-permute-start.55 = (bf16[4,128,2048]{2,1,0:T(8,128)(2,1)}, bf16[4,128,2048]{2,1,0:T(8,128)(2,1)}, u32[]{:S(2)}, u32[]{:S(2)}) collective-permute-start(bf16[4,128,2048]{2,1,0:T(8,128)(2,1)} %fusion.35), channel_id=1, source_target_pairs={{0,2},{2,0},{1,3},{3,1},{4,6},{6,4},{5,7},{7,5},{8,10},{10,8},{9,1... | collective-permute-start | bytes 6291464 | tf_op jit(solution)/shard_map/ppermute | solution.py:41
  1001.1 146.9 %collective-permute-start.30 = (bf16[256,2048]{1,0:T(8,128)(2,1)}, bf16[256,2048]{1,0:T(8,128)(2,1)}, u32[]{:S(2)}, u32[]{:S(2)}) collective-permute-start(bf16[256,2048]{1,0:T(8,128)(2,1)} %fusion.40), channel_id=1, source_target_pairs={{0,4},{4,0},{1,5},{5,1},{2,6},{6,2},{3,7},{7,3},{8,12},{12,8},{9,1... | collective-permute-start | bytes 3145736 | tf_op jit(solution)/shard_map/ppermute | solution.py:41
  1004.9 75.2 %collective-permute-start.57 = (bf16[128,2048]{1,0:T(8,128)(2,1)S(1)}, bf16[128,2048]{1,0:T(8,128)(2,1)S(1)}, u32[]{:S(2)}, u32[]{:S(2)}) collective-permute-start(bf16[128,2048]{1,0:T(8,128)(2,1)S(1)} %get-tuple-element.109), channel_id=1, source_target_pairs={{0,16},{8,24},{16,0},{24,8},{1,17},{9,25},{17,1},{25,9},{2,18},{10... | collective-permute-start | bytes 1572872 | tf_op jit(solution)/shard_map/ppermute | solution.py:865
  1005.6 74.5 %collective-permute-start.56 = (bf16[128,2048]{1,0:T(8,128)(2,1)S(1)}, bf16[128,2048]{1,0:T(8,128)(2,1)S(1)}, u32[]{:S(2)}, u32[]{:S(2)}) collective-permute-start(bf16[128,2048]{1,0:T(8,128)(2,1)S(1)} %get-tuple-element.107), channel_id=1, source_target_pairs={{0,8},{8,16},{16,24},{24,0},{1,9},{9,17},{17,25},{25,1},{2,10},{10... | collective-permute-start | bytes 1572872 | tf_op jit(solution)/shard_map/ppermute | solution.py:865
  1010.7 80.5 %collective-permute-start.49 = (bf16[256,2048]{1,0:T(8,128)(2,1)}, bf16[256,2048]{1,0:T(8,128)(2,1)}, u32[]{:S(2)}, u32[]{:S(2)}) collective-permute-start(bf16[256,2048]{1,0:T(8,128)(2,1)} %fusion.46), channel_id=1, source_target_pairs={{0,4},{4,0},{1,5},{5,1},{2,6},{6,2},{3,7},{7,3},{8,12},{12,8},{9,1... | collective-permute-start | bytes 3145736 | tf_op jit(solution)/shard_map/ppermute | solution.py:41
  (171 other events, 3793.0 us)
Sparse Core Ops, SparseCore 0:
  26.1 97.6 all-gather.4
  126.5 117.9 all-gather.6
  246.7 177.2 all-gather.8
  428.3 95.7 all-gather.10
  553.7 86.2 reduce-scatter.4
  643.9 174.7 reduce-scatter.6
  822.3 137.0 reduce-scatter.8
  981.1 153.4 reduce-scatter.10

commit v6 on v5

--- a/solution.py
+++ b/solution.py
@@ -912,14 +912,15 @@
     key16 = rotate(rest[..., None, AT_K:AT_V], cosine, sine).astype(bf16)[:, :, 0]
     kv16 = jnp.stack([key16, rest[..., AT_V:].astype(bf16)])
     state_in = chained(own_state, 1, kv16)
-    kv_all = jnp.concatenate([shifted(kv16, d) for d in range(nz - 1, 0, -1)] + [kv16], axis=2)
+    kv_before = [shifted(kv16, d) for d in range(nz - 1, 0, -1)]
     keys_at = (zi - nz + 1) * span_all + jnp.arange(nz * span_all, dtype=jnp.int32)
     query_place = jnp.broadcast_to(positions[:, None], (span_all, 128))
     key_place = jnp.broadcast_to(keys_at[None], (8, nz * span_all))
     values, flat, square = scan_values(
         mixed, steps, starts, prefix, state_in, rest, 0, skip, lift
     )
-    attended, log_sum = attend(after(query16, flat), kv_all[0], kv_all[1], query_place, key_place)
+    kv_all = jnp.concatenate(list(after(tuple(kv_before), flat)) + [kv16], axis=2)
+    attended, log_sum = attend(query16, kv_all[0], kv_all[1], query_place, key_place)
     attended16 = attended.reshape(tokens, QP).astype(bf16)
 
     root = lax.rsqrt(group_total(square[..., :1]) / INNER + epsilon)
@@ -962,6 +963,16 @@
     gated_grad = back_dot(mix16, full_out).reshape(2, span_all, PART)
     grad_out_w = weight_grad(gated16, mix16).astype(bf16)
     grad_o = weight_grad(attended16, mix16).astype(bf16)
+    if aligned:
+        rows_grad = jnp.concatenate(
+            [grad_out_w.reshape(nz, 2, out_rows, D), grad_o.reshape(nz, 2, o_rows, D)], axis=2
+        )
+        other_y = lax.dynamic_index_in_dim(rows_grad, 1 - yi, 1, keepdims=False)
+        both_y = lax.dynamic_index_in_dim(rows_grad, yi, 1, keepdims=False).astype(f32) + swap(
+            other_y, "y"
+        ).astype(f32)
+    else:
+        both_y = grad_o
 
     inner = jnp.sum(gated_grad * gain * flat, axis=-1, keepdims=True) * root
     inner_mean = group_total(inner) / INNER
@@ -1019,7 +1030,7 @@
         starts,
         prefix,
         state_in,
-        after(state_grad, ff_owned),
+        after(state_grad, ff_owned, both_y),
         mixed_grad,
         step_grad,
         taps,
@@ -1034,17 +1045,11 @@
         scan_grad16, last_rows.astype(bf16), (0, span_all - edge_count, 0)
     ).reshape(tokens, SCAN_COLS)
     if aligned:
-        rows_grad = jnp.concatenate(
-            [grad_out_w.reshape(nz, 2, out_rows, D), grad_o.reshape(nz, 2, o_rows, D)], axis=2
-        )
-        other_y = lax.dynamic_index_in_dim(rows_grad, 1 - yi, 1, keepdims=False)
-        both_y = lax.dynamic_index_in_dim(rows_grad, yi, 1, keepdims=False).astype(f32) + swap(
-            other_y, "y"
-        ).astype(f32)
         rows_owned = lax.dynamic_index_in_dim(both_y, zi, 0, keepdims=False)
+        waiting = after(both_y.astype(bf16), state_grad)
         for d in range(1, nz):
-            leaving = lax.dynamic_index_in_dim(both_y, (zi + d) % nz, 0, keepdims=False)
-            rows_owned = rows_owned + turned(leaving.astype(bf16), d).astype(f32)
+            leaving = lax.dynamic_index_in_dim(waiting, (zi + d) % nz, 0, keepdims=False)
+            rows_owned = rows_owned + turned(leaving, d).astype(f32)
         rows_owned = rows_owned.astype(bf16)
         result_out = lax.ppermute(rows_owned[:out_rows], ("y", "c"), turn).astype(f32)
         result_o = lax.ppermute(rows_owned[out_rows:], ("z", "y", "c"), back_place).astype(f32)
@@ -1061,28 +1066,18 @@
         result_o = lax.psum_scatter(every_o, EVERY, scatter_dimension=0, tiled=True)
         result_out, result_o = result_out.astype(f32), result_o.astype(f32)
     rest_owned = to_owners(
-        after(weight_grad(normed_rows, rest_grad16).astype(bf16), ff_owned, mixed_grad)
+        after(weight_grad(normed_rows, rest_grad16).astype(bf16), ff_owned, state_grad)
     )
     rest_parts = to_ranks(rest_owned.reshape(4, rows, REST_COLS)).astype(f32)
     scan_owned = to_owners(
         after(weight_grad(normed_rows, scan_grad16).astype(bf16), rest_owned)
     )
-    scan_parts = to_ranks(scan_owned.reshape(4, rows, SCAN_COLS)).astype(f32)
 
     normed_grad = back_dot(scan_grad16, full_scan) + back_dot(rest_grad16, full_rest)
     normed_grad = restored(scatter_sequences(normed_grad.reshape(2, span_all, D)))
     resident_grad, norm_gain_grad = norm_back(normed_grad)
     input_grad = hidden_grad + resident_grad
 
-    result_in = jnp.concatenate(
-        [
-            heads_join(rest_parts[..., :PART], MAMBA_HEAD),
-            heads_join(scan_parts[..., :PART], MAMBA_HEAD),
-            jnp.sum(scan_parts[..., PART:CONV_COLS], axis=0),
-            heads_join(scan_parts[..., CONV_COLS : CONV_COLS + HEADS], 1),
-        ],
-        axis=1,
-    )
     result_q = jnp.transpose(
         rest_parts[..., AT_Q:AT_K].reshape(2, 2, rows, 2, HEAD_DIM), (2, 1, 3, 0, 4)
     ).reshape(rows, ATT_HEADS * HEAD_DIM)
@@ -1110,6 +1105,31 @@
     for v in small:
         parts.append(summed[at : at + v.size].reshape(v.shape))
         at += v.size
+    scan_owned = after(
+        scan_owned,
+        summed,
+        input_grad,
+        output,
+        rest_parts,
+        result_gate,
+        result_up,
+        result_down,
+        result_q,
+        result_k,
+        result_v,
+        result_out,
+        result_o,
+    )
+    scan_parts = to_ranks(scan_owned.reshape(4, rows, SCAN_COLS)).astype(f32)
+    result_in = jnp.concatenate(
+        [
+            heads_join(rest_parts[..., :PART], MAMBA_HEAD),
+            heads_join(scan_parts[..., :PART], MAMBA_HEAD),
+            jnp.sum(scan_parts[..., PART:CONV_COLS], axis=0),
+            heads_join(scan_parts[..., CONV_COLS : CONV_COLS + HEADS], 1),
+        ],
+        axis=1,
+    )
     return (
         output[None],
         input_grad[None],

time: 1200 us -> 1160 us (0.967)
  waiting for transfers between devices: 547 us -> 501 us
    reduce_scatter x4, waiting for transfers between devices: 65.5 us -> 21.1 us  [to_owners(): return lax.psum_scatter(array, SHARDS, scatter_dimension=0, tiled=True)]
    all_gather x4, waiting for transfers between devices: 64.4 us -> 96.1 us  [gathered(): return lax.all_gather(array, SHARDS, axis=0, tiled=True)]
    ppermute x12, waiting for transfers between devices: 118 us -> 96.9 us  [chained(): lax.ppermute(leaving.astype(bf16), 'z', [(at, at + step)]).astype(f32)]
    unnamed x288 -> x296, local copies, waits for them, and re-layouts: 53.3 us -> 44.9 us
  transfers between devices with their start and end apart: 74 -> 74, of which waited for: 32 -> 31; matrix products, arithmetic and copies ran while one was open for 27% -> 29% of each run, Pallas kernels for 10% -> 10%
where the time goes in v6:
time: 1160 us; the launch traced here: 1150 us
  waiting for transfers between devices  501 us (43%)
  matrix products  154 us (13%)
  local copies, waits for them, and re-layouts  125 us (11%)
  other arithmetic  115 us (10%)
  Pallas kernels  113 us (10%)
  starting transfers between devices  109 us (9%)
  between operations  17.6 us (2%)
  blocking collectives  15.1 us (1%)
    ppermute x26, waiting for transfers between devices, swap(): return lax.ppermute(array, axis, [(0, 1), (1, 0)])  132 us
    ppermute x12, waiting for transfers between devices, chained(): lax.ppermute(leaving.astype(bf16), 'z', [(at, at + step)]).astype(f32)  96.9 us
    all_gather x4, waiting for transfers between devices, gathered(): return lax.all_gather(array, SHARDS, axis=0, tiled=True)  96.1 us
    ppermute x6, waiting for transfers between devices, turned(): lax.ppermute(array, 'z', [(i, (i + distance) % nz) for i in range(nz)])  73.7 us
    dot_general x6, matrix products, back_dot(): lax.dot_general(grad_rows, weight, (((1,), (1,)), ((), ())), preferred_el...  60.6 us
    ppermute x8, waiting for transfers between devices, shifted(): lax.ppermute(array, 'z', [(i - distance, i) for i in devices if i - dista...  59.3 us
    dot_general x7, matrix products, low_dot(): return jnp.dot(left, right, preferred_element_type=f32)  47.5 us
    dot_general x6, matrix products, weight_grad(): lax.dot_general(left, right, (((0,), (0,)), ((), ())), preferred_element_...  46.2 us
  transfers between devices with their start and end apart: 74, of which 31 were waited for; matrix products, arithmetic and copies ran while one was open for 29% of the time, Pallas kernels for 10%

profile of v6, /device:TPU:0, one launch (start us, length us, event | category | flops | bytes accessed | tf_op | source)
XLA Modules:
  0.0 1149.8 jit_solution(3305307372171309499)
XLA Ops:
  10.9 15.1 %all_to_all.30 = bf16[4,64,1408]{2,1,0:T(8,128)(2,1)} all-to-all(bf16[4,64,1408]{2,1,0:T(8,128)(2,1)S(1)} %fusion.62), channel_id=1, replica_groups=mesh['z'=4,'x'=2,'y'=2,'c'=2] {'x','c'}, dimensions={0} | all-to-all | bytes 1441792 | tf_op jit(solution)/shard_map/all_to_all | solution.py:755
  35.5 24.8 %collective-permute-done = bf16[256,2048]{1,0:T(8,128)(2,1)} collective-permute-done((bf16[256,2048]{1,0:T(8,128)(2,1)}, bf16[256,2048]{1,0:T(8,128)(2,1)}, u32[]{:S(2)}, u32[]{:S(2)}) %collective-permute-start) | collective-permute-done | bytes 1048608 | tf_op jit(solution)/shard_map/ppermute | solution.py:41
  143.1 14.0 %shard_map.330 = (f32[2,512,1280]{2,1,0:T(8,128)}, f32[2,512,256]{2,1,0:T(8,128)S(1)}, f32[2,4,8,128]{3,2,1,0:T(8,128)S(1)}, f32[2,4,256,768]{3,2,1,0:T(8,128)}, f32[2,256,768]{2,1,0:T(8,128)S(1)}) custom-call(f32[2,512,1408]{2,1,0:T(8,128)} %bitcast.351, f32[2,4,8,1280]{3,2,1,0:T(8,128)S(1)} %pad_maximum_fusion.21.before, ...), custom_call_target="tpu_custom_call" | custom-call | flops 8000000000 | bytes 30000000 | tf_op jit(solution)/shard_map/pallas_call | solution.py:428
  165.3 26.9 %collective-permute-done.4 = bf16[256,768]{1,0:T(8,128)(2,1)S(1)} collective-permute-done((bf16[256,768]{1,0:T(8,128)(2,1)}, bf16[256,768]{1,0:T(8,128)(2,1)S(1)}, u32[]{:S(2)}, u32[]{:S(2)}) %collective-permute-start.4) | collective-permute-done | bytes 393248 | tf_op jit(solution)/shard_map/ppermute | solution.py:896
  220.3 37.8 %all-gather.7.cloned.1.call-done = bf16[2048,1280]{1,0:T(8,128)(2,1)} async-done(((bf16[256,1280]{1,0:T(8,128)(2,1)}), bf16[2048,1280]{1,0:T(8,128)(2,1)}) %all-gather.7.cloned.1.call-update) | async-done | bytes 5242896 | tf_op jit(solution)/shard_map/all_gather | solution.py:798
  270.5 18.0 %collective-permute-start.18 = (bf16[2,2,512,128]{3,2,1,0:T(8,128)(2,1)}, bf16[2,2,512,128]{3,2,1,0:T(8,128)(2,1)}, u32[]{:S(2)}, u32[]{:S(2)}) collective-permute-start(bf16[2,2,512,128]{3,2,1,0:T(8,128)(2,1)} %pad_maximum_fusion.17), channel_id=1, source_target_pairs={{0,24},{1,25},{2,26},{3,27},{4,28},{5,29},{6,30},{7,31}} | collective-permute-start | bytes 1572872 | tf_op jit(solution)/shard_map/ppermute | solution.py:46
  320.4 13.6 %collective-permute-done.19 = bf16[2,2,512,128]{3,2,1,0:T(8,128)(2,1)} collective-permute-done((bf16[2,2,512,128]{3,2,1,0:T(8,128)(2,1)}, bf16[2,2,512,128]{3,2,1,0:T(8,128)(2,1)}, u32[]{:S(2)}, u32[]{:S(2)}) %collective-permute-start.19) | collective-permute-done | bytes 524320 | tf_op jit(solution)/shard_map/ppermute | solution.py:46
  334.0 16.5 %collective-permute-done.20 = bf16[2,2,512,128]{3,2,1,0:T(8,128)(2,1)} collective-permute-done((bf16[2,2,512,128]{3,2,1,0:T(8,128)(2,1)}, bf16[2,2,512,128]{3,2,1,0:T(8,128)(2,1)}, u32[]{:S(2)}, u32[]{:S(2)}) %collective-permute-start.20) | collective-permute-done | bytes 524320 | tf_op jit(solution)/shard_map/ppermute | solution.py:46
  355.4 12.8 %shard_map.332 = (f32[2,512,256]{2,1,0:T(8,128)S(1)}, f32[2,512,256]{2,1,0:T(8,128)S(1)}) custom-call(bf16[2,512,256]{2,1,0:T(8,128)(2,1)S(1)} %convert_element_type.373.query, bf16[2,2048,128]{2,1,0:T(8,128)(2,1)S(1)} %get-tuple-element.130.key, bf16[2,2048,128]{2,1,0:T(8,128)(2,1)} %get-tuple-element.129.value, ...), custom_call_target="tpu_custom_call" | custom-call | flops 12000000000 | bytes 20000000 | tf_op jit(solution)/shard_map/pallas_call | solution.py:621
  392.7 24.7 %collective-permute-done.22 = bf16[256,2048]{1,0:T(8,128)(2,1)S(1)} collective-permute-done((bf16[256,2048]{1,0:T(8,128)(2,1)S(1)}, bf16[256,2048]{1,0:T(8,128)(2,1)S(1)}, u32[]{:S(2)}, u32[]{:S(2)}) %collective-permute-start.22) | collective-permute-done | bytes 1048608 | tf_op jit(solution)/shard_map/ppermute | solution.py:41
  420.7 24.1 %collective-permute-done.24 = bf16[256,2048]{1,0:T(8,128)(2,1)S(1)} collective-permute-done((bf16[256,2048]{1,0:T(8,128)(2,1)S(1)}, bf16[256,2048]{1,0:T(8,128)(2,1)S(1)}, u32[]{:S(2)}, u32[]{:S(2)}) %collective-permute-start.24) | collective-permute-done | bytes 1048608 | tf_op jit(solution)/shard_map/ppermute | solution.py:41
  473.0 52.1 %all-gather.11.cloned.1.call-done = bf16[1024,2048]{1,0:T(8,128)(2,1)} async-done(((bf16[128,2048]{1,0:T(8,128)(2,1)}), bf16[1024,2048]{1,0:T(8,128)(2,1)}) %all-gather.11.cloned.1.call-update) | async-done | bytes 4194320 | tf_op jit(solution)/shard_map/all_gather | solution.py:798
  536.9 14.7 %fusion.96 = (bf16[1024,2048]{1,0:T(8,128)(2,1)S(1)}, f32[1024,2048]{1,0:T(8,128)}) fusion(bf16[2048,2048]{1,0:T(8,128)(2,1)} %all-gather.9.cloned.1.call-done, bf16[1024,1024]{1,0:T(8,128)(2,1)S(1)} %get-tuple-element.116, bf16[1024,1024]{1,0:T(8,128)(2,1)S(1)} %get-tuple-element.115), kind=kOutput, calls=%fused_computation.336 | convolution fusion | flops 8600420352 | bytes 25165824 | tf_op jit(solution)/shard_map/dot_general | solution.py:69
  560.0 13.9 %convolution_convert_fusion = bf16[2048,2048]{1,0:T(8,128)(2,1)} fusion(bf16[1024,1024]{1,0:T(8,128)(2,1)} %copy-done.119, bf16[1024,1024]{1,0:T(8,128)(2,1)} %copy-done.118, bf16[256,2048]{1,0:T(8,128)(2,1)} %collective-permute-done.25, bf16[256,2048]{1,0:T(8,128)(2,1)S(1)} %copy-done.114, bf16[256,2048]{1,0:T(8,128)(2,1)S(1)} %copy-done.116, ...), kind=kOutput, calls=%fused_computation.2 | convolution fusion | flops 8619294720 | bytes 16777216 | tf_op jit(solution)/shard_map/dot_general | solution.py:73
  592.5 23.1 %collective-permute-done.33 = bf16[256,2048]{1,0:T(8,128)(2,1)S(1)} collective-permute-done((bf16[256,2048]{1,0:T(8,128)(2,1)S(1)}, bf16[256,2048]{1,0:T(8,128)(2,1)S(1)}, u32[]{:S(2)}, u32[]{:S(2)}) %collective-permute-start.33) | collective-permute-done | bytes 1048608 | tf_op jit(solution)/shard_map/ppermute | solution.py:41
  624.6 14.1 %reduce-scatter.5.cloned.1.call-done = bf16[128,2048]{1,0:T(8,128)(2,1)} async-done(((bf16[1024,2048]{1,0:T(8,128)(2,1)}), bf16[128,2048]{1,0:T(8,128)(2,1)}) %reduce-scatter.5.cloned.1.call-update) | async-done | bytes 524304 | tf_op jit(solution)/shard_map/reduce_scatter | solution.py:946
  694.5 18.9 %shard_map.336 = (f32[2,512,256]{2,1,0:T(8,128)S(1)}, f32[2,2,2048,128]{3,2,1,0:T(8,128)}) custom-call(bf16[2,512,256]{2,1,0:T(8,128)(2,1)S(1)} %copy-done.7, bf16[2,2048,128]{2,1,0:T(8,128)(2,1)S(1)} %copy-done.5, bf16[2,2048,128]{2,1,0:T(8,128)(2,1)} %get-tuple-element.129.value, bf16[2,512,256]{2,1,0:T(8,128)(2,1)S(1)} %bitcast.304, ...), custom_call_target="tpu_custom_call" | custom-call | flops 20000000000 | bytes 30000000 | tf_op jit(solution)/shard_map/pallas_call | solution.py:640
  736.1 13.1 %collective-permute-done.48 = bf16[2,2,512,128]{3,2,1,0:T(8,128)(2,1)} collective-permute-done((bf16[2,2,512,128]{3,2,1,0:T(8,128)(2,1)}, bf16[2,2,512,128]{3,2,1,0:T(8,128)(2,1)}, u32[]{:S(2)}, u32[]{:S(2)}) %collective-permute-start.48) | collective-permute-done | bytes 524320 | tf_op jit(solution)/shard_map/ppermute | solution.py:46
  750.0 13.5 %collective-permute-done.47 = bf16[2,2,512,128]{3,2,1,0:T(8,128)(2,1)} collective-permute-done((bf16[2,2,512,128]{3,2,1,0:T(8,128)(2,1)}, bf16[2,2,512,128]{3,2,1,0:T(8,128)(2,1)}, u32[]{:S(2)}, u32[]{:S(2)}) %collective-permute-start.47) | collective-permute-done | bytes 524320 | tf_op jit(solution)/shard_map/ppermute | solution.py:46
  780.2 46.2 %collective-permute-done.43 = bf16[256,768]{1,0:T(8,128)(2,1)} collective-permute-done((bf16[256,768]{1,0:T(8,128)(2,1)}, bf16[256,768]{1,0:T(8,128)(2,1)}, u32[]{:S(2)}, u32[]{:S(2)}) %collective-permute-start.43) | collective-permute-done | bytes 393248 | tf_op jit(solution)/shard_map/ppermute | solution.py:896
  862.6 22.0 %shard_map.334 = (f32[2,512,1280]{2,1,0:T(8,128)}, f32[2,512,256]{2,1,0:T(8,128)S(1)}, f32[8,128]{1,0:T(8,128)S(1)}) custom-call(f32[2,512,1280]{2,1,0:T(8,128)} %get-tuple-element.62.mixed.c_part, f32[2,512,256]{2,1,0:T(8,128)S(1)} %get-tuple-element.63.steps, f32[2,4,8,128]{3,2,1,0:T(8,128)S(1)} %copy-done.17, ...), custom_call_target="tpu_custom_call" | custom-call | flops 30000001024 | bytes 40000000 | tf_op jit(solution)/shard_map/pallas_call | solution.py:513
  884.7 21.7 %shard_map.335 = (bf16[2,512,1408]{2,1,0:T(8,128)(2,1)}, f32[2,8,1280]{2,1,0:T(8,128)S(1)}, f32[8,1280]{1,0:T(8,128)S(1)}, f32[8,128]{1,0:T(8,128)S(1)}) custom-call(f32[2,512,1408]{2,1,0:T(8,128)} %bitcast.352, f32[2,4,8,1280]{3,2,1,0:T(8,128)S(1)} %copy-done.9, f32[2,512,1280]{2,1,0:T(8,128)} %get-tuple-element.62.mixed.c_part, ...), custom_call_target="tpu_custom_call" | custom-call | flops 15000000512 | bytes 50000000 | tf_op jit(solution)/shard_map/pallas_call | solution.py:544
  975.2 19.1 %collective-permute-done.58 = bf16[128,2048]{1,0:T(8,128)(2,1)S(1)} collective-permute-done((bf16[128,2048]{1,0:T(8,128)(2,1)S(1)}, bf16[128,2048]{1,0:T(8,128)(2,1)S(1)}, u32[]{:S(2)}, u32[]{:S(2)}) %collective-permute-start.58) | collective-permute-done | bytes 524320 | tf_op jit(solution)/shard_map/ppermute | solution.py:865
  994.3 54.5 %collective-permute-done.57 = bf16[128,2048]{1,0:T(8,128)(2,1)S(1)} collective-permute-done((bf16[128,2048]{1,0:T(8,128)(2,1)S(1)}, bf16[128,2048]{1,0:T(8,128)(2,1)S(1)}, u32[]{:S(2)}, u32[]{:S(2)}) %collective-permute-start.57) | collective-permute-done | bytes 524320 | tf_op jit(solution)/shard_map/ppermute | solution.py:865
  (721 shorter events, 577.2 us)
Async XLA Ops:
  7.2 116.6 %all-gather.5.cloned.1.call-start = ((), (), s32[]{:S(2)}) async-start(), calls=%async_computation.10 | async-start | bytes 6488064 | tf_op jit(solution)/shard_map/all_gather | solution.py:798
  66.4 191.6 %all-gather.7.cloned.1.call-start = ((), (), s32[]{:S(2)}) async-start(), calls=%async_computation.11 | async-start | bytes 5898240 | tf_op jit(solution)/shard_map/all_gather | solution.py:798
  94.4 70.8 %all-to-all-start.2 = ((bf16[4,64,2048]{2,1,0:T(8,128)(2,1)}), bf16[4,64,2048]{2,1,0:T(8,128)(2,1)}, u32[]{:S(2)}, u32[]{:S(2)}) async-start(bf16[4,64,2048]{2,1,0:T(8,128)(2,1)} %pad_maximum_fusion.13), calls=%async_computation.2 | async-start | bytes 2097152 | tf_op jit(solution)/shard_map/all_to_all | solution.py:755
  98.9 348.6 %all-gather.9.cloned.1.call-start = ((), (), s32[]{:S(2)}) async-start(), calls=%async_computation.12 | async-start | bytes 9437184 | tf_op jit(solution)/shard_map/all_gather | solution.py:798
  123.8 84.9 %collective-permute-start.14 = (bf16[128,2048]{1,0:T(8,128)(2,1)}, bf16[128,2048]{1,0:T(8,128)(2,1)}, u32[]{:S(2)}, u32[]{:S(2)}) collective-permute-start(bf16[128,2048]{1,0:T(8,128)(2,1)} %pad_maximum_fusion.18), channel_id=1, source_target_pairs={{0,24},{8,0},{16,8},{24,16},{1,25},{9,1},{17,9},{25,17},{2,26},{10... | collective-permute-start | bytes 1572872 | tf_op jit(solution)/shard_map/ppermute | solution.py:865
  127.5 82.2 %collective-permute-start.15 = (bf16[128,2048]{1,0:T(8,128)(2,1)}, bf16[128,2048]{1,0:T(8,128)(2,1)}, u32[]{:S(2)}, u32[]{:S(2)}) collective-permute-start(bf16[128,2048]{1,0:T(8,128)(2,1)} %pad_maximum_fusion.18), channel_id=1, source_target_pairs={{0,16},{8,24},{16,0},{24,8},{1,17},{9,25},{17,1},{25,9},{2,18},{10... | collective-permute-start | bytes 1572872 | tf_op jit(solution)/shard_map/ppermute | solution.py:865
  128.2 82.6 %collective-permute-start.16 = (bf16[128,2048]{1,0:T(8,128)(2,1)}, bf16[128,2048]{1,0:T(8,128)(2,1)}, u32[]{:S(2)}, u32[]{:S(2)}) collective-permute-start(bf16[128,2048]{1,0:T(8,128)(2,1)} %pad_maximum_fusion.18), channel_id=1, source_target_pairs={{0,8},{8,16},{16,24},{24,0},{1,9},{9,17},{17,25},{25,1},{2,10},{10... | collective-permute-start | bytes 1572872 | tf_op jit(solution)/shard_map/ppermute | solution.py:865
  165.3 359.8 %all-gather.11.cloned.1.call-start = ((), (), s32[]{:S(2)}) async-start(), calls=%async_computation.13 | async-start | bytes 4718592 | tf_op jit(solution)/shard_map/all_gather | solution.py:798
  205.4 88.8 %collective-permute-start.5 = (bf16[256,768]{1,0:T(8,128)(2,1)}, bf16[256,768]{1,0:T(8,128)(2,1)}, u32[]{:S(2)}, u32[]{:S(2)}) collective-permute-start(bf16[256,768]{1,0:T(8,128)(2,1)} %get-tuple-element.143), channel_id=1, source_target_pairs={{8,16},{9,17},{10,18},{11,19},{12,20},{13,21},{14,22},{15,23}} | collective-permute-start | bytes 1179656 | tf_op jit(solution)/shard_map/ppermute | solution.py:896
  206.9 87.4 %collective-permute-start.8 = (bf16[256,768]{1,0:T(8,128)(2,1)}, bf16[256,768]{1,0:T(8,128)(2,1)}, u32[]{:S(2)}, u32[]{:S(2)}) collective-permute-start(bf16[256,768]{1,0:T(8,128)(2,1)} %get-tuple-element.144), channel_id=1, source_target_pairs={{8,16},{9,17},{10,18},{11,19},{12,20},{13,21},{14,22},{15,23}} | collective-permute-start | bytes 1179656 | tf_op jit(solution)/shard_map/ppermute | solution.py:896
  220.3 149.7 %collective-permute-start.17 = (bf16[4,128,2048]{2,1,0:T(8,128)(2,1)}, bf16[4,128,2048]{2,1,0:T(8,128)(2,1)}, u32[]{:S(2)}, u32[]{:S(2)}) collective-permute-start(bf16[4,128,2048]{2,1,0:T(8,128)(2,1)} %constant_dynamic-slice_fusion), channel_id=1, source_target_pairs={{0,2},{2,0},{1,3},{3,1},{4,6},{6,4},{5,7},{7,5},{8,10},{10,8},{9,1... | collective-permute-start | bytes 6291464 | tf_op jit(solution)/shard_map/ppermute | solution.py:41
  270.5 49.8 %collective-permute-start.18 = (bf16[2,2,512,128]{3,2,1,0:T(8,128)(2,1)}, bf16[2,2,512,128]{3,2,1,0:T(8,128)(2,1)}, u32[]{:S(2)}, u32[]{:S(2)}) collective-permute-start(bf16[2,2,512,128]{3,2,1,0:T(8,128)(2,1)} %pad_maximum_fusion.17), channel_id=1, source_target_pairs={{0,24},{1,25},{2,26},{3,27},{4,28},{5,29},{6,30},{7,31}} | collective-permute-start | bytes 1572872 | tf_op jit(solution)/shard_map/ppermute | solution.py:46
  420.0 218.7 %reduce-scatter.5.cloned.1.call-start = ((), (), s32[]{:S(2)}) async-start(), calls=%async_computation.14 | async-start | bytes 4718592 | tf_op jit(solution)/shard_map/reduce_scatter | solution.py:946
  552.0 291.2 %reduce-scatter.7.cloned.1.call-start = ((), (), s32[]{:S(2)}) async-start(), calls=%async_computation.15 | async-start | bytes 9437184 | tf_op jit(solution)/shard_map/reduce_scatter | solution.py:946
  638.6 305.4 %reduce-scatter.9.cloned.1.call-start = ((), (), s32[]{:S(2)}) async-start(), calls=%async_computation.16 | async-start | bytes 5898240 | tf_op jit(solution)/shard_map/reduce_scatter | solution.py:946
  731.9 123.8 %collective-permute-start.44 = (bf16[4,128,2048]{2,1,0:T(8,128)(2,1)}, bf16[4,128,2048]{2,1,0:T(8,128)(2,1)}, u32[]{:S(2)}, u32[]{:S(2)}) collective-permute-start(bf16[4,128,2048]{2,1,0:T(8,128)(2,1)} %fusion.34), channel_id=1, source_target_pairs={{0,2},{2,0},{1,3},{3,1},{4,6},{6,4},{5,7},{7,5},{8,10},{10,8},{9,1... | collective-permute-start | bytes 6291464 | tf_op jit(solution)/shard_map/ppermute | solution.py:41
  770.0 56.4 %collective-permute-start.43 = (bf16[256,768]{1,0:T(8,128)(2,1)}, bf16[256,768]{1,0:T(8,128)(2,1)}, u32[]{:S(2)}, u32[]{:S(2)}) collective-permute-start(bf16[256,768]{1,0:T(8,128)(2,1)} %get-tuple-element.134), channel_id=1, source_target_pairs={{8,0},{9,1},{10,2},{11,3},{12,4},{13,5},{14,6},{15,7}} | collective-permute-start | bytes 1179656 | tf_op jit(solution)/shard_map/ppermute | solution.py:896
  771.3 69.2 %collective-permute-start.40 = (bf16[256,768]{1,0:T(8,128)(2,1)}, bf16[256,768]{1,0:T(8,128)(2,1)}, u32[]{:S(2)}, u32[]{:S(2)}) collective-permute-start(bf16[256,768]{1,0:T(8,128)(2,1)} %get-tuple-element.133), channel_id=1, source_target_pairs={{8,0},{9,1},{10,2},{11,3},{12,4},{13,5},{14,6},{15,7}} | collective-permute-start | bytes 1179656 | tf_op jit(solution)/shard_map/ppermute | solution.py:896
  843.2 280.2 %reduce-scatter.11.cloned.1.call-start = ((), (), s32[]{:S(2)}) async-start(), calls=%async_computation.17 | async-start | bytes 6488064 | tf_op jit(solution)/shard_map/reduce_scatter | solution.py:946
  855.7 103.3 %collective-permute-start.29 = (bf16[2,256,2048]{2,1,0:T(8,128)(2,1)}, bf16[2,256,2048]{2,1,0:T(8,128)(2,1)}, u32[]{:S(2)}, u32[]{:S(2)}) collective-permute-start(bf16[2,256,2048]{2,1,0:T(8,128)(2,1)} %pad_maximum_fusion.8), channel_id=1, source_target_pairs={{0,1},{1,0},{2,3},{3,2},{4,5},{5,4},{6,7},{7,6},{8,9},{9,8},{10,11... | collective-permute-start | bytes 6291464 | tf_op jit(solution)/shard_map/ppermute | solution.py:41
  962.1 146.9 %collective-permute-start.30 = (bf16[256,2048]{1,0:T(8,128)(2,1)}, bf16[256,2048]{1,0:T(8,128)(2,1)}, u32[]{:S(2)}, u32[]{:S(2)}) collective-permute-start(bf16[256,2048]{1,0:T(8,128)(2,1)} %fusion.39), channel_id=1, source_target_pairs={{0,4},{4,0},{1,5},{5,1},{2,6},{6,2},{3,7},{7,3},{8,12},{12,8},{9,1... | collective-permute-start | bytes 3145736 | tf_op jit(solution)/shard_map/ppermute | solution.py:41
  967.8 81.0 %collective-permute-start.57 = (bf16[128,2048]{1,0:T(8,128)(2,1)S(1)}, bf16[128,2048]{1,0:T(8,128)(2,1)S(1)}, u32[]{:S(2)}, u32[]{:S(2)}) collective-permute-start(bf16[128,2048]{1,0:T(8,128)(2,1)S(1)} %get-tuple-element.123), channel_id=1, source_target_pairs={{0,16},{8,24},{16,0},{24,8},{1,17},{9,25},{17,1},{25,9},{2,18},{10... | collective-permute-start | bytes 1572872 | tf_op jit(solution)/shard_map/ppermute | solution.py:865
  968.6 80.2 %collective-permute-start.56 = (bf16[128,2048]{1,0:T(8,128)(2,1)S(1)}, bf16[128,2048]{1,0:T(8,128)(2,1)S(1)}, u32[]{:S(2)}, u32[]{:S(2)}) collective-permute-start(bf16[128,2048]{1,0:T(8,128)(2,1)S(1)} %get-tuple-element.121), channel_id=1, source_target_pairs={{0,8},{8,16},{16,24},{24,0},{1,9},{9,17},{17,25},{25,1},{2,10},{10... | collective-permute-start | bytes 1572872 | tf_op jit(solution)/shard_map/ppermute | solution.py:865
  974.6 85.9 %collective-permute-start.50 = (bf16[256,2048]{1,0:T(8,128)(2,1)}, bf16[256,2048]{1,0:T(8,128)(2,1)}, u32[]{:S(2)}, u32[]{:S(2)}) collective-permute-start(bf16[256,2048]{1,0:T(8,128)(2,1)} %fusion.45), channel_id=1, source_target_pairs={{0,4},{4,0},{1,5},{5,1},{2,6},{6,2},{3,7},{7,3},{8,12},{12,8},{9,1... | collective-permute-start | bytes 3145736 | tf_op jit(solution)/shard_map/ppermute | solution.py:41
  (175 other events, 3355.4 us)
Sparse Core Ops, SparseCore 0:
  26.1 97.6 all-gather.4
  126.5 131.4 all-gather.6
  260.2 175.8 all-gather.8
  438.0 87.0 all-gather.10
  552.1 86.4 reduce-scatter.4
  642.5 196.2 reduce-scatter.6
  843.3 100.6 reduce-scatter.8
  947.7 156.2 reduce-scatter.10

commit v7 on v6

--- a/solution.py
+++ b/solution.py
@@ -23,6 +23,8 @@
 QP = 2 * HEAD_DIM
 CONV_COLS = PART + BC
 SCAN_COLS = CONV_COLS + DT_PAD
+QUARTER = BC // 4
+SENT_COLS = PART + QUARTER + DT_PAD
 AT_Q = PART
 AT_K = AT_Q + QP
 AT_V = AT_K + HEAD_DIM
@@ -777,7 +779,9 @@
     packed_scan = jnp.concatenate(
         [
             heads_split(w_in[:, INNER : 2 * INNER], MAMBA_HEAD),
-            jnp.broadcast_to(w_in[None, :, 2 * INNER : 2 * INNER + BC], (4, rows, BC)),
+            jnp.swapaxes(
+                w_in[:, 2 * INNER : 2 * INNER + BC].reshape(rows, 4, QUARTER), 0, 1
+            ),
             jnp.pad(
                 heads_split(w_in[:, 2 * INNER + BC :], 1), ((0, 0), (0, 0), (0, DT_PAD - HEADS))
             ),
@@ -808,7 +812,7 @@
         w = w.reshape(2, 2, rows, nz, ny, ff_rows)
         return jnp.transpose(w, (2, 3, 0, 4, 1, 5)).reshape(rows, 4 * hidden_part)
 
-    full_scan = gathered(to_ranks(packed_scan).reshape(4 * rows, SCAN_COLS))
+    full_scan = gathered(to_ranks(packed_scan).reshape(4 * rows, SENT_COLS))
 
     tokens = 2 * span_all
     resident = inputs[0].astype(f32)
@@ -832,12 +836,32 @@
     full_rest = gathered(after(rest_mine, normed_rows, edges16))
     cotangent16 = jnp.concatenate(gather_tokens(out_grad[0]), 0)
 
-    scan_in = low_dot(normed_rows, full_scan).reshape(2, span_all, SCAN_COLS)
-    edge_rows = low_dot(edges16, full_scan).reshape(2, 1, 8, SCAN_COLS)
+    def beside(own, other, index):
+        return jnp.where(
+            index == 0,
+            jnp.concatenate([own, other], axis=-1),
+            jnp.concatenate([other, own], axis=-1),
+        )
+
     n = span_all // SPAN
+    sent_in = low_dot(normed_rows, full_scan).reshape(2, span_all, SENT_COLS)
+    sent_edge = low_dot(edges16, full_scan).reshape(2, 8, SENT_COLS)
+    quarter = jnp.concatenate(
+        [sent_edge[..., PART : PART + QUARTER], sent_in[..., PART : PART + QUARTER]], axis=1
+    ).astype(bf16)
+    half = beside(quarter, swap(quarter[::-1], "c"), ci)
+    every_bc = beside(half, swap(half, "x"), xi).astype(f32)
+    scan_in = jnp.concatenate(
+        [sent_in[..., :PART], every_bc[:, 8:], sent_in[..., PART + QUARTER :]], axis=-1
+    )
+    edge_rows = jnp.concatenate([sent_edge[..., :PART], every_bc[:, :8]], axis=-1)[:, None]
     before = jnp.concatenate(
-        [edge_rows, scan_in.reshape(2, n, SPAN, SCAN_COLS)[:, : n - 1, SPAN - 8 :]], axis=1
-    )[..., :CONV_COLS]
+        [
+            edge_rows,
+            scan_in.reshape(2, n, SPAN, SCAN_COLS)[:, : n - 1, SPAN - 8 :, :CONV_COLS],
+        ],
+        axis=1,
+    )
 
     def rank_channels(array):
         return jnp.concatenate(
@@ -989,7 +1013,10 @@
         steps,
         lift,
     )
-    state_grad = chained(first_grad, -1)
+    mixed_grad, step_grad, skip_grad = scan_backward(
+        mixed, steps, starts, prefix, state_in, suffix, value_grad, skip, lift
+    )
+    state_grad = chained(first_grad, -1, mixed_grad)
 
     query_grad, kv_grads = attend_backward(
         after(query16, first_grad),
@@ -1019,9 +1046,6 @@
         axis=-1,
     ).reshape(tokens, REST_COLS)
 
-    mixed_grad, step_grad, skip_grad = scan_backward(
-        mixed, steps, starts, prefix, state_in, suffix, value_grad, skip, lift
-    )
     scan_grad16, edge_grad, conv_grad, small_grad = finish_backward(
         scan_in,
         before,
@@ -1043,7 +1067,20 @@
     last_rows = scan_grad16[:, span_all - edge_count :, :CONV_COLS].astype(f32) + edge_back
     scan_grad16 = lax.dynamic_update_slice(
         scan_grad16, last_rows.astype(bf16), (0, span_all - edge_count, 0)
-    ).reshape(tokens, SCAN_COLS)
+    )
+    bc_grad = scan_grad16[..., PART:CONV_COLS].reshape(2, span_all, 2, 2 * QUARTER)
+    half_grad = lax.dynamic_index_in_dim(bc_grad, xi, 2, keepdims=False).astype(f32) + swap(
+        lax.dynamic_index_in_dim(bc_grad, 1 - xi, 2, keepdims=False), "x"
+    ).astype(f32)
+    half_grad = half_grad.reshape(2, span_all, 2, QUARTER)
+    leaving = lax.dynamic_index_in_dim(half_grad, 1 - ci, 2, keepdims=False)
+    quarter_grad = lax.dynamic_index_in_dim(half_grad, ci, 2, keepdims=False) + swap(
+        leaving[::-1].astype(bf16), "c"
+    ).astype(f32)
+    sent_grad16 = jnp.concatenate(
+        [scan_grad16[..., :PART], quarter_grad.astype(bf16), scan_grad16[..., CONV_COLS:]],
+        axis=-1,
+    ).reshape(tokens, SENT_COLS)
     if aligned:
         rows_owned = lax.dynamic_index_in_dim(both_y, zi, 0, keepdims=False)
         waiting = after(both_y.astype(bf16), state_grad)
@@ -1070,10 +1107,10 @@
     )
     rest_parts = to_ranks(rest_owned.reshape(4, rows, REST_COLS)).astype(f32)
     scan_owned = to_owners(
-        after(weight_grad(normed_rows, scan_grad16).astype(bf16), rest_owned)
-    )
-
-    normed_grad = back_dot(scan_grad16, full_scan) + back_dot(rest_grad16, full_rest)
+        after(weight_grad(normed_rows, sent_grad16).astype(bf16), rest_owned)
+    )
+
+    normed_grad = back_dot(sent_grad16, full_scan) + back_dot(rest_grad16, full_rest)
     normed_grad = restored(scatter_sequences(normed_grad.reshape(2, span_all, D)))
     resident_grad, norm_gain_grad = norm_back(normed_grad)
     input_grad = hidden_grad + resident_grad
@@ -1120,13 +1157,13 @@
         result_out,
         result_o,
     )
-    scan_parts = to_ranks(scan_owned.reshape(4, rows, SCAN_COLS)).astype(f32)
+    scan_parts = to_ranks(scan_owned.reshape(4, rows, SENT_COLS)).astype(f32)
     result_in = jnp.concatenate(
         [
             heads_join(rest_parts[..., :PART], MAMBA_HEAD),
             heads_join(scan_parts[..., :PART], MAMBA_HEAD),
-            jnp.sum(scan_parts[..., PART:CONV_COLS], axis=0),
-            heads_join(scan_parts[..., CONV_COLS : CONV_COLS + HEADS], 1),
+            jnp.swapaxes(scan_parts[..., PART : PART + QUARTER], 0, 1).reshape(rows, BC),
+            heads_join(scan_parts[..., PART + QUARTER : PART + QUARTER + HEADS], 1),
         ],
         axis=1,
     )

time: 1160 us -> 1140 us (0.983)
  waiting for transfers between devices: 501 us -> 442 us
  starting transfers between devices: 109 us -> 140 us
  local copies, waits for them, and re-layouts: 125 us -> 143 us
    ppermute x6, waiting for transfers between devices: 73.7 us -> 129 us  [turned(): lax.ppermute(array, 'z', [(i, (i + distance) % nz) for i in range(nz)])]
    ppermute x8, waiting for transfers between devices: 59.3 us -> 6.61 us  [shifted(): lax.ppermute(array, 'z', [(i - distance, i) for i in devices if i - dista...]
    all_gather x4, waiting for transfers between devices: 96.1 us -> 46.3 us  [gathered(): return lax.all_gather(array, SHARDS, axis=0, tiled=True)]
    ppermute x8, starting transfers between devices: 33 us -> 65.3 us  [shifted(): lax.ppermute(array, 'z', [(i - distance, i) for i in devices if i - dista...]
    ppermute x12, waiting for transfers between devices: 96.9 us -> 77.5 us  [chained(): lax.ppermute(leaving.astype(bf16), 'z', [(at, at + step)]).astype(f32)]
    ppermute x26 -> x30, waiting for transfers between devices: 132 us -> 145 us  [swap(): return lax.ppermute(array, axis, [(0, 1), (1, 0)])]
    unnamed x296 -> x351, local copies, waits for them, and re-layouts: 44.9 us -> 49.4 us
  transfers between devices with their start and end apart: 74 -> 78, of which waited for: 31 -> 30; matrix products, arithmetic and copies ran while one was open for 29% -> 30% of each run, Pallas kernels for 10% -> 10%
where the time goes in v7:
time: 1140 us; the launch traced here: 1130 us
  waiting for transfers between devices  442 us (39%)
  matrix products  145 us (13%)
  local copies, waits for them, and re-layouts  143 us (13%)
  starting transfers between devices  140 us (12%)
  other arithmetic  114 us (10%)
  Pallas kernels  113 us (10%)
  between operations  17.8 us (2%)
  blocking collectives  13 us (1%)
    ppermute x30, waiting for transfers between devices, swap(): return lax.ppermute(array, axis, [(0, 1), (1, 0)])  145 us
    ppermute x6, waiting for transfers between devices, turned(): lax.ppermute(array, 'z', [(i, (i + distance) % nz) for i in range(nz)])  129 us
    ppermute x12, waiting for transfers between devices, chained(): lax.ppermute(leaving.astype(bf16), 'z', [(at, at + step)]).astype(f32)  77.5 us
    ppermute x8, starting transfers between devices, shifted(): lax.ppermute(array, 'z', [(i - distance, i) for i in devices if i - dista...  65.3 us
    dot_general x6, matrix products, back_dot(): lax.dot_general(grad_rows, weight, (((1,), (1,)), ((), ())), preferred_el...  57.2 us
    unnamed x351, local copies, waits for them, and re-layouts  49.4 us
    all_gather x4, waiting for transfers between devices, gathered(): return lax.all_gather(array, SHARDS, axis=0, tiled=True)  46.3 us
    dot_general x7, matrix products, low_dot(): return jnp.dot(left, right, preferred_element_type=f32)  45.1 us
  transfers between devices with their start and end apart: 78, of which 30 were waited for; matrix products, arithmetic and copies ran while one was open for 30% of the time, Pallas kernels for 10%

profile of v7, /device:TPU:0, one launch (start us, length us, event | category | flops | bytes accessed | tf_op | source)
XLA Modules:
  0.0 1128.2 jit_solution(4314986831733056510)
XLA Ops:
  11.7 13.0 %all_to_all.30 = bf16[4,64,1024]{2,1,0:T(8,128)(2,1)} all-to-all(bf16[4,64,1024]{2,1,0:T(8,128)(2,1)S(1)} %fusion.61), channel_id=1, replica_groups=mesh['z'=4,'x'=2,'y'=2,'c'=2] {'x','c'}, dimensions={0} | all-to-all | bytes 1048576 | tf_op jit(solution)/shard_map/all_to_all | solution.py:757
  72.4 17.3 %collective-permute-done.29 = bf16[256,2048]{1,0:T(8,128)(2,1)} collective-permute-done((bf16[256,2048]{1,0:T(8,128)(2,1)S(1)}, bf16[256,2048]{1,0:T(8,128)(2,1)}, u32[]{:S(2)}, u32[]{:S(2)}) %collective-permute-start.29) | collective-permute-done | bytes 1048608 | tf_op jit(solution)/shard_map/ppermute | solution.py:43
  121.3 23.9 %collective-permute-done.16 = bf16[128,2048]{1,0:T(8,128)(2,1)} collective-permute-done((bf16[128,2048]{1,0:T(8,128)(2,1)S(1)}, bf16[128,2048]{1,0:T(8,128)(2,1)}, u32[]{:S(2)}, u32[]{:S(2)}) %collective-permute-start.16) | collective-permute-done | bytes 524320 | tf_op jit(solution)/shard_map/ppermute | solution.py:889
  146.3 45.5 %collective-permute-done.17 = bf16[128,2048]{1,0:T(8,128)(2,1)S(1)} collective-permute-done((bf16[128,2048]{1,0:T(8,128)(2,1)S(1)}, bf16[128,2048]{1,0:T(8,128)(2,1)S(1)}, u32[]{:S(2)}, u32[]{:S(2)}) %collective-permute-start.17) | collective-permute-done | bytes 524320 | tf_op jit(solution)/shard_map/ppermute | solution.py:889
  200.5 13.9 %shard_map.330 = (f32[2,512,1280]{2,1,0:T(8,128)}, f32[2,512,256]{2,1,0:T(8,128)S(1)}, f32[2,4,8,128]{3,2,1,0:T(8,128)S(1)}, f32[2,4,256,768]{3,2,1,0:T(8,128)}, f32[2,256,768]{2,1,0:T(8,128)S(1)}) custom-call(f32[2,512,1408]{2,1,0:T(8,128)} %copy-done.67, f32[2,4,8,1280]{3,2,1,0:T(8,128)S(1)} %pad_maximum_fusion.23.before, ...), custom_call_target="tpu_custom_call" | custom-call | flops 8000000000 | bytes 30000000 | tf_op jit(solution)/shard_map/pallas_call | solution.py:430
  266.1 51.4 %collective-permute-start.21 = (bf16[2,2,512,128]{3,2,1,0:T(8,128)(2,1)}, bf16[2,2,512,128]{3,2,1,0:T(8,128)(2,1)}, u32[]{:S(2)}, u32[]{:S(2)}) collective-permute-start(bf16[2,2,512,128]{3,2,1,0:T(8,128)(2,1)} %pad_maximum_fusion.19), channel_id=1, source_target_pairs={{0,16},{8,24},{1,17},{9,25},{2,18},{10,26},{3,19},{11,27},{4,20},{... | collective-permute-start | bytes 1572872 | tf_op jit(solution)/shard_map/ppermute | solution.py:48
  324.0 12.1 %shard_map.331 = (f32[2,512,768]{2,1,0:T(8,128)}, f32[2,512,768]{2,1,0:T(8,128)}, f32[2,512,128]{2,1,0:T(8,128)S(1)}) custom-call(f32[2,512,1280]{2,1,0:T(8,128)} %get-tuple-element.63.mixed.c_part, f32[2,512,256]{2,1,0:T(8,128)S(1)} %get-tuple-element.64.steps, f32[2,4,8,128]{3,2,1,0:T(8,128)S(1)} %get-tuple-element.65.starts, ...), custom_call_target="tpu_custom_call" | custom-call | flops 12000000000 | bytes 30000000 | tf_op jit(solution)/shard_map/pallas_call | solution.py:458
  341.1 11.1 collective-permute-done.13
  359.2 13.0 %shard_map.332 = (f32[2,512,256]{2,1,0:T(8,128)S(1)}, f32[2,512,256]{2,1,0:T(8,128)S(1)}) custom-call(bf16[2,512,256]{2,1,0:T(8,128)(2,1)S(1)} %convert_element_type.396.query, bf16[2,2048,128]{2,1,0:T(8,128)(2,1)S(1)} %get-tuple-element.132.key, bf16[2,2048,128]{2,1,0:T(8,128)(2,1)} %get-tuple-element.131.value, ...), custom_call_target="tpu_custom_call" | custom-call | flops 12000000000 | bytes 20000000 | tf_op jit(solution)/shard_map/pallas_call | solution.py:623
  397.6 24.2 %collective-permute-done.24 = bf16[256,2048]{1,0:T(8,128)(2,1)S(1)} collective-permute-done((bf16[256,2048]{1,0:T(8,128)(2,1)S(1)}, bf16[256,2048]{1,0:T(8,128)(2,1)S(1)}, u32[]{:S(2)}, u32[]{:S(2)}) %collective-permute-start.24) | collective-permute-done | bytes 1048608 | tf_op jit(solution)/shard_map/ppermute | solution.py:43
  436.8 23.6 %collective-permute-done.26 = bf16[256,2048]{1,0:T(8,128)(2,1)S(1)} collective-permute-done((bf16[256,2048]{1,0:T(8,128)(2,1)}, bf16[256,2048]{1,0:T(8,128)(2,1)S(1)}, u32[]{:S(2)}, u32[]{:S(2)}) %collective-permute-start.26) | collective-permute-done | bytes 1048608 | tf_op jit(solution)/shard_map/ppermute | solution.py:43
  464.1 12.6 %fusion.60 = f32[1024,2048]{1,0:T(8,128)S(1)} fusion(bf16[2048,2048]{1,0:T(8,128)(2,1)} %all-gather.9.cloned.1.call-done, bf16[256,2048]{1,0:T(8,128)(2,1)} %collective-permute-done.27, bf16[256,2048]{1,0:T(8,128)(2,1)} %copy-done.142, bf16[256,2048]{1,0:T(8,128)(2,1)} %collective-permute-done.25, bf16[256,2048]{1,0:T(8,128)(2,1)} %constant_dynamic-update-slice_fusion.10), kind=kOutput, calls=%fused_computation.173 | convolution fusion | flops 8606711808 | bytes 20971520 | tf_op jit(solution)/shard_map/dot_general | solution.py:67
  489.8 46.2 %all-gather.11.cloned.1.call-done = bf16[1024,2048]{1,0:T(8,128)(2,1)} async-done(((bf16[128,2048]{1,0:T(8,128)(2,1)}), bf16[1024,2048]{1,0:T(8,128)(2,1)}) %all-gather.11.cloned.1.call-update) | async-done | bytes 4194320 | tf_op jit(solution)/shard_map/all_gather | solution.py:802
  536.0 13.0 %fusion.4 = (bf16[1024,1024]{1,0:T(8,128)(2,1)S(1)}, bf16[1024,1024]{1,0:T(8,128)(2,1)}) fusion(f32[1024,2048]{1,0:T(8,128)} %copy-done.50, bf16[1024,2048]{1,0:T(8,128)(2,1)} %pad_maximum_fusion.3, bf16[1024,2048]{1,0:T(8,128)(2,1)} %all-gather.11.cloned.1.call-done), kind=kOutput, calls=%fused_computation.15 | convolution fusion | flops 4309647360 | bytes 20971520 | tf_op jit(solution)/shard_map/dot_general | solution.py:71
  549.1 14.6 %fusion.93 = (bf16[1024,2048]{1,0:T(8,128)(2,1)S(1)}, f32[1024,2048]{1,0:T(8,128)}) fusion(bf16[2048,2048]{1,0:T(8,128)(2,1)} %all-gather.9.cloned.1.call-done, bf16[1024,1024]{1,0:T(8,128)(2,1)} %get-tuple-element.118, bf16[1024,1024]{1,0:T(8,128)(2,1)S(1)} %get-tuple-element.117), kind=kOutput, calls=%fused_computation.354 | convolution fusion | flops 8600420352 | bytes 25165824 | tf_op jit(solution)/shard_map/dot_general | solution.py:71
  574.6 13.5 %convolution_convert_fusion = bf16[2048,2048]{1,0:T(8,128)(2,1)} fusion(bf16[1024,1024]{1,0:T(8,128)(2,1)} %get-tuple-element.118, bf16[1024,1024]{1,0:T(8,128)(2,1)S(1)} %copy-done.146, bf16[256,2048]{1,0:T(8,128)(2,1)} %collective-permute-done.27, bf16[256,2048]{1,0:T(8,128)(2,1)S(1)} %copy-done.143, bf16[256,2048]{1,0:T(8,128)(2,1)} %collective-permute-done.25, ...), kind=kOutput, calls=%fused_computation.2 | convolution fusion | flops 8619294720 | bytes 16777216 | tf_op jit(solution)/shard_map/dot_general | solution.py:75
  605.9 23.1 %collective-permute-done.35 = bf16[256,2048]{1,0:T(8,128)(2,1)S(1)} collective-permute-done((bf16[256,2048]{1,0:T(8,128)(2,1)S(1)}, bf16[256,2048]{1,0:T(8,128)(2,1)S(1)}, u32[]{:S(2)}, u32[]{:S(2)}) %collective-permute-start.35) | collective-permute-done | bytes 1048608 | tf_op jit(solution)/shard_map/ppermute | solution.py:43
  638.0 14.0 %reduce-scatter.5.cloned.1.call-done = bf16[128,2048]{1,0:T(8,128)(2,1)} async-done(((bf16[1024,2048]{1,0:T(8,128)(2,1)}), bf16[128,2048]{1,0:T(8,128)(2,1)}) %reduce-scatter.5.cloned.1.call-update) | async-done | bytes 524304 | tf_op jit(solution)/shard_map/reduce_scatter | solution.py:970
  689.1 11.5 %shard_map.333 = (f32[2,512,768]{2,1,0:T(8,128)}, bf16[2,512,768]{2,1,0:T(8,128)(2,1)S(1)}, f32[8,768]{1,0:T(8,128)S(1)}, f32[2,4,256,768]{3,2,1,0:T(8,128)}, f32[2,256,768]{2,1,0:T(8,128)}) custom-call(f32[2,512,768]{2,1,0:T(8,128)} %get-tuple-element.81.gated_grad, f32[2,512,768]{2,1,0:T(8,128)} %get-tuple-element.82.values, f32[2,512,1280]{2,1,0:T(8,128)} %copy-done.108, ...), custom_call_target="tpu_custom_call" | custom-call | flops 8000000000 | bytes 30000000 | tf_op jit(solution)/shard_map/pallas_call | solution.py:485
  705.9 18.8 %shard_map.336 = (f32[2,512,256]{2,1,0:T(8,128)S(1)}, f32[2,2,2048,128]{3,2,1,0:T(8,128)}) custom-call(bf16[2,512,256]{2,1,0:T(8,128)(2,1)S(1)} %copy-done.11, bf16[2,2048,128]{2,1,0:T(8,128)(2,1)S(1)} %copy-done.9, bf16[2,2048,128]{2,1,0:T(8,128)(2,1)} %get-tuple-element.131.value, bf16[2,512,256]{2,1,0:T(8,128)(2,1)S(1)} %bitcast.322, ...), custom_call_target="tpu_custom_call" | custom-call | flops 20000000000 | bytes 30000000 | tf_op jit(solution)/shard_map/pallas_call | solution.py:642
  737.3 21.9 %shard_map.334 = (f32[2,512,1280]{2,1,0:T(8,128)}, f32[2,512,256]{2,1,0:T(8,128)S(1)}, f32[8,128]{1,0:T(8,128)S(1)}) custom-call(f32[2,512,1280]{2,1,0:T(8,128)} %get-tuple-element.63.mixed.c_part, f32[2,512,256]{2,1,0:T(8,128)S(1)} %copy-done.5, f32[2,4,8,128]{3,2,1,0:T(8,128)S(1)} %copy-done.27, f32[2,4,256,768]{3,2,1,0:T(8,128)} %get-tuple-element.66.prefix, ...), custom_call_target="tpu_custom_call" | custom-call | flops 30000001024 | bytes 40000000 | tf_op jit(solution)/shard_map/pallas_call | solution.py:515
  792.6 54.2 %collective-permute-done.45 = bf16[256,768]{1,0:T(8,128)(2,1)S(1)} collective-permute-done((bf16[256,768]{1,0:T(8,128)(2,1)}, bf16[256,768]{1,0:T(8,128)(2,1)S(1)}, u32[]{:S(2)}, u32[]{:S(2)}) %collective-permute-start.45) | collective-permute-done | bytes 393248 | tf_op jit(solution)/shard_map/ppermute | solution.py:920
  863.8 21.7 %shard_map.335 = (bf16[2,512,1408]{2,1,0:T(8,128)(2,1)}, f32[2,8,1280]{2,1,0:T(8,128)S(1)}, f32[8,1280]{1,0:T(8,128)S(1)}, f32[8,128]{1,0:T(8,128)S(1)}) custom-call(f32[2,512,1408]{2,1,0:T(8,128)} %copy-done.67, f32[2,4,8,1280]{3,2,1,0:T(8,128)S(1)} %copy-done.13, f32[2,512,1280]{2,1,0:T(8,128)} %get-tuple-element.63.mixed.c_part, ...), custom_call_target="tpu_custom_call" | custom-call | flops 15000000512 | bytes 50000000 | tf_op jit(solution)/shard_map/pallas_call | solution.py:546
  974.5 59.9 %collective-permute-done.61 = bf16[128,2048]{1,0:T(8,128)(2,1)} collective-permute-done((bf16[128,2048]{1,0:T(8,128)(2,1)}, bf16[128,2048]{1,0:T(8,128)(2,1)}, u32[]{:S(2)}, u32[]{:S(2)}) %collective-permute-start.61) | collective-permute-done | bytes 524320 | tf_op jit(solution)/shard_map/ppermute | solution.py:889
  (808 shorter events, 536.3 us)
Async XLA Ops:
  7.2 95.5 %all-gather.5.cloned.1.call-start = ((), (), s32[]{:S(2)}) async-start(), calls=%async_computation.10 | async-start | bytes 4718592 | tf_op jit(solution)/shard_map/all_gather | solution.py:802
  67.1 175.1 %all-to-all-start.2 = ((bf16[4,64,2048]{2,1,0:T(8,128)(2,1)}), bf16[4,64,2048]{2,1,0:T(8,128)(2,1)}, u32[]{:S(2)}, u32[]{:S(2)}) async-start(bf16[4,64,2048]{2,1,0:T(8,128)(2,1)} %pad_maximum_fusion.15), calls=%async_computation.2 | async-start | bytes 2097152 | tf_op jit(solution)/shard_map/all_to_all | solution.py:757
  71.4 173.8 %all-gather.7.cloned.1.call-start = ((), (), s32[]{:S(2)}) async-start(), calls=%async_computation.11 | async-start | bytes 5898240 | tf_op jit(solution)/shard_map/all_gather | solution.py:802
  72.1 392.0 %all-gather.9.cloned.1.call-start = ((), (), s32[]{:S(2)}) async-start(), calls=%async_computation.12 | async-start | bytes 9437184 | tf_op jit(solution)/shard_map/all_gather | solution.py:802
  117.7 74.1 %collective-permute-start.17 = (bf16[128,2048]{1,0:T(8,128)(2,1)S(1)}, bf16[128,2048]{1,0:T(8,128)(2,1)S(1)}, u32[]{:S(2)}, u32[]{:S(2)}) collective-permute-start(bf16[128,2048]{1,0:T(8,128)(2,1)S(1)} %pad_maximum_fusion.20), channel_id=1, source_target_pairs={{0,16},{8,24},{16,0},{24,8},{1,17},{9,25},{17,1},{25,9},{2,18},{10... | collective-permute-start | bytes 1572872 | tf_op jit(solution)/shard_map/ppermute | solution.py:889
  119.1 72.7 %collective-permute-start.18 = (bf16[128,2048]{1,0:T(8,128)(2,1)S(1)}, bf16[128,2048]{1,0:T(8,128)(2,1)S(1)}, u32[]{:S(2)}, u32[]{:S(2)}) collective-permute-start(bf16[128,2048]{1,0:T(8,128)(2,1)S(1)} %pad_maximum_fusion.20), channel_id=1, source_target_pairs={{0,8},{8,16},{16,24},{24,0},{1,9},{9,17},{17,25},{25,1},{2,10},{10... | collective-permute-start | bytes 1572872 | tf_op jit(solution)/shard_map/ppermute | solution.py:889
  120.9 74.2 %collective-permute-start.5 = (bf16[2,520,256]{2,1,0:T(8,128)(2,1)S(1)}, bf16[2,520,256]{2,1,0:T(8,128)(2,1)S(1)}, u32[]{:S(2)}, u32[]{:S(2)}) collective-permute-start(bf16[2,520,256]{2,1,0:T(8,128)(2,1)S(1)} %maximum_select_fusion.2), channel_id=1, source_target_pairs={{0,4},{4,0},{1,5},{5,1},{2,6},{6,2},{3,7},{7,3},{8,12},{12,8},{9,1... | collective-permute-start | bytes 1597448 | tf_op jit(solution)/shard_map/ppermute | solution.py:43
  242.3 293.8 %all-gather.11.cloned.1.call-start = ((), (), s32[]{:S(2)}) async-start(), calls=%async_computation.13 | async-start | bytes 4718592 | tf_op jit(solution)/shard_map/all_gather | solution.py:802
  255.5 63.7 %collective-permute-start.11 = (bf16[256,768]{1,0:T(8,128)(2,1)}, bf16[256,768]{1,0:T(8,128)(2,1)}, u32[]{:S(2)}, u32[]{:S(2)}) collective-permute-start(bf16[256,768]{1,0:T(8,128)(2,1)} %get-tuple-element.69), channel_id=1, source_target_pairs={{16,24},{17,25},{18,26},{19,27},{20,28},{21,29},{22,30},{23,31}} | collective-permute-start | bytes 1179656 | tf_op jit(solution)/shard_map/ppermute | solution.py:920
  262.4 109.9 %collective-permute-start.19 = (bf16[4,128,2048]{2,1,0:T(8,128)(2,1)}, bf16[4,128,2048]{2,1,0:T(8,128)(2,1)}, u32[]{:S(2)}, u32[]{:S(2)}) collective-permute-start(bf16[4,128,2048]{2,1,0:T(8,128)(2,1)} %constant_dynamic-slice_fusion.4), channel_id=1, source_target_pairs={{0,2},{2,0},{1,3},{3,1},{4,6},{6,4},{5,7},{7,5},{8,10},{10,8},{9,1... | collective-permute-start | bytes 6291464 | tf_op jit(solution)/shard_map/ppermute | solution.py:43
  263.9 92.1 %collective-permute-start.20 = (bf16[2,2,512,128]{3,2,1,0:T(8,128)(2,1)}, bf16[2,2,512,128]{3,2,1,0:T(8,128)(2,1)}, u32[]{:S(2)}, u32[]{:S(2)}) collective-permute-start(bf16[2,2,512,128]{3,2,1,0:T(8,128)(2,1)} %pad_maximum_fusion.19), channel_id=1, source_target_pairs={{0,24},{1,25},{2,26},{3,27},{4,28},{5,29},{6,30},{7,31}} | collective-permute-start | bytes 1572872 | tf_op jit(solution)/shard_map/ppermute | solution.py:48
  266.1 90.0 %collective-permute-start.21 = (bf16[2,2,512,128]{3,2,1,0:T(8,128)(2,1)}, bf16[2,2,512,128]{3,2,1,0:T(8,128)(2,1)}, u32[]{:S(2)}, u32[]{:S(2)}) collective-permute-start(bf16[2,2,512,128]{3,2,1,0:T(8,128)(2,1)} %pad_maximum_fusion.19), channel_id=1, source_target_pairs={{0,16},{8,24},{1,17},{9,25},{2,18},{10,26},{3,19},{11,27},{4,20},{... | collective-permute-start | bytes 1572872 | tf_op jit(solution)/shard_map/ppermute | solution.py:48
  428.3 223.7 %reduce-scatter.5.cloned.1.call-start = ((), (), s32[]{:S(2)}) async-start(), calls=%async_computation.14 | async-start | bytes 4718592 | tf_op jit(solution)/shard_map/reduce_scatter | solution.py:970
  565.4 292.1 %reduce-scatter.7.cloned.1.call-start = ((), (), s32[]{:S(2)}) async-start(), calls=%async_computation.15 | async-start | bytes 9437184 | tf_op jit(solution)/shard_map/reduce_scatter | solution.py:970
  652.0 316.2 %reduce-scatter.9.cloned.1.call-start = ((), (), s32[]{:S(2)}) async-start(), calls=%async_computation.16 | async-start | bytes 5898240 | tf_op jit(solution)/shard_map/reduce_scatter | solution.py:970
  704.5 63.2 %collective-permute-start.43 = (bf16[256,768]{1,0:T(8,128)(2,1)}, bf16[256,768]{1,0:T(8,128)(2,1)}, u32[]{:S(2)}, u32[]{:S(2)}) collective-permute-start(bf16[256,768]{1,0:T(8,128)(2,1)} %get-tuple-element.140), channel_id=1, source_target_pairs={{24,16},{25,17},{26,18},{27,19},{28,20},{29,21},{30,22},{31,23}} | collective-permute-start | bytes 1179656 | tf_op jit(solution)/shard_map/ppermute | solution.py:920
  766.1 91.5 %collective-permute-start.46 = (bf16[4,128,2048]{2,1,0:T(8,128)(2,1)}, bf16[4,128,2048]{2,1,0:T(8,128)(2,1)}, u32[]{:S(2)}, u32[]{:S(2)}) collective-permute-start(bf16[4,128,2048]{2,1,0:T(8,128)(2,1)} %fusion.33), channel_id=1, source_target_pairs={{0,2},{2,0},{1,3},{3,1},{4,6},{6,4},{5,7},{7,5},{8,10},{10,8},{9,1... | collective-permute-start | bytes 6291464 | tf_op jit(solution)/shard_map/ppermute | solution.py:43
  782.5 64.4 %collective-permute-start.45 = (bf16[256,768]{1,0:T(8,128)(2,1)}, bf16[256,768]{1,0:T(8,128)(2,1)S(1)}, u32[]{:S(2)}, u32[]{:S(2)}) collective-permute-start(bf16[256,768]{1,0:T(8,128)(2,1)} %get-tuple-element.88), channel_id=1, source_target_pairs={{8,0},{9,1},{10,2},{11,3},{12,4},{13,5},{14,6},{15,7}} | collective-permute-start | bytes 1179656 | tf_op jit(solution)/shard_map/ppermute | solution.py:920
  783.8 71.1 %collective-permute-start.42 = (bf16[256,768]{1,0:T(8,128)(2,1)}, bf16[256,768]{1,0:T(8,128)(2,1)}, u32[]{:S(2)}, u32[]{:S(2)}) collective-permute-start(bf16[256,768]{1,0:T(8,128)(2,1)} %get-tuple-element.87), channel_id=1, source_target_pairs={{8,0},{9,1},{10,2},{11,3},{12,4},{13,5},{14,6},{15,7}} | collective-permute-start | bytes 1179656 | tf_op jit(solution)/shard_map/ppermute | solution.py:920
  857.6 246.4 %reduce-scatter.11.cloned.1.call-start = ((), (), s32[]{:S(2)}) async-start(), calls=%async_computation.17 | async-start | bytes 4718592 | tf_op jit(solution)/shard_map/reduce_scatter | solution.py:970
  951.4 138.2 %collective-permute-start.32 = (bf16[256,2048]{1,0:T(8,128)(2,1)}, bf16[256,2048]{1,0:T(8,128)(2,1)}, u32[]{:S(2)}, u32[]{:S(2)}) collective-permute-start(bf16[256,2048]{1,0:T(8,128)(2,1)} %fusion.38), channel_id=1, source_target_pairs={{0,4},{4,0},{1,5},{5,1},{2,6},{6,2},{3,7},{7,3},{8,12},{12,8},{9,1... | collective-permute-start | bytes 3145736 | tf_op jit(solution)/shard_map/ppermute | solution.py:43
  955.9 78.4 %collective-permute-start.61 = (bf16[128,2048]{1,0:T(8,128)(2,1)}, bf16[128,2048]{1,0:T(8,128)(2,1)}, u32[]{:S(2)}, u32[]{:S(2)}) collective-permute-start(bf16[128,2048]{1,0:T(8,128)(2,1)} %get-tuple-element.125), channel_id=1, source_target_pairs={{0,16},{8,24},{16,0},{24,8},{1,17},{9,25},{17,1},{25,9},{2,18},{10... | collective-permute-start | bytes 1572872 | tf_op jit(solution)/shard_map/ppermute | solution.py:889
  959.7 74.7 %collective-permute-start.60 = (bf16[128,2048]{1,0:T(8,128)(2,1)}, bf16[128,2048]{1,0:T(8,128)(2,1)}, u32[]{:S(2)}, u32[]{:S(2)}) collective-permute-start(bf16[128,2048]{1,0:T(8,128)(2,1)} %get-tuple-element.123), channel_id=1, source_target_pairs={{0,8},{8,16},{16,24},{24,0},{1,9},{9,17},{17,25},{25,1},{2,10},{10... | collective-permute-start | bytes 1572872 | tf_op jit(solution)/shard_map/ppermute | solution.py:889
  973.9 72.5 %collective-permute-start.54 = (bf16[256,2048]{1,0:T(8,128)(2,1)S(1)}, bf16[256,2048]{1,0:T(8,128)(2,1)}, u32[]{:S(2)}, u32[]{:S(2)}) collective-permute-start(bf16[256,2048]{1,0:T(8,128)(2,1)S(1)} %fusion.44), channel_id=1, source_target_pairs={{0,4},{4,0},{1,5},{5,1},{2,6},{6,2},{3,7},{7,3},{8,12},{12,8},{9,1... | collective-permute-start | bytes 3145736 | tf_op jit(solution)/shard_map/ppermute | solution.py:43
  (208 other events, 4784.2 us)
Sparse Core Ops, SparseCore 0:
  24.8 76.9 all-gather.4
  104.6 119.4 all-gather.6
  242.4 172.7 all-gather.8
  428.4 107.5 all-gather.10
  565.5 86.4 reduce-scatter.4
  655.9 188.4 reduce-scatter.6
  857.6 100.6 reduce-scatter.8
  968.4 115.4 reduce-scatter.10

commit v8 on v7

--- a/solution.py
+++ b/solution.py
@@ -834,8 +834,6 @@
         sent_o = lax.ppermute(w_o, ("z", "y", "c"), place)
         sent_rows = jnp.concatenate([sent_out, sent_o], 0)
     full_rest = gathered(after(rest_mine, normed_rows, edges16))
-    cotangent16 = jnp.concatenate(gather_tokens(out_grad[0]), 0)
-
     def beside(own, other, index):
         return jnp.where(
             index == 0,
@@ -884,6 +882,8 @@
     )
     log_decay = starts[:, n - 1, 0] + steps[:, span_all - 1, DT_PAD:]
     own_decay = jnp.repeat(jnp.exp(log_decay[:, :HEADS]), MAMBA_HEAD, axis=-1)
+
+    cotangent16 = jnp.concatenate(gather_tokens(after(out_grad[0], mixed)), 0)
 
     def turned(array, distance):
         return lax.ppermute(array, "z", [(i, (i + distance) % nz) for i in range(nz)])
@@ -943,14 +943,14 @@
     values, flat, square = scan_values(
         mixed, steps, starts, prefix, state_in, rest, 0, skip, lift
     )
-    kv_all = jnp.concatenate(list(after(tuple(kv_before), flat)) + [kv16], axis=2)
+    kv_all = jnp.concatenate(list(after(tuple(kv_before), flat, cotangent16)) + [kv16], axis=2)
     attended, log_sum = attend(query16, kv_all[0], kv_all[1], query_place, key_place)
     attended16 = attended.reshape(tokens, QP).astype(bf16)
 
     root = lax.rsqrt(group_total(square[..., :1]) / INNER + epsilon)
     gated16 = (flat * root * gain).astype(bf16).reshape(tokens, PART)
     full_ff = gathered(
-        after(to_ranks(packed_ff).reshape(4 * rows, 2 * hidden_part), mixed, cotangent16)
+        after(to_ranks(packed_ff).reshape(4 * rows, 2 * hidden_part), mixed)
     )
     mixture = low_dot(gated16, full_out) + low_dot(attended16, full_o)
     hidden_state = resident + scatter_sequences(mixture.reshape(2, span_all, D))
@@ -1082,14 +1082,11 @@
         axis=-1,
     ).reshape(tokens, SENT_COLS)
     if aligned:
-        rows_owned = lax.dynamic_index_in_dim(both_y, zi, 0, keepdims=False)
         waiting = after(both_y.astype(bf16), state_grad)
-        for d in range(1, nz):
-            leaving = lax.dynamic_index_in_dim(waiting, (zi + d) % nz, 0, keepdims=False)
-            rows_owned = rows_owned + turned(leaving, d).astype(f32)
-        rows_owned = rows_owned.astype(bf16)
-        result_out = lax.ppermute(rows_owned[:out_rows], ("y", "c"), turn).astype(f32)
-        result_o = lax.ppermute(rows_owned[out_rows:], ("z", "y", "c"), back_place).astype(f32)
+        arriving = tuple(
+            turned(lax.dynamic_index_in_dim(waiting, (zi + d) % nz, 0, keepdims=False), d)
+            for d in range(1, nz)
+        )
     else:
         every_out = lax.dynamic_update_slice_in_dim(
             jnp.zeros((INNER, D), bf16), grad_out_w, (2 * xi + ci) * PART, 0
@@ -1111,8 +1108,8 @@
     )
 
     normed_grad = back_dot(sent_grad16, full_scan) + back_dot(rest_grad16, full_rest)
-    normed_grad = restored(scatter_sequences(normed_grad.reshape(2, span_all, D)))
-    resident_grad, norm_gain_grad = norm_back(normed_grad)
+    normed_grad = scatter_sequences(normed_grad.reshape(2, span_all, D))
+    resident_grad, norm_gain_grad = norm_back(restored(after(normed_grad, rest_parts)))
     input_grad = hidden_grad + resident_grad
 
     result_q = jnp.transpose(
@@ -1137,7 +1134,16 @@
         heads_spread(gain_grad[0], MAMBA_HEAD),
         mid_gain_grad,
     ]
-    summed = total(jnp.concatenate([v.reshape(-1) for v in small]))
+    summed = total(
+        after(jnp.concatenate([v.reshape(-1) for v in small]), input_grad, output)
+    )
+    if aligned:
+        rows_owned = lax.dynamic_index_in_dim(both_y, zi, 0, keepdims=False)
+        for part in after(arriving, summed):
+            rows_owned = rows_owned + part.astype(f32)
+        rows_owned = rows_owned.astype(bf16)
+        result_out = lax.ppermute(rows_owned[:out_rows], ("y", "c"), turn).astype(f32)
+        result_o = lax.ppermute(rows_owned[out_rows:], ("z", "y", "c"), back_place).astype(f32)
     parts, at = [], 0
     for v in small:
         parts.append(summed[at : at + v.size].reshape(v.shape))

time: 1140 us -> 1180 us (1.035)
  waiting for transfers between devices: 442 us -> 484 us
    ppermute x6, waiting for transfers between devices: 129 us -> 65.6 us  [turned(): lax.ppermute(array, 'z', [(i, (i + distance) % nz) for i in range(nz)])]
    ppermute x5, waiting for transfers between devices: 12.7 us -> 41.4 us  [total(): lax.ppermute(array, axis, [(i, i ^ bit) for i in range(size)])]
    all_to_all x5, waiting for transfers between devices: 10.1 us -> 37.2 us  [to_ranks(): return lax.all_to_all(array, GROUP, 0, 0, tiled=True)]
    all_gather x4, waiting for transfers between devices: 46.3 us -> 65.4 us  [gathered(): return lax.all_gather(array, SHARDS, axis=0, tiled=True)]
    ppermute x8, waiting for transfers between devices: 6.61 us -> 19.9 us  [shifted(): lax.ppermute(array, 'z', [(i - distance, i) for i in devices if i - dista...]
    unnamed x351 -> x344, local copies, waits for them, and re-layouts: 49.4 us -> 55.8 us
  transfers between devices with their start and end apart: 78 -> 78, of which waited for: 30 -> 31; matrix products, arithmetic and copies ran while one was open for 30% -> 28% of each run, Pallas kernels for 10% -> 10%
where the time goes in v8:
time: 1180 us; the launch traced here: 1170 us
  waiting for transfers between devices  484 us (41%)
  matrix products  146 us (12%)
  starting transfers between devices  144 us (12%)
  local copies, waits for them, and re-layouts  139 us (12%)
  Pallas kernels  113 us (10%)
  other arithmetic  110 us (9%)
  between operations  17.9 us (2%)
  blocking collectives  13 us (1%)
    ppermute x30, waiting for transfers between devices, swap(): return lax.ppermute(array, axis, [(0, 1), (1, 0)])  155 us
    ppermute x12, waiting for transfers between devices, chained(): lax.ppermute(leaving.astype(bf16), 'z', [(at, at + step)]).astype(f32)  86.2 us
    ppermute x6, waiting for transfers between devices, turned(): lax.ppermute(array, 'z', [(i, (i + distance) % nz) for i in range(nz)])  65.6 us
    all_gather x4, waiting for transfers between devices, gathered(): return lax.all_gather(array, SHARDS, axis=0, tiled=True)  65.4 us
    dot_general x6, matrix products, back_dot(): lax.dot_general(grad_rows, weight, (((1,), (1,)), ((), ())), preferred_el...  57.5 us
    ppermute x8, starting transfers between devices, shifted(): lax.ppermute(array, 'z', [(i - distance, i) for i in devices if i - dista...  57.4 us
    unnamed x344, local copies, waits for them, and re-layouts  55.8 us
    dot_general x7, matrix products, low_dot(): return jnp.dot(left, right, preferred_element_type=f32)  50.1 us
  transfers between devices with their start and end apart: 78, of which 31 were waited for; matrix products, arithmetic and copies ran while one was open for 28% of the time, Pallas kernels for 10%

profile of v8, /device:TPU:0, one launch (start us, length us, event | category | flops | bytes accessed | tf_op | source)
XLA Modules:
  0.0 1166.1 jit_solution(7964982766384550124)
XLA Ops:
  11.7 13.0 %all_to_all.30 = bf16[4,64,1024]{2,1,0:T(8,128)(2,1)} all-to-all(bf16[4,64,1024]{2,1,0:T(8,128)(2,1)S(1)} %fusion.61), channel_id=1, replica_groups=mesh['z'=4,'x'=2,'y'=2,'c'=2] {'x','c'}, dimensions={0} | all-to-all | bytes 1048576 | tf_op jit(solution)/shard_map/all_to_all | solution.py:757
  47.8 12.8 %collective-permute-done = bf16[256,2048]{1,0:T(8,128)(2,1)} collective-permute-done((bf16[256,2048]{1,0:T(8,128)(2,1)}, bf16[256,2048]{1,0:T(8,128)(2,1)}, u32[]{:S(2)}, u32[]{:S(2)}) %collective-permute-start) | collective-permute-done | bytes 1048608 | tf_op jit(solution)/shard_map/ppermute | solution.py:43
  85.5 16.2 %all-gather.5.cloned.1.call-done = bf16[2048,1024]{1,0:T(8,128)(2,1)} async-done(((bf16[256,1024]{1,0:T(8,128)(2,1)}), bf16[2048,1024]{1,0:T(8,128)(2,1)}) %all-gather.5.cloned.1.call-update) | async-done | bytes 4194320 | tf_op jit(solution)/shard_map/all_gather | solution.py:802
  118.8 20.5 %collective-permute-done.16 = bf16[128,2048]{1,0:T(8,128)(2,1)S(1)} collective-permute-done((bf16[128,2048]{1,0:T(8,128)(2,1)S(1)}, bf16[128,2048]{1,0:T(8,128)(2,1)S(1)}, u32[]{:S(2)}, u32[]{:S(2)}) %collective-permute-start.16) | collective-permute-done | bytes 524320 | tf_op jit(solution)/shard_map/ppermute | solution.py:889
  139.3 45.1 %collective-permute-done.17 = bf16[128,2048]{1,0:T(8,128)(2,1)S(1)} collective-permute-done((bf16[128,2048]{1,0:T(8,128)(2,1)S(1)}, bf16[128,2048]{1,0:T(8,128)(2,1)S(1)}, u32[]{:S(2)}, u32[]{:S(2)}) %collective-permute-start.17) | collective-permute-done | bytes 524320 | tf_op jit(solution)/shard_map/ppermute | solution.py:889
  195.5 13.9 %shard_map.330 = (f32[2,512,1280]{2,1,0:T(8,128)}, f32[2,512,256]{2,1,0:T(8,128)S(1)}, f32[2,4,8,128]{3,2,1,0:T(8,128)S(1)}, f32[2,4,256,768]{3,2,1,0:T(8,128)}, f32[2,256,768]{2,1,0:T(8,128)S(1)}) custom-call(f32[2,512,1408]{2,1,0:T(8,128)} %copy-done.61, f32[2,4,8,1280]{3,2,1,0:T(8,128)S(1)} %pad_maximum_fusion.22.before, ...), custom_call_target="tpu_custom_call" | custom-call | flops 8000000000 | bytes 30000000 | tf_op jit(solution)/shard_map/pallas_call | solution.py:430
  237.8 13.4 %collective-permute-done.9 = bf16[256,768]{1,0:T(8,128)(2,1)} collective-permute-done((bf16[256,768]{1,0:T(8,128)(2,1)}, bf16[256,768]{1,0:T(8,128)(2,1)}, u32[]{:S(2)}, u32[]{:S(2)}) %collective-permute-start.9) | collective-permute-done | bytes 393248 | tf_op jit(solution)/shard_map/ppermute | solution.py:920
  287.1 41.2 %collective-permute-start.21 = (bf16[2,2,512,128]{3,2,1,0:T(8,128)(2,1)}, bf16[2,2,512,128]{3,2,1,0:T(8,128)(2,1)}, u32[]{:S(2)}, u32[]{:S(2)}) collective-permute-start(bf16[2,2,512,128]{3,2,1,0:T(8,128)(2,1)} %pad_maximum_fusion.18), channel_id=1, source_target_pairs={{0,16},{8,24},{1,17},{9,25},{2,18},{10,26},{3,19},{11,27},{4,20},{... | collective-permute-start | bytes 1572872 | tf_op jit(solution)/shard_map/ppermute | solution.py:48
  331.1 12.3 %shard_map.331 = (f32[2,512,768]{2,1,0:T(8,128)}, f32[2,512,768]{2,1,0:T(8,128)}, f32[2,512,128]{2,1,0:T(8,128)S(1)}) custom-call(f32[2,512,1280]{2,1,0:T(8,128)} %get-tuple-element.69.mixed.c_part, f32[2,512,256]{2,1,0:T(8,128)S(1)} %get-tuple-element.70.steps, f32[2,4,8,128]{3,2,1,0:T(8,128)S(1)} %get-tuple-element.71.starts, ...), custom_call_target="tpu_custom_call" | custom-call | flops 12000000000 | bytes 30000000 | tf_op jit(solution)/shard_map/pallas_call | solution.py:458
  390.0 12.6 %shard_map.332 = (f32[2,512,256]{2,1,0:T(8,128)S(1)}, f32[2,512,256]{2,1,0:T(8,128)S(1)}) custom-call(bf16[2,512,256]{2,1,0:T(8,128)(2,1)S(1)} %convert_element_type.396.query, bf16[2,2048,128]{2,1,0:T(8,128)(2,1)S(1)} %get-tuple-element.144.key, bf16[2,2048,128]{2,1,0:T(8,128)(2,1)} %get-tuple-element.143.value, ...), custom_call_target="tpu_custom_call" | custom-call | flops 12000000000 | bytes 20000000 | tf_op jit(solution)/shard_map/pallas_call | solution.py:623
  421.5 24.1 %collective-permute-done.27 = bf16[256,2048]{1,0:T(8,128)(2,1)S(1)} collective-permute-done((bf16[256,2048]{1,0:T(8,128)(2,1)S(1)}, bf16[256,2048]{1,0:T(8,128)(2,1)S(1)}, u32[]{:S(2)}, u32[]{:S(2)}) %collective-permute-start.27) | collective-permute-done | bytes 1048608 | tf_op jit(solution)/shard_map/ppermute | solution.py:43
  457.8 23.4 %collective-permute-done.29 = bf16[256,2048]{1,0:T(8,128)(2,1)S(1)} collective-permute-done((bf16[256,2048]{1,0:T(8,128)(2,1)}, bf16[256,2048]{1,0:T(8,128)(2,1)S(1)}, u32[]{:S(2)}, u32[]{:S(2)}) %collective-permute-start.29) | collective-permute-done | bytes 1048608 | tf_op jit(solution)/shard_map/ppermute | solution.py:43
  508.0 49.2 %all-gather.11.cloned.1.call-done = bf16[1024,2048]{1,0:T(8,128)(2,1)} async-done(((bf16[128,2048]{1,0:T(8,128)(2,1)}), bf16[1024,2048]{1,0:T(8,128)(2,1)}) %all-gather.11.cloned.1.call-update) | async-done | bytes 4194320 | tf_op jit(solution)/shard_map/all_gather | solution.py:802
  557.2 13.0 %fusion.4 = (bf16[1024,1024]{1,0:T(8,128)(2,1)S(1)}, bf16[1024,1024]{1,0:T(8,128)(2,1)}) fusion(f32[1024,2048]{1,0:T(8,128)} %copy-done.43, bf16[1024,2048]{1,0:T(8,128)(2,1)} %constant_dynamic-update-slice_fusion.13, bf16[1024,2048]{1,0:T(8,128)(2,1)} %all-gather.11.cloned.1.call-done), kind=kOutput, calls=%fused_computation.15 | convolution fusion | flops 4309647360 | bytes 20971520 | tf_op jit(solution)/shard_map/dot_general | solution.py:71
  570.2 14.7 %fusion.93 = (bf16[1024,2048]{1,0:T(8,128)(2,1)S(1)}, f32[1024,2048]{1,0:T(8,128)}) fusion(bf16[2048,2048]{1,0:T(8,128)(2,1)} %all-gather.9.cloned.1.call-done, bf16[1024,1024]{1,0:T(8,128)(2,1)} %get-tuple-element.130, bf16[1024,1024]{1,0:T(8,128)(2,1)S(1)} %get-tuple-element.129), kind=kOutput, calls=%fused_computation.357 | convolution fusion | flops 8600420352 | bytes 25165824 | tf_op jit(solution)/shard_map/dot_general | solution.py:71
  596.2 13.5 %convolution_convert_fusion = bf16[2048,2048]{1,0:T(8,128)(2,1)} fusion(bf16[1024,1024]{1,0:T(8,128)(2,1)} %get-tuple-element.130, bf16[1024,1024]{1,0:T(8,128)(2,1)S(1)} %copy-done.141, bf16[256,2048]{1,0:T(8,128)(2,1)} %collective-permute-done.30, bf16[256,2048]{1,0:T(8,128)(2,1)S(1)} %copy-done.138, bf16[256,2048]{1,0:T(8,128)(2,1)} %collective-permute-done.28, ...), kind=kOutput, calls=%fused_computation.2 | convolution fusion | flops 8619294720 | bytes 16777216 | tf_op jit(solution)/shard_map/dot_general | solution.py:75
  629.0 23.0 %collective-permute-done.35 = bf16[256,2048]{1,0:T(8,128)(2,1)S(1)} collective-permute-done((bf16[256,2048]{1,0:T(8,128)(2,1)S(1)}, bf16[256,2048]{1,0:T(8,128)(2,1)S(1)}, u32[]{:S(2)}, u32[]{:S(2)}) %collective-permute-start.35) | collective-permute-done | bytes 1048608 | tf_op jit(solution)/shard_map/ppermute | solution.py:43
  727.2 18.8 %shard_map.336 = (f32[2,512,256]{2,1,0:T(8,128)S(1)}, f32[2,2,2048,128]{3,2,1,0:T(8,128)}) custom-call(bf16[2,512,256]{2,1,0:T(8,128)(2,1)S(1)} %convert_element_type.396.query, bf16[2,2048,128]{2,1,0:T(8,128)(2,1)S(1)} %get-tuple-element.144.key, bf16[2,2048,128]{2,1,0:T(8,128)(2,1)} %get-tuple-element.143.value, bf16[2,512,256]{2,1,0:T(8,128)(2,1)S(1)} %bitcast.323, ...), custom_call_target="tpu_custom_call" | custom-call | flops 20000000000 | bytes 30000000 | tf_op jit(solution)/shard_map/pallas_call | solution.py:642
  758.5 21.9 %shard_map.334 = (f32[2,512,1280]{2,1,0:T(8,128)}, f32[2,512,256]{2,1,0:T(8,128)S(1)}, f32[8,128]{1,0:T(8,128)S(1)}) custom-call(f32[2,512,1280]{2,1,0:T(8,128)} %get-tuple-element.69.mixed.c_part, f32[2,512,256]{2,1,0:T(8,128)S(1)} %copy-done.5, f32[2,4,8,128]{3,2,1,0:T(8,128)S(1)} %copy-done.20, f32[2,4,256,768]{3,2,1,0:T(8,128)} %get-tuple-element.72.prefix, ...), custom_call_target="tpu_custom_call" | custom-call | flops 30000001024 | bytes 40000000 | tf_op jit(solution)/shard_map/pallas_call | solution.py:515
  813.8 54.0 %collective-permute-done.45 = bf16[256,768]{1,0:T(8,128)(2,1)S(1)} collective-permute-done((bf16[256,768]{1,0:T(8,128)(2,1)}, bf16[256,768]{1,0:T(8,128)(2,1)S(1)}, u32[]{:S(2)}, u32[]{:S(2)}) %collective-permute-start.45) | collective-permute-done | bytes 393248 | tf_op jit(solution)/shard_map/ppermute | solution.py:920
  885.0 21.6 %shard_map.335 = (bf16[2,512,1408]{2,1,0:T(8,128)(2,1)}, f32[2,8,1280]{2,1,0:T(8,128)S(1)}, f32[8,1280]{1,0:T(8,128)S(1)}, f32[8,128]{1,0:T(8,128)S(1)}) custom-call(f32[2,512,1408]{2,1,0:T(8,128)} %copy-done.61, f32[2,4,8,1280]{3,2,1,0:T(8,128)S(1)} %copy-done.9, f32[2,512,1280]{2,1,0:T(8,128)} %get-tuple-element.69.mixed.c_part, ...), custom_call_target="tpu_custom_call" | custom-call | flops 15000000512 | bytes 50000000 | tf_op jit(solution)/shard_map/pallas_call | solution.py:546
  1003.0 15.8 %collective-permute-done.54 = bf16[256,2048]{1,0:T(8,128)(2,1)} collective-permute-done((bf16[256,2048]{1,0:T(8,128)(2,1)S(1)}, bf16[256,2048]{1,0:T(8,128)(2,1)}, u32[]{:S(2)}, u32[]{:S(2)}) %collective-permute-start.54) | collective-permute-done | bytes 1048608 | tf_op jit(solution)/shard_map/ppermute | solution.py:43
  1021.2 26.2 %all-to-all-done.3 = bf16[4,64,1280]{2,1,0:T(8,128)(2,1)S(1)} async-done(((bf16[4,64,1280]{2,1,0:T(8,128)(2,1)}), bf16[4,64,1280]{2,1,0:T(8,128)(2,1)S(1)}, u32[]{:S(2)}, u32[]{:S(2)}) %all-to-all-start.3) | async-done | bytes 655392 | tf_op jit(solution)/shard_map/all_to_all | solution.py:757
  1077.9 28.0 %collective-permute-done.56 = f32[25232]{0:T(1024)S(1)} collective-permute-done((f32[25232]{0:T(1024)S(1)}, f32[25232]{0:T(1024)S(1)}, u32[]{:S(2)}, u32[]{:S(2)}) %collective-permute-start.56) | collective-permute-done | bytes 100960 | tf_op jit(solution)/shard_map/ppermute | solution.py:56
  (802 shorter events, 599.9 us)
Async XLA Ops:
  7.2 94.5 %all-gather.5.cloned.1.call-start = ((), (), s32[]{:S(2)}) async-start(), calls=%async_computation.10 | async-start | bytes 4718592 | tf_op jit(solution)/shard_map/all_gather | solution.py:802
  67.2 192.1 %all-to-all-start.2 = ((bf16[4,64,2048]{2,1,0:T(8,128)(2,1)}), bf16[4,64,2048]{2,1,0:T(8,128)(2,1)}, u32[]{:S(2)}, u32[]{:S(2)}) async-start(bf16[4,64,2048]{2,1,0:T(8,128)(2,1)} %pad_maximum_fusion.14), calls=%async_computation.2 | async-start | bytes 2097152 | tf_op jit(solution)/shard_map/all_to_all | solution.py:757
  71.5 193.2 %all-gather.7.cloned.1.call-start = ((), (), s32[]{:S(2)}) async-start(), calls=%async_computation.11 | async-start | bytes 5898240 | tf_op jit(solution)/shard_map/all_gather | solution.py:802
  72.2 411.8 %all-gather.9.cloned.1.call-start = ((), (), s32[]{:S(2)}) async-start(), calls=%async_computation.12 | async-start | bytes 9437184 | tf_op jit(solution)/shard_map/all_gather | solution.py:802
  115.4 69.1 %collective-permute-start.17 = (bf16[128,2048]{1,0:T(8,128)(2,1)S(1)}, bf16[128,2048]{1,0:T(8,128)(2,1)S(1)}, u32[]{:S(2)}, u32[]{:S(2)}) collective-permute-start(bf16[128,2048]{1,0:T(8,128)(2,1)S(1)} %pad_maximum_fusion.19), channel_id=1, source_target_pairs={{0,16},{8,24},{16,0},{24,8},{1,17},{9,25},{17,1},{25,9},{2,18},{10... | collective-permute-start | bytes 1572872 | tf_op jit(solution)/shard_map/ppermute | solution.py:889
  115.7 68.8 %collective-permute-start.18 = (bf16[128,2048]{1,0:T(8,128)(2,1)S(1)}, bf16[128,2048]{1,0:T(8,128)(2,1)S(1)}, u32[]{:S(2)}, u32[]{:S(2)}) collective-permute-start(bf16[128,2048]{1,0:T(8,128)(2,1)S(1)} %pad_maximum_fusion.19), channel_id=1, source_target_pairs={{0,8},{8,16},{16,24},{24,0},{1,9},{9,17},{17,25},{25,1},{2,10},{10... | collective-permute-start | bytes 1572872 | tf_op jit(solution)/shard_map/ppermute | solution.py:889
  117.2 72.1 %collective-permute-start.5 = (bf16[2,520,256]{2,1,0:T(8,128)(2,1)S(1)}, bf16[2,520,256]{2,1,0:T(8,128)(2,1)S(1)}, u32[]{:S(2)}, u32[]{:S(2)}) collective-permute-start(bf16[2,520,256]{2,1,0:T(8,128)(2,1)S(1)} %maximum_select_fusion.2), channel_id=1, source_target_pairs={{0,4},{4,0},{1,5},{5,1},{2,6},{6,2},{3,7},{7,3},{8,12},{12,8},{9,1... | collective-permute-start | bytes 1597448 | tf_op jit(solution)/shard_map/ppermute | solution.py:43
  187.4 179.2 %collective-permute-start.19 = (bf16[4,128,2048]{2,1,0:T(8,128)(2,1)}, bf16[4,128,2048]{2,1,0:T(8,128)(2,1)}, u32[]{:S(2)}, u32[]{:S(2)}) collective-permute-start(bf16[4,128,2048]{2,1,0:T(8,128)(2,1)} %constant_dynamic-slice_fusion.4), channel_id=1, source_target_pairs={{0,2},{2,0},{1,3},{3,1},{4,6},{6,4},{5,7},{7,5},{8,10},{10,8},{9,1... | collective-permute-start | bytes 6291464 | tf_op jit(solution)/shard_map/ppermute | solution.py:43
  259.3 297.9 %all-gather.11.cloned.1.call-start = ((), (), s32[]{:S(2)}) async-start(), calls=%async_computation.13 | async-start | bytes 4718592 | tf_op jit(solution)/shard_map/all_gather | solution.py:802
  264.1 111.8 %collective-permute-start.25 = (bf16[256,2048]{1,0:T(8,128)(2,1)}, bf16[256,2048]{1,0:T(8,128)(2,1)}, u32[]{:S(2)}, u32[]{:S(2)}) collective-permute-start(bf16[256,2048]{1,0:T(8,128)(2,1)} %collective-permute-done.24), channel_id=1, source_target_pairs={{0,1},{1,0},{2,3},{3,2},{4,5},{5,4},{6,7},{7,6},{8,9},{9,8},{10,11... | collective-permute-start | bytes 3145736 | tf_op jit(solution)/shard_map/ppermute | solution.py:43
  283.2 95.5 %collective-permute-start.20 = (bf16[2,2,512,128]{3,2,1,0:T(8,128)(2,1)}, bf16[2,2,512,128]{3,2,1,0:T(8,128)(2,1)}, u32[]{:S(2)}, u32[]{:S(2)}) collective-permute-start(bf16[2,2,512,128]{3,2,1,0:T(8,128)(2,1)} %pad_maximum_fusion.18), channel_id=1, source_target_pairs={{0,24},{1,25},{2,26},{3,27},{4,28},{5,29},{6,30},{7,31}} | collective-permute-start | bytes 1572872 | tf_op jit(solution)/shard_map/ppermute | solution.py:48
  287.1 91.6 %collective-permute-start.21 = (bf16[2,2,512,128]{3,2,1,0:T(8,128)(2,1)}, bf16[2,2,512,128]{3,2,1,0:T(8,128)(2,1)}, u32[]{:S(2)}, u32[]{:S(2)}) collective-permute-start(bf16[2,2,512,128]{3,2,1,0:T(8,128)(2,1)} %pad_maximum_fusion.18), channel_id=1, source_target_pairs={{0,16},{8,24},{1,17},{9,25},{2,18},{10,26},{3,19},{11,27},{4,20},{... | collective-permute-start | bytes 1572872 | tf_op jit(solution)/shard_map/ppermute | solution.py:48
  451.8 221.3 %reduce-scatter.5.cloned.1.call-start = ((), (), s32[]{:S(2)}) async-start(), calls=%async_computation.14 | async-start | bytes 4718592 | tf_op jit(solution)/shard_map/reduce_scatter | solution.py:970
  586.6 292.0 %reduce-scatter.7.cloned.1.call-start = ((), (), s32[]{:S(2)}) async-start(), calls=%async_computation.15 | async-start | bytes 9437184 | tf_op jit(solution)/shard_map/reduce_scatter | solution.py:970
  673.1 321.3 %reduce-scatter.9.cloned.1.call-start = ((), (), s32[]{:S(2)}) async-start(), calls=%async_computation.16 | async-start | bytes 5898240 | tf_op jit(solution)/shard_map/reduce_scatter | solution.py:970
  724.3 63.1 %collective-permute-start.40 = (bf16[256,768]{1,0:T(8,128)(2,1)}, bf16[256,768]{1,0:T(8,128)(2,1)}, u32[]{:S(2)}, u32[]{:S(2)}) collective-permute-start(bf16[256,768]{1,0:T(8,128)(2,1)} %get-tuple-element.151), channel_id=1, source_target_pairs={{24,16},{25,17},{26,18},{27,19},{28,20},{29,21},{30,22},{31,23}} | collective-permute-start | bytes 1179656 | tf_op jit(solution)/shard_map/ppermute | solution.py:920
  725.7 63.3 %collective-permute-start.43 = (bf16[256,768]{1,0:T(8,128)(2,1)}, bf16[256,768]{1,0:T(8,128)(2,1)}, u32[]{:S(2)}, u32[]{:S(2)}) collective-permute-start(bf16[256,768]{1,0:T(8,128)(2,1)} %get-tuple-element.152), channel_id=1, source_target_pairs={{24,16},{25,17},{26,18},{27,19},{28,20},{29,21},{30,22},{31,23}} | collective-permute-start | bytes 1179656 | tf_op jit(solution)/shard_map/ppermute | solution.py:920
  787.3 91.4 %collective-permute-start.46 = (bf16[4,128,2048]{2,1,0:T(8,128)(2,1)}, bf16[4,128,2048]{2,1,0:T(8,128)(2,1)}, u32[]{:S(2)}, u32[]{:S(2)}) collective-permute-start(bf16[4,128,2048]{2,1,0:T(8,128)(2,1)} %fusion.33), channel_id=1, source_target_pairs={{0,2},{2,0},{1,3},{3,1},{4,6},{6,4},{5,7},{7,5},{8,10},{10,8},{9,1... | collective-permute-start | bytes 6291464 | tf_op jit(solution)/shard_map/ppermute | solution.py:43
  803.6 64.2 %collective-permute-start.45 = (bf16[256,768]{1,0:T(8,128)(2,1)}, bf16[256,768]{1,0:T(8,128)(2,1)S(1)}, u32[]{:S(2)}, u32[]{:S(2)}) collective-permute-start(bf16[256,768]{1,0:T(8,128)(2,1)} %get-tuple-element.95), channel_id=1, source_target_pairs={{8,0},{9,1},{10,2},{11,3},{12,4},{13,5},{14,6},{15,7}} | collective-permute-start | bytes 1179656 | tf_op jit(solution)/shard_map/ppermute | solution.py:920
  804.9 71.0 %collective-permute-start.42 = (bf16[256,768]{1,0:T(8,128)(2,1)}, bf16[256,768]{1,0:T(8,128)(2,1)}, u32[]{:S(2)}, u32[]{:S(2)}) collective-permute-start(bf16[256,768]{1,0:T(8,128)(2,1)} %get-tuple-element.94), channel_id=1, source_target_pairs={{8,0},{9,1},{10,2},{11,3},{12,4},{13,5},{14,6},{15,7}} | collective-permute-start | bytes 1179656 | tf_op jit(solution)/shard_map/ppermute | solution.py:920
  878.7 258.5 %reduce-scatter.11.cloned.1.call-start = ((), (), s32[]{:S(2)}) async-start(), calls=%async_computation.17 | async-start | bytes 4718592 | tf_op jit(solution)/shard_map/reduce_scatter | solution.py:970
  1047.4 60.2 %all-to-all-start.4 = ((bf16[4,64,2048]{2,1,0:T(8,128)(2,1)}), bf16[4,64,2048]{2,1,0:T(8,128)(2,1)}, u32[]{:S(2)}, u32[]{:S(2)}) async-start(bf16[4,64,2048]{2,1,0:T(8,128)(2,1)} %bitcast.358), calls=%async_computation.8 | async-start | bytes 2097152 | tf_op jit(solution)/shard_map/all_to_all | solution.py:757
  1071.9 57.0 %collective-permute-start.60 = (bf16[128,2048]{1,0:T(8,128)(2,1)}, bf16[128,2048]{1,0:T(8,128)(2,1)}, u32[]{:S(2)}, u32[]{:S(2)}) collective-permute-start(bf16[128,2048]{1,0:T(8,128)(2,1)} %get-tuple-element.137), channel_id=1, source_target_pairs={{0,8},{8,16},{16,24},{24,0},{1,9},{9,17},{17,25},{25,1},{2,10},{10... | collective-permute-start | bytes 1572872 | tf_op jit(solution)/shard_map/ppermute | solution.py:889
  1071.9 57.0 %collective-permute-start.61 = (bf16[128,2048]{1,0:T(8,128)(2,1)}, bf16[128,2048]{1,0:T(8,128)(2,1)}, u32[]{:S(2)}, u32[]{:S(2)}) collective-permute-start(bf16[128,2048]{1,0:T(8,128)(2,1)} %get-tuple-element.136), channel_id=1, source_target_pairs={{0,16},{8,24},{16,0},{24,8},{1,17},{9,25},{17,1},{25,9},{2,18},{10... | collective-permute-start | bytes 1572872 | tf_op jit(solution)/shard_map/ppermute | solution.py:889
  (204 other events, 3776.3 us)
Sparse Core Ops, SparseCore 0:
  24.8 76.8 all-gather.4
  104.5 146.1 all-gather.6
  259.4 158.6 all-gather.8
  451.9 105.2 all-gather.10
  586.7 86.3 reduce-scatter.4
  677.0 188.0 reduce-scatter.6
  878.7 100.5 reduce-scatter.8
  994.6 113.3 reduce-scatter.10

commit v9 on v7

--- a/solution.py
+++ b/solution.py
@@ -888,8 +888,37 @@
     def turned(array, distance):
         return lax.ppermute(array, "z", [(i, (i + distance) % nz) for i in range(nz)])
 
+    def chained(local, step, pin=None):
+        entering = []
+        for s in range(2):
+            held = jnp.zeros(local.shape[1:], f32)
+            for hop in range(nz - 1):
+                at = hop if step == 1 else nz - 1 - hop
+                leaving = local[s] + own_decay[s][None] * held if hop else local[s]
+                if pin is not None and hop == nz - 2:
+                    leaving = after(leaving, pin)
+                held = held + lax.ppermute(
+                    leaving.astype(bf16), "z", [(at, at + step)]
+                ).astype(f32)
+            entering.append(held)
+        return jnp.stack(entering)
+
+    packed_ff = jnp.concatenate([split_ff(w_gate), split_ff(w_up)], axis=2)
+    rest = low_dot(normed_rows, full_rest).reshape(2, span_all, REST_COLS)
+
+    positions = zi * span_all + jnp.arange(span_all, dtype=jnp.int32)
+    cosine, sine = rope_tables(positions)
+    query16 = (
+        rotate(rest[..., AT_Q:AT_K].reshape(2, span_all, 2, HEAD_DIM), cosine, sine)
+        .astype(bf16)
+        .reshape(2, span_all, QP)
+    )
+    key16 = rotate(rest[..., None, AT_K:AT_V], cosine, sine).astype(bf16)[:, :, 0]
+    kv16 = jnp.stack([key16, rest[..., AT_V:].astype(bf16)])
+    state_in = chained(own_state, 1, kv16)
+    kv_before = [shifted(kv16, d) for d in range(nz - 1, 0, -1)]
     if aligned:
-        first_rows = after(sent_rows, full_scan)
+        first_rows = after(sent_rows, kv_before[-1])
         along_z = jnp.stack([turned(first_rows, d) for d in range(nz - 1, 0, -1)] + [first_rows])
         along_z = lax.dynamic_slice_in_dim(
             jnp.concatenate([along_z, along_z], 0), nz - 1 - zi, nz, 0
@@ -908,35 +937,6 @@
         every_o = lax.dynamic_index_in_dim(every_o, xi, 2, keepdims=False)
         full_o = lax.dynamic_index_in_dim(every_o, ci, 0, keepdims=False).reshape(QP, D)
 
-    def chained(local, step, pin=None):
-        entering = []
-        for s in range(2):
-            held = jnp.zeros(local.shape[1:], f32)
-            for hop in range(nz - 1):
-                at = hop if step == 1 else nz - 1 - hop
-                leaving = local[s] + own_decay[s][None] * held if hop else local[s]
-                if pin is not None and hop == nz - 2:
-                    leaving = after(leaving, pin)
-                held = held + lax.ppermute(
-                    leaving.astype(bf16), "z", [(at, at + step)]
-                ).astype(f32)
-            entering.append(held)
-        return jnp.stack(entering)
-
-    packed_ff = jnp.concatenate([split_ff(w_gate), split_ff(w_up)], axis=2)
-    rest = low_dot(normed_rows, full_rest).reshape(2, span_all, REST_COLS)
-
-    positions = zi * span_all + jnp.arange(span_all, dtype=jnp.int32)
-    cosine, sine = rope_tables(positions)
-    query16 = (
-        rotate(rest[..., AT_Q:AT_K].reshape(2, span_all, 2, HEAD_DIM), cosine, sine)
-        .astype(bf16)
-        .reshape(2, span_all, QP)
-    )
-    key16 = rotate(rest[..., None, AT_K:AT_V], cosine, sine).astype(bf16)[:, :, 0]
-    kv16 = jnp.stack([key16, rest[..., AT_V:].astype(bf16)])
-    state_in = chained(own_state, 1, kv16)
-    kv_before = [shifted(kv16, d) for d in range(nz - 1, 0, -1)]
     keys_at = (zi - nz + 1) * span_all + jnp.arange(nz * span_all, dtype=jnp.int32)
     query_place = jnp.broadcast_to(positions[:, None], (span_all, 128))
     key_place = jnp.broadcast_to(keys_at[None], (8, nz * span_all))
@@ -957,7 +957,7 @@
 
     middle, mid_back = jax.vjp(rms_scale, hidden_state, mid_gain)
     middle16 = jnp.concatenate(gather_tokens(permuted(middle.astype(bf16))), 0)
-    full_down = gathered(after(w_down, hidden_state))
+    full_down = gathered(after(w_down, flat, attended))
     both = low_dot(middle16, full_ff)
     activated, swish_back = jax.vjp(
         swish_product, both[:, :hidden_part], both[:, hidden_part:]

time: 1140 us -> 1160 us (1.018)
  waiting for transfers between devices: 442 us -> 476 us
  local copies, waits for them, and re-layouts: 143 us -> 129 us
    ppermute x30, waiting for transfers between devices: 145 us -> 217 us  [swap(): return lax.ppermute(array, axis, [(0, 1), (1, 0)])]
    all_gather x4, waiting for transfers between devices: 46.3 us -> 11.8 us  [gathered(): return lax.all_gather(array, SHARDS, axis=0, tiled=True)]
    ppermute x8, starting transfers between devices: 65.3 us -> 35.7 us  [shifted(): lax.ppermute(array, 'z', [(i - distance, i) for i in devices if i - dista...]
    ppermute x6, waiting for transfers between devices: 129 us -> 101 us  [turned(): lax.ppermute(array, 'z', [(i, (i + distance) % nz) for i in range(nz)])]
    ppermute x6, starting transfers between devices: 8.21 us -> 26.6 us  [turned(): lax.ppermute(array, 'z', [(i, (i + distance) % nz) for i in range(nz)])]
    ppermute x12, waiting for transfers between devices: 77.5 us -> 92.4 us  [chained(): lax.ppermute(leaving.astype(bf16), 'z', [(at, at + step)]).astype(f32)]
    unnamed x351 -> x339, local copies, waits for them, and re-layouts: 49.4 us -> 39.1 us
  transfers between devices with their start and end apart: 78 -> 78, of which waited for: 30 -> 34; matrix products, arithmetic and copies ran while one was open for 30% -> 28% of each run, Pallas kernels for 10% -> 10%
where the time goes in v9:
time: 1160 us; the launch traced here: 1150 us
  waiting for transfers between devices  476 us (41%)
  matrix products  146 us (13%)
  starting transfers between devices  136 us (12%)
  local copies, waits for them, and re-layouts  129 us (11%)
  other arithmetic  116 us (10%)
  Pallas kernels  113 us (10%)
  between operations  17.8 us (2%)
  blocking collectives  13 us (1%)
    ppermute x30, waiting for transfers between devices, swap(): return lax.ppermute(array, axis, [(0, 1), (1, 0)])  217 us
    ppermute x6, waiting for transfers between devices, turned(): lax.ppermute(array, 'z', [(i, (i + distance) % nz) for i in range(nz)])  101 us
    ppermute x12, waiting for transfers between devices, chained(): lax.ppermute(leaving.astype(bf16), 'z', [(at, at + step)]).astype(f32)  92.4 us
    dot_general x6, matrix products, back_dot(): lax.dot_general(grad_rows, weight, (((1,), (1,)), ((), ())), preferred_el...  57.3 us
    dot_general x7, matrix products, low_dot(): return jnp.dot(left, right, preferred_element_type=f32)  44.6 us
    dot_general x6, matrix products, weight_grad(): lax.dot_general(left, right, (((0,), (0,)), ((), ())), preferred_element_...  43.7 us
    unnamed x339, local copies, waits for them, and re-layouts  39.1 us
    ppermute x8, starting transfers between devices, shifted(): lax.ppermute(array, 'z', [(i - distance, i) for i in devices if i - dista...  35.7 us
  transfers between devices with their start and end apart: 78, of which 34 were waited for; matrix products, arithmetic and copies ran while one was open for 28% of the time, Pallas kernels for 10%

profile of v9, /device:TPU:0, one launch (start us, length us, event | category | flops | bytes accessed | tf_op | source)
XLA Modules:
  0.0 1146.4 jit_solution(3608772077183376957)
XLA Ops:
  11.7 13.0 %all_to_all.30 = bf16[4,64,1024]{2,1,0:T(8,128)(2,1)} all-to-all(bf16[4,64,1024]{2,1,0:T(8,128)(2,1)S(1)} %fusion.61), channel_id=1, replica_groups=mesh['z'=4,'x'=2,'y'=2,'c'=2] {'x','c'}, dimensions={0} | all-to-all | bytes 1048576 | tf_op jit(solution)/shard_map/all_to_all | solution.py:757
  43.6 24.8 %collective-permute-done = bf16[256,2048]{1,0:T(8,128)(2,1)} collective-permute-done((bf16[256,2048]{1,0:T(8,128)(2,1)}, bf16[256,2048]{1,0:T(8,128)(2,1)}, u32[]{:S(2)}, u32[]{:S(2)}) %collective-permute-start) | collective-permute-done | bytes 1048608 | tf_op jit(solution)/shard_map/ppermute | solution.py:43
  129.9 14.0 %shard_map.330 = (f32[2,512,1280]{2,1,0:T(8,128)}, f32[2,512,256]{2,1,0:T(8,128)S(1)}, f32[2,4,8,128]{3,2,1,0:T(8,128)S(1)}, f32[2,4,256,768]{3,2,1,0:T(8,128)}, f32[2,256,768]{2,1,0:T(8,128)S(1)}) custom-call(f32[2,512,1408]{2,1,0:T(8,128)} %copy-done.63, f32[2,4,8,1280]{3,2,1,0:T(8,128)S(1)} %pad_maximum_fusion.23.before, ...), custom_call_target="tpu_custom_call" | custom-call | flops 8000000000 | bytes 30000000 | tf_op jit(solution)/shard_map/pallas_call | solution.py:430
  153.3 14.9 %collective-permute-done.6 = bf16[256,768]{1,0:T(8,128)(2,1)S(1)} collective-permute-done((bf16[256,768]{1,0:T(8,128)(2,1)}, bf16[256,768]{1,0:T(8,128)(2,1)S(1)}, u32[]{:S(2)}, u32[]{:S(2)}) %collective-permute-start.6) | collective-permute-done | bytes 393248 | tf_op jit(solution)/shard_map/ppermute | solution.py:900
  168.3 16.3 %collective-permute-done.9 = bf16[256,768]{1,0:T(8,128)(2,1)} collective-permute-done((bf16[256,768]{1,0:T(8,128)(2,1)}, bf16[256,768]{1,0:T(8,128)(2,1)}, u32[]{:S(2)}, u32[]{:S(2)}) %collective-permute-start.9) | collective-permute-done | bytes 393248 | tf_op jit(solution)/shard_map/ppermute | solution.py:900
  221.1 18.1 %collective-permute-start.16 = (bf16[2,2,512,128]{3,2,1,0:T(8,128)(2,1)}, bf16[2,2,512,128]{3,2,1,0:T(8,128)(2,1)}, u32[]{:S(2)}, u32[]{:S(2)}) collective-permute-start(bf16[2,2,512,128]{3,2,1,0:T(8,128)(2,1)} %pad_maximum_fusion.19), channel_id=1, source_target_pairs={{0,8},{8,16},{16,24},{1,9},{9,17},{17,25},{2,10},{10,18},{18,26},{... | collective-permute-start | bytes 1572872 | tf_op jit(solution)/shard_map/ppermute | solution.py:48
  268.6 22.5 %collective-permute-start.17 = (bf16[128,2048]{1,0:T(8,128)(2,1)}, bf16[128,2048]{1,0:T(8,128)(2,1)S(1)}, u32[]{:S(2)}, u32[]{:S(2)}) collective-permute-start(bf16[128,2048]{1,0:T(8,128)(2,1)} %pad_maximum_fusion.20), channel_id=1, source_target_pairs={{0,24},{8,0},{16,8},{24,16},{1,25},{9,1},{17,9},{25,17},{2,26},{10... | collective-permute-start | bytes 1572872 | tf_op jit(solution)/shard_map/ppermute | solution.py:889
  300.0 18.6 %collective-permute-done.17 = bf16[128,2048]{1,0:T(8,128)(2,1)S(1)} collective-permute-done((bf16[128,2048]{1,0:T(8,128)(2,1)}, bf16[128,2048]{1,0:T(8,128)(2,1)S(1)}, u32[]{:S(2)}, u32[]{:S(2)}) %collective-permute-start.17) | collective-permute-done | bytes 524320 | tf_op jit(solution)/shard_map/ppermute | solution.py:889
  318.5 20.7 %collective-permute-done.18 = bf16[128,2048]{1,0:T(8,128)(2,1)S(1)} collective-permute-done((bf16[128,2048]{1,0:T(8,128)(2,1)}, bf16[128,2048]{1,0:T(8,128)(2,1)S(1)}, u32[]{:S(2)}, u32[]{:S(2)}) %collective-permute-start.18) | collective-permute-done | bytes 524320 | tf_op jit(solution)/shard_map/ppermute | solution.py:889
  348.1 12.9 %shard_map.332 = (f32[2,512,256]{2,1,0:T(8,128)S(1)}, f32[2,512,256]{2,1,0:T(8,128)S(1)}) custom-call(bf16[2,512,256]{2,1,0:T(8,128)(2,1)S(1)} %convert_element_type.396.query, bf16[2,2048,128]{2,1,0:T(8,128)(2,1)S(1)} %get-tuple-element.132.key, bf16[2,2048,128]{2,1,0:T(8,128)(2,1)} %get-tuple-element.131.value, ...), custom_call_target="tpu_custom_call" | custom-call | flops 12000000000 | bytes 20000000 | tf_op jit(solution)/shard_map/pallas_call | solution.py:623
  362.4 67.5 %collective-permute-done.20 = bf16[4,128,2048]{2,1,0:T(8,128)(2,1)} collective-permute-done((bf16[4,128,2048]{2,1,0:T(8,128)(2,1)}, bf16[4,128,2048]{2,1,0:T(8,128)(2,1)}, u32[]{:S(2)}, u32[]{:S(2)}) %collective-permute-start.20) | collective-permute-done | bytes 2097184 | tf_op jit(solution)/shard_map/ppermute | solution.py:43
  456.8 23.8 %collective-permute-done.24 = bf16[256,2048]{1,0:T(8,128)(2,1)} collective-permute-done((bf16[256,2048]{1,0:T(8,128)(2,1)S(1)}, bf16[256,2048]{1,0:T(8,128)(2,1)}, u32[]{:S(2)}, u32[]{:S(2)}) %collective-permute-start.24) | collective-permute-done | bytes 1048608 | tf_op jit(solution)/shard_map/ppermute | solution.py:43
  485.4 23.1 %collective-permute-done.26 = bf16[256,2048]{1,0:T(8,128)(2,1)S(1)} collective-permute-done((bf16[256,2048]{1,0:T(8,128)(2,1)S(1)}, bf16[256,2048]{1,0:T(8,128)(2,1)S(1)}, u32[]{:S(2)}, u32[]{:S(2)}) %collective-permute-start.26) | collective-permute-done | bytes 1048608 | tf_op jit(solution)/shard_map/ppermute | solution.py:43
  511.3 12.7 %fusion.60 = f32[1024,2048]{1,0:T(8,128)S(1)} fusion(bf16[2048,2048]{1,0:T(8,128)(2,1)} %all-gather.9.cloned.1.call-done, bf16[256,2048]{1,0:T(8,128)(2,1)} %collective-permute-done.27, bf16[256,2048]{1,0:T(8,128)(2,1)} %copy-done.135, bf16[256,2048]{1,0:T(8,128)(2,1)} %copy-done.137, bf16[256,2048]{1,0:T(8,128)(2,1)} %copy-done.130), kind=kOutput, calls=%fused_computation.173 | convolution fusion | flops 8606711808 | bytes 20971520 | tf_op jit(solution)/shard_map/dot_general | solution.py:67
  544.3 13.0 %fusion.4 = (bf16[1024,1024]{1,0:T(8,128)(2,1)S(1)}, bf16[1024,1024]{1,0:T(8,128)(2,1)}) fusion(f32[1024,2048]{1,0:T(8,128)} %copy-done.47, bf16[1024,2048]{1,0:T(8,128)(2,1)} %pad_maximum_fusion.3, bf16[1024,2048]{1,0:T(8,128)(2,1)} %all-gather.11.cloned.1.call-done), kind=kOutput, calls=%fused_computation.15 | convolution fusion | flops 4309647360 | bytes 20971520 | tf_op jit(solution)/shard_map/dot_general | solution.py:71
  557.3 14.7 %fusion.93 = (bf16[1024,2048]{1,0:T(8,128)(2,1)S(1)}, f32[1024,2048]{1,0:T(8,128)}) fusion(bf16[2048,2048]{1,0:T(8,128)(2,1)} %all-gather.9.cloned.1.call-done, bf16[1024,1024]{1,0:T(8,128)(2,1)} %get-tuple-element.118, bf16[1024,1024]{1,0:T(8,128)(2,1)S(1)} %get-tuple-element.117), kind=kOutput, calls=%fused_computation.354 | convolution fusion | flops 8600420352 | bytes 25165824 | tf_op jit(solution)/shard_map/dot_general | solution.py:71
  582.7 13.8 %convolution_convert_fusion = bf16[2048,2048]{1,0:T(8,128)(2,1)} fusion(bf16[1024,1024]{1,0:T(8,128)(2,1)} %get-tuple-element.118, bf16[1024,1024]{1,0:T(8,128)(2,1)} %copy-done.140, bf16[256,2048]{1,0:T(8,128)(2,1)} %collective-permute-done.27, bf16[256,2048]{1,0:T(8,128)(2,1)S(1)} %copy-done.136, bf16[256,2048]{1,0:T(8,128)(2,1)S(1)} %copy-done.138, ...), kind=kOutput, calls=%fused_computation.2 | convolution fusion | flops 8619294720 | bytes 16777216 | tf_op jit(solution)/shard_map/dot_general | solution.py:75
  614.7 22.9 %collective-permute-done.35 = bf16[256,2048]{1,0:T(8,128)(2,1)S(1)} collective-permute-done((bf16[256,2048]{1,0:T(8,128)(2,1)S(1)}, bf16[256,2048]{1,0:T(8,128)(2,1)S(1)}, u32[]{:S(2)}, u32[]{:S(2)}) %collective-permute-start.35) | collective-permute-done | bytes 1048608 | tf_op jit(solution)/shard_map/ppermute | solution.py:43
  646.7 23.1 %reduce-scatter.5.cloned.1.call-done = bf16[128,2048]{1,0:T(8,128)(2,1)} async-done(((bf16[1024,2048]{1,0:T(8,128)(2,1)}), bf16[128,2048]{1,0:T(8,128)(2,1)}) %reduce-scatter.5.cloned.1.call-update) | async-done | bytes 524304 | tf_op jit(solution)/shard_map/reduce_scatter | solution.py:970
  723.9 18.8 %shard_map.336 = (f32[2,512,256]{2,1,0:T(8,128)S(1)}, f32[2,2,2048,128]{3,2,1,0:T(8,128)}) custom-call(bf16[2,512,256]{2,1,0:T(8,128)(2,1)S(1)} %copy-done.11, bf16[2,2048,128]{2,1,0:T(8,128)(2,1)S(1)} %copy-done.9, bf16[2,2048,128]{2,1,0:T(8,128)(2,1)} %get-tuple-element.131.value, bf16[2,512,256]{2,1,0:T(8,128)(2,1)S(1)} %bitcast.322, ...), custom_call_target="tpu_custom_call" | custom-call | flops 20000000000 | bytes 30000000 | tf_op jit(solution)/shard_map/pallas_call | solution.py:642
  755.2 21.9 %shard_map.334 = (f32[2,512,1280]{2,1,0:T(8,128)}, f32[2,512,256]{2,1,0:T(8,128)S(1)}, f32[8,128]{1,0:T(8,128)S(1)}) custom-call(f32[2,512,1280]{2,1,0:T(8,128)} %get-tuple-element.63.mixed.c_part, f32[2,512,256]{2,1,0:T(8,128)S(1)} %copy-done.5, f32[2,4,8,128]{3,2,1,0:T(8,128)S(1)} %copy-done.27, f32[2,4,256,768]{3,2,1,0:T(8,128)} %get-tuple-element.66.prefix, ...), custom_call_target="tpu_custom_call" | custom-call | flops 30000001024 | bytes 40000000 | tf_op jit(solution)/shard_map/pallas_call | solution.py:515
  810.5 54.1 %collective-permute-done.45 = bf16[256,768]{1,0:T(8,128)(2,1)S(1)} collective-permute-done((bf16[256,768]{1,0:T(8,128)(2,1)}, bf16[256,768]{1,0:T(8,128)(2,1)S(1)}, u32[]{:S(2)}, u32[]{:S(2)}) %collective-permute-start.45) | collective-permute-done | bytes 393248 | tf_op jit(solution)/shard_map/ppermute | solution.py:900
  881.8 21.7 %shard_map.335 = (bf16[2,512,1408]{2,1,0:T(8,128)(2,1)}, f32[2,8,1280]{2,1,0:T(8,128)S(1)}, f32[8,1280]{1,0:T(8,128)S(1)}, f32[8,128]{1,0:T(8,128)S(1)}) custom-call(f32[2,512,1408]{2,1,0:T(8,128)} %copy-done.63, f32[2,4,8,1280]{3,2,1,0:T(8,128)S(1)} %copy-done.13, f32[2,512,1280]{2,1,0:T(8,128)} %get-tuple-element.63.mixed.c_part, ...), custom_call_target="tpu_custom_call" | custom-call | flops 15000000512 | bytes 50000000 | tf_op jit(solution)/shard_map/pallas_call | solution.py:546
  990.6 61.8 %collective-permute-done.61 = bf16[128,2048]{1,0:T(8,128)(2,1)} collective-permute-done((bf16[128,2048]{1,0:T(8,128)(2,1)}, bf16[128,2048]{1,0:T(8,128)(2,1)}, u32[]{:S(2)}, u32[]{:S(2)}) %collective-permute-start.61) | collective-permute-done | bytes 524320 | tf_op jit(solution)/shard_map/ppermute | solution.py:889
  (797 shorter events, 559.9 us)
Async XLA Ops:
  7.2 92.2 %all-gather.5.cloned.1.call-start = ((), (), s32[]{:S(2)}) async-start(), calls=%async_computation.10 | async-start | bytes 4718592 | tf_op jit(solution)/shard_map/all_gather | solution.py:802
  30.8 169.3 %all-gather.7.cloned.1.call-start = ((), (), s32[]{:S(2)}) async-start(), calls=%async_computation.11 | async-start | bytes 5898240 | tf_op jit(solution)/shard_map/all_gather | solution.py:802
  68.3 124.5 %collective-permute-start.29 = (bf16[256,2048]{1,0:T(8,128)(2,1)}, bf16[256,2048]{1,0:T(8,128)(2,1)}, u32[]{:S(2)}, u32[]{:S(2)}) collective-permute-start(bf16[256,2048]{1,0:T(8,128)(2,1)} %bitcast.52), channel_id=1, source_target_pairs={{0,4},{4,0},{1,5},{5,1},{2,6},{6,2},{3,7},{7,3},{8,12},{12,8},{9,1... | collective-permute-start | bytes 3145736 | tf_op jit(solution)/shard_map/ppermute | solution.py:43
  68.9 148.3 %collective-permute-start.28 = (bf16[256,2048]{1,0:T(8,128)(2,1)}, bf16[256,2048]{1,0:T(8,128)(2,1)}, u32[]{:S(2)}, u32[]{:S(2)}) collective-permute-start(bf16[256,2048]{1,0:T(8,128)(2,1)} %bitcast.52), channel_id=1, source_target_pairs={{0,1},{1,0},{2,3},{3,2},{4,5},{5,4},{6,7},{7,6},{8,9},{9,8},{10,11... | collective-permute-start | bytes 3145736 | tf_op jit(solution)/shard_map/ppermute | solution.py:43
  69.2 144.8 %collective-permute-start.15 = (bf16[32,2048]{1,0:T(8,128)(2,1)}, bf16[32,2048]{1,0:T(8,128)(2,1)}, u32[]{:S(2)}, u32[]{:S(2)}) collective-permute-start(bf16[32,2048]{1,0:T(8,128)(2,1)} %param.33), channel_id=1, source_target_pairs={{0,0},{1,2},{2,8},{3,10},{8,16},{9,18},{10,24},{11,26},{16,1},{17,... | collective-permute-start | bytes 393224 | tf_op jit(solution)/shard_map/ppermute | solution.py:834
  75.5 145.5 %all-to-all-start.2 = ((bf16[4,64,2048]{2,1,0:T(8,128)(2,1)}), bf16[4,64,2048]{2,1,0:T(8,128)(2,1)}, u32[]{:S(2)}, u32[]{:S(2)}) async-start(bf16[4,64,2048]{2,1,0:T(8,128)(2,1)} %pad_maximum_fusion.15), calls=%async_computation.2 | async-start | bytes 2097152 | tf_op jit(solution)/shard_map/all_to_all | solution.py:757
  79.8 431.5 %all-gather.9.cloned.1.call-start = ((), (), s32[]{:S(2)}) async-start(), calls=%async_computation.12 | async-start | bytes 9437184 | tf_op jit(solution)/shard_map/all_gather | solution.py:802
  221.0 323.3 %all-gather.11.cloned.1.call-start = ((), (), s32[]{:S(2)}) async-start(), calls=%async_computation.13 | async-start | bytes 4718592 | tf_op jit(solution)/shard_map/all_gather | solution.py:802
  241.5 55.8 %collective-permute-start.21 = (bf16[2,2,512,128]{3,2,1,0:T(8,128)(2,1)}, bf16[2,2,512,128]{3,2,1,0:T(8,128)(2,1)}, u32[]{:S(2)}, u32[]{:S(2)}) collective-permute-start(bf16[2,2,512,128]{3,2,1,0:T(8,128)(2,1)} %pad_maximum_fusion.19), channel_id=1, source_target_pairs={{0,24},{1,25},{2,26},{3,27},{4,28},{5,29},{6,30},{7,31}} | collective-permute-start | bytes 1572872 | tf_op jit(solution)/shard_map/ppermute | solution.py:48
  243.6 56.4 %collective-permute-start.22 = (bf16[2,2,512,128]{3,2,1,0:T(8,128)(2,1)}, bf16[2,2,512,128]{3,2,1,0:T(8,128)(2,1)}, u32[]{:S(2)}, u32[]{:S(2)}) collective-permute-start(bf16[2,2,512,128]{3,2,1,0:T(8,128)(2,1)} %pad_maximum_fusion.19), channel_id=1, source_target_pairs={{0,16},{8,24},{1,17},{9,25},{2,18},{10,26},{3,19},{11,27},{4,20},{... | collective-permute-start | bytes 1572872 | tf_op jit(solution)/shard_map/ppermute | solution.py:48
  343.6 86.3 %collective-permute-start.20 = (bf16[4,128,2048]{2,1,0:T(8,128)(2,1)}, bf16[4,128,2048]{2,1,0:T(8,128)(2,1)}, u32[]{:S(2)}, u32[]{:S(2)}) collective-permute-start(bf16[4,128,2048]{2,1,0:T(8,128)(2,1)} %constant_dynamic-slice_fusion.4), channel_id=1, source_target_pairs={{0,2},{2,0},{1,3},{3,1},{4,6},{6,4},{5,7},{7,5},{8,10},{10,8},{9,1... | collective-permute-start | bytes 6291464 | tf_op jit(solution)/shard_map/ppermute | solution.py:43
  456.7 213.1 %reduce-scatter.5.cloned.1.call-start = ((), (), s32[]{:S(2)}) async-start(), calls=%async_computation.14 | async-start | bytes 4718592 | tf_op jit(solution)/shard_map/reduce_scatter | solution.py:970
  573.6 301.8 %reduce-scatter.7.cloned.1.call-start = ((), (), s32[]{:S(2)}) async-start(), calls=%async_computation.15 | async-start | bytes 9437184 | tf_op jit(solution)/shard_map/reduce_scatter | solution.py:970
  669.8 316.4 %reduce-scatter.9.cloned.1.call-start = ((), (), s32[]{:S(2)}) async-start(), calls=%async_computation.16 | async-start | bytes 5898240 | tf_op jit(solution)/shard_map/reduce_scatter | solution.py:970
  721.0 63.1 %collective-permute-start.40 = (bf16[256,768]{1,0:T(8,128)(2,1)}, bf16[256,768]{1,0:T(8,128)(2,1)}, u32[]{:S(2)}, u32[]{:S(2)}) collective-permute-start(bf16[256,768]{1,0:T(8,128)(2,1)} %get-tuple-element.139), channel_id=1, source_target_pairs={{24,16},{25,17},{26,18},{27,19},{28,20},{29,21},{30,22},{31,23}} | collective-permute-start | bytes 1179656 | tf_op jit(solution)/shard_map/ppermute | solution.py:900
  722.4 63.2 %collective-permute-start.43 = (bf16[256,768]{1,0:T(8,128)(2,1)}, bf16[256,768]{1,0:T(8,128)(2,1)}, u32[]{:S(2)}, u32[]{:S(2)}) collective-permute-start(bf16[256,768]{1,0:T(8,128)(2,1)} %get-tuple-element.140), channel_id=1, source_target_pairs={{24,16},{25,17},{26,18},{27,19},{28,20},{29,21},{30,22},{31,23}} | collective-permute-start | bytes 1179656 | tf_op jit(solution)/shard_map/ppermute | solution.py:900
  784.1 91.5 %collective-permute-start.46 = (bf16[4,128,2048]{2,1,0:T(8,128)(2,1)}, bf16[4,128,2048]{2,1,0:T(8,128)(2,1)}, u32[]{:S(2)}, u32[]{:S(2)}) collective-permute-start(bf16[4,128,2048]{2,1,0:T(8,128)(2,1)} %fusion.33), channel_id=1, source_target_pairs={{0,2},{2,0},{1,3},{3,1},{4,6},{6,4},{5,7},{7,5},{8,10},{10,8},{9,1... | collective-permute-start | bytes 6291464 | tf_op jit(solution)/shard_map/ppermute | solution.py:43
  800.3 64.3 %collective-permute-start.45 = (bf16[256,768]{1,0:T(8,128)(2,1)}, bf16[256,768]{1,0:T(8,128)(2,1)S(1)}, u32[]{:S(2)}, u32[]{:S(2)}) collective-permute-start(bf16[256,768]{1,0:T(8,128)(2,1)} %get-tuple-element.88), channel_id=1, source_target_pairs={{8,0},{9,1},{10,2},{11,3},{12,4},{13,5},{14,6},{15,7}} | collective-permute-start | bytes 1179656 | tf_op jit(solution)/shard_map/ppermute | solution.py:900
  801.6 71.2 %collective-permute-start.42 = (bf16[256,768]{1,0:T(8,128)(2,1)}, bf16[256,768]{1,0:T(8,128)(2,1)}, u32[]{:S(2)}, u32[]{:S(2)}) collective-permute-start(bf16[256,768]{1,0:T(8,128)(2,1)} %get-tuple-element.87), channel_id=1, source_target_pairs={{8,0},{9,1},{10,2},{11,3},{12,4},{13,5},{14,6},{15,7}} | collective-permute-start | bytes 1179656 | tf_op jit(solution)/shard_map/ppermute | solution.py:900
  875.5 246.6 %reduce-scatter.11.cloned.1.call-start = ((), (), s32[]{:S(2)}) async-start(), calls=%async_computation.17 | async-start | bytes 4718592 | tf_op jit(solution)/shard_map/reduce_scatter | solution.py:970
  969.4 138.3 %collective-permute-start.32 = (bf16[256,2048]{1,0:T(8,128)(2,1)}, bf16[256,2048]{1,0:T(8,128)(2,1)}, u32[]{:S(2)}, u32[]{:S(2)}) collective-permute-start(bf16[256,2048]{1,0:T(8,128)(2,1)} %fusion.38), channel_id=1, source_target_pairs={{0,4},{4,0},{1,5},{5,1},{2,6},{6,2},{3,7},{7,3},{8,12},{12,8},{9,1... | collective-permute-start | bytes 3145736 | tf_op jit(solution)/shard_map/ppermute | solution.py:43
  973.9 78.5 %collective-permute-start.61 = (bf16[128,2048]{1,0:T(8,128)(2,1)}, bf16[128,2048]{1,0:T(8,128)(2,1)}, u32[]{:S(2)}, u32[]{:S(2)}) collective-permute-start(bf16[128,2048]{1,0:T(8,128)(2,1)} %get-tuple-element.125), channel_id=1, source_target_pairs={{0,16},{8,24},{16,0},{24,8},{1,17},{9,25},{17,1},{25,9},{2,18},{10... | collective-permute-start | bytes 1572872 | tf_op jit(solution)/shard_map/ppermute | solution.py:889
  977.7 74.7 %collective-permute-start.60 = (bf16[128,2048]{1,0:T(8,128)(2,1)}, bf16[128,2048]{1,0:T(8,128)(2,1)}, u32[]{:S(2)}, u32[]{:S(2)}) collective-permute-start(bf16[128,2048]{1,0:T(8,128)(2,1)} %get-tuple-element.123), channel_id=1, source_target_pairs={{0,8},{8,16},{16,24},{24,0},{1,9},{9,17},{17,25},{25,1},{2,10},{10... | collective-permute-start | bytes 1572872 | tf_op jit(solution)/shard_map/ppermute | solution.py:889
  989.9 74.5 %collective-permute-start.54 = (bf16[256,2048]{1,0:T(8,128)(2,1)S(1)}, bf16[256,2048]{1,0:T(8,128)(2,1)}, u32[]{:S(2)}, u32[]{:S(2)}) collective-permute-start(bf16[256,2048]{1,0:T(8,128)(2,1)S(1)} %fusion.44), channel_id=1, source_target_pairs={{0,4},{4,0},{1,5},{5,1},{2,6},{6,2},{3,7},{7,3},{8,12},{12,8},{9,1... | collective-permute-start | bytes 3145736 | tf_op jit(solution)/shard_map/ppermute | solution.py:43
  (202 other events, 3754.7 us)
Sparse Core Ops, SparseCore 0:
  24.8 74.5 all-gather.4
  102.2 97.8 all-gather.6
  221.1 237.2 all-gather.8
  460.4 83.8 all-gather.10
  573.8 96.0 reduce-scatter.4
  673.7 188.2 reduce-scatter.6
  875.5 100.3 reduce-scatter.8
  986.4 114.9 reduce-scatter.10
